TPU v7x, 32 devices: a whole 2x2x4 slice. The times are simulated.
32 devices in a mesh: wide: 8 (over y, x, core), narrow: 4 (over z).
Axes of the slice: x: 2, y: 2, z: 4, core: 2. Of those that a mesh axis runs over, the one named last changes fastest.
Arguments:
- images: bfloat16 [64, 7, 7, 2048], P(('wide', 'narrow')), may hold values from 0 to 4
- tile_maps: bfloat16 [576, 2, 2, 2048], P(('wide', 'narrow')), may hold values from 0 to 4
- map_sizes: int32 [64], P(('wide', 'narrow')), may hold values from 0 to 7, as said below
- w_reduce: bfloat16 [2, 2048, 512], replicated, may hold values from -0.125 to 0.125
- w_spatial: bfloat16 [2, 3, 3, 512, 512], replicated, may hold values from -0.09375 to 0.09375
- w_expand: bfloat16 [2, 512, 2048], replicated, may hold values from -0.25 to 0.25
- gain_mid: float32 [2, 2, 512], replicated, may hold values from 0.5 to 1.5
- bias_mid: float32 [2, 2, 512], replicated, may hold values from -4 to 4
- gain_out: float32 [2, 2048], replicated, may hold values from 0.5 to 1.5
- bias_out: float32 [2, 2048], replicated, may hold values from -4 to 4
- grad_images: bfloat16 [64, 7, 7, 2048], P(('wide', 'narrow')), may hold values from -6 to 6
- grad_tiles: bfloat16 [576, 2, 2, 2048], P(('wide', 'narrow')), may hold values from -6 to 6
Outputs:
- out_images: float32 [64, 7, 7, 2048], P(('wide', 'narrow'))
- out_tiles: float32 [576, 2, 2, 2048], P(('wide', 'narrow'))
- grad_in_images: float32 [64, 7, 7, 2048], P(('wide', 'narrow'))
- grad_in_tiles: float32 [576, 2, 2, 2048], P(('wide', 'narrow'))
- grad_w_reduce: float32 [2, 2048, 512], P(None, 'narrow')
- grad_w_spatial: float32 [2, 3, 3, 512, 512], P(None, None, None, 'narrow')
- grad_w_expand: float32 [2, 512, 2048], P(None, 'narrow')
- grad_gain_mid: float32 [2, 2, 512], replicated
- grad_bias_mid: float32 [2, 2, 512], replicated
- grad_gain_out: float32 [2, 2048], replicated
- grad_bias_out: float32 [2, 2048], replicated
Inputs may be any that keep to these rules, and one draw needn't show every extreme that they name: 0 marks an empty image slot, whose 9 tiles are empty too; a live image's map is the top-left map_sizes[i] x map_sizes[i] cells of its slot, with map_sizes[i] one of 5, 6, 7. On each device (aligned blocks of 2 slots) the live images fill the first slots, at least half of them, and one device has every slot live.
All inputs are finite; a program needn't handle non-finite values.
Results may differ from a plain program's by a relative error of at most 0.019.
Values sent between devices are 32-bit elements; how exact they have to be, the bound alone decides.
No kernel may reach another device: no remote copies, remote signals or barrier semaphores. Data moves between devices by JAX's collectives and lax.ppermute only.
A program may use at most 192 MiB of HBM per device.

v0:
```python
import jax
import jax.numpy as jnp
from jax import lax
from jax.sharding import PartitionSpec as P

BLOCKS = 2
MAP = 7
TILE = 2
PIECES = 9


epsilon = 1e-05


def make_masks(map_sizes):
    position = jnp.arange(MAP)
    inside = (position[None, :, None] < map_sizes[:, None, None]) & (
        position[None, None, :] < map_sizes[:, None, None]
    )
    image_mask = inside.astype(jnp.float32)[..., None]
    occupied = jnp.repeat((map_sizes > 0).astype(jnp.float32), PIECES)
    tile_mask = jnp.broadcast_to(occupied[:, None, None, None], (occupied.shape[0], TILE, TILE, 1))
    return (image_mask, tile_mask)


def silu_slope(values):
    sigmoid_value = jax.nn.sigmoid(values)
    return sigmoid_value * (1.0 + values * (1.0 - sigmoid_value))


def channel_sums(values):
    return jnp.sum(values, axis=(0, 1, 2))


def project(values, weight):
    return jnp.einsum("nhwc,cd->nhwd", values, weight, preferred_element_type=jnp.float32)


def weight_term(values, gradient):
    return jnp.einsum("nhwc,nhwd->cd", values, gradient, preferred_element_type=jnp.float32)


def back_project(gradient, weight):
    return jnp.einsum("nhwd,cd->nhwc", gradient, weight, preferred_element_type=jnp.float32)


def columns(values):
    map_height, map_width = (values.shape[1], values.shape[2])
    padded = jnp.pad(values, ((0, 0), (1, 1), (1, 1), (0, 0)))
    return jnp.concatenate(
        [
            padded[:, offset_y : offset_y + map_height, offset_x : offset_x + map_width, :]
            for offset_y in range(3)
            for offset_x in range(3)
        ],
        axis=3,
    )


def uncolumns(gradient):
    map_height, map_width = (gradient.shape[1], gradient.shape[2])
    channels = gradient.shape[3] // 9
    padded = jnp.zeros((gradient.shape[0], map_height + 2, map_width + 2, channels), jnp.float32)
    for offset_y in range(3):
        for offset_x in range(3):
            tap_index = 3 * offset_y + offset_x
            padded = padded.at[
                :, offset_y : offset_y + map_height, offset_x : offset_x + map_width, :
            ].add(gradient[..., tap_index * channels : (tap_index + 1) * channels])
    return padded[:, 1:-1, 1:-1, :]


def moments(values, mask_pair, local_counts):
    image_vals, tile_vals = values
    image_mask, tile_mask = mask_pair
    image_total, tile_total, image_count, tile_count = lax.psum(
        (
            channel_sums(image_vals * image_mask),
            channel_sums(tile_vals * tile_mask),
            local_counts[0],
            local_counts[1],
        ),
        ("wide", "narrow"),
    )
    image_average = image_total / image_count
    tile_average = tile_total / tile_count
    image_centered = (image_vals - image_average) * image_mask
    tile_centered = (tile_vals - tile_average) * tile_mask
    image_square, tile_square = lax.psum(
        (
            channel_sums(image_centered * image_centered),
            channel_sums(tile_centered * tile_centered),
        ),
        ("wide", "narrow"),
    )
    image_spread = image_square / image_count
    tile_spread = tile_square / tile_count
    return (
        (image_average, lax.rsqrt(image_spread + epsilon), image_count),
        (tile_average, lax.rsqrt(tile_spread + epsilon), tile_count),
    )


def norm_back(pre_grads, normed, mask_pair, statistics, scale_gain):
    image_plain, image_cross, tile_plain, tile_cross = lax.psum(
        (
            channel_sums(pre_grads[0]),
            channel_sums(pre_grads[0] * normed[0]),
            channel_sums(pre_grads[1]),
            channel_sums(pre_grads[1] * normed[1]),
        ),
        ("wide", "narrow"),
    )
    plain_sums = (image_plain, tile_plain)
    cross_sums = (image_cross, tile_cross)
    results = []
    for stream in range(2):
        total_count = statistics[stream][2]
        inv_root = statistics[stream][1]
        gradient = (
            mask_pair[stream]
            * scale_gain
            * inv_root
            * (
                pre_grads[stream]
                - plain_sums[stream] / total_count
                - normed[stream] * cross_sums[stream] / total_count
            )
        )
        results.append(gradient.astype(jnp.bfloat16))
    return (results, image_cross + tile_cross, image_plain + tile_plain)


def per_device(
    images,
    tile_maps,
    map_sizes,
    w_reduce,
    w_spatial,
    w_expand,
    gain_mid,
    bias_mid,
    gain_out,
    bias_out,
    grad_images,
    grad_tiles,
):
    mask_pair = make_masks(map_sizes)
    local_counts = (jnp.sum(mask_pair[0]), jnp.sum(mask_pair[1]))
    activations = [images.astype(jnp.float32), tile_maps.astype(jnp.float32)]
    mid_width = w_spatial.shape[4]
    kept_values = []
    for number in range(BLOCKS):
        spatial_weight = w_spatial[number].reshape(9 * mid_width, mid_width)
        lowered = [activation.astype(jnp.bfloat16) for activation in activations]
        reduced = [project(lowered[stream], w_reduce[number]) for stream in range(2)]
        moments_one = moments(reduced, mask_pair, local_counts)
        normed_one = [
            (reduced[stream] - moments_one[stream][0]) * moments_one[stream][1]
            for stream in range(2)
        ]
        before_one = [
            normed_one[stream] * gain_mid[number, 0] + bias_mid[number, 0] for stream in range(2)
        ]
        hidden_one = [
            (jax.nn.silu(before_one[stream]) * mask_pair[stream]).astype(jnp.bfloat16)
            for stream in range(2)
        ]
        spatial_out = [project(columns(hidden_one[stream]), spatial_weight) for stream in range(2)]
        moments_two = moments(spatial_out, mask_pair, local_counts)
        normed_two = [
            (spatial_out[stream] - moments_two[stream][0]) * moments_two[stream][1]
            for stream in range(2)
        ]
        before_two = [
            normed_two[stream] * gain_mid[number, 1] + bias_mid[number, 1] for stream in range(2)
        ]
        hidden_two = [
            (jax.nn.silu(before_two[stream]) * mask_pair[stream]).astype(jnp.bfloat16)
            for stream in range(2)
        ]
        expanded = [project(hidden_two[stream], w_expand[number]) for stream in range(2)]
        moments_three = moments(expanded, mask_pair, local_counts)
        normed_three = [
            (expanded[stream] - moments_three[stream][0]) * moments_three[stream][1]
            for stream in range(2)
        ]
        before_three = [
            normed_three[stream] * gain_out[number] + bias_out[number] + activations[stream]
            for stream in range(2)
        ]
        block_out = [jax.nn.silu(before_three[stream]) * mask_pair[stream] for stream in range(2)]
        kept_values.append(
            (
                lowered,
                moments_one,
                normed_one,
                hidden_one,
                before_one,
                moments_two,
                normed_two,
                hidden_two,
                before_two,
                moments_three,
                normed_three,
                before_three,
            )
        )
        activations = block_out
    out_grads = [grad_images.astype(jnp.float32), grad_tiles.astype(jnp.float32)]
    reduce_grads = [None] * BLOCKS
    spatial_grads = [None] * BLOCKS
    expand_grads = [None] * BLOCKS
    mid_gain_grads = [None] * BLOCKS
    mid_bias_grads = [None] * BLOCKS
    last_gain_grads = [None] * BLOCKS
    last_bias_grads = [None] * BLOCKS
    for number in reversed(range(BLOCKS)):
        (
            lowered,
            moments_one,
            normed_one,
            hidden_one,
            before_one,
            moments_two,
            normed_two,
            hidden_two,
            before_two,
            moments_three,
            normed_three,
            before_three,
        ) = kept_values[number]
        spatial_weight = w_spatial[number].reshape(9 * mid_width, mid_width)
        pre_three = [
            out_grads[stream] * mask_pair[stream] * silu_slope(before_three[stream])
            for stream in range(2)
        ]
        grad_expanded, last_gain_grads[number], last_bias_grads[number] = norm_back(
            pre_three, normed_three, mask_pair, moments_three, gain_out[number]
        )
        expand_grads[number] = weight_term(hidden_two[0], grad_expanded[0]) + weight_term(
            hidden_two[1], grad_expanded[1]
        )
        pre_two = [
            back_project(grad_expanded[stream], w_expand[number])
            * mask_pair[stream]
            * silu_slope(before_two[stream])
            for stream in range(2)
        ]
        grad_spatial, gain_second, bias_second = norm_back(
            pre_two, normed_two, mask_pair, moments_two, gain_mid[number, 1]
        )
        patch_image = columns(hidden_one[0])
        patch_tile = columns(hidden_one[1])
        spatial_grads[number] = (
            weight_term(patch_image, grad_spatial[0]) + weight_term(patch_tile, grad_spatial[1])
        ).reshape(3, 3, mid_width, mid_width)
        pre_one = [
            uncolumns(back_project(grad_spatial[stream], spatial_weight))
            * mask_pair[stream]
            * silu_slope(before_one[stream])
            for stream in range(2)
        ]
        grad_reduced, gain_first, bias_first = norm_back(
            pre_one, normed_one, mask_pair, moments_one, gain_mid[number, 0]
        )
        reduce_grads[number] = weight_term(lowered[0], grad_reduced[0]) + weight_term(
            lowered[1], grad_reduced[1]
        )
        mid_gain_grads[number] = jnp.stack([gain_first, gain_second])
        mid_bias_grads[number] = jnp.stack([bias_first, bias_second])
        out_grads = [
            pre_three[stream] + back_project(grad_reduced[stream], w_reduce[number])
            for stream in range(2)
        ]
    full_grads = (jnp.stack(reduce_grads), jnp.stack(spatial_grads), jnp.stack(expand_grads))
    partial_value = (
        lax.psum_scatter(full_grads[0], "narrow", scatter_dimension=1, tiled=True),
        lax.psum_scatter(full_grads[1], "narrow", scatter_dimension=3, tiled=True),
        lax.psum_scatter(full_grads[2], "narrow", scatter_dimension=1, tiled=True),
    )
    shards = lax.psum((partial_value[0], partial_value[1], partial_value[2]), "wide")
    return (
        activations[0],
        activations[1],
        out_grads[0],
        out_grads[1],
        shards[0],
        shards[1],
        shards[2],
        jnp.stack(mid_gain_grads),
        jnp.stack(mid_bias_grads),
        jnp.stack(last_gain_grads),
        jnp.stack(last_bias_grads),
    )


def solution(mesh):
    placed = (
        P(("wide", "narrow"), None, None, None),
        P(("wide", "narrow"), None, None, None),
        P(("wide", "narrow")),
        P(),
        P(),
        P(),
        P(),
        P(),
        P(),
        P(),
        P(("wide", "narrow"), None, None, None),
        P(("wide", "narrow"), None, None, None),
    )
    return jax.shard_map(
        per_device,
        mesh=mesh,
        in_specs=placed,
        out_specs=(
            P(("wide", "narrow"), None, None, None),
            P(("wide", "narrow"), None, None, None),
            P(("wide", "narrow"), None, None, None),
            P(("wide", "narrow"), None, None, None),
            P(None, "narrow", None),
            P(None, None, None, "narrow", None),
            P(None, "narrow", None),
            P(),
            P(),
            P(),
            P(),
        ),
        check_vma=False,
    )
```

profile of v0, /device:TPU:0, one launch (start us, length us, event | category | flops | bytes accessed | tf_op | source)
XLA Modules:
  0.0 1597.2 jit_solution(2967983598770522694)
XLA Ops:
  19.4 42.3 %all-reduce.25 = (f32[512]{0:T(512)S(1)}, f32[]{:T(128)}, f32[512]{0:T(512)S(1)}, f32[]{:T(128)}) all-reduce(f32[512]{0:T(512)S(1)} %get-tuple-element.586, f32[]{:T(128)} %fusion.153, f32[512]{0:T(512)S(1)} %get-tuple-element.588, f32[]{:T(128)} %broadcast_reduce_fusion), channel_id=1, replica_groups=mesh['wide'=8,'narrow'=4] {'wide','narrow'}, use_global_device_ids=true, to_apply=%region_1.0 | all-reduce | flops 1026 | bytes 8208 | tf_op jit(solution)/shard_map/psum | solution.py:76
  63.2 40.5 %all-reduce.24 = (f32[512]{0:T(512)S(1)}, f32[512]{0:T(512)S(1)}) all-reduce(f32[512]{0:T(512)S(1)} %multiply_reduce_fusion.22, f32[512]{0:T(512)S(1)} %multiply_reduce_fusion.34), channel_id=1, replica_groups=mesh['wide'=8,'narrow'=4] {'wide','narrow'}, use_global_device_ids=true, to_apply=%region_5.0 | all-reduce | flops 1024 | bytes 8192 | tf_op jit(solution)/shard_map/psum | solution.py:89
  105.9 6.9 fusion.171
  115.2 40.0 %all-reduce.23 = (f32[512]{0:T(512)S(1)}, f32[512]{0:T(512)S(1)}) all-reduce(f32[512]{0:T(512)S(1)} %get-tuple-element.590, f32[512]{0:T(512)S(1)} %get-tuple-element.592), channel_id=1, replica_groups=mesh['wide'=8,'narrow'=4] {'wide','narrow'}, use_global_device_ids=true, to_apply=%region_7.0 | all-reduce | flops 1024 | bytes 8192 | tf_op jit(solution)/shard_map/psum | solution.py:76
  156.8 40.1 %all-reduce.22 = (f32[512]{0:T(512)S(1)}, f32[512]{0:T(512)S(1)}) all-reduce(f32[512]{0:T(512)S(1)} %multiply_reduce_fusion.20, f32[512]{0:T(512)S(1)} %multiply_reduce_fusion.32), channel_id=1, replica_groups=mesh['wide'=8,'narrow'=4] {'wide','narrow'}, use_global_device_ids=true, to_apply=%region_9.0 | all-reduce | flops 1024 | bytes 8192 | tf_op jit(solution)/shard_map/psum | solution.py:89
  202.8 40.1 %all-reduce.21 = (f32[2048]{0:T(1024)S(1)}, f32[2048]{0:T(1024)S(1)}) all-reduce(f32[2048]{0:T(1024)S(1)} %get-tuple-element.594, f32[2048]{0:T(1024)S(1)} %get-tuple-element.596), channel_id=1, replica_groups=mesh['wide'=8,'narrow'=4] {'wide','narrow'}, use_global_device_ids=true, to_apply=%region_11.0 | all-reduce | flops 4096 | bytes 32768 | tf_op jit(solution)/shard_map/psum | solution.py:76
  244.7 40.5 %all-reduce.20 = (f32[2048]{0:T(1024)S(1)}, f32[2048]{0:T(1024)S(1)}) all-reduce(f32[2048]{0:T(1024)S(1)} %multiply_reduce_fusion.4, f32[2048]{0:T(1024)S(1)} %multiply_reduce_fusion.10), channel_id=1, replica_groups=mesh['wide'=8,'narrow'=4] {'wide','narrow'}, use_global_device_ids=true, to_apply=%region_13.14 | all-reduce | flops 4096 | bytes 32768 | tf_op jit(solution)/shard_map/psum | solution.py:89
  290.3 39.9 %all-reduce.19 = (f32[512]{0:T(512)S(1)}, f32[512]{0:T(512)S(1)}) all-reduce(f32[512]{0:T(512)S(1)} %get-tuple-element.598, f32[512]{0:T(512)S(1)} %get-tuple-element.600), channel_id=1, replica_groups=mesh['wide'=8,'narrow'=4] {'wide','narrow'}, use_global_device_ids=true, to_apply=%region_15.16 | all-reduce | flops 1024 | bytes 8192 | tf_op jit(solution)/shard_map/psum | solution.py:76
  331.8 40.1 %all-reduce.18 = (f32[512]{0:T(512)S(1)}, f32[512]{0:T(512)S(1)}) all-reduce(f32[512]{0:T(512)S(1)} %multiply_reduce_fusion.18, f32[512]{0:T(512)S(1)} %multiply_reduce_fusion.30), channel_id=1, replica_groups=mesh['wide'=8,'narrow'=4] {'wide','narrow'}, use_global_device_ids=true, to_apply=%region_17.18 | all-reduce | flops 1024 | bytes 8192 | tf_op jit(solution)/shard_map/psum | solution.py:89
  374.7 4.0 multiply_reduce_fusion.29
  380.7 39.8 %all-reduce.17 = (f32[512]{0:T(512)S(1)}, f32[512]{0:T(512)S(1)}) all-reduce(f32[512]{0:T(512)S(1)} %get-tuple-element.602, f32[512]{0:T(512)S(1)} %get-tuple-element.604), channel_id=1, replica_groups=mesh['wide'=8,'narrow'=4] {'wide','narrow'}, use_global_device_ids=true, to_apply=%region_19.20 | all-reduce | flops 1024 | bytes 8192 | tf_op jit(solution)/shard_map/psum | solution.py:76
  423.0 40.2 %all-reduce.16 = (f32[512]{0:T(512)S(1)}, f32[512]{0:T(512)S(1)}) all-reduce(f32[512]{0:T(512)S(1)} %multiply_reduce_fusion.16, f32[512]{0:T(512)S(1)} %multiply_reduce_fusion.28), channel_id=1, replica_groups=mesh['wide'=8,'narrow'=4] {'wide','narrow'}, use_global_device_ids=true, to_apply=%region_21.22 | all-reduce | flops 1024 | bytes 8192 | tf_op jit(solution)/shard_map/psum | solution.py:89
  465.2 3.6 multiply_reduce_fusion.9
  468.8 3.1 multiply_reduce_fusion.3
  471.8 40.1 %all-reduce.15 = (f32[2048]{0:T(1024)}, f32[2048]{0:T(1024)}) all-reduce(f32[2048]{0:T(1024)} %get-tuple-element.606, f32[2048]{0:T(1024)} %get-tuple-element.608), channel_id=1, replica_groups=mesh['wide'=8,'narrow'=4] {'wide','narrow'}, use_global_device_ids=true, to_apply=%region_23.24 | all-reduce | flops 4096 | bytes 32768 | tf_op jit(solution)/shard_map/psum | solution.py:76
  518.0 41.6 %all-reduce.14 = (f32[2048]{0:T(1024)}, f32[2048]{0:T(1024)}) all-reduce(f32[2048]{0:T(1024)} %multiply_reduce_fusion.2, f32[2048]{0:T(1024)} %multiply_reduce_fusion.8), channel_id=1, replica_groups=mesh['wide'=8,'narrow'=4] {'wide','narrow'}, use_global_device_ids=true, to_apply=%region_25.26 | all-reduce | flops 4096 | bytes 32768 | tf_op jit(solution)/shard_map/psum | solution.py:89
  562.2 4.1 fusion.158
  566.2 4.1 fusion.156
  570.4 41.5 %all-reduce.13 = (f32[2048]{0:T(1024)}, f32[2048]{0:T(1024)}, f32[2048]{0:T(1024)}, f32[2048]{0:T(1024)}) all-reduce(f32[2048]{0:T(1024)} %get-tuple-element.468, f32[2048]{0:T(1024)} %get-tuple-element.467, f32[2048]{0:T(1024)} %get-tuple-element.472, ...), channel_id=1, replica_groups=mesh['wide'=8,'narrow'=4] {'wide','narrow'}, use_global_device_ids=true, to_apply=%region_55.56 | all-reduce | flops 8192 | bytes 65536 | tf_op jit(solution)/shard_map/psum | solution.py:105
  611.8 2.6 fusion.175
  616.6 3.2 fusion.162
  619.9 3.7 fusion.80
  627.4 40.7 %all-reduce.12 = (f32[512]{0:T(512)S(1)}, f32[512]{0:T(512)S(1)}, f32[512]{0:T(512)S(1)}, f32[512]{0:T(512)S(1)}) all-reduce(f32[512]{0:T(512)S(1)} %get-tuple-element.480, f32[512]{0:T(512)S(1)} %get-tuple-element.479, f32[512]{0:T(512)S(1)} %get-tuple-element.488, ...), channel_id=1, replica_groups=mesh['wide'=8,'narrow'=4] {'wide','narrow'}, use_global_device_ids=true, to_apply=%region_59.60 | all-reduce | flops 2048 | bytes 16384 | tf_op jit(solution)/shard_map/psum | solution.py:105
  671.7 4.1 fusion.186
  675.8 4.6 fusion.184
  686.6 3.5 add_select_fusion.1
  714.0 2.8 fusion.97
  723.6 39.6 %all-reduce.11 = (f32[512]{0:T(512)S(1)}, f32[512]{0:T(512)S(1)}, f32[512]{0:T(512)S(1)}, f32[512]{0:T(512)S(1)}) all-reduce(f32[512]{0:T(512)S(1)} %get-tuple-element.478, f32[512]{0:T(512)S(1)} %get-tuple-element.477, f32[512]{0:T(512)S(1)} %get-tuple-element.486, ...), channel_id=1, replica_groups=mesh['wide'=8,'narrow'=4] {'wide','narrow'}, use_global_device_ids=true, to_apply=%region_64.65 | all-reduce | flops 2048 | bytes 16384 | tf_op jit(solution)/shard_map/psum | solution.py:105
  766.8 4.1 fusion.155
  771.0 2.6 fusion.157
  773.6 41.1 %all-reduce.10 = (f32[2048]{0:T(1024)S(1)}, f32[2048]{0:T(1024)S(1)}, f32[2048]{0:T(1024)S(1)}, f32[2048]{0:T(1024)S(1)}) all-reduce(f32[2048]{0:T(1024)S(1)} %get-tuple-element.466, f32[2048]{0:T(1024)S(1)} %get-tuple-element.465, f32[2048]{0:T(1024)S(1)} %get-tuple-element.470, ...), channel_id=1, replica_groups=mesh['wide'=8,'narrow'=4] {'wide','narrow'}, use_global_device_ids=true, to_apply=%region_68.69 | all-reduce | flops 8192 | bytes 65536 | tf_op jit(solution)/shard_map/psum | solution.py:105
  824.1 3.9 pad_maximum_fusion.2
  830.6 3.3 fusion.160
  833.9 43.2 %all-reduce.9 = (f32[512]{0:T(512)S(1)}, f32[512]{0:T(512)S(1)}, f32[512]{0:T(512)S(1)}, f32[512]{0:T(512)S(1)}) all-reduce(f32[512]{0:T(512)S(1)} %get-tuple-element.476, f32[512]{0:T(512)S(1)} %get-tuple-element.475, f32[512]{0:T(512)S(1)} %get-tuple-element.484, ...), channel_id=1, replica_groups=mesh['wide'=8,'narrow'=4] {'wide','narrow'}, use_global_device_ids=true, to_apply=%region_72.73 | all-reduce | flops 2048 | bytes 16384 | tf_op jit(solution)/shard_map/psum | solution.py:105
  878.9 5.0 fusion.185
  892.0 2.8 add_select_fusion
  908.4 2.8 fusion.98
  918.9 47.3 %all-reduce.8 = (f32[512]{0:T(512)S(1)}, f32[512]{0:T(512)S(1)}, f32[512]{0:T(512)S(1)}, f32[512]{0:T(512)S(1)}) all-reduce(f32[512]{0:T(512)S(1)} %get-tuple-element.474, f32[512]{0:T(512)S(1)} %get-tuple-element.473, f32[512]{0:T(512)S(1)} %get-tuple-element.482, ...), channel_id=1, replica_groups=mesh['wide'=8,'narrow'=4] {'wide','narrow'}, use_global_device_ids=true, to_apply=%region_76.77 | all-reduce | flops 2048 | bytes 16384 | tf_op jit(solution)/shard_map/psum | solution.py:105
  970.0 2.6 fusion.3
  975.1 3.8 pad_maximum_fusion.1
  979.9 2.9 fusion.78
  989.1 7.0 pad_maximum_fusion
  996.5 128.8 %reduce-scatter.4.cloned.1.call-done = f32[2,512,512]{1,2,0:T(8,128)} async-done(((f32[2,2048,512]{1,2,0:T(8,128)}), f32[2,512,512]{1,2,0:T(8,128)}) %reduce-scatter.4.cloned.1.call-update) | async-done | bytes 2097168 | tf_op jit(solution)/shard_map/reduce_scatter | solution.py:278
  1125.3 316.9 %reduce-scatter.6.cloned.1.call-done = f32[2,3,3,128,512]{4,3,2,1,0:T(8,128)} async-done(((f32[2,3,3,512,512]{4,3,2,1,0:T(8,128)}), f32[2,3,3,128,512]{4,3,2,1,0:T(8,128)}) %reduce-scatter.6.cloned.1.call-update) | async-done | bytes 4718608 | tf_op jit(solution)/shard_map/reduce_scatter | solution.py:279
  1447.1 3.1 convolution_add_fusion.2
  1456.5 124.2 %all-reduce.29.cloned.1.call-done = (f32[2,512,512]{1,2,0:T(8,128)}, f32[2,3,3,128,512]{4,3,2,1,0:T(8,128)}, f32[2,128,2048]{2,1,0:T(8,128)}) async-done(((f32[2,512,512]{1,2,0:T(8,128)}, f32[2,3,3,128,512]{4,3,2,1,0:T(8,128)}, f32[2,128,2048]{2,1,0:T(8,128)}), (f32[2,512,512]{1,2,0:T(8,128)}, f32[2,3,3,128,512]{4,3,2,1,0:T(8,128)}, f32[2,128,2048]{2,1,0:T(8,128)})) %all-reduce.29.cloned.1.call-update) | async-done | bytes 8912912 | tf_op jit(solution)/shard_map/psum | solution.py:282
  1580.6 2.9 copy.75
  1583.5 5.4 copy.231
  (498 shorter events, 169.2 us)
Async XLA Ops:
  7.2 989.3 %reduce-scatter.8.cloned.1.call-start = ((), (), s32[]{:S(2)}) async-start(), calls=%async_computation.5 | async-start | bytes 10485760 | tf_op jit(solution)/shard_map/reduce_scatter | solution.py:280
  11.6 188.8 %copy-start.83 = (f32[1,1,512]{2,1,0:T(1,128)}, f32[1,1,512]{2,1,0:T(1,128)S(1)}, u32[]{:S(2)}) copy-start(f32[1,1,512]{2,1,0:T(1,128)S(1)} %get-tuple-element.563) | copy-start | bytes 6148
  11.6 453.0 %copy-start.81 = (f32[1,1,512]{2,1,0:T(1,128)}, f32[1,1,512]{2,1,0:T(1,128)S(1)}, u32[]{:S(2)}) copy-start(f32[1,1,512]{2,1,0:T(1,128)S(1)} %get-tuple-element.562) | copy-start | bytes 6148
  12.4 93.2 %copy-start.62 = (f32[1,1,512]{2,1,0:T(1,128)}, f32[1,1,512]{2,1,0:T(1,128)S(1)}, u32[]{:S(2)}) copy-start(f32[1,1,512]{2,1,0:T(1,128)S(1)} %get-tuple-element.568) | copy-start | bytes 6148
  12.4 188.0 %copy-start.129 = (f32[1,1,512]{2,1,0:T(1,128)}, f32[1,1,512]{2,1,0:T(1,128)S(1)}, u32[]{:S(2)}) copy-start(f32[1,1,512]{2,1,0:T(1,128)S(1)} %get-tuple-element.567) | copy-start | bytes 6148
  12.4 361.5 %copy-start.64 = (f32[1,1,512]{2,1,0:T(1,128)}, f32[1,1,512]{2,1,0:T(1,128)S(1)}, u32[]{:S(2)}) copy-start(f32[1,1,512]{2,1,0:T(1,128)S(1)} %get-tuple-element.569) | copy-start | bytes 6148
  12.4 452.2 %copy-start.132 = (f32[1,1,512]{2,1,0:T(1,128)}, f32[1,1,512]{2,1,0:T(1,128)S(1)}, u32[]{:S(2)}) copy-start(f32[1,1,512]{2,1,0:T(1,128)S(1)} %get-tuple-element.566) | copy-start | bytes 6148
  62.3 50.5 %copy-start.68 = (f32[512]{0:T(512)}, f32[512]{0:T(512)S(1)}, u32[]{:S(2)}) copy-start(f32[512]{0:T(512)S(1)} %broadcast_divide_fusion.23) | copy-start | bytes 6148
  113.8 84.4 %copy-start.6 = (f32[18,2,2,512]{3,0,2,1:T(8,128)}, f32[18,2,2,512]{3,0,2,1:T(8,128)S(1)}, u32[]{:S(2)}) copy-start(f32[18,2,2,512]{3,0,2,1:T(8,128)S(1)} %get-tuple-element.593) | copy-start | bytes 442372
  115.2 87.5 %copy-start.28 = (f32[2,7,7,512]{3,2,1,0:T(8,128)}, f32[2,7,7,512]{3,2,1,0:T(8,128)S(1)}, u32[]{:S(2)}) copy-start(f32[2,7,7,512]{3,2,1,0:T(8,128)S(1)} %get-tuple-element.591) | copy-start | bytes 602116
  155.8 46.9 %copy-start.110 = (f32[512]{0:T(512)}, f32[512]{0:T(512)S(1)}, u32[]{:S(2)}) copy-start(f32[512]{0:T(512)S(1)} %broadcast_divide_fusion.22) | copy-start | bytes 6148
  156.5 46.2 %copy-start.77 = (f32[512]{0:T(512)}, f32[512]{0:T(512)S(1)}, u32[]{:S(2)}) copy-start(f32[512]{0:T(512)S(1)} %broadcast_divide_fusion.14) | copy-start | bytes 6148
  198.2 88.3 %copy-start.18 = (bf16[18,2,2,2048]{3,2,1,0:T(2,128)(2,1)S(1)}, bf16[18,2,2,2048]{3,2,1,0:T(2,128)(2,1)}, u32[]{:S(2)}) copy-start(bf16[18,2,2,2048]{3,2,1,0:T(2,128)(2,1)} %param.85) | copy-start | bytes 884740
  244.4 44.6 %copy-start.40 = (bf16[2,7,7,2048]{3,0,2,1:T(2,128)(2,1)S(1)}, bf16[2,7,7,2048]{3,0,2,1:T(2,128)(2,1)}, u32[]{:S(2)}) copy-start(bf16[2,7,7,2048]{3,0,2,1:T(2,128)(2,1)} %param.84) | copy-start | bytes 1204228
  289.5 89.2 %slice-start.2 = ((s8[4718592]{0:T(1024)(128)(4,1)}), s8[524288]{0:T(1024)(128)(4,1)S(1)}, s32[]{:S(2)}) async-start(s8[4718592]{0:T(1024)(128)(4,1)} %bitcast.242), calls=%async_computation.9 | async-start | bytes 1048576
  330.9 43.3 %copy-start.72 = (f32[512]{0:T(512)}, f32[512]{0:T(512)S(1)}, u32[]{:S(2)}) copy-start(f32[512]{0:T(512)S(1)} %broadcast_divide_fusion.21) | copy-start | bytes 6148
  331.6 42.6 %copy-start.70 = (f32[512]{0:T(512)}, f32[512]{0:T(512)S(1)}, u32[]{:S(2)}) copy-start(f32[512]{0:T(512)S(1)} %broadcast_divide_fusion.13) | copy-start | bytes 6148
  378.8 85.9 %copy-start.8 = (f32[18,2,2,512]{3,0,2,1:T(8,128)}, f32[18,2,2,512]{3,0,2,1:T(8,128)S(1)}, u32[]{:S(2)}) copy-start(f32[18,2,2,512]{3,0,2,1:T(8,128)S(1)} %get-tuple-element.605) | copy-start | bytes 442372
  421.2 42.7 %copy-start.112 = (f32[512]{0:T(512)}, f32[512]{0:T(512)S(1)}, u32[]{:S(2)}) copy-start(f32[512]{0:T(512)S(1)} %broadcast_divide_fusion.20) | copy-start | bytes 6148
  421.9 42.8 %copy-start.79 = (f32[512]{0:T(512)}, f32[512]{0:T(512)S(1)}, u32[]{:S(2)}) copy-start(f32[512]{0:T(512)S(1)} %broadcast_divide_fusion.12) | copy-start | bytes 6148
  623.6 46.3 %copy-start.32 = (f32[2,7,7,512]{3,2,1,0:T(8,128)S(1)}, f32[2,7,7,512]{3,2,1,0:T(8,128)}, u32[]{:S(2)}) copy-start(f32[2,7,7,512]{3,2,1,0:T(8,128)} %get-tuple-element.603) | copy-start | bytes 602116
  623.7 46.3 %copy-start.113 = (f32[512]{0:T(512)S(1)}, f32[512]{0:T(512)}, u32[]{:S(2)}) copy-start(f32[512]{0:T(512)} %copy-done.112) | copy-start | bytes 6148
  623.7 46.3 %copy-start.123 = (f32[512]{0:T(512)S(1)}, f32[512]{0:T(512)}, u32[]{:S(2)}) copy-start(f32[512]{0:T(512)} %copy-done.122) | copy-start | bytes 6148
  627.4 53.0 %copy-start.45 = (f32[18,2,2,512]{3,0,2,1:T(8,128)}, f32[18,2,2,512]{3,0,2,1:T(8,128)S(1)}, u32[]{:S(2)}) copy-start(f32[18,2,2,512]{3,0,2,1:T(8,128)S(1)} %get-tuple-element.611) | copy-start | bytes 442372
  684.1 25.7 %copy-start.65 = (f32[1,1,512]{2,1,0:T(1,128)S(1)}, f32[1,1,512]{2,1,0:T(1,128)}, u32[]{:S(2)}) copy-start(f32[1,1,512]{2,1,0:T(1,128)} %copy-done.64) | copy-start | bytes 6148
  684.1 25.7 %copy-start.73 = (f32[512]{0:T(512)S(1)}, f32[512]{0:T(512)}, u32[]{:S(2)}) copy-start(f32[512]{0:T(512)} %copy-done.72) | copy-start | bytes 6148
  684.1 25.7 %copy-start.91 = (f32[512]{0:T(512)S(1)}, f32[512]{0:T(512)}, u32[]{:S(2)}) copy-start(f32[512]{0:T(512)} %copy-done.90) | copy-start | bytes 6148
  704.0 18.7 %copy-start.71 = (f32[512]{0:T(512)S(1)}, f32[512]{0:T(512)}, u32[]{:S(2)}) copy-start(f32[512]{0:T(512)} %copy-done.70) | copy-start | bytes 6148
  704.0 18.7 %copy-start.88 = (f32[512]{0:T(512)S(1)}, f32[512]{0:T(512)}, u32[]{:S(2)}) copy-start(f32[512]{0:T(512)} %copy-done.87) | copy-start | bytes 6148
  710.7 56.1 %copy-start.41 = (bf16[2,7,7,2048]{3,0,2,1:T(2,128)(2,1)S(1)}, bf16[2,7,7,2048]{3,0,2,1:T(2,128)(2,1)}, u32[]{:S(2)}) copy-start(bf16[2,7,7,2048]{3,0,2,1:T(2,128)(2,1)} %param.84) | copy-start | bytes 1204228
  770.9 47.7 %copy-start.29 = (f32[2,7,7,512]{3,2,1,0:T(8,128)S(1)}, f32[2,7,7,512]{3,2,1,0:T(8,128)}, u32[]{:S(2)}) copy-start(f32[2,7,7,512]{3,2,1,0:T(8,128)} %copy-done.28) | copy-start | bytes 602116
  770.9 47.7 %copy-start.84 = (f32[1,1,512]{2,1,0:T(1,128)S(1)}, f32[1,1,512]{2,1,0:T(1,128)}, u32[]{:S(2)}) copy-start(f32[1,1,512]{2,1,0:T(1,128)} %copy-done.83) | copy-start | bytes 6148
  770.9 47.7 %copy-start.111 = (f32[512]{0:T(512)S(1)}, f32[512]{0:T(512)}, u32[]{:S(2)}) copy-start(f32[512]{0:T(512)} %copy-done.110) | copy-start | bytes 6148
  770.9 47.7 %copy-start.121 = (f32[512]{0:T(512)S(1)}, f32[512]{0:T(512)}, u32[]{:S(2)}) copy-start(f32[512]{0:T(512)} %copy-done.120) | copy-start | bytes 6148
  771.0 47.7 %copy-start.130 = (f32[1,1,512]{2,1,0:T(1,128)S(1)}, f32[1,1,512]{2,1,0:T(1,128)}, u32[]{:S(2)}) copy-start(f32[1,1,512]{2,1,0:T(1,128)} %copy-done.129) | copy-start | bytes 6148
  828.1 297.3 %reduce-scatter.4.cloned.1.call-start = ((), (), s32[]{:S(2)}) async-start(), calls=%async_computation.3 | async-start | bytes 10485760 | tf_op jit(solution)/shard_map/reduce_scatter | solution.py:278
  830.6 53.3 %copy-start.47 = (f32[18,2,2,512]{3,0,2,1:T(8,128)}, f32[18,2,2,512]{3,0,2,1:T(8,128)S(1)}, u32[]{:S(2)}) copy-start(f32[18,2,2,512]{3,0,2,1:T(8,128)S(1)} %get-tuple-element.615) | copy-start | bytes 442372
  830.6 55.3 %slice-start = ((s8[4718592]{0:T(1024)(128)(4,1)}), s8[524288]{0:T(1024)(128)(4,1)S(1)}, s32[]{:S(2)}) async-start(s8[4718592]{0:T(1024)(128)(4,1)} %bitcast.236), calls=%async_computation.7 | async-start | bytes 1048576
  833.9 51.3 %copy-start.58 = (f32[2,7,7,512]{3,2,1,0:T(8,128)S(1)}, f32[2,7,7,512]{3,2,1,0:T(8,128)}, u32[]{:S(2)}) copy-start(f32[2,7,7,512]{3,2,1,0:T(8,128)} %get-tuple-element.614) | copy-start | bytes 602116
  901.8 16.3 %copy-start.69 = (f32[512]{0:T(512)S(1)}, f32[512]{0:T(512)}, u32[]{:S(2)}) copy-start(f32[512]{0:T(512)} %copy-done.68) | copy-start | bytes 6148
  901.8 16.3 %copy-start.86 = (f32[512]{0:T(512)S(1)}, f32[512]{0:T(512)}, u32[]{:S(2)}) copy-start(f32[512]{0:T(512)} %copy-done.85) | copy-start | bytes 6148
  904.8 64.3 %copy-start.34 = (bf16[2,7,7,2048]{3,2,1,0:T(8,128)(2,1)S(1)}, bf16[2,7,7,2048]{3,2,1,0:T(8,128)(2,1)}, u32[]{:S(2)}) copy-start(bf16[2,7,7,2048]{3,2,1,0:T(8,128)(2,1)} %copy-done.33) | copy-start | bytes 1204228
  914.1 55.8 %copy-start.20 = (bf16[18,2,2,2048]{3,2,1,0:T(2,128)(2,1)S(1)}, bf16[18,2,2,2048]{3,2,1,0:T(2,128)(2,1)}, u32[]{:S(2)}) copy-start(bf16[18,2,2,2048]{3,2,1,0:T(2,128)(2,1)} %param.85) | copy-start | bytes 884740
  914.2 55.8 %copy-start.89 = (f32[512]{0:T(512)S(1)}, f32[512]{0:T(512)}, u32[]{:S(2)}) copy-start(f32[512]{0:T(512)} %copy-done.87) | copy-start | bytes 6148
  914.2 55.8 %copy-start.119 = (f32[512]{0:T(512)S(1)}, f32[512]{0:T(512)}, u32[]{:S(2)}) copy-start(f32[512]{0:T(512)} %copy-done.118) | copy-start | bytes 6148
  914.2 55.8 %copy-start.125 = (f32[512]{0:T(512)S(1)}, f32[512]{0:T(512)}, u32[]{:S(2)}) copy-start(f32[512]{0:T(512)} %copy-done.124) | copy-start | bytes 6148
  979.0 463.2 %reduce-scatter.6.cloned.1.call-start = ((), (), s32[]{:S(2)}) async-start(), calls=%async_computation.4 | async-start | bytes 23592960 | tf_op jit(solution)/shard_map/reduce_scatter | solution.py:279
  996.1 584.5 %all-reduce.29.cloned.1.call-start = ((), (), s32[]{:S(2)}) async-start(), calls=%async_computation.6 | async-start | bytes 17825792 | tf_op jit(solution)/shard_map/psum | solution.py:282
  (98 other events, 448.5 us)
Sparse Core Ops, SparseCore 0:
  828.1 147.1 reduce-scatter.7
  979.1 146.1 reduce-scatter.3
  1127.7 314.5 reduce-scatter.5
  1446.6 133.9 all-reduce.28
where the time goes:
time: 1610 us; the launch traced here: 1600 us
  blocking collectives  739 us (46%)
  waiting for transfers between devices  570 us (35%)
  other arithmetic  128 us (8%)
  matrix products  84.1 us (5%)
  local copies, waits for them, and re-layouts  59 us (4%)
  between operations  17 us (1%)
    reduce_scatter x1, waiting for transfers between devices, per_device(): lax.psum_scatter(full_grads[1], 'narrow', scatter_dimension=3, tiled=True)  317 us
    psum x6, blocking collectives, norm_back(): lax.psum((channel_sums(pre_grads[0]), channel_sums(pre_grads[0] * normed[...  253 us
    psum x6, blocking collectives, moments(): lax.psum((channel_sums(image_centered * image_centered), channel_sums(til...  243 us
    psum x6, blocking collectives, moments(): lax.psum((channel_sums(image_vals * image_mask), channel_sums(tile_vals *...  242 us
    reduce_scatter x1, waiting for transfers between devices, per_device(): lax.psum_scatter(full_grads[0], 'narrow', scatter_dimension=1, tiled=True)  129 us
    psum x1, waiting for transfers between devices, per_device(): lax.psum((partial_value[0], partial_value[1], partial_value[2]), 'wide')  124 us
    dot_general x12, matrix products, back_project(): jnp.einsum('nhwd,cd->nhwc', gradient, weight, preferred_element_type=jnp....  35.8 us
  transfers between devices with their start and end apart: 4, of which 3 were waited for; matrix products, arithmetic and copies ran while one was open for 5% of the time, Pallas kernels for 0%

commit v1 on v0

v1 whole, which is shorter than its diff:
```python
import functools

import jax
import jax.numpy as jnp
from jax import lax
from jax.experimental import pallas as pl
from jax.experimental.pallas import tpu as pltpu
from jax.sharding import PartitionSpec as P

BLOCKS = 2
MAP = 7
MAPW = 8
TILE = 2
PIECES = 9
SLOTS = 2
IMG_ROWS = MAP * MAPW * SLOTS
EPS = 1e-05
CH = 512
BF = jnp.bfloat16
F32 = jnp.float32
VMEM_LIMIT = 48 * 1024 * 1024
AXES = ("wide", "narrow")


class Grid:
    def __init__(self, wide, narrow):
        chips = wide // 2
        side = 1
        while side * side < chips:
            side *= 2
        self.y, self.x, self.c, self.z = chips // side, side, 2, narrow

    def index(self):
        wide = lax.axis_index("wide")
        core = wide % 2
        chip = wide // 2
        return chip // self.x, chip % self.x, core, lax.axis_index("narrow")

    def swap(self, value, dy=0, dx=0, dc=0, dz=0):
        pairs = []
        for y in range(self.y):
            for x in range(self.x):
                for c in range(self.c):
                    for z in range(self.z):
                        src = ((y * self.x + x) * 2 + c) * self.z + z
                        dst = (((y ^ dy) * self.x + (x ^ dx)) * 2 + (c ^ dc)) * self.z + (z ^ dz)
                        pairs.append((src, dst))
        return lax.ppermute(value, AXES, pairs)

    def phases(self):
        found = [[dict(dc=1)]]
        step = 1
        while step < max(self.x, self.y):
            group = []
            for dy in (0, step):
                for dx in (0, step):
                    if (dy or dx) and dy < self.y and dx < self.x:
                        group.append(dict(dy=dy, dx=dx))
            found.append(group)
            step *= 2
        found.append([dict(dz=k) for k in range(1, min(self.z, 4))])
        step = 4
        while step < self.z:
            found.append([dict(dz=step)])
            step *= 2
        return found


def merge_moments(members, counts):
    total = sum(counts)
    out = []
    for stream in range(2):
        whole = total[stream]
        plain = sum(m[2 * stream] for m in members)
        mean = plain / whole
        square = sum(m[2 * stream + 1] for m in members)
        for m, n in zip(members, counts):
            gap = m[2 * stream] / jnp.maximum(n[stream], 1.0) - mean
            square = square + n[stream] * gap * gap
        out += [plain, square]
    return jnp.stack(out), total


class Sync:
    def __init__(self, grid, local_counts):
        self.grid = grid
        self.local = local_counts
        self.levels = None

    def moments(self, stats):
        grid = self.grid
        first = self.levels is None
        value = stats
        count = self.local
        levels = [] if first else self.levels
        for number, group in enumerate(grid.phases()):
            if first:
                width = value.shape[1]
                packed = jnp.concatenate(
                    [value, jnp.broadcast_to(count[:, None], (2, width)), jnp.zeros((2, width), F32)]
                )
                got = [grid.swap(packed, **step) for step in group]
                counts = [count] + [g[4:6, 0] for g in got]
                got = [g[0:4] for g in got]
                levels.append(counts)
            else:
                got = [grid.swap(value, **step) for step in group]
                counts = levels[number]
            value, count = merge_moments([value] + got, counts)
        if first:
            self.levels = levels
            self.total = count
        out = []
        for stream in range(2):
            out.append(value[2 * stream] / self.total[stream])
            out.append(lax.rsqrt(value[2 * stream + 1] / self.total[stream] + EPS))
        return jnp.stack(out)

    def sums(self, value):
        for group in self.grid.phases():
            value = value + sum(self.grid.swap(value, **step) for step in group)
        return value

    def shares(self, sums):
        return sums / jnp.stack([self.total[0], self.total[0], self.total[1], self.total[1]])[:, None]


def parts(rows):
    return ((0, 0, IMG_ROWS), (1, IMG_ROWS, rows))


def sigmoid(v):
    return 0.5 * jnp.tanh(0.5 * v) + 0.5


def slope(v):
    s = sigmoid(v)
    return s * (1.0 + v * (1.0 - s))


def local_moments(value, mask, inv_ref, stats_ref):
    for stream, lo, hi in parts(value.shape[0]):
        v = value[lo:hi]
        m = mask[lo:hi]
        plain = jnp.sum(v * m, axis=0, keepdims=True)
        gap = (v - plain * inv_ref[stream]) * m
        stats_ref[2 * stream : 2 * stream + 1, :] = plain
        stats_ref[2 * stream + 1 : 2 * stream + 2, :] = jnp.sum(gap * gap, axis=0, keepdims=True)


def normed_of(value, mr_ref, stream):
    return (value - mr_ref[2 * stream : 2 * stream + 1, :]) * mr_ref[2 * stream + 1 : 2 * stream + 2, :]


def shifted(image_ref, tile_ref, dy, dx, tile_rows):
    start = 24 + 2 * MAPW * dy + 2 * dx
    image = image_ref[start : start + IMG_ROWS, :]
    start = 8 + TILE * dy + dx
    tile = tile_ref[start : start + tile_rows, :]
    if dy or dx:
        place = lax.broadcasted_iota(jnp.int32, (tile_rows, 1), 0)
        ty = (place // TILE) % TILE + dy
        tx = place % TILE + dx
        valid = (ty >= 0) & (ty < TILE) & (tx >= 0) & (tx < TILE)
        tile = jnp.where(valid, tile, 0.0)
    return image, tile


def fill_patches(value, image_ref, tile_ref, patch_ref, sign):
    rows = value.shape[0]
    tile_rows = rows - IMG_ROWS
    width = value.shape[1]
    image_ref[0:24, :] = jnp.zeros((24, width), F32)
    image_ref[24 + IMG_ROWS : 48 + IMG_ROWS, :] = jnp.zeros((24, width), F32)
    image_ref[24 : 24 + IMG_ROWS, :] = value[0:IMG_ROWS]
    tile_ref[0:8, :] = jnp.zeros((8, width), F32)
    tile_ref[8 + tile_rows : 16 + tile_rows, :] = jnp.zeros((8, width), F32)
    tile_ref[8 : 8 + tile_rows, :] = value[IMG_ROWS:]
    for tap in range(9):
        dy, dx = tap // 3 - 1, tap % 3 - 1
        image, tile = shifted(image_ref, tile_ref, sign * dy, sign * dx, tile_rows)
        patch_ref[tap, 0:IMG_ROWS, :] = image.astype(BF)
        patch_ref[tap, IMG_ROWS:rows, :] = tile.astype(BF)


def dot(a, b):
    return jnp.dot(a, b, preferred_element_type=F32)


def dot_nt(a, b):
    return lax.dot_general(a, b, (((1,), (1,)), ((), ())), preferred_element_type=F32)


def full(shape):
    zeros = (0,) * len(shape)
    return pl.BlockSpec(shape, lambda k: zeros)


def cols(rows):
    return pl.BlockSpec((rows, CH), lambda k: (0, k))


def smem():
    return pl.BlockSpec(memory_space=pltpu.SMEM)


def call(body, steps, in_specs, out_specs, out_shape, scratch=(), name=None, flops=0, transcendentals=0):
    return pl.pallas_call(
        body,
        grid=(steps,),
        in_specs=in_specs,
        out_specs=out_specs,
        out_shape=out_shape,
        scratch_shapes=list(scratch),
        compiler_params=pltpu.CompilerParams(
            vmem_limit_bytes=VMEM_LIMIT, dimension_semantics=("arbitrary",)
        ),
        cost_estimate=pl.CostEstimate(flops=flops, bytes_accessed=4_000_000, transcendentals=transcendentals),
        name=name,
    )


def sds(shape, dtype=F32):
    return jax.ShapeDtypeStruct(shape, dtype)


def reduce_first(x, w_reduce, mask, inv):
    rows, d_in = x.shape
    mid = w_reduce.shape[2]

    def body(inv_ref, x_ref, w_ref, mask_ref, red_ref, stats_ref):
        k = pl.program_id(0)
        part = dot(x_ref[...], w_ref[0])

        @pl.when(k == 0)
        def _():
            red_ref[...] = part

        @pl.when(k > 0)
        def _():
            red_ref[...] += part

        @pl.when(k == pl.num_programs(0) - 1)
        def _():
            local_moments(red_ref[...], mask_ref[...], inv_ref, stats_ref)

    return call(
        body,
        d_in // CH,
        [smem(), cols(rows), pl.BlockSpec((1, CH, mid), lambda k: (0, k, 0)), full((rows, 1))],
        [full((rows, mid)), full((4, mid))],
        [sds((rows, mid)), sds((4, mid))],
        name="reduce_first",
        flops=2 * rows * d_in * mid,
    )(inv, x, w_reduce, mask)


def spatial_stage(number, red, mr, gain, bias, mask, w9, inv):
    rows, mid = red.shape

    def body(inv_ref, red_ref, mr_ref, gain_ref, bias_ref, mask_ref, w_ref, hid_ref, out_ref, stats_ref, image, tile, patch):
        k = pl.program_id(0)

        @pl.when(k == 0)
        def _():
            pieces = []
            for stream, lo, hi in parts(rows):
                z = normed_of(red_ref[lo:hi, :], mr_ref, stream) * gain_ref[...] + bias_ref[...]
                pieces.append(z * sigmoid(z) * mask_ref[lo:hi, :])
            hidden = jnp.concatenate(pieces, axis=0)
            hid_ref[...] = hidden.astype(BF)
            fill_patches(hidden, image, tile, patch, 1)
            out_ref[...] = jnp.zeros((rows, mid), F32)

        total = out_ref[...]
        for j in range(3):
            total += dot(patch[3 * k + j], w_ref[0, j])
        out_ref[...] = total

        @pl.when(k == 2)
        def _():
            local_moments(out_ref[...], mask_ref[...], inv_ref, stats_ref)

    return call(
        body,
        3,
        [
            smem(),
            full((rows, mid)),
            full((4, mid)),
            full((1, mid)),
            full((1, mid)),
            full((rows, 1)),
            pl.BlockSpec((1, 3, mid, mid), lambda k: (number, k, 0, 0)),
        ],
        [full((rows, mid)), full((rows, mid)), full((4, mid))],
        [sds((rows, mid), BF), sds((rows, mid)), sds((4, mid))],
        [
            pltpu.VMEM((IMG_ROWS + 48, mid), F32),
            pltpu.VMEM((rows - IMG_ROWS + 16, mid), F32),
            pltpu.VMEM((9, rows, mid), BF),
        ],
        name="spatial_stage",
        flops=2 * rows * 9 * mid * mid,
    )(inv, red, mr, gain, bias, mask, w9)


def expand_stage(number, spa, mr, gain, bias, mask, w_expand, inv):
    rows, mid = spa.shape
    d_in = w_expand.shape[2]

    def body(inv_ref, spa_ref, mr_ref, gain_ref, bias_ref, mask_ref, w_ref, hid_ref, out_ref, stats_ref):
        @pl.when(pl.program_id(0) == 0)
        def _():
            for stream, lo, hi in parts(rows):
                z = normed_of(spa_ref[lo:hi, :], mr_ref, stream) * gain_ref[...] + bias_ref[...]
                hid_ref[lo:hi, :] = (z * sigmoid(z) * mask_ref[lo:hi, :]).astype(BF)

        value = dot(hid_ref[...], w_ref[0])
        out_ref[...] = value
        local_moments(value, mask_ref[...], inv_ref, stats_ref)

    return call(
        body,
        d_in // CH,
        [
            smem(),
            full((rows, mid)),
            full((4, mid)),
            full((1, mid)),
            full((1, mid)),
            full((rows, 1)),
            pl.BlockSpec((1, mid, CH), lambda k: (number, 0, k)),
        ],
        [full((rows, mid)), cols(rows), cols(4)],
        [sds((rows, mid), BF), sds((rows, d_in)), sds((4, d_in))],
        name="expand_stage",
        flops=2 * rows * d_in * mid,
    )(inv, spa, mr, gain, bias, mask, w_expand)


def join_stage(number, exp, mr, gain, bias, act, mask, w_reduce, inv):
    rows, d_in = exp.shape
    mid = w_reduce.shape[2]

    def body(inv_ref, exp_ref, mr_ref, gain_ref, bias_ref, act_ref, mask_ref, w_ref, out_ref, low_ref, red_ref, stats_ref):
        k = pl.program_id(0)
        for stream, lo, hi in parts(rows):
            z = (
                normed_of(exp_ref[lo:hi, :], mr_ref, stream) * gain_ref[...]
                + bias_ref[...]
                + act_ref[lo:hi, :].astype(F32)
            )
            out = z * sigmoid(z) * mask_ref[lo:hi, :]
            out_ref[lo:hi, :] = out
            low_ref[lo:hi, :] = out.astype(BF)
        part = dot(low_ref[...], w_ref[0])

        @pl.when(k == 0)
        def _():
            red_ref[...] = part

        @pl.when(k > 0)
        def _():
            red_ref[...] += part

        @pl.when(k == pl.num_programs(0) - 1)
        def _():
            local_moments(red_ref[...], mask_ref[...], inv_ref, stats_ref)

    return call(
        body,
        d_in // CH,
        [
            smem(),
            cols(rows),
            cols(4),
            cols(1),
            cols(1),
            cols(rows),
            full((rows, 1)),
            pl.BlockSpec((1, CH, mid), lambda k: (number, k, 0)),
        ],
        [cols(rows), cols(rows), full((rows, mid)), full((4, mid))],
        [sds((rows, d_in)), sds((rows, d_in), BF), sds((rows, mid)), sds((4, mid))],
        name="join_stage",
        flops=2 * rows * d_in * mid,
        transcendentals=rows * d_in,
    )(inv, exp, mr, gain, bias, act, mask, w_reduce)


def put_sums(stream, pre, normed, sums_ref):
    sums_ref[2 * stream : 2 * stream + 1, :] = jnp.sum(pre, axis=0, keepdims=True)
    sums_ref[2 * stream + 1 : 2 * stream + 2, :] = jnp.sum(pre * normed, axis=0, keepdims=True)


def turn_stage(exp, mr, gain, bias, act, mask, grad):
    rows, d_in = exp.shape

    def body(exp_ref, mr_ref, gain_ref, bias_ref, act_ref, mask_ref, grad_ref, out_ref, pre_ref, sums_ref):
        for stream, lo, hi in parts(rows):
            n = normed_of(exp_ref[lo:hi, :], mr_ref, stream)
            z = n * gain_ref[...] + bias_ref[...] + act_ref[lo:hi, :].astype(F32)
            s = sigmoid(z)
            m = mask_ref[lo:hi, :]
            out_ref[lo:hi, :] = z * s * m
            pre = grad_ref[lo:hi, :].astype(F32) * m * (s * (1.0 + z * (1.0 - s)))
            pre_ref[lo:hi, :] = pre
            put_sums(stream, pre, n, sums_ref)

    return call(
        body,
        d_in // CH,
        [cols(rows), cols(4), cols(1), cols(1), cols(rows), full((rows, 1)), cols(rows)],
        [cols(rows), cols(rows), cols(4)],
        [sds((rows, d_in)), sds((rows, d_in)), sds((4, d_in))],
        name="turn_stage",
        flops=20 * rows * d_in,
        transcendentals=rows * d_in,
    )(exp, mr, gain, bias, act, mask, grad)


def norm_back(pre, normed, share_ref, mr_ref, gain_ref, mask, stream):
    return (
        mask
        * (gain_ref[...] * mr_ref[2 * stream + 1 : 2 * stream + 2, :])
        * (
            pre
            - share_ref[2 * stream : 2 * stream + 1, :]
            - normed * share_ref[2 * stream + 1 : 2 * stream + 2, :]
        )
    )


def back_expand(number, pre3, exp, mr3, share3, gain3, mask, w_expand, spa, mr2, gain2, bias2):
    rows, d_in = exp.shape
    mid = spa.shape[1]

    def body(pre3_ref, exp_ref, mr3_ref, share_ref, gain3_ref, mask_ref, w_ref, spa_ref, mr2_ref, gain2_ref, bias2_ref, ge_ref, pre2_ref, sums_ref):
        k = pl.program_id(0)
        for stream, lo, hi in parts(rows):
            n = normed_of(exp_ref[lo:hi, :], mr3_ref, stream)
            ge_ref[lo:hi, :] = norm_back(
                pre3_ref[lo:hi, :], n, share_ref, mr3_ref, gain3_ref, mask_ref[lo:hi, :], stream
            ).astype(BF)
        part = dot_nt(ge_ref[...], w_ref[0])

        @pl.when(k == 0)
        def _():
            pre2_ref[...] = part

        @pl.when(k > 0)
        def _():
            pre2_ref[...] += part

        @pl.when(k == pl.num_programs(0) - 1)
        def _():
            for stream, lo, hi in parts(rows):
                n2 = normed_of(spa_ref[lo:hi, :], mr2_ref, stream)
                z2 = n2 * gain2_ref[...] + bias2_ref[...]
                pre2 = pre2_ref[lo:hi, :] * mask_ref[lo:hi, :] * slope(z2)
                pre2_ref[lo:hi, :] = pre2
                put_sums(stream, pre2, n2, sums_ref)

    return call(
        body,
        d_in // CH,
        [
            cols(rows),
            cols(rows),
            cols(4),
            cols(4),
            cols(1),
            full((rows, 1)),
            pl.BlockSpec((1, mid, CH), lambda k: (number, 0, k)),
            full((rows, mid)),
            full((4, mid)),
            full((1, mid)),
            full((1, mid)),
        ],
        [cols(rows), full((rows, mid)), full((4, mid))],
        [sds((rows, d_in), BF), sds((rows, mid)), sds((4, mid))],
        name="back_expand",
        flops=2 * rows * d_in * mid,
    )(pre3, exp, mr3, share3, gain3, mask, w_expand, spa, mr2, gain2, bias2)


def back_spatial(number, pre2, spa, mr2, share2, gain2, mask, w9, red, mr1, gain1, bias1):
    rows, mid = spa.shape

    def body(pre2_ref, spa_ref, mr2_ref, share_ref, gain2_ref, mask_ref, w_ref, red_ref, mr1_ref, gain1_ref, bias1_ref, gs_ref, pre1_ref, sums_ref, image, tile, patch):
        k = pl.program_id(0)

        @pl.when(k == 0)
        def _():
            pieces = []
            for stream, lo, hi in parts(rows):
                n = normed_of(spa_ref[lo:hi, :], mr2_ref, stream)
                pieces.append(
                    norm_back(pre2_ref[lo:hi, :], n, share_ref, mr2_ref, gain2_ref, mask_ref[lo:hi, :], stream)
                )
            value = jnp.concatenate(pieces, axis=0)
            gs_ref[...] = value.astype(BF)
            fill_patches(value, image, tile, patch, -1)
            pre1_ref[...] = jnp.zeros((rows, mid), F32)

        total = pre1_ref[...]
        for j in range(3):
            total += dot_nt(patch[3 * k + j], w_ref[0, j])
        pre1_ref[...] = total

        @pl.when(k == 2)
        def _():
            for stream, lo, hi in parts(rows):
                n1 = normed_of(red_ref[lo:hi, :], mr1_ref, stream)
                z1 = n1 * gain1_ref[...] + bias1_ref[...]
                pre1 = pre1_ref[lo:hi, :] * mask_ref[lo:hi, :] * slope(z1)
                pre1_ref[lo:hi, :] = pre1
                put_sums(stream, pre1, n1, sums_ref)

    return call(
        body,
        3,
        [
            full((rows, mid)),
            full((rows, mid)),
            full((4, mid)),
            full((4, mid)),
            full((1, mid)),
            full((rows, 1)),
            pl.BlockSpec((1, 3, mid, mid), lambda k: (number, k, 0, 0)),
            full((rows, mid)),
            full((4, mid)),
            full((1, mid)),
            full((1, mid)),
        ],
        [full((rows, mid)), full((rows, mid)), full((4, mid))],
        [sds((rows, mid), BF), sds((rows, mid)), sds((4, mid))],
        [
            pltpu.VMEM((IMG_ROWS + 48, mid), F32),
            pltpu.VMEM((rows - IMG_ROWS + 16, mid), F32),
            pltpu.VMEM((9, rows, mid), BF),
        ],
        name="back_spatial",
        flops=2 * rows * 9 * mid * mid,
    )(pre2, spa, mr2, share2, gain2, mask, w9, red, mr1, gain1, bias1)


def back_reduce(number, pre1, red, mr1, share1, gain1, mask, w_reduce, pre3, below):
    rows, mid = red.shape
    d_in = pre3.shape[1]

    def head(k, pre1_ref, red_ref, mr1_ref, share_ref, gain1_ref, mask_ref, gr_ref):
        @pl.when(k == 0)
        def _():
            for stream, lo, hi in parts(rows):
                n = normed_of(red_ref[lo:hi, :], mr1_ref, stream)
                gr_ref[lo:hi, :] = norm_back(
                    pre1_ref[lo:hi, :], n, share_ref, mr1_ref, gain1_ref, mask_ref[lo:hi, :], stream
                ).astype(BF)

    specs = [
        full((rows, mid)),
        full((rows, mid)),
        full((4, mid)),
        full((4, mid)),
        full((1, mid)),
        full((rows, 1)),
        pl.BlockSpec((1, CH, mid), lambda k: (number, k, 0)),
        cols(rows),
    ]
    args = [pre1, red, mr1, share1, gain1, mask, w_reduce, pre3]
    if below is None:

        def body(pre1_ref, red_ref, mr1_ref, share_ref, gain1_ref, mask_ref, w_ref, pre3_ref, gr_ref, out_ref):
            head(pl.program_id(0), pre1_ref, red_ref, mr1_ref, share_ref, gain1_ref, mask_ref, gr_ref)
            out_ref[...] = pre3_ref[...] + dot_nt(gr_ref[...], w_ref[0])

        return call(
            body,
            d_in // CH,
            specs,
            [full((rows, mid)), cols(rows)],
            [sds((rows, mid), BF), sds((rows, d_in))],
            name="back_reduce_last",
            flops=2 * rows * d_in * mid,
        )(*args)

    def body(pre1_ref, red_ref, mr1_ref, share_ref, gain1_ref, mask_ref, w_ref, pre3_ref, exp_ref, mr3_ref, gain3_ref, bias3_ref, act_ref, gr_ref, out_ref, sums_ref):
        head(pl.program_id(0), pre1_ref, red_ref, mr1_ref, share_ref, gain1_ref, mask_ref, gr_ref)
        grad = pre3_ref[...] + dot_nt(gr_ref[...], w_ref[0])
        for stream, lo, hi in parts(rows):
            n = normed_of(exp_ref[lo:hi, :], mr3_ref, stream)
            z = n * gain3_ref[...] + bias3_ref[...] + act_ref[lo:hi, :].astype(F32)
            pre = grad[lo:hi] * mask_ref[lo:hi, :] * slope(z)
            out_ref[lo:hi, :] = pre
            put_sums(stream, pre, n, sums_ref)

    return call(
        body,
        d_in // CH,
        specs + [cols(rows), cols(4), cols(1), cols(1), cols(rows)],
        [full((rows, mid)), cols(rows), cols(4)],
        [sds((rows, mid), BF), sds((rows, d_in)), sds((4, d_in))],
        name="back_reduce",
        flops=2 * rows * d_in * mid,
        transcendentals=rows * d_in,
    )(*args, *below)


def weight_dot(a, b):
    return lax.dot_general(a, b, (((0,), (0,)), ((), ())), preferred_element_type=F32)


def patches_xla(value):
    rows, width = value.shape
    image = value[:IMG_ROWS].reshape(MAP, MAPW, SLOTS, width)
    tile = value[IMG_ROWS:].reshape(-1, TILE, TILE, width)
    image = jnp.pad(image, ((1, 1), (1, 1), (0, 0), (0, 0)))
    tile = jnp.pad(tile, ((0, 0), (1, 1), (1, 1), (0, 0)))
    taps = []
    for i in range(3):
        for j in range(3):
            a = image[i : i + MAP, j : j + MAPW].reshape(IMG_ROWS, width)
            b = tile[:, i : i + TILE, j : j + TILE].reshape(-1, width)
            taps.append(jnp.concatenate([a, b], axis=0))
    return jnp.stack(taps, axis=1)


def to_rows(image, tile, rows):
    width = image.shape[-1]
    image = jnp.transpose(image, (1, 2, 0, 3))
    image = jnp.pad(image, ((0, 0), (0, 1), (0, 0), (0, 0))).reshape(IMG_ROWS, width)
    tile = tile.reshape(-1, width)
    pad = jnp.zeros((rows - IMG_ROWS - tile.shape[0], width), tile.dtype)
    return jnp.concatenate([image, tile, pad], axis=0)


def from_rows(value, tiles):
    width = value.shape[1]
    image = value[:IMG_ROWS].reshape(MAP, MAPW, SLOTS, width)[:, :MAP]
    image = jnp.transpose(image, (2, 0, 1, 3))
    tile = value[IMG_ROWS : IMG_ROWS + tiles * 4].reshape(tiles, TILE, TILE, width)
    return image, tile


def row_mask(map_sizes, rows):
    row = jnp.arange(MAP)
    col = jnp.arange(MAPW)
    inside = (row[:, None, None] < map_sizes[None, None, :]) & (col[None, :, None] < map_sizes[None, None, :])
    image = inside.astype(F32).reshape(IMG_ROWS)
    tile = jnp.repeat((map_sizes > 0).astype(F32), PIECES * TILE * TILE)
    pad = jnp.zeros((rows - IMG_ROWS - tile.shape[0],), F32)
    return jnp.concatenate([image, tile, pad])[:, None]


def per_device(
    grid,
    images,
    tile_maps,
    map_sizes,
    w_reduce,
    w_spatial,
    w_expand,
    gain_mid,
    bias_mid,
    gain_out,
    bias_out,
    grad_images,
    grad_tiles,
):
    tiles = tile_maps.shape[0]
    rows = -(-(IMG_ROWS + tiles * TILE * TILE) // 16) * 16
    mid = w_reduce.shape[2]
    mask = row_mask(map_sizes, rows)
    counts = jnp.stack([jnp.sum(mask[:IMG_ROWS]), jnp.sum(mask[IMG_ROWS:])])
    inv = 1.0 / jnp.maximum(counts, 1.0)
    sync = Sync(grid, counts)
    w9 = w_spatial.reshape(BLOCKS, 9, mid, mid)
    x = to_rows(images, tile_maps, rows)
    grad = to_rows(grad_images, grad_tiles, rows)

    def row(table, *at):
        return table[at][None]

    acts, lows, reds, spas, exps = [x], [x], [], [], []
    mr1, mr2, mr3, hid1, hid2 = [], [], [], [], []
    red, stats = reduce_first(x, w_reduce, mask, inv)
    for b in range(BLOCKS):
        reds.append(red)
        mr1.append(sync.moments(stats))
        hidden, spa, stats = spatial_stage(
            b, red, mr1[b], row(gain_mid, b, 0), row(bias_mid, b, 0), mask, w9, inv
        )
        hid1.append(hidden)
        spas.append(spa)
        mr2.append(sync.moments(stats))
        hidden, exp, stats = expand_stage(
            b, spa, mr2[b], row(gain_mid, b, 1), row(bias_mid, b, 1), mask, w_expand, inv
        )
        hid2.append(hidden)
        exps.append(exp)
        mr3.append(sync.moments(stats))
        if b + 1 < BLOCKS:
            out, low, red, stats = join_stage(
                b + 1, exp, mr3[b], row(gain_out, b), row(bias_out, b), acts[b], mask, w_reduce, inv
            )
            acts.append(out)
            lows.append(low)
    last = BLOCKS - 1
    out, pre3, sums3 = turn_stage(
        exps[last], mr3[last], row(gain_out, last), row(bias_out, last), acts[last], mask, grad
    )

    g_reduce, g_spatial, g_expand = [None] * BLOCKS, [None] * BLOCKS, [None] * BLOCKS
    g_gain, g_bias = [[None, None] for _ in range(BLOCKS)], [[None, None] for _ in range(BLOCKS)]
    g_gain3, g_bias3 = [None] * BLOCKS, [None] * BLOCKS
    for b in reversed(range(BLOCKS)):
        total = sync.sums(sums3)
        g_gain3[b], g_bias3[b] = total[1] + total[3], total[0] + total[2]
        ge, pre2, sums2 = back_expand(
            b, pre3, exps[b], mr3[b], sync.shares(total), row(gain_out, b), mask, w_expand,
            spas[b], mr2[b], row(gain_mid, b, 1), row(bias_mid, b, 1),
        )
        g_expand[b] = weight_dot(hid2[b], ge)
        total = sync.sums(sums2)
        g_gain[b][1], g_bias[b][1] = total[1] + total[3], total[0] + total[2]
        gs, pre1, sums1 = back_spatial(
            b, pre2, spas[b], mr2[b], sync.shares(total), row(gain_mid, b, 1), mask, w9,
            reds[b], mr1[b], row(gain_mid, b, 0), row(bias_mid, b, 0),
        )
        g_spatial[b] = weight_dot(patches_xla(hid1[b]).reshape(rows, 9 * mid), gs).reshape(3, 3, mid, mid)
        total = sync.sums(sums1)
        g_gain[b][0], g_bias[b][0] = total[1] + total[3], total[0] + total[2]
        below = None
        if b > 0:
            below = (exps[b - 1], mr3[b - 1], row(gain_out, b - 1), row(bias_out, b - 1), acts[b - 1])
        result = back_reduce(
            b, pre1, reds[b], mr1[b], sync.shares(total), row(gain_mid, b, 0), mask, w_reduce, pre3, below
        )
        g_reduce[b] = weight_dot(lows[b], result[0])
        if b > 0:
            pre3, sums3 = result[1], result[2]
        else:
            grad_in = result[1]

    shards = lax.psum(
        (
            lax.psum_scatter(jnp.stack(g_reduce), "narrow", scatter_dimension=1, tiled=True),
            lax.psum_scatter(jnp.stack(g_spatial), "narrow", scatter_dimension=3, tiled=True),
            lax.psum_scatter(jnp.stack(g_expand), "narrow", scatter_dimension=1, tiled=True),
        ),
        "wide",
    )
    out_images, out_tiles = from_rows(out, tiles)
    in_images, in_tiles = from_rows(grad_in, tiles)
    return (
        out_images,
        out_tiles,
        in_images,
        in_tiles,
        shards[0],
        shards[1],
        shards[2],
        jnp.stack([jnp.stack(g) for g in g_gain]),
        jnp.stack([jnp.stack(g) for g in g_bias]),
        jnp.stack(g_gain3),
        jnp.stack(g_bias3),
    )


def solution(mesh):
    both = ("wide", "narrow")
    batch = P(both, None, None, None)
    grid = Grid(mesh.shape["wide"], mesh.shape["narrow"])
    return jax.shard_map(
        functools.partial(per_device, grid),
        mesh=mesh,
        in_specs=(batch, batch, P(both), P(), P(), P(), P(), P(), P(), P(), batch, batch),
        out_specs=(
            batch,
            batch,
            batch,
            batch,
            P(None, "narrow", None),
            P(None, None, None, "narrow", None),
            P(None, "narrow", None),
            P(),
            P(),
            P(),
            P(),
        ),
        check_vma=False,
    )
```

time: 1610 us -> 1110 us (0.69)
  blocking collectives: 739 us -> 0 us
  waiting for transfers between devices: 570 us -> 734 us
  starting transfers between devices: 0.46 us -> 97.6 us
  matrix products: 84.1 us -> 6.01 us
  Pallas kernels: 0 us -> 51.8 us
    psum x18 -> x0, blocking collectives: 739 us -> none  [the longest x6 253 us: norm_back(): lax.psum((channel_sums(pre_grads[0]), channel_sums(pre_grads[0] * normed[...]
    ppermute x0 -> x84, starting transfers between devices: none -> 97.4 us  [swap(): return lax.ppermute(value, AXES, pairs)]
    reduce_scatter x3, waiting for transfers between devices: 446 us -> 536 us  [the longest x1 317 us: per_device(): lax.psum_scatter(jnp.stack(g_spatial), 'narrow', scatter_dimension=3, til...]
    dot_general x36 -> x6, matrix products: 84.1 us -> 6.01 us  [weight_dot(): lax.dot_general(a, b, (((0,), (0,)), ((), ())), preferred_element_type=F32)]
    ppermute x0 -> x84, waiting for transfers between devices: none -> 71.2 us  [swap(): return lax.ppermute(value, AXES, pairs)]
    pallas_call x0 -> x13, Pallas kernels: none -> 51.8 us  [the longest x2 10.4 us: back_spatial(): call(body, 3, [full((rows, mid)), full((rows, mid)), full((4, mid)), full...]
    add x26 -> x41, other arithmetic: 31.4 us -> 65.8 us  [the longest x18 62.8 us: merge_moments(): square = square + n[stream] * gap * gap]
    rsqrt x11 -> x12, other arithmetic: 8.55 us -> 39.6 us  [moments(): out.append(lax.rsqrt(value[2 * stream + 1] / self.total[stream] + EPS))]
  transfers between devices with their start and end apart: 4 -> 88, of which waited for: 3 -> 82; matrix products, arithmetic and copies ran while one was open for 5% -> 4% of each run, Pallas kernels for 0% -> 1%
where the time goes in v1:
time: 1110 us; the launch traced here: 1100 us
  waiting for transfers between devices  734 us (66%)
  other arithmetic  139 us (13%)
  starting transfers between devices  97.6 us (9%)
  Pallas kernels  51.8 us (5%)
  local copies, waits for them, and re-layouts  45.5 us (4%)
  between operations  28.7 us (3%)
    reduce_scatter x1, waiting for transfers between devices, per_device(): lax.psum_scatter(jnp.stack(g_spatial), 'narrow', scatter_dimension=3, til...  317 us
    reduce_scatter x1, waiting for transfers between devices, per_device(): lax.psum_scatter(jnp.stack(g_reduce), 'narrow', scatter_dimension=1, tile...  148 us
    psum x1, waiting for transfers between devices, per_device(): lax.psum((lax.psum_scatter(jnp.stack(g_reduce), 'narrow', scatter_dimensi...  127 us
    ppermute x84, starting transfers between devices, swap(): return lax.ppermute(value, AXES, pairs)  97.4 us
    reduce_scatter x1, waiting for transfers between devices, per_device(): lax.psum_scatter(jnp.stack(g_expand), 'narrow', scatter_dimension=1, tile...  71.5 us
    ppermute x84, waiting for transfers between devices, swap(): return lax.ppermute(value, AXES, pairs)  71.2 us
    add x18, other arithmetic, merge_moments(): square = square + n[stream] * gap * gap  62.8 us
    rsqrt x12, other arithmetic, moments(): out.append(lax.rsqrt(value[2 * stream + 1] / self.total[stream] + EPS))  39.6 us
  transfers between devices with their start and end apart: 88, of which 82 were waited for; matrix products, arithmetic and copies ran while one was open for 4% of the time, Pallas kernels for 1%

profile of v1, /device:TPU:0, one launch (start us, length us, event | category | flops | bytes accessed | tf_op | source)
XLA Modules:
  0.0 1102.2 jit_solution(10469384789669990460)
XLA Ops:
  26.9 3.9 fusion.60
  31.0 3.5 collective-permute-start.3
  45.5 3.3 fusion.70
  48.8 3.2 fusion.66
  52.1 3.7 collective-permute-start.6
  66.7 3.3 add_rsqrt_fusion.10
  73.3 4.6 spatial_stage.2
  79.1 3.9 fusion.80
  88.9 3.3 fusion.90
  101.7 3.3 add_rsqrt_fusion.8
  105.0 3.2 add_rsqrt_fusion.9
  108.3 3.5 expand_stage.2
  113.1 4.0 fusion.20
  123.9 3.4 fusion.30
  127.2 3.3 fusion.26
  138.1 3.4 add_rsqrt_fusion.2
  141.6 3.3 add_rsqrt_fusion.3
  144.9 3.9 join_stage.1
  150.1 3.9 fusion.100
  159.9 3.3 fusion.110
  172.6 3.3 add_rsqrt_fusion.6
  175.9 3.2 add_rsqrt_fusion.7
  179.2 4.6 spatial_stage.3
  185.1 3.9 fusion.120
  195.5 3.3 fusion.130
  209.2 3.3 add_rsqrt_fusion.4
  212.5 3.2 add_rsqrt_fusion.5
  215.8 3.5 expand_stage.3
  220.6 4.0 fusion.40
  230.7 3.4 fusion.50
  234.1 3.3 fusion.46
  244.1 3.4 add_rsqrt_fusion
  247.5 3.3 add_rsqrt_fusion.1
  250.8 3.2 turn_stage.1
  270.7 4.0 back_expand.2
  289.3 5.0 back_spatial.2
  309.8 4.1 back_reduce.1
  329.3 3.8 back_expand.3
  333.9 4.1 pad_maximum_fusion.2
  354.7 5.4 back_spatial.3
  375.0 3.4 back_reduce_last.1
  379.6 4.3 pad_maximum_fusion.1
  403.8 7.3 pad_maximum_fusion
  411.2 71.5 %reduce-scatter.8.cloned.1.call-done = f32[2,128,2048]{2,1,0:T(8,128)} async-done(((f32[2,512,2048]{2,1,0:T(8,128)}), f32[2,128,2048]{2,1,0:T(8,128)}) %reduce-scatter.8.cloned.1.call-update) | async-done | bytes 2097168 | tf_op jit(solution)/shard_map/reduce_scatter | solution.py:751
  482.8 147.6 %reduce-scatter.4.cloned.1.call-done = f32[2,512,512]{2,1,0:T(8,128)} async-done(((f32[2,2048,512]{2,1,0:T(8,128)}), f32[2,512,512]{2,1,0:T(8,128)}) %reduce-scatter.4.cloned.1.call-update) | async-done | bytes 2097168 | tf_op jit(solution)/shard_map/reduce_scatter | solution.py:749
  630.4 316.9 %reduce-scatter.6.cloned.1.call-done = f32[2,3,3,128,512]{4,3,2,1,0:T(8,128)} async-done(((f32[2,3,3,512,512]{4,3,2,1,0:T(8,128)}), f32[2,3,3,128,512]{4,3,2,1,0:T(8,128)}) %reduce-scatter.6.cloned.1.call-update) | async-done | bytes 4718608 | tf_op jit(solution)/shard_map/reduce_scatter | solution.py:750
  959.0 126.7 %all-reduce.10.cloned.1.call-done = (f32[2,512,512]{2,1,0:T(8,128)}, f32[2,3,3,128,512]{4,3,2,1,0:T(8,128)}, f32[2,128,2048]{2,1,0:T(8,128)}) async-done(((f32[2,512,512]{2,1,0:T(8,128)}, f32[2,3,3,128,512]{4,3,2,1,0:T(8,128)}, f32[2,128,2048]{2,1,0:T(8,128)}), (f32[2,512,512]{2,1,0:T(8,128)}, f32[2,3,3,128,512]{4,3,2,1,0:T(8,128)}, f32[2,128,2048]{2,1,0:T(8,128)})) %all-reduce.10.cloned.1.call-update) | async-done | bytes 8912912 | tf_op jit(solution)/shard_map/psum | solution.py:747
  1088.7 5.4 copy.70
  (442 shorter events, 243.8 us)
Async XLA Ops:
  7.2 475.6 %reduce-scatter.8.cloned.1.call-start = ((), (), s32[]{:S(2)}) async-start(), calls=%async_computation.5 | async-start | bytes 10485760 | tf_op jit(solution)/shard_map/reduce_scatter | solution.py:751
  31.0 5.5 collective-permute-start.3
  35.0 5.1 collective-permute-start.1
  52.1 5.8 collective-permute-start.6
  55.8 4.7 collective-permute-start.5
  55.9 6.5 collective-permute-start.4
  83.1 4.6 collective-permute-start.10
  95.5 5.5 collective-permute-start.13
  97.1 4.5 collective-permute-start.12
  97.1 4.5 collective-permute-start.11
  117.1 4.9 collective-permute-start.17
  130.5 6.1 collective-permute-start.20
  132.8 5.0 collective-permute-start.19
  134.0 4.2 collective-permute-start.18
  154.0 4.6 collective-permute-start.24
  166.4 5.5 collective-permute-start.27
  167.9 4.6 collective-permute-start.26
  189.0 4.6 collective-permute-start.31
  202.1 5.5 collective-permute-start.34
  204.4 4.5 collective-permute-start.33
  224.6 4.9 collective-permute-start.38
  237.4 5.8 collective-permute-start.41
  238.9 4.8 collective-permute-start.40
  239.9 4.2 collective-permute-start.39
  256.4 5.0 collective-permute-start.45
  263.4 6.1 collective-permute-start.48
  265.8 4.0 collective-permute-start.46
  265.8 4.8 collective-permute-start.47
  276.0 4.5 collective-permute-start.52
  281.6 5.5 collective-permute-start.55
  284.2 4.5 collective-permute-start.54
  295.6 4.5 collective-permute-start.59
  302.3 5.5 collective-permute-start.62
  304.6 4.5 collective-permute-start.61
  315.2 4.9 collective-permute-start.66
  321.2 6.1 collective-permute-start.69
  323.5 4.0 collective-permute-start.67
  323.8 4.8 collective-permute-start.68
  338.0 292.3 %reduce-scatter.4.cloned.1.call-start = ((), (), s32[]{:S(2)}) async-start(), calls=%async_computation.3 | async-start | bytes 10485760 | tf_op jit(solution)/shard_map/reduce_scatter | solution.py:749
  339.3 4.5 collective-permute-start.73
  346.0 5.7 collective-permute-start.76
  348.4 4.8 collective-permute-start.75
  361.4 4.5 collective-permute-start.80
  366.9 5.9 collective-permute-start.83
  369.1 4.7 collective-permute-start.81
  369.5 4.9 collective-permute-start.82
  383.9 563.4 %reduce-scatter.6.cloned.1.call-start = ((), (), s32[]{:S(2)}) async-start(), calls=%async_computation.4 | async-start | bytes 23592960 | tf_op jit(solution)/shard_map/reduce_scatter | solution.py:750
  411.2 674.5 %all-reduce.10.cloned.1.call-start = ((), (), s32[]{:S(2)}) async-start(), calls=%async_computation.6 | async-start | bytes 17825792 | tf_op jit(solution)/shard_map/psum | solution.py:747
  (82 other events, 606.2 us)
Sparse Core Ops, SparseCore 0:
  338.2 144.5 reduce-scatter.7
  485.1 145.1 reduce-scatter.3
  632.7 314.4 reduce-scatter.5
  951.7 133.9 all-reduce.9

commit v2 on v1

v2 whole, which is shorter than its diff:
```python
import functools

import jax
import jax.numpy as jnp
from jax import lax
from jax.experimental import pallas as pl
from jax.experimental.pallas import tpu as pltpu
from jax.sharding import PartitionSpec as P

BLOCKS = 2
MAP = 7
MAPW = 8
TILE = 2
PIECES = 9
SLOTS = 2
IMG_ROWS = MAP * MAPW * SLOTS
EPS = 1e-05
CH = 512
BF = jnp.bfloat16
F32 = jnp.float32
VMEM_LIMIT = 48 * 1024 * 1024
AXES = ("wide", "narrow")


class Grid:
    def __init__(self, wide, narrow):
        chips = wide // 2
        side = 1
        while side * side < chips:
            side *= 2
        self.y, self.x, self.c, self.z = chips // side, side, 2, narrow

    def index(self):
        wide = lax.axis_index("wide")
        core = wide % 2
        chip = wide // 2
        return chip // self.x, chip % self.x, core, lax.axis_index("narrow")

    def swap(self, value, dy=0, dx=0, dc=0, dz=0):
        pairs = []
        for y in range(self.y):
            for x in range(self.x):
                for c in range(self.c):
                    for z in range(self.z):
                        src = ((y * self.x + x) * 2 + c) * self.z + z
                        dst = (((y ^ dy) * self.x + (x ^ dx)) * 2 + (c ^ dc)) * self.z + (z ^ dz)
                        pairs.append((src, dst))
        return lax.ppermute(value, AXES, pairs)

    def phases(self):
        found = [[dict(dc=1)]]
        step = 1
        while step < max(self.x, self.y):
            group = []
            for dy in (0, step):
                for dx in (0, step):
                    if (dy or dx) and dy < self.y and dx < self.x:
                        group.append(dict(dy=dy, dx=dx))
            found.append(group)
            step *= 2
        self.far_groups = found[2:]
        found.append([dict(dz=k) for k in range(1, min(self.z, 4))])
        step = 4
        while step < self.z:
            found.append([dict(dz=step)])
            step *= 2
        return found

    def far(self):
        self.phases()
        return self.far_groups


def exchange(grid, payload, join):
    groups = grid.phases()
    for number, group in enumerate(groups):
        members = [payload] + [grid.swap(payload, **step) for step in group]
        if number + 1 < len(groups):
            payload = join(members)
    return members


def add_members(members):
    return sum(members[1:], members[0])


def read_moments(members, stream, width):
    at = slice(2 * stream, 2 * stream + 1)
    counts = [m[at, width : width + 1] for m in members]
    sums = [m[at, 0:width] for m in members]
    count = sum(counts[1:], counts[0])
    plain = sum(sums[1:], sums[0])
    mean = plain / count
    square = None
    for m, n, v in zip(members, counts, sums):
        gap = v / jnp.maximum(n, 1.0) - mean
        term = m[2 * stream + 1 : 2 * stream + 2, 0:width] + n * (gap * gap)
        square = term if square is None else square + term
    return count, plain, mean, square


def join_moments(members):
    width = members[0].shape[1] - 128
    size = len(members)

    def body(*refs):
        out_ref = refs[size]
        for stream in range(2):
            count, plain, _, square = read_moments(refs[:size], stream, width)
            out_ref[2 * stream : 2 * stream + 1, 0:width] = plain
            out_ref[2 * stream + 1 : 2 * stream + 2, 0:width] = square
            out_ref[2 * stream : 2 * stream + 2, width : width + 128] = jnp.broadcast_to(count, (2, 128))

    return pl.pallas_call(body, out_shape=sds((4, width + 128)), name="join_moments")(*members)


def put_statistics(members, out_ref):
    width = out_ref.shape[1]
    for stream in range(2):
        count, _, mean, square = read_moments(members, stream, width)
        out_ref[2 * stream : 2 * stream + 1, :] = mean
        out_ref[2 * stream + 1 : 2 * stream + 2, :] = lax.rsqrt(square / count + EPS)
        out_ref[4 + stream : 5 + stream, :] = jnp.broadcast_to(1.0 / count, (1, width))
    out_ref[6:8, :] = jnp.zeros((2, width), F32)


def put_shares(members, mr_ref, share_ref, both_ref):
    total = members[0][...]
    for m in members[1:]:
        total += m[...]
    for stream in range(2):
        inv = mr_ref[4 + stream : 5 + stream, :]
        share_ref[2 * stream : 2 * stream + 2, :] = total[2 * stream : 2 * stream + 2] * inv
    both_ref[...] = total[0:2] + total[2:4]


def parts(rows):
    return ((0, 0, IMG_ROWS), (1, IMG_ROWS, rows))


def sigmoid(v):
    return 0.5 * jnp.tanh(0.5 * v) + 0.5


def slope(v):
    s = sigmoid(v)
    return s * (1.0 + v * (1.0 - s))


def local_moments(value, mask_ref, stats_ref, at):
    width = value.shape[1]
    for stream, lo, hi in parts(value.shape[0]):
        v = value[lo:hi]
        m = mask_ref[lo:hi, :]
        count = jnp.sum(m, axis=0, keepdims=True)
        plain = jnp.sum(v * m, axis=0, keepdims=True)
        gap = (v - plain / jnp.maximum(count, 1.0)) * m
        stats_ref[2 * stream : 2 * stream + 1, pl.ds(at, width)] = plain
        stats_ref[2 * stream + 1 : 2 * stream + 2, pl.ds(at, width)] = jnp.sum(gap * gap, axis=0, keepdims=True)
        last = stats_ref.shape[1] - 128
        stats_ref[2 * stream : 2 * stream + 2, last : last + 128] = jnp.broadcast_to(count, (2, 128))


def normed_of(value, mr_ref, stream):
    return (value - mr_ref[2 * stream : 2 * stream + 1, :]) * mr_ref[2 * stream + 1 : 2 * stream + 2, :]


def shifted(image_ref, tile_ref, dy, dx, tile_rows):
    start = 24 + 2 * MAPW * dy + 2 * dx
    image = image_ref[start : start + IMG_ROWS, :]
    start = 8 + TILE * dy + dx
    tile = tile_ref[start : start + tile_rows, :]
    if dy or dx:
        place = lax.broadcasted_iota(jnp.int32, (tile_rows, 1), 0)
        ty = (place // TILE) % TILE + dy
        tx = place % TILE + dx
        valid = (ty >= 0) & (ty < TILE) & (tx >= 0) & (tx < TILE)
        tile = jnp.where(valid, tile, 0.0)
    return image, tile


def fill_patches(value, image_ref, tile_ref, patch_ref, sign):
    rows = value.shape[0]
    tile_rows = rows - IMG_ROWS
    width = value.shape[1]
    image_ref[0:24, :] = jnp.zeros((24, width), F32)
    image_ref[24 + IMG_ROWS : 48 + IMG_ROWS, :] = jnp.zeros((24, width), F32)
    image_ref[24 : 24 + IMG_ROWS, :] = value[0:IMG_ROWS]
    tile_ref[0:8, :] = jnp.zeros((8, width), F32)
    tile_ref[8 + tile_rows : 16 + tile_rows, :] = jnp.zeros((8, width), F32)
    tile_ref[8 : 8 + tile_rows, :] = value[IMG_ROWS:]
    for tap in range(9):
        dy, dx = tap // 3 - 1, tap % 3 - 1
        image, tile = shifted(image_ref, tile_ref, sign * dy, sign * dx, tile_rows)
        patch_ref[tap, 0:IMG_ROWS, :] = image.astype(BF)
        patch_ref[tap, IMG_ROWS:rows, :] = tile.astype(BF)


def dot(a, b):
    return jnp.dot(a, b, preferred_element_type=F32)


def dot_nt(a, b):
    return lax.dot_general(a, b, (((1,), (1,)), ((), ())), preferred_element_type=F32)


def full(shape):
    zeros = (0,) * len(shape)
    return pl.BlockSpec(shape, lambda k: zeros)


def cols(rows):
    return pl.BlockSpec((rows, CH), lambda k: (0, k))


def smem():
    return pl.BlockSpec(memory_space=pltpu.SMEM)


def call(body, steps, in_specs, out_specs, out_shape, scratch=(), name=None, flops=0, transcendentals=0):
    return pl.pallas_call(
        body,
        grid=(steps,),
        in_specs=in_specs,
        out_specs=out_specs,
        out_shape=out_shape,
        scratch_shapes=list(scratch),
        compiler_params=pltpu.CompilerParams(
            vmem_limit_bytes=VMEM_LIMIT, dimension_semantics=("arbitrary",)
        ),
        cost_estimate=pl.CostEstimate(flops=flops, bytes_accessed=4_000_000, transcendentals=transcendentals),
        name=name,
    )


def sds(shape, dtype=F32):
    return jax.ShapeDtypeStruct(shape, dtype)


def rounded(value):
    return value.astype(BF).astype(F32)


def payload_shape(width):
    return sds((4, width + 128))


def reduce_first(x, w_reduce, mask):
    rows, d_in = x.shape
    mid = w_reduce.shape[2]

    def body(x_ref, w_ref, mask_ref, red_ref, stats_ref):
        k = pl.program_id(0)
        part = dot(x_ref[...], w_ref[0])

        @pl.when(k == 0)
        def _():
            red_ref[...] = part

        @pl.when(k > 0)
        def _():
            red_ref[...] += part

        @pl.when(k == pl.num_programs(0) - 1)
        def _():
            local_moments(red_ref[...], mask_ref, stats_ref, 0)

    return call(
        body,
        d_in // CH,
        [cols(rows), pl.BlockSpec((1, CH, mid), lambda k: (0, k, 0)), full((rows, 1))],
        [full((rows, mid)), full((4, mid + 128))],
        [sds((rows, mid)), payload_shape(mid)],
        name="reduce_first",
        flops=2 * rows * d_in * mid,
    )(x, w_reduce, mask)


def spatial_stage(number, red, members, gain, bias, mask, w9, select):
    rows, mid = red.shape
    size = len(members)

    def body(red_ref, gain_ref, bias_ref, mask_ref, w_ref, select_ref, *refs):
        got, (mr_ref, keep_ref, send_ref, out_ref, stats_ref, image, tile, patch) = refs[:size], refs[size:]
        k = pl.program_id(0)

        @pl.when(k == 0)
        def _():
            put_statistics(got, mr_ref)
            pieces = []
            for stream, lo, hi in parts(rows):
                z = normed_of(red_ref[lo:hi, :], mr_ref, stream) * gain_ref[...] + bias_ref[...]
                pieces.append(z * sigmoid(z) * mask_ref[lo:hi, :])
            hidden = jnp.concatenate(pieces, axis=0)
            fill_patches(hidden, image, tile, patch, 1)
            halves = dot(hidden.astype(BF), select_ref[...])
            keep_ref[...] = halves[:, : mid // 2]
            send_ref[...] = halves[:, mid // 2 :]
            out_ref[...] = jnp.zeros((rows, mid), F32)

        total = out_ref[...]
        for j in range(3):
            total += dot(patch[3 * k + j], w_ref[0, j])
        out_ref[...] = total

        @pl.when(k == 2)
        def _():
            local_moments(out_ref[...], mask_ref, stats_ref, 0)

    return call(
        body,
        3,
        [
            full((rows, mid)),
            full((1, mid)),
            full((1, mid)),
            full((rows, 1)),
            pl.BlockSpec((1, 3, mid, mid), lambda k: (number, k, 0, 0)),
            full((mid, mid)),
        ]
        + [full((4, mid + 128))] * size,
        [
            full((8, mid)),
            full((rows, mid // 2)),
            full((rows, mid // 2)),
            full((rows, mid)),
            full((4, mid + 128)),
        ],
        [
            sds((8, mid)),
            sds((rows, mid // 2)),
            sds((rows, mid // 2)),
            sds((rows, mid)),
            payload_shape(mid),
        ],
        [
            pltpu.VMEM((IMG_ROWS + 48, mid), F32),
            pltpu.VMEM((rows - IMG_ROWS + 16, mid), F32),
            pltpu.VMEM((9, rows, mid), BF),
        ],
        name="spatial_stage",
        flops=2 * rows * 9 * mid * mid,
    )(red, gain, bias, mask, w9, select, *members)


def expand_stage(number, spa, members, gain, bias, mask, w_expand):
    rows, mid = spa.shape
    d_in = w_expand.shape[2]
    size = len(members)

    def body(spa_ref, gain_ref, bias_ref, mask_ref, w_ref, *refs):
        got, (mr_ref, hid_ref, out_ref, stats_ref) = refs[:size], refs[size:]
        k = pl.program_id(0)

        @pl.when(k == 0)
        def _():
            put_statistics(got, mr_ref)
            for stream, lo, hi in parts(rows):
                z = normed_of(spa_ref[lo:hi, :], mr_ref, stream) * gain_ref[...] + bias_ref[...]
                hid_ref[lo:hi, :] = rounded(z * sigmoid(z) * mask_ref[lo:hi, :])

        value = dot(hid_ref[...].astype(BF), w_ref[0])
        out_ref[...] = value
        local_moments(value, mask_ref, stats_ref, pl.multiple_of(k * CH, CH))

    return call(
        body,
        d_in // CH,
        [
            full((rows, mid)),
            full((1, mid)),
            full((1, mid)),
            full((rows, 1)),
            pl.BlockSpec((1, mid, CH), lambda k: (number, 0, k)),
        ]
        + [full((4, mid + 128))] * size,
        [full((8, mid)), full((rows, mid)), cols(rows), full((4, d_in + 128))],
        [sds((8, mid)), sds((rows, mid)), sds((rows, d_in)), payload_shape(d_in)],
        name="expand_stage",
        flops=2 * rows * d_in * mid,
    )(spa, gain, bias, mask, w_expand, *members)


def pick(ref, k, stream, row):
    return ref[2 * stream + row : 2 * stream + row + 1, pl.ds(pl.multiple_of(k * CH, CH), CH)]


def normed_at(value, mr_ref, k, stream):
    return (value - pick(mr_ref, k, stream, 0)) * pick(mr_ref, k, stream, 1)


def join_stage(number, exp, members, gain, bias, act, mask, w_reduce):
    rows, d_in = exp.shape
    mid = w_reduce.shape[2]
    size = len(members)

    def body(exp_ref, gain_ref, bias_ref, act_ref, mask_ref, w_ref, *refs):
        got, (mr_ref, out_ref, low_ref, red_ref, stats_ref) = refs[:size], refs[size:]
        k = pl.program_id(0)

        @pl.when(k == 0)
        def _():
            put_statistics(got, mr_ref)

        for stream, lo, hi in parts(rows):
            z = (
                normed_at(exp_ref[lo:hi, :], mr_ref, k, stream) * gain_ref[...]
                + bias_ref[...]
                + act_ref[lo:hi, :].astype(F32)
            )
            out = z * sigmoid(z) * mask_ref[lo:hi, :]
            out_ref[lo:hi, :] = out
            low_ref[lo:hi, :] = rounded(out)
        part = dot(low_ref[...].astype(BF), w_ref[0])

        @pl.when(k == 0)
        def _():
            red_ref[...] = part

        @pl.when(k > 0)
        def _():
            red_ref[...] += part

        @pl.when(k == pl.num_programs(0) - 1)
        def _():
            local_moments(red_ref[...], mask_ref, stats_ref, 0)

    return call(
        body,
        d_in // CH,
        [
            cols(rows),
            cols(1),
            cols(1),
            cols(rows),
            full((rows, 1)),
            pl.BlockSpec((1, CH, mid), lambda k: (number, k, 0)),
        ]
        + [full((4, d_in + 128))] * size,
        [full((8, d_in)), cols(rows), cols(rows), full((rows, mid)), full((4, mid + 128))],
        [sds((8, d_in)), sds((rows, d_in)), sds((rows, d_in)), sds((rows, mid)), payload_shape(mid)],
        name="join_stage",
        flops=2 * rows * d_in * mid,
        transcendentals=rows * d_in,
    )(exp, gain, bias, act, mask, w_reduce, *members)


def put_sums(stream, pre, normed, sums_ref):
    sums_ref[2 * stream : 2 * stream + 1, :] = jnp.sum(pre, axis=0, keepdims=True)
    sums_ref[2 * stream + 1 : 2 * stream + 2, :] = jnp.sum(pre * normed, axis=0, keepdims=True)


def turn_stage(exp, members, gain, bias, act, mask, grad):
    rows, d_in = exp.shape
    size = len(members)

    def body(exp_ref, gain_ref, bias_ref, act_ref, mask_ref, grad_ref, *refs):
        got, (mr_ref, out_ref, pre_ref, sums_ref) = refs[:size], refs[size:]
        k = pl.program_id(0)

        @pl.when(k == 0)
        def _():
            put_statistics(got, mr_ref)

        for stream, lo, hi in parts(rows):
            n = normed_at(exp_ref[lo:hi, :], mr_ref, k, stream)
            z = n * gain_ref[...] + bias_ref[...] + act_ref[lo:hi, :].astype(F32)
            s = sigmoid(z)
            m = mask_ref[lo:hi, :]
            out_ref[lo:hi, :] = z * s * m
            pre = grad_ref[lo:hi, :].astype(F32) * m * (s * (1.0 + z * (1.0 - s)))
            pre_ref[lo:hi, :] = pre
            put_sums(stream, pre, n, sums_ref)

    return call(
        body,
        d_in // CH,
        [cols(rows), cols(1), cols(1), cols(rows), full((rows, 1)), cols(rows)]
        + [full((4, d_in + 128))] * size,
        [full((8, d_in)), cols(rows), cols(rows), cols(4)],
        [sds((8, d_in)), sds((rows, d_in)), sds((rows, d_in)), sds((4, d_in))],
        name="turn_stage",
        flops=20 * rows * d_in,
        transcendentals=rows * d_in,
    )(exp, gain, bias, act, mask, grad, *members)


def norm_back(pre, normed, plain, cross, scale, mask):
    return mask * scale * (pre - plain - normed * cross)


def rows_of(ref, stream):
    return ref[2 * stream : 2 * stream + 1, :], ref[2 * stream + 1 : 2 * stream + 2, :]


def back_expand(number, me, pre3, exp, mr3, members, gain3, mask, w_expand, spa, mr2, gain2, bias2):
    rows, d_in = exp.shape
    mid = spa.shape[1]
    half = d_in // 2
    size = len(members)

    def body(me_ref, pre3_ref, exp_ref, mr3_ref, gain3_ref, mask_ref, w_ref, spa_ref, mr2_ref, gain2_ref, bias2_ref, *refs):
        got, (both_ref, keep_ref, send_ref, pre2_ref, sums_ref, share, grad) = refs[:size], refs[size:]
        k = pl.program_id(0)

        @pl.when(k == 0)
        def _():
            put_shares(got, mr3_ref, share, both_ref)

        for stream, lo, hi in parts(rows):
            n = normed_at(exp_ref[lo:hi, :], mr3_ref, k, stream)
            grad[lo:hi, :] = norm_back(
                pre3_ref[lo:hi, :],
                n,
                pick(share, k, stream, 0),
                pick(share, k, stream, 1),
                gain3_ref[...] * pick(mr3_ref, k, stream, 1),
                mask_ref[lo:hi, :],
            ).astype(BF)
        per_half = half // CH
        at = pl.ds(pl.multiple_of(lax.rem(k, per_half) * CH, CH), CH)
        mine = k // per_half == me_ref[0]

        @pl.when(mine)
        def _():
            keep_ref[:, at] = grad[...].astype(F32)

        @pl.when(jnp.logical_not(mine))
        def _():
            send_ref[:, at] = grad[...].astype(F32)

        part = dot_nt(grad[...], w_ref[0])

        @pl.when(k == 0)
        def _():
            pre2_ref[...] = part

        @pl.when(k > 0)
        def _():
            pre2_ref[...] += part

        @pl.when(k == pl.num_programs(0) - 1)
        def _():
            for stream, lo, hi in parts(rows):
                n2 = normed_of(spa_ref[lo:hi, :], mr2_ref, stream)
                z2 = n2 * gain2_ref[...] + bias2_ref[...]
                pre2 = pre2_ref[lo:hi, :] * mask_ref[lo:hi, :] * slope(z2)
                pre2_ref[lo:hi, :] = pre2
                put_sums(stream, pre2, n2, sums_ref)

    return call(
        body,
        d_in // CH,
        [
            smem(),
            cols(rows),
            cols(rows),
            full((8, d_in)),
            cols(1),
            full((rows, 1)),
            pl.BlockSpec((1, mid, CH), lambda k: (number, 0, k)),
            full((rows, mid)),
            full((8, mid)),
            full((1, mid)),
            full((1, mid)),
        ]
        + [full((4, d_in))] * size,
        [full((2, d_in)), full((rows, half)), full((rows, half)), full((rows, mid)), full((4, mid))],
        [sds((2, d_in)), sds((rows, half)), sds((rows, half)), sds((rows, mid)), sds((4, mid))],
        [pltpu.VMEM((4, d_in), F32), pltpu.VMEM((rows, CH), BF)],
        name="back_expand",
        flops=2 * rows * d_in * mid,
    )(me, pre3, exp, mr3, gain3, mask, w_expand, spa, mr2, gain2, bias2, *members)


def back_spatial(number, me, pre2, spa, mr2, members, gain2, mask, w9, red, mr1, gain1, bias1):
    rows, mid = spa.shape
    size = len(members)
    quarter = mid // 4

    def body(me_ref, pre2_ref, spa_ref, mr2_ref, gain2_ref, mask_ref, w_ref, red_ref, mr1_ref, gain1_ref, bias1_ref, *refs):
        got, rest = refs[:size], refs[size:]
        both_ref, gs_ref, pre1_ref, sums_ref, share, image, tile, patch = rest
        k = pl.program_id(0)

        @pl.when(k == 0)
        def _():
            put_shares(got, mr2_ref, share, both_ref)
            pieces = []
            for stream, lo, hi in parts(rows):
                n = normed_of(spa_ref[lo:hi, :], mr2_ref, stream)
                plain, cross = rows_of(share, stream)
                scale = gain2_ref[...] * mr2_ref[2 * stream + 1 : 2 * stream + 2, :]
                pieces.append(norm_back(pre2_ref[lo:hi, :], n, plain, cross, scale, mask_ref[lo:hi, :]))
            value = rounded(jnp.concatenate(pieces, axis=0))
            fill_patches(value, image, tile, patch, -1)
            pre1_ref[...] = value
            for m in range(4):
                at = pl.ds(pl.multiple_of((me_ref[1] ^ m) * quarter, quarter), quarter)
                gs_ref[m, :, :] = pre1_ref[:, at]
            pre1_ref[...] = jnp.zeros((rows, mid), F32)

        total = pre1_ref[...]
        for j in range(3):
            total += dot_nt(patch[3 * k + j], w_ref[0, j])
        pre1_ref[...] = total

        @pl.when(k == 2)
        def _():
            for stream, lo, hi in parts(rows):
                n1 = normed_of(red_ref[lo:hi, :], mr1_ref, stream)
                z1 = n1 * gain1_ref[...] + bias1_ref[...]
                pre1 = pre1_ref[lo:hi, :] * mask_ref[lo:hi, :] * slope(z1)
                pre1_ref[lo:hi, :] = pre1
                put_sums(stream, pre1, n1, sums_ref)

    return call(
        body,
        3,
        [
            smem(),
            full((rows, mid)),
            full((rows, mid)),
            full((8, mid)),
            full((1, mid)),
            full((rows, 1)),
            pl.BlockSpec((1, 3, mid, mid), lambda k: (number, k, 0, 0)),
            full((rows, mid)),
            full((8, mid)),
            full((1, mid)),
            full((1, mid)),
        ]
        + [full((4, mid))] * size,
        [full((2, mid)), full((4, rows, quarter)), full((rows, mid)), full((4, mid))],
        [sds((2, mid)), sds((4, rows, quarter)), sds((rows, mid)), sds((4, mid))],
        [
            pltpu.VMEM((4, mid), F32),
            pltpu.VMEM((IMG_ROWS + 48, mid), F32),
            pltpu.VMEM((rows - IMG_ROWS + 16, mid), F32),
            pltpu.VMEM((9, rows, mid), BF),
        ],
        name="back_spatial",
        flops=2 * rows * 9 * mid * mid,
    )(me, pre2, spa, mr2, gain2, mask, w9, red, mr1, gain1, bias1, *members)


def back_reduce(number, pre1, red, mr1, members, gain1, mask, w_reduce, pre3, below):
    rows, mid = red.shape
    d_in = pre3.shape[1]
    size = len(members)

    def head(k, got, pre1_ref, red_ref, mr1_ref, gain1_ref, mask_ref, both_ref, gr_ref, share):
        @pl.when(k == 0)
        def _():
            put_shares(got, mr1_ref, share, both_ref)
            for stream, lo, hi in parts(rows):
                n = normed_of(red_ref[lo:hi, :], mr1_ref, stream)
                plain, cross = rows_of(share, stream)
                scale = gain1_ref[...] * mr1_ref[2 * stream + 1 : 2 * stream + 2, :]
                gr_ref[lo:hi, :] = rounded(
                    norm_back(pre1_ref[lo:hi, :], n, plain, cross, scale, mask_ref[lo:hi, :])
                )

    specs = [
        full((rows, mid)),
        full((rows, mid)),
        full((8, mid)),
        full((1, mid)),
        full((rows, 1)),
        pl.BlockSpec((1, CH, mid), lambda k: (number, k, 0)),
        cols(rows),
    ]
    args = [pre1, red, mr1, gain1, mask, w_reduce, pre3]
    if below is None:

        def body(pre1_ref, red_ref, mr1_ref, gain1_ref, mask_ref, w_ref, pre3_ref, *refs):
            got, (both_ref, gr_ref, out_ref, share) = refs[:size], refs[size:]
            head(pl.program_id(0), got, pre1_ref, red_ref, mr1_ref, gain1_ref, mask_ref, both_ref, gr_ref, share)
            out_ref[...] = pre3_ref[...] + dot_nt(gr_ref[...].astype(BF), w_ref[0])

        return call(
            body,
            d_in // CH,
            specs + [full((4, mid))] * size,
            [full((2, mid)), full((rows, mid)), cols(rows)],
            [sds((2, mid)), sds((rows, mid)), sds((rows, d_in))],
            [pltpu.VMEM((4, mid), F32)],
            name="back_reduce_last",
            flops=2 * rows * d_in * mid,
        )(*args, *members)

    def body(pre1_ref, red_ref, mr1_ref, gain1_ref, mask_ref, w_ref, pre3_ref, exp_ref, mr3_ref, gain3_ref, bias3_ref, act_ref, *refs):
        got, (both_ref, gr_ref, out_ref, sums_ref, share) = refs[:size], refs[size:]
        k = pl.program_id(0)
        head(k, got, pre1_ref, red_ref, mr1_ref, gain1_ref, mask_ref, both_ref, gr_ref, share)
        grad = pre3_ref[...] + dot_nt(gr_ref[...].astype(BF), w_ref[0])
        for stream, lo, hi in parts(rows):
            n = normed_at(exp_ref[lo:hi, :], mr3_ref, k, stream)
            z = n * gain3_ref[...] + bias3_ref[...] + act_ref[lo:hi, :].astype(F32)
            pre = grad[lo:hi] * mask_ref[lo:hi, :] * slope(z)
            out_ref[lo:hi, :] = pre
            put_sums(stream, pre, n, sums_ref)

    return call(
        body,
        d_in // CH,
        specs + [cols(rows), full((8, d_in)), cols(1), cols(1), cols(rows)] + [full((4, mid))] * size,
        [full((2, mid)), full((rows, mid)), cols(rows), cols(4)],
        [sds((2, mid)), sds((rows, mid)), sds((rows, d_in)), sds((4, d_in))],
        [pltpu.VMEM((4, mid), F32)],
        name="back_reduce",
        flops=2 * rows * d_in * mid,
        transcendentals=rows * d_in,
    )(*args, *below, *members)


def dot_tn(a, b):
    return lax.dot_general(a, b, (((0,), (0,)), ((), ())), preferred_element_type=F32)


def spot(index, size):
    place, bit = 0, 1
    while bit < size:
        place = place * 2 + (index // bit) % 2
        bit *= 2
    return place


def weight_call(body, args, shape, flops, scratch=(), name=None):
    vmem = pl.BlockSpec(memory_space=pltpu.VMEM)
    return pl.pallas_call(
        body,
        in_specs=[smem()] + [vmem] * (len(args) - 1),
        out_specs=vmem,
        out_shape=sds(shape),
        scratch_shapes=list(scratch),
        compiler_params=pltpu.CompilerParams(vmem_limit_bytes=VMEM_LIMIT),
        cost_estimate=pl.CostEstimate(flops=flops, bytes_accessed=4_000_000, transcendentals=0),
        name=name,
    )(*args)


def weight_expand(me, own, peer, keep, got, nz):
    rows, mid = own.shape
    half = keep.shape[1]
    step = half // 4
    deep = mid // nz

    def body(me_ref, own_ref, peer_ref, keep_ref, got_ref, out_ref):
        a = jnp.concatenate([own_ref[...].astype(BF), peer_ref[...].astype(BF)], axis=0)
        for m in range(4):
            at = pl.ds(pl.multiple_of((me_ref[3] ^ m) * step, step), step)
            b = jnp.concatenate([keep_ref[:, at].astype(BF), got_ref[:, at].astype(BF)], axis=0)
            value = dot_tn(a, b)
            for z in range(nz):
                place = spot(me_ref[2] ^ z, nz)
                for t in range(step // 128):
                    out_ref[m * (step // 128) + t, place] = value[z * deep : (z + 1) * deep, t * 128 : (t + 1) * 128]

    return weight_call(
        body,
        (me, own, peer, keep, got),
        (half // 128, nz, deep, 128),
        4 * rows * mid * half,
        name="weight_expand",
    )


def weight_reduce(me, own, peer, keep, got, nz):
    rows, width = own.shape
    mid = keep.shape[1]
    step = mid // 4
    deep = width // nz

    def body(me_ref, own_ref, peer_ref, keep_ref, got_ref, out_ref):
        b = jnp.concatenate([keep_ref[...].astype(BF), got_ref[...].astype(BF)], axis=0)
        for z in range(nz):
            at = slice(z * deep, (z + 1) * deep)
            a = jnp.concatenate([own_ref[:, at].astype(BF), peer_ref[:, at].astype(BF)], axis=0)
            value = dot_tn(a, b)
            place = spot(me_ref[2] ^ z, nz)
            for m in range(4):
                out_ref[me_ref[1] ^ m, place] = value[:, m * step : (m + 1) * step]

    return weight_call(
        body,
        (me, own, peer, keep, got),
        (4, nz, deep, step),
        4 * rows * mid * width,
        name="weight_reduce",
    )


def weight_spatial(me, hidden, near, far, nz):
    both, half = hidden[0].shape
    rows = both // 2
    width = near.shape[2]
    deep = half // nz

    def body(me_ref, h0, h1, h2, h3, near_ref, far_ref, out_ref, image, tile, patch):
        for m in range(4):
            for core, ref in enumerate((near_ref, far_ref)):
                tile_rows = rows - IMG_ROWS
                at = (2 * m + core) * rows
                image[0:24, :] = jnp.zeros((24, width), F32)
                image[24 + IMG_ROWS : 48 + IMG_ROWS, :] = jnp.zeros((24, width), F32)
                image[24 : 24 + IMG_ROWS, :] = ref[m, 0:IMG_ROWS, :]
                tile[0:8, :] = jnp.zeros((8, width), F32)
                tile[8 + tile_rows : 16 + tile_rows, :] = jnp.zeros((8, width), F32)
                tile[8 : 8 + tile_rows, :] = ref[m, IMG_ROWS:rows, :]
                for tap in range(9):
                    dy, dx = tap // 3 - 1, tap % 3 - 1
                    part, rest = shifted(image, tile, -dy, -dx, tile_rows)
                    patch[at : at + IMG_ROWS, tap * width : (tap + 1) * width] = part.astype(BF)
                    patch[at + IMG_ROWS : at + rows, tap * width : (tap + 1) * width] = rest.astype(BF)
        a = jnp.concatenate([r[...].astype(BF) for r in (h0, h1, h2, h3)], axis=0)
        for tap in range(9):
            value = dot_tn(a, patch[:, tap * width : (tap + 1) * width])
            for z in range(nz):
                out_ref[spot(me_ref[2] ^ z, nz), tap] = value[z * deep : (z + 1) * deep]

    return weight_call(
        body,
        (me, *hidden, near, far),
        (nz, 9, deep, width),
        2 * 8 * rows * 9 * half * width,
        [
            pltpu.VMEM((IMG_ROWS + 48, width), F32),
            pltpu.VMEM((rows - IMG_ROWS + 16, width), F32),
            pltpu.VMEM((8 * rows, 9 * width), BF),
        ],
        name="weight_spatial",
    )


class Collect:
    def __init__(self, grid, me, core):
        self.grid, self.me, self.core = grid, me, core

    def over_z(self, value, axis):
        step = 1
        while step < self.grid.z:
            size = value.shape[axis] // 2
            keep = lax.slice_in_dim(value, 0, size, axis=axis)
            send = lax.slice_in_dim(value, size, 2 * size, axis=axis)
            value = keep + self.grid.swap(send, dz=step)
            step *= 2
        return lax.squeeze(value, (axis,))

    def over_plane(self, value, order):
        for name in order:
            size = value.shape[0] // 2
            value = value[:size] + self.grid.swap(value[size:], **{name: 1})
        return value

    def expand(self, own, peer, keep, send):
        got = self.grid.swap(send, dc=1)
        value = weight_expand(self.me, own, peer, keep, got, self.grid.z)
        return self.over_z(self.over_plane(value, ("dx", "dy")), 1)

    def reduce(self, own, peer, grad):
        got = self.grid.swap(grad, dc=1)
        value = weight_reduce(self.me, own, peer, grad, got, self.grid.z)
        return self.over_z(self.over_plane(value, ("dy", "dx")), 1)

    def spatial(self, hidden, grad):
        near = jnp.stack([grad[0]] + [self.grid.swap(grad[m], dy=m >> 1, dx=m & 1) for m in (1, 2, 3)])
        far = self.grid.swap(near, dc=1)
        return self.over_z(weight_spatial(self.me, hidden, near, far, self.grid.z), 0)

    def gather(self, pieces):
        flat = jnp.concatenate([p.reshape(-1, 128) for p in pieces], axis=0)
        for group in self.grid.far():
            flat = flat + sum(self.grid.swap(flat, **step) for step in group)
        own = jnp.stack([flat] + [self.grid.swap(flat, dy=m >> 1, dx=m & 1) for m in (1, 2, 3)])
        return own, self.grid.swap(own, dc=1)


def place_slices(me, number, own, other, shapes, before):
    (e_rows, d_in), (r_rows, mid), (s_rows, _) = shapes
    length = own.shape[1]
    e_len, r_len = 2 * e_rows, r_rows // 2
    dims = ((BLOCKS, r_rows, mid), (BLOCKS, 9, s_rows, mid), (BLOCKS, e_rows, d_in))

    def body(me_ref, own_ref, other_ref, *refs):
        red_ref, spa_ref, exp_ref = refs[-3:]

        def put(ref):
            for t in range(2):
                exp_ref[0, :, t * 128 : (t + 1) * 128] = ref[0, t * e_rows : (t + 1) * e_rows, :]
            red_ref[0] = ref[0, e_len : e_len + r_len, :]
            for tap in range(9):
                at = e_len + r_len + tap * (s_rows // 2)
                spa_ref[0, tap] = ref[0, at : at + s_rows // 2, :]

        mine = pl.program_id(0) // 4 == me_ref[0]

        @pl.when(mine)
        def _():
            put(own_ref)

        @pl.when(jnp.logical_not(mine))
        def _():
            put(other_ref)

    def piece(a, me):
        return (a % 4) ^ me[1], 0, 0

    def e_place(a, me):
        return number, 0, (a // 4) * 4 + (a % 2) * 2 + (a // 2) % 2

    in_specs = [pl.BlockSpec((1, length, 128), piece)] * 2
    out_specs = [
        pl.BlockSpec((1, r_rows // 2, 128), lambda a, me: (number, a // 4, a % 4)),
        pl.BlockSpec((1, 9, s_rows // 2, 128), lambda a, me: (number, 0, a // 4, a % 4)),
        pl.BlockSpec((1, e_rows, 256), e_place),
    ]
    args = (me, own, other)
    aliases = {}
    if before is not None:
        in_specs = in_specs + [pl.BlockSpec(memory_space=pl.ANY)] * 3
        args = args + before
        aliases = {3: 0, 4: 1, 5: 2}
    return pl.pallas_call(
        body,
        grid_spec=pltpu.PrefetchScalarGridSpec(
            num_scalar_prefetch=1, grid=(8,), in_specs=in_specs, out_specs=out_specs
        ),
        out_shape=[sds(d) for d in dims],
        input_output_aliases=aliases,
        compiler_params=pltpu.CompilerParams(dimension_semantics=("arbitrary",)),
        name="place_slices",
    )(*args)


def to_rows(image, tile, rows):
    width = image.shape[-1]
    image = jnp.transpose(image, (1, 2, 0, 3))
    image = jnp.pad(image, ((0, 0), (0, 1), (0, 0), (0, 0))).reshape(IMG_ROWS, width)
    tile = tile.reshape(-1, width)
    pad = jnp.zeros((rows - IMG_ROWS - tile.shape[0], width), tile.dtype)
    return jnp.concatenate([image, tile, pad], axis=0)


def from_rows(value, tiles):
    width = value.shape[1]
    image = value[:IMG_ROWS].reshape(MAP, MAPW, SLOTS, width)[:, :MAP]
    image = jnp.transpose(image, (2, 0, 1, 3))
    tile = value[IMG_ROWS : IMG_ROWS + tiles * 4].reshape(tiles, TILE, TILE, width)
    return image, tile


def row_mask(map_sizes, rows):
    row = jnp.arange(MAP)
    col = jnp.arange(MAPW)
    inside = (row[:, None, None] < map_sizes[None, None, :]) & (col[None, :, None] < map_sizes[None, None, :])
    image = inside.astype(F32).reshape(IMG_ROWS)
    tile = jnp.repeat((map_sizes > 0).astype(F32), PIECES * TILE * TILE)
    pad = jnp.zeros((rows - IMG_ROWS - tile.shape[0],), F32)
    return jnp.concatenate([image, tile, pad])[:, None]


def core_halves(value, core, nz):
    deep = value.shape[1] // (2 * nz)
    low = [value[:, 2 * z * deep : (2 * z + 1) * deep] for z in range(nz)]
    high = [value[:, (2 * z + 1) * deep : (2 * z + 2) * deep] for z in range(nz)]
    low, high = jnp.concatenate(low, axis=1), jnp.concatenate(high, axis=1)
    keep = jnp.where(core == 0, low, high).astype(F32)
    send = jnp.where(core == 0, high, low).astype(F32)
    return keep, send


def core_select(core, mid, nz):
    deep = mid // (2 * nz)
    at = jnp.arange(mid)
    side = at // (mid // 2)
    inner = at % (mid // 2)
    source = (inner // deep) * 2 * deep + (side ^ core) * deep + inner % deep
    return (jnp.arange(mid)[:, None] == source[None, :]).astype(BF)


def per_device(
    grid,
    images,
    tile_maps,
    map_sizes,
    w_reduce,
    w_spatial,
    w_expand,
    gain_mid,
    bias_mid,
    gain_out,
    bias_out,
    grad_images,
    grad_tiles,
):
    tiles = tile_maps.shape[0]
    rows = -(-(IMG_ROWS + tiles * TILE * TILE) // 16) * 16
    d_in, mid = w_reduce.shape[1:]
    nz = grid.z
    y, x, core, z = grid.index()
    chip = (y % 2) * 2 + x % 2
    turned = (x % 2) * 2 + y % 2
    me = jnp.stack([core, chip, z, turned]).astype(jnp.int32)
    mask = row_mask(map_sizes, rows)
    w9 = w_spatial.reshape(BLOCKS, 9, mid, mid)
    start = to_rows(images, tile_maps, rows)
    grad = to_rows(grad_images, grad_tiles, rows)
    select = core_select(core, mid, nz)
    collect = Collect(grid, me, core)

    def row(table, *at):
        return table[at][None]

    def moments(stats):
        return exchange(grid, stats, join_moments)

    def sums(value):
        return exchange(grid, value, add_members)

    acts, lows, reds, spas, exps = [start], [], [], [], []
    mr1, mr2, mr3, hid1, hid2 = [], [], [], [], []
    red, stats = reduce_first(start, w_reduce, mask)
    low = start
    for b in range(BLOCKS):
        keep, send = core_halves(low, core, nz)
        lows.append((keep, grid.swap(send, dc=1)))
        reds.append(red)
        mr, keep, send, spa, stats = spatial_stage(
            b, red, moments(stats), row(gain_mid, b, 0), row(bias_mid, b, 0), mask, w9, select
        )
        mr1.append(mr)
        hidden = jnp.concatenate([keep, grid.swap(send, dc=1)], axis=0)
        hid1.append([hidden] + [grid.swap(hidden, dy=m >> 1, dx=m & 1) for m in (1, 2, 3)])
        spas.append(spa)
        mr, hidden, exp, stats = expand_stage(
            b, spa, moments(stats), row(gain_mid, b, 1), row(bias_mid, b, 1), mask, w_expand
        )
        mr2.append(mr)
        hid2.append((hidden, grid.swap(hidden, dc=1)))
        exps.append(exp)
        if b + 1 < BLOCKS:
            mr, out, low, red, stats = join_stage(
                b + 1, exp, moments(stats), row(gain_out, b), row(bias_out, b), acts[b], mask, w_reduce
            )
            mr3.append(mr)
            acts.append(out)
    last = BLOCKS - 1
    mr, out, pre3, sums3 = turn_stage(
        exps[last], moments(stats), row(gain_out, last), row(bias_out, last), acts[last], mask, grad
    )
    mr3.append(mr)

    both1, both2, both3 = [None] * BLOCKS, [None] * BLOCKS, [None] * BLOCKS
    shapes = ((mid // nz, d_in), (d_in // nz, mid), (mid // nz, mid))
    slices = None
    for b in reversed(range(BLOCKS)):
        both3[b], keep, send, pre2, sums2 = back_expand(
            b, me, pre3, exps[b], mr3[b], sums(sums3), row(gain_out, b), mask, w_expand,
            spas[b], mr2[b], row(gain_mid, b, 1), row(bias_mid, b, 1),
        )
        part_e = collect.expand(*hid2[b], keep, send)
        both2[b], gs, pre1, sums1 = back_spatial(
            b, me, pre2, spas[b], mr2[b], sums(sums2), row(gain_mid, b, 1), mask, w9,
            reds[b], mr1[b], row(gain_mid, b, 0), row(bias_mid, b, 0),
        )
        part_s = collect.spatial(hid1[b], gs)
        below = None
        if b > 0:
            below = (exps[b - 1], mr3[b - 1], row(gain_out, b - 1), row(bias_out, b - 1), acts[b - 1])
        result = back_reduce(
            b, pre1, reds[b], mr1[b], sums(sums1), row(gain_mid, b, 0), mask, w_reduce, pre3, below
        )
        both1[b] = result[0]
        part_r = collect.reduce(*lows[b], result[1])
        own, other = collect.gather((part_e, part_r, part_s))
        slices = place_slices(me, b, own, other, shapes, slices)
        if b > 0:
            pre3, sums3 = result[2], result[3]
        else:
            grad_in = result[2]

    out_images, out_tiles = from_rows(out, tiles)
    in_images, in_tiles = from_rows(grad_in, tiles)
    g_reduce, g_spatial, g_expand = slices

    def table(at):
        return jnp.stack([jnp.stack([both1[b][at], both2[b][at]]) for b in range(BLOCKS)])

    return (
        out_images,
        out_tiles,
        in_images,
        in_tiles,
        g_reduce,
        g_spatial.reshape(BLOCKS, 3, 3, mid // nz, mid),
        g_expand,
        table(1),
        table(0),
        jnp.stack([both3[b][1] for b in range(BLOCKS)]),
        jnp.stack([both3[b][0] for b in range(BLOCKS)]),
    )


def solution(mesh):
    both = ("wide", "narrow")
    batch = P(both, None, None, None)
    grid = Grid(mesh.shape["wide"], mesh.shape["narrow"])
    return jax.shard_map(
        functools.partial(per_device, grid),
        mesh=mesh,
        in_specs=(batch, batch, P(both), P(), P(), P(), P(), P(), P(), P(), batch, batch),
        out_specs=(
            batch,
            batch,
            batch,
            batch,
            P(None, "narrow", None),
            P(None, None, None, "narrow", None),
            P(None, "narrow", None),
            P(),
            P(),
            P(),
            P(),
        ),
        check_vma=False,
    )
```

time: 1110 us -> 575 us (0.52)
  waiting for transfers between devices: 734 us -> 216 us
  other arithmetic: 139 us -> 21.3 us
  Pallas kernels: 51.8 us -> 112 us
  starting transfers between devices: 97.6 us -> 144 us
  between operations: 28.7 us -> 2.14 us
  local copies, waits for them, and re-layouts: 45.5 us -> 70.8 us
    reduce_scatter x3 -> x0, waiting for transfers between devices: 536 us -> none  [the longest x1 317 us: per_device(): lax.psum_scatter(jnp.stack(g_spatial), 'narrow', scatter_dimension=3, til...]
    ppermute x84 -> x136, waiting for transfers between devices: 71.2 us -> 216 us  [swap(): return lax.ppermute(value, AXES, pairs)]
    psum x1 -> x0, waiting for transfers between devices: 127 us -> none  [per_device(): lax.psum((lax.psum_scatter(jnp.stack(g_reduce), 'narrow', scatter_dimensi...]
    pallas_call x13 -> x33, Pallas kernels: 51.8 us -> 112 us  [the longest x12 17.5 us: join_moments(): pl.pallas_call(body, out_shape=sds((4, width + 128)), name='join_moments')]
    add x41 -> x31, other arithmetic: 65.8 us -> 7.8 us  [the longest x8 3.13 us: over_plane(): value = value[:size] + self.grid.swap(value[size:], **{name: 1})]
    ppermute x84 -> x136, starting transfers between devices: 97.4 us -> 144 us  [swap(): return lax.ppermute(value, AXES, pairs)]
    rsqrt x12 -> x0, other arithmetic: 39.6 us -> none  [moments(): out.append(lax.rsqrt(value[2 * stream + 1] / self.total[stream] + EPS))]
    unnamed x89 -> x264, local copies, waits for them, and re-layouts: 15.9 us -> 41.9 us
  transfers between devices with their start and end apart: 88 -> 136, of which waited for: 82 -> 92; matrix products, arithmetic and copies ran while one was open for 4% -> 7% of each run, Pallas kernels for 1% -> 8%
where the time goes in v2:
time: 575 us; the launch traced here: 567 us
  waiting for transfers between devices  216 us (38%)
  starting transfers between devices  144 us (25%)
  Pallas kernels  112 us (19%)
  local copies, waits for them, and re-layouts  70.8 us (12%)
  other arithmetic  21.3 us (4%)
    ppermute x136, waiting for transfers between devices, swap(): return lax.ppermute(value, AXES, pairs)  216 us
    ppermute x136, starting transfers between devices, swap(): return lax.ppermute(value, AXES, pairs)  144 us
    unnamed x264, local copies, waits for them, and re-layouts  41.9 us
    pallas_call x12, Pallas kernels, join_moments(): pl.pallas_call(body, out_shape=sds((4, width + 128)), name='join_moments')  17.5 us
    pallas_call x2, Pallas kernels, place_slices(): pl.pallas_call(body, grid_spec=pltpu.PrefetchScalarGridSpec(num_scalar_pr...  16.8 us
    pallas_call x6, Pallas kernels, weight_call(): pl.pallas_call(body, in_specs=[smem()] + [vmem] * (len(args) - 1), out_sp...  14.8 us
    pallas_call x1, Pallas kernels, back_reduce(): call(body, d_in // CH, specs + [full((4, mid))] * size, [full((2, mid)),...  13.6 us
  transfers between devices with their start and end apart: 136, of which 92 were waited for; matrix products, arithmetic and copies ran while one was open for 7% of the time, Pallas kernels for 8%

profile of v2, /device:TPU:0, one launch (start us, length us, event | category | flops | bytes accessed | tf_op | source)
XLA Modules:
  0.0 566.8 jit_solution(3152398980298374104)
XLA Ops:
  16.0 3.8 collective-permute-start.3
  26.3 3.6 collective-permute-start.6
  32.0 2.7 collective-permute-done.5.refs_2_
  35.4 4.7 spatial_stage.2
  54.0 2.4 collective-permute-start.11
  59.1 3.5 expand_stage.2
  67.9 2.4 collective-permute-start.17
  77.2 2.5 collective-permute-start.20
  85.8 4.3 join_stage.1
  110.5 4.7 spatial_stage.3
  120.4 2.4 collective-permute-start.31
  129.3 2.3 collective-permute-start.34
  137.4 3.5 expand_stage.3
  165.2 3.4 turn_stage.1
  172.3 2.3 collective-permute-start.45
  180.3 2.5 collective-permute-start.48
  193.2 4.2 back_expand.2
  210.9 5.4 back_spatial.2
  218.3 2.4 collective-permute-start.59
  224.9 2.3 collective-permute-start.62
  232.0 4.8 back_reduce.1
  255.2 4.3 back_expand.3
  275.1 5.2 back_spatial.3
  290.3 2.6 collective-permute-done.128
  303.8 14.3 %collective-permute-done.101 = f32[192,128]{1,0:T(8,128)S(1)} collective-permute-done((f32[192,128]{1,0:T(8,128)S(1)}, f32[192,128]{1,0:T(8,128)S(1)}, u32[]{:S(2)}, u32[]{:S(2)}) %collective-permute-start.101) | collective-permute-done | bytes 98336 | tf_op jit(solution)/shard_map/ppermute | solution.py:48
  333.7 13.6 %back_reduce_last.1 = (f32[2,512]{1,0:T(2,128)S(1)}, f32[192,512]{1,0:T(8,128)S(1)}, f32[192,2048]{1,0:T(8,128)S(1)}) custom-call(f32[192,512]{1,0:T(8,128)S(1)} %copy-done.33, f32[192,512]{1,0:T(8,128)S(1)} %get-tuple-element.71.red_ref, f32[8,512]{1,0:T(8,128)S(1)} %get-tuple-element.99.mr1_ref, f32[1,512]{1,0:T(1,128)S(1)} %copy-done.66, ...), custom_call_target="tpu_custom_call" | custom-call | flops 402653184 | bytes 4000000 | tf_op jit(solution)/shard_map/back_reduce_last/pallas_call | solution.py:681
  347.4 4.0 weight_spatial.3
  352.9 3.8 weight_spatial.2
  366.3 7.6 %collective-permute-done.130 = f32[2,9,64,128]{3,2,1,0:T(8,128)S(1)} collective-permute-done((f32[2,9,64,128]{3,2,1,0:T(8,128)}, f32[2,9,64,128]{3,2,1,0:T(8,128)S(1)}, u32[]{:S(2)}, u32[]{:S(2)}) %collective-permute-start.130) | collective-permute-done | bytes 589856 | tf_op jit(solution)/shard_map/ppermute | solution.py:48
  378.6 7.5 %collective-permute-done.104 = f32[2,9,64,128]{3,2,1,0:T(8,128)S(1)} collective-permute-done((f32[2,9,64,128]{3,2,1,0:T(8,128)}, f32[2,9,64,128]{3,2,1,0:T(8,128)S(1)}, u32[]{:S(2)}, u32[]{:S(2)}) %collective-permute-start.104) | collective-permute-done | bytes 589856 | tf_op jit(solution)/shard_map/ppermute | solution.py:48
  395.3 13.6 %collective-permute-done.131 = f32[1,9,64,128]{3,2,1,0:T(8,128)} collective-permute-done((f32[1,9,64,128]{3,2,1,0:T(8,128)}, f32[1,9,64,128]{3,2,1,0:T(8,128)}, u32[]{:S(2)}, u32[]{:S(2)}) %collective-permute-start.131) | collective-permute-done | bytes 294944 | tf_op jit(solution)/shard_map/ppermute | solution.py:48
  410.8 4.0 collective-permute-done.105
  417.5 4.3 collective-permute-done.92
  425.2 15.8 %collective-permute-done.86 = f32[4,4,128,128]{3,2,1,0:T(8,128)S(1)} collective-permute-done((f32[4,4,128,128]{3,2,1,0:T(8,128)S(1)}, f32[4,4,128,128]{3,2,1,0:T(8,128)S(1)}, u32[]{:S(2)}, u32[]{:S(2)}) %collective-permute-start.86) | collective-permute-done | bytes 1048608 | tf_op jit(solution)/shard_map/ppermute | solution.py:48
  442.4 9.9 %collective-permute-done.119 = f32[1,4,256,128]{3,2,1,0:T(8,128)S(1)} collective-permute-done((f32[1,4,256,128]{3,2,1,0:T(8,128)S(1)}, f32[1,4,256,128]{3,2,1,0:T(8,128)S(1)}, u32[]{:S(2)}, u32[]{:S(2)}) %collective-permute-start.119) | collective-permute-done | bytes 524320 | tf_op jit(solution)/shard_map/ppermute | solution.py:48
  453.1 8.5 %collective-permute-done.93 = f32[1,4,256,128]{3,2,1,0:T(8,128)S(1)} collective-permute-done((f32[1,4,256,128]{3,2,1,0:T(8,128)S(1)}, f32[1,4,256,128]{3,2,1,0:T(8,128)S(1)}, u32[]{:S(2)}, u32[]{:S(2)}) %collective-permute-start.93) | collective-permute-done | bytes 524320 | tf_op jit(solution)/shard_map/ppermute | solution.py:48
  465.7 7.1 %collective-permute-done.94 = f32[1,2,256,128]{3,2,1,0:T(8,128)S(1)} collective-permute-done((f32[1,2,256,128]{3,2,1,0:T(8,128)S(1)}, f32[1,2,256,128]{3,2,1,0:T(8,128)S(1)}, u32[]{:S(2)}, u32[]{:S(2)}) %collective-permute-start.94) | collective-permute-done | bytes 262176 | tf_op jit(solution)/shard_map/ppermute | solution.py:48
  474.7 4.9 collective-permute-done.114
  480.7 5.9 %collective-permute-done.115 = f32[2,1,128,128]{3,2,1,0:T(8,128)S(1)} collective-permute-done((f32[2,1,128,128]{3,2,1,0:T(8,128)S(1)}, f32[2,1,128,128]{3,2,1,0:T(8,128)S(1)}, u32[]{:S(2)}, u32[]{:S(2)}) %collective-permute-start.115) | collective-permute-done | bytes 131104 | tf_op jit(solution)/shard_map/ppermute | solution.py:48
  492.7 2.7 collective-permute-done.89
  497.7 6.7 %collective-permute-done.133 = f32[1088,128]{1,0:T(8,128)S(1)} collective-permute-done((f32[1088,128]{1,0:T(8,128)S(1)}, f32[1088,128]{1,0:T(8,128)S(1)}, u32[]{:S(2)}, u32[]{:S(2)}) %collective-permute-start.133) | collective-permute-done | bytes 557088 | tf_op jit(solution)/shard_map/ppermute | solution.py:48
  504.4 2.6 collective-permute-start.108
  507.1 11.2 %collective-permute-done.134 = f32[1088,128]{1,0:T(8,128)S(1)} collective-permute-done((f32[1088,128]{1,0:T(8,128)S(1)}, f32[1088,128]{1,0:T(8,128)S(1)}, u32[]{:S(2)}, u32[]{:S(2)}) %collective-permute-start.134) | collective-permute-done | bytes 557088 | tf_op jit(solution)/shard_map/ppermute | solution.py:48
  518.5 3.6 collective-permute-done.107
  522.0 7.4 %collective-permute-done.106 = f32[1088,128]{1,0:T(8,128)S(1)} collective-permute-done((f32[1088,128]{1,0:T(8,128)S(1)}, f32[1088,128]{1,0:T(8,128)S(1)}, u32[]{:S(2)}, u32[]{:S(2)}) %collective-permute-start.106) | collective-permute-done | bytes 557088 | tf_op jit(solution)/shard_map/ppermute | solution.py:48
  529.4 9.7 %collective-permute-done.108 = f32[1088,128]{1,0:T(8,128)S(1)} collective-permute-done((f32[1088,128]{1,0:T(8,128)S(1)}, f32[1088,128]{1,0:T(8,128)S(1)}, u32[]{:S(2)}, u32[]{:S(2)}) %collective-permute-start.108) | collective-permute-done | bytes 557088 | tf_op jit(solution)/shard_map/ppermute | solution.py:48
  549.8 8.4 %place_slices.2 = (f32[2,512,512]{2,1,0:T(8,128)}, f32[2,9,128,512]{3,2,1,0:T(8,128)}, f32[2,128,2048]{2,1,0:T(8,128)}) custom-call(s32[4]{0:T(128)} %copy-done.44, f32[4,1088,128]{2,1,0:T(8,128)} %copy-done.96, f32[4,1088,128]{2,1,0:T(8,128)} %collective-permute-done.135.other_ref), custom_call_target="tpu_custom_call" | custom-call | tf_op jit(solution)/shard_map/place_slices/pallas_call | solution.py:924
  558.2 8.4 %place_slices.3 = (f32[2,512,512]{2,1,0:T(8,128)}, f32[2,9,128,512]{3,2,1,0:T(8,128)}, f32[2,128,2048]{2,1,0:T(8,128)}) custom-call(s32[4]{0:T(128)} %copy-done.44, f32[4,1088,128]{2,1,0:T(8,128)} %pad_maximum_fusion.own_ref, f32[4,1088,128]{2,1,0:T(8,128)} %collective-permute-done.109.other_ref, ...), custom_call_target="tpu_custom_call", output_to_operand_aliasing={{0}: (3, {}), {1}: (4, {}), {2}: (5, {})} | custom-call | tf_op jit(solution)/shard_map/place_slices/pallas_call | solution.py:924
  (636 shorter events, 297.2 us)
Async XLA Ops:
  247.4 17.8 %collective-permute-start.96 = (f32[192,256]{1,0:T(8,128)}, f32[192,256]{1,0:T(8,128)S(1)}, u32[]{:S(2)}, u32[]{:S(2)}) collective-permute-start(f32[192,256]{1,0:T(8,128)} %copy-done.93), channel_id=1, source_target_pairs={{0,4},{1,5},{2,6},{3,7},{4,0},{5,1},{6,2},{7,3},{8,12},{9,13},{10,... | collective-permute-start | bytes 589832 | tf_op jit(solution)/shard_map/ppermute | solution.py:48
  261.2 10.1 %collective-permute-start.122 = (f32[192,256]{1,0:T(8,128)S(1)}, f32[192,256]{1,0:T(8,128)S(1)}, u32[]{:S(2)}, u32[]{:S(2)}) collective-permute-start(f32[192,256]{1,0:T(8,128)S(1)} %copy-done.95), channel_id=1, source_target_pairs={{0,4},{1,5},{2,6},{3,7},{4,0},{5,1},{6,2},{7,3},{8,12},{9,13},{10,... | collective-permute-start | bytes 589832 | tf_op jit(solution)/shard_map/ppermute | solution.py:48
  265.2 31.9 %collective-permute-start.99 = (f32[384,256]{1,0:T(8,128)S(1)}, f32[384,256]{1,0:T(8,128)S(1)}, u32[]{:S(2)}, u32[]{:S(2)}) collective-permute-start(f32[384,256]{1,0:T(8,128)S(1)} %constant_dynamic-update-slice_fusion.h0), channel_id=1, source_target_pairs={{0,24},{1,25},{2,26},{3,27},{4,28},{5,29},{6,30},{7,31},{8,16},{9,... | collective-permute-start | bytes 1179656 | tf_op jit(solution)/shard_map/ppermute | solution.py:48
  267.4 31.4 %collective-permute-start.98 = (f32[384,256]{1,0:T(8,128)S(1)}, f32[384,256]{1,0:T(8,128)S(1)}, u32[]{:S(2)}, u32[]{:S(2)}) collective-permute-start(f32[384,256]{1,0:T(8,128)S(1)} %constant_dynamic-update-slice_fusion.h0), channel_id=1, source_target_pairs={{0,16},{1,17},{2,18},{3,19},{4,20},{5,21},{6,22},{7,23},{8,24},{9,... | collective-permute-start | bytes 1179656 | tf_op jit(solution)/shard_map/ppermute | solution.py:48
  293.0 9.5 %collective-permute-start.102 = (f32[192,128]{1,0:T(8,128)S(1)}, f32[192,128]{1,0:T(8,128)S(1)}, u32[]{:S(2)}, u32[]{:S(2)}) collective-permute-start(f32[192,128]{1,0:T(8,128)S(1)} %get-tuple-element.160), channel_id=1, source_target_pairs={{0,24},{1,25},{2,26},{3,27},{4,28},{5,29},{6,30},{7,31},{8,16},{9,... | collective-permute-start | bytes 294920 | tf_op jit(solution)/shard_map/ppermute | solution.py:48
  298.9 25.9 %collective-permute-start.125 = (f32[384,256]{1,0:T(8,128)}, f32[384,256]{1,0:T(8,128)}, u32[]{:S(2)}, u32[]{:S(2)}) collective-permute-start(f32[384,256]{1,0:T(8,128)} %constant_dynamic-update-slice_fusion.2.h0), channel_id=1, source_target_pairs={{0,24},{1,25},{2,26},{3,27},{4,28},{5,29},{6,30},{7,31},{8,16},{9,... | collective-permute-start | bytes 1179656 | tf_op jit(solution)/shard_map/ppermute | solution.py:48
  300.4 24.9 %collective-permute-start.124 = (f32[384,256]{1,0:T(8,128)}, f32[384,256]{1,0:T(8,128)}, u32[]{:S(2)}, u32[]{:S(2)}) collective-permute-start(f32[384,256]{1,0:T(8,128)} %constant_dynamic-update-slice_fusion.2.h0), channel_id=1, source_target_pairs={{0,16},{1,17},{2,18},{3,19},{4,20},{5,21},{6,22},{7,23},{8,24},{9,... | collective-permute-start | bytes 1179656 | tf_op jit(solution)/shard_map/ppermute | solution.py:48
  301.5 23.9 %collective-permute-start.123 = (f32[384,256]{1,0:T(8,128)}, f32[384,256]{1,0:T(8,128)}, u32[]{:S(2)}, u32[]{:S(2)}) collective-permute-start(f32[384,256]{1,0:T(8,128)} %constant_dynamic-update-slice_fusion.2.h0), channel_id=1, source_target_pairs={{0,8},{1,9},{2,10},{3,11},{4,12},{5,13},{6,14},{7,15},{8,0},{9,1},... | collective-permute-start | bytes 1179656 | tf_op jit(solution)/shard_map/ppermute | solution.py:48
  302.5 23.9 %collective-permute-start.129 = (f32[4,192,128]{2,1,0:T(8,128)S(1)}, f32[4,192,128]{2,1,0:T(8,128)}, u32[]{:S(2)}, u32[]{:S(2)}) collective-permute-start(f32[4,192,128]{2,1,0:T(8,128)S(1)} %pad_maximum_fusion.9.near_ref), channel_id=1, source_target_pairs={{0,4},{1,5},{2,6},{3,7},{4,0},{5,1},{6,2},{7,3},{8,12},{9,13},{10,... | collective-permute-start | bytes 1179656 | tf_op jit(solution)/shard_map/ppermute | solution.py:48
  302.5 15.7 %collective-permute-start.101 = (f32[192,128]{1,0:T(8,128)S(1)}, f32[192,128]{1,0:T(8,128)S(1)}, u32[]{:S(2)}, u32[]{:S(2)}) collective-permute-start(f32[192,128]{1,0:T(8,128)S(1)} %get-tuple-element.161), channel_id=1, source_target_pairs={{0,16},{1,17},{2,18},{3,19},{4,20},{5,21},{6,22},{7,23},{8,24},{9,... | collective-permute-start | bytes 294920 | tf_op jit(solution)/shard_map/ppermute | solution.py:48
  323.1 35.2 %collective-permute-start.90 = (f32[192,1024]{1,0:T(8,128)}, f32[192,1024]{1,0:T(8,128)}, u32[]{:S(2)}, u32[]{:S(2)}) collective-permute-start(f32[192,1024]{1,0:T(8,128)} %get-tuple-element.141), channel_id=1, source_target_pairs={{0,4},{1,5},{2,6},{3,7},{4,0},{5,1},{6,2},{7,3},{8,12},{9,13},{10,... | collective-permute-start | bytes 2359304 | tf_op jit(solution)/shard_map/ppermute | solution.py:48
  324.8 32.7 %collective-permute-start.84 = (f32[192,512]{1,0:T(8,128)}, f32[192,512]{1,0:T(8,128)}, u32[]{:S(2)}, u32[]{:S(2)}) collective-permute-start(f32[192,512]{1,0:T(8,128)} %copy-done.26), channel_id=1, source_target_pairs={{0,4},{1,5},{2,6},{3,7},{4,0},{5,1},{6,2},{7,3},{8,12},{9,13},{10,... | collective-permute-start | bytes 1179656 | tf_op jit(solution)/shard_map/ppermute | solution.py:48
  325.3 34.3 %collective-permute-start.116 = (f32[192,1024]{1,0:T(8,128)}, f32[192,1024]{1,0:T(8,128)}, u32[]{:S(2)}, u32[]{:S(2)}) collective-permute-start(f32[192,1024]{1,0:T(8,128)} %get-tuple-element.131), channel_id=1, source_target_pairs={{0,4},{1,5},{2,6},{3,7},{4,0},{5,1},{6,2},{7,3},{8,12},{9,13},{10,... | collective-permute-start | bytes 2359304 | tf_op jit(solution)/shard_map/ppermute | solution.py:48
  325.4 26.8 %collective-permute-start.97 = (f32[384,256]{1,0:T(8,128)}, f32[384,256]{1,0:T(8,128)}, u32[]{:S(2)}, u32[]{:S(2)}) collective-permute-start(f32[384,256]{1,0:T(8,128)} %copy-done.20), channel_id=1, source_target_pairs={{0,8},{1,9},{2,10},{3,11},{4,12},{5,13},{6,14},{7,15},{8,0},{9,1},... | collective-permute-start | bytes 1179656 | tf_op jit(solution)/shard_map/ppermute | solution.py:48
  326.3 26.3 %collective-permute-start.103 = (f32[4,192,128]{2,1,0:T(8,128)}, f32[4,192,128]{2,1,0:T(8,128)}, u32[]{:S(2)}, u32[]{:S(2)}) collective-permute-start(f32[4,192,128]{2,1,0:T(8,128)} %pad_maximum_fusion.8.near_ref), channel_id=1, source_target_pairs={{0,4},{1,5},{2,6},{3,7},{4,0},{5,1},{6,2},{7,3},{8,12},{9,13},{10,... | collective-permute-start | bytes 1179656 | tf_op jit(solution)/shard_map/ppermute | solution.py:48
  352.2 7.3 %collective-permute-start.117 = (f32[192,512]{1,0:T(8,128)S(1)}, f32[192,512]{1,0:T(8,128)S(1)}, u32[]{:S(2)}, u32[]{:S(2)}) collective-permute-start(f32[192,512]{1,0:T(8,128)S(1)} %copy-done.31), channel_id=1, source_target_pairs={{0,4},{1,5},{2,6},{3,7},{4,0},{5,1},{6,2},{7,3},{8,12},{9,13},{10,... | collective-permute-start | bytes 1179656 | tf_op jit(solution)/shard_map/ppermute | solution.py:48
  352.6 7.5 %collective-permute-start.91 = (f32[192,512]{1,0:T(8,128)S(1)}, f32[192,512]{1,0:T(8,128)S(1)}, u32[]{:S(2)}, u32[]{:S(2)}) collective-permute-start(f32[192,512]{1,0:T(8,128)S(1)} %get-tuple-element.107.keep_ref), channel_id=1, source_target_pairs={{0,4},{1,5},{2,6},{3,7},{4,0},{5,1},{6,2},{7,3},{8,12},{9,13},{10,... | collective-permute-start | bytes 1179656 | tf_op jit(solution)/shard_map/ppermute | solution.py:48
  357.5 16.3 %collective-permute-start.130 = (f32[2,9,64,128]{3,2,1,0:T(8,128)}, f32[2,9,64,128]{3,2,1,0:T(8,128)S(1)}, u32[]{:S(2)}, u32[]{:S(2)}) collective-permute-start(f32[2,9,64,128]{3,2,1,0:T(8,128)} %slice.439), channel_id=1, source_target_pairs={{0,1},{1,0},{2,3},{3,2},{4,5},{5,4},{6,7},{7,6},{8,9},{9,8},{10,11... | collective-permute-start | bytes 1769480 | tf_op jit(solution)/shard_map/ppermute | solution.py:48
  358.3 27.8 %collective-permute-start.104 = (f32[2,9,64,128]{3,2,1,0:T(8,128)}, f32[2,9,64,128]{3,2,1,0:T(8,128)S(1)}, u32[]{:S(2)}, u32[]{:S(2)}) collective-permute-start(f32[2,9,64,128]{3,2,1,0:T(8,128)} %slice.419), channel_id=1, source_target_pairs={{0,1},{1,0},{2,3},{3,2},{4,5},{5,4},{6,7},{7,6},{8,9},{9,8},{10,11... | collective-permute-start | bytes 1769480 | tf_op jit(solution)/shard_map/ppermute | solution.py:48
  359.6 18.1 %collective-permute-start.110 = (f32[192,512]{1,0:T(8,128)S(1)}, f32[192,512]{1,0:T(8,128)S(1)}, u32[]{:S(2)}, u32[]{:S(2)}) collective-permute-start(f32[192,512]{1,0:T(8,128)S(1)} %copy-done.29), channel_id=1, source_target_pairs={{0,4},{1,5},{2,6},{3,7},{4,0},{5,1},{6,2},{7,3},{8,12},{9,13},{10,... | collective-permute-start | bytes 1179656 | tf_op jit(solution)/shard_map/ppermute | solution.py:48
  359.7 28.8 %collective-permute-start.111 = (f32[192,1024]{1,0:T(8,128)S(1)}, f32[192,1024]{1,0:T(8,128)S(1)}, u32[]{:S(2)}, u32[]{:S(2)}) collective-permute-start(f32[192,1024]{1,0:T(8,128)S(1)} %copy-done.90), channel_id=1, source_target_pairs={{0,4},{1,5},{2,6},{3,7},{4,0},{5,1},{6,2},{7,3},{8,12},{9,13},{10,... | collective-permute-start | bytes 2359304 | tf_op jit(solution)/shard_map/ppermute | solution.py:48
  360.2 32.1 %collective-permute-start.85 = (f32[192,1024]{1,0:T(8,128)S(1)}, f32[192,1024]{1,0:T(8,128)S(1)}, u32[]{:S(2)}, u32[]{:S(2)}) collective-permute-start(f32[192,1024]{1,0:T(8,128)S(1)} %copy-done.92), channel_id=1, source_target_pairs={{0,4},{1,5},{2,6},{3,7},{4,0},{5,1},{6,2},{7,3},{8,12},{9,13},{10,... | collective-permute-start | bytes 2359304 | tf_op jit(solution)/shard_map/ppermute | solution.py:48
  374.7 40.2 %collective-permute-start.118 = (f32[2,4,256,128]{3,2,1,0:T(8,128)}, f32[2,4,256,128]{3,2,1,0:T(8,128)}, u32[]{:S(2)}, u32[]{:S(2)}) collective-permute-start(f32[2,4,256,128]{3,2,1,0:T(8,128)} %slice.431), channel_id=1, source_target_pairs={{0,16},{1,17},{2,18},{3,19},{4,20},{5,21},{6,22},{7,23},{8,24},{9,... | collective-permute-start | bytes 3145736 | tf_op jit(solution)/shard_map/ppermute | solution.py:48
  377.7 44.1 %collective-permute-start.92 = (f32[2,4,256,128]{3,2,1,0:T(8,128)}, f32[2,4,256,128]{3,2,1,0:T(8,128)}, u32[]{:S(2)}, u32[]{:S(2)}) collective-permute-start(f32[2,4,256,128]{3,2,1,0:T(8,128)} %slice.411), channel_id=1, source_target_pairs={{0,16},{1,17},{2,18},{3,19},{4,20},{5,21},{6,22},{7,23},{8,24},{9,... | collective-permute-start | bytes 3145736 | tf_op jit(solution)/shard_map/ppermute | solution.py:48
  386.1 22.8 %collective-permute-start.131 = (f32[1,9,64,128]{3,2,1,0:T(8,128)}, f32[1,9,64,128]{3,2,1,0:T(8,128)}, u32[]{:S(2)}, u32[]{:S(2)}) collective-permute-start(f32[1,9,64,128]{3,2,1,0:T(8,128)} %slice.441), channel_id=1, source_target_pairs={{0,2},{1,3},{2,0},{3,1},{4,6},{5,7},{6,4},{7,5},{8,10},{9,11},{10,... | collective-permute-start | bytes 884744 | tf_op jit(solution)/shard_map/ppermute | solution.py:48
  388.5 26.4 %collective-permute-start.105 = (f32[1,9,64,128]{3,2,1,0:T(8,128)}, f32[1,9,64,128]{3,2,1,0:T(8,128)S(1)}, u32[]{:S(2)}, u32[]{:S(2)}) collective-permute-start(f32[1,9,64,128]{3,2,1,0:T(8,128)} %slice.421), channel_id=1, source_target_pairs={{0,2},{1,3},{2,0},{3,1},{4,6},{5,7},{6,4},{7,5},{8,10},{9,11},{10,... | collective-permute-start | bytes 884744 | tf_op jit(solution)/shard_map/ppermute | solution.py:48
  392.2 32.1 %collective-permute-start.112 = (f32[4,4,128,128]{3,2,1,0:T(8,128)}, f32[4,4,128,128]{3,2,1,0:T(8,128)S(1)}, u32[]{:S(2)}, u32[]{:S(2)}) collective-permute-start(f32[4,4,128,128]{3,2,1,0:T(8,128)} %slice.423), channel_id=1, source_target_pairs={{0,8},{1,9},{2,10},{3,11},{4,12},{5,13},{6,14},{7,15},{8,0},{9,1},... | collective-permute-start | bytes 3145736 | tf_op jit(solution)/shard_map/ppermute | solution.py:48
  408.9 32.1 %collective-permute-start.86 = (f32[4,4,128,128]{3,2,1,0:T(8,128)S(1)}, f32[4,4,128,128]{3,2,1,0:T(8,128)S(1)}, u32[]{:S(2)}, u32[]{:S(2)}) collective-permute-start(f32[4,4,128,128]{3,2,1,0:T(8,128)S(1)} %slice.395), channel_id=1, source_target_pairs={{0,8},{1,9},{2,10},{3,11},{4,12},{5,13},{6,14},{7,15},{8,0},{9,1},... | collective-permute-start | bytes 3145736 | tf_op jit(solution)/shard_map/ppermute | solution.py:48
  416.3 36.0 %collective-permute-start.119 = (f32[1,4,256,128]{3,2,1,0:T(8,128)S(1)}, f32[1,4,256,128]{3,2,1,0:T(8,128)S(1)}, u32[]{:S(2)}, u32[]{:S(2)}) collective-permute-start(f32[1,4,256,128]{3,2,1,0:T(8,128)S(1)} %slice.433), channel_id=1, source_target_pairs={{0,8},{1,9},{2,10},{3,11},{4,12},{5,13},{6,14},{7,15},{8,0},{9,1},... | collective-permute-start | bytes 1572872 | tf_op jit(solution)/shard_map/ppermute | solution.py:48
  423.1 38.5 %collective-permute-start.93 = (f32[1,4,256,128]{3,2,1,0:T(8,128)S(1)}, f32[1,4,256,128]{3,2,1,0:T(8,128)S(1)}, u32[]{:S(2)}, u32[]{:S(2)}) collective-permute-start(f32[1,4,256,128]{3,2,1,0:T(8,128)S(1)} %slice.413), channel_id=1, source_target_pairs={{0,8},{1,9},{2,10},{3,11},{4,12},{5,13},{6,14},{7,15},{8,0},{9,1},... | collective-permute-start | bytes 1572872 | tf_op jit(solution)/shard_map/ppermute | solution.py:48
  424.5 39.6 %collective-permute-start.113 = (f32[2,4,128,128]{3,2,1,0:T(8,128)S(1)}, f32[2,4,128,128]{3,2,1,0:T(8,128)S(1)}, u32[]{:S(2)}, u32[]{:S(2)}) collective-permute-start(f32[2,4,128,128]{3,2,1,0:T(8,128)S(1)} %slice.425), channel_id=1, source_target_pairs={{0,16},{1,17},{2,18},{3,19},{4,20},{5,21},{6,22},{7,23},{8,24},{9,... | collective-permute-start | bytes 1572872 | tf_op jit(solution)/shard_map/ppermute | solution.py:48
  441.2 38.7 %collective-permute-start.87 = (f32[2,4,128,128]{3,2,1,0:T(8,128)S(1)}, f32[2,4,128,128]{3,2,1,0:T(8,128)S(1)}, u32[]{:S(2)}, u32[]{:S(2)}) collective-permute-start(f32[2,4,128,128]{3,2,1,0:T(8,128)S(1)} %slice.397), channel_id=1, source_target_pairs={{0,16},{1,17},{2,18},{3,19},{4,20},{5,21},{6,22},{7,23},{8,24},{9,... | collective-permute-start | bytes 1572872 | tf_op jit(solution)/shard_map/ppermute | solution.py:48
  452.3 10.2 %collective-permute-start.120 = (f32[1,2,256,128]{3,2,1,0:T(8,128)S(1)}, f32[1,2,256,128]{3,2,1,0:T(8,128)S(1)}, u32[]{:S(2)}, u32[]{:S(2)}) collective-permute-start(f32[1,2,256,128]{3,2,1,0:T(8,128)S(1)} %slice.435), channel_id=1, source_target_pairs={{0,1},{1,0},{2,3},{3,2},{4,5},{5,4},{6,7},{7,6},{8,9},{9,8},{10,11... | collective-permute-start | bytes 786440 | tf_op jit(solution)/shard_map/ppermute | solution.py:48
  461.8 11.0 %collective-permute-start.94 = (f32[1,2,256,128]{3,2,1,0:T(8,128)S(1)}, f32[1,2,256,128]{3,2,1,0:T(8,128)S(1)}, u32[]{:S(2)}, u32[]{:S(2)}) collective-permute-start(f32[1,2,256,128]{3,2,1,0:T(8,128)S(1)} %slice.415), channel_id=1, source_target_pairs={{0,1},{1,0},{2,3},{3,2},{4,5},{5,4},{6,7},{7,6},{8,9},{9,8},{10,11... | collective-permute-start | bytes 786440 | tf_op jit(solution)/shard_map/ppermute | solution.py:48
  462.6 12.1 %collective-permute-start.121 = (f32[1,1,256,128]{3,2,1,0:T(8,128)S(1)}, f32[1,1,256,128]{3,2,1,0:T(8,128)S(1)}, u32[]{:S(2)}, u32[]{:S(2)}) collective-permute-start(f32[1,1,256,128]{3,2,1,0:T(8,128)S(1)} %slice.437), channel_id=1, source_target_pairs={{0,2},{1,3},{2,0},{3,1},{4,6},{5,7},{6,4},{7,5},{8,10},{9,11},{10,... | collective-permute-start | bytes 393224 | tf_op jit(solution)/shard_map/ppermute | solution.py:48
  464.3 15.3 %collective-permute-start.114 = (f32[2,2,128,128]{3,2,1,0:T(8,128)S(1)}, f32[2,2,128,128]{3,2,1,0:T(8,128)S(1)}, u32[]{:S(2)}, u32[]{:S(2)}) collective-permute-start(f32[2,2,128,128]{3,2,1,0:T(8,128)S(1)} %slice.427), channel_id=1, source_target_pairs={{0,1},{1,0},{2,3},{3,2},{4,5},{5,4},{6,7},{7,6},{8,9},{9,8},{10,11... | collective-permute-start | bytes 786440 | tf_op jit(solution)/shard_map/ppermute | solution.py:48
  472.8 17.0 %collective-permute-start.95 = (f32[1,1,256,128]{3,2,1,0:T(8,128)S(1)}, f32[1,1,256,128]{3,2,1,0:T(8,128)S(1)}, u32[]{:S(2)}, u32[]{:S(2)}) collective-permute-start(f32[1,1,256,128]{3,2,1,0:T(8,128)S(1)} %slice.417), channel_id=1, source_target_pairs={{0,2},{1,3},{2,0},{3,1},{4,6},{5,7},{6,4},{7,5},{8,10},{9,11},{10,... | collective-permute-start | bytes 393224 | tf_op jit(solution)/shard_map/ppermute | solution.py:48
  479.6 7.0 %collective-permute-start.115 = (f32[2,1,128,128]{3,2,1,0:T(8,128)S(1)}, f32[2,1,128,128]{3,2,1,0:T(8,128)S(1)}, u32[]{:S(2)}, u32[]{:S(2)}) collective-permute-start(f32[2,1,128,128]{3,2,1,0:T(8,128)S(1)} %slice.429), channel_id=1, source_target_pairs={{0,2},{1,3},{2,0},{3,1},{4,6},{5,7},{6,4},{7,5},{8,10},{9,11},{10,... | collective-permute-start | bytes 393224 | tf_op jit(solution)/shard_map/ppermute | solution.py:48
  479.9 8.1 %collective-permute-start.88 = (f32[2,2,128,128]{3,2,1,0:T(8,128)S(1)}, f32[2,2,128,128]{3,2,1,0:T(8,128)S(1)}, u32[]{:S(2)}, u32[]{:S(2)}) collective-permute-start(f32[2,2,128,128]{3,2,1,0:T(8,128)S(1)} %slice.399), channel_id=1, source_target_pairs={{0,1},{1,0},{2,3},{3,2},{4,5},{5,4},{6,7},{7,6},{8,9},{9,8},{10,11... | collective-permute-start | bytes 786440 | tf_op jit(solution)/shard_map/ppermute | solution.py:48
  486.7 17.7 %collective-permute-start.133 = (f32[1088,128]{1,0:T(8,128)S(1)}, f32[1088,128]{1,0:T(8,128)S(1)}, u32[]{:S(2)}, u32[]{:S(2)}) collective-permute-start(f32[1088,128]{1,0:T(8,128)S(1)} %get-tuple-element.152), channel_id=1, source_target_pairs={{0,16},{1,17},{2,18},{3,19},{4,20},{5,21},{6,22},{7,23},{8,24},{9,... | collective-permute-start | bytes 1671176 | tf_op jit(solution)/shard_map/ppermute | solution.py:48
  488.1 7.3 %collective-permute-start.89 = (f32[2,1,128,128]{3,2,1,0:T(8,128)S(1)}, f32[2,1,128,128]{3,2,1,0:T(8,128)S(1)}, u32[]{:S(2)}, u32[]{:S(2)}) collective-permute-start(f32[2,1,128,128]{3,2,1,0:T(8,128)S(1)} %slice.401), channel_id=1, source_target_pairs={{0,2},{1,3},{2,0},{3,1},{4,6},{5,7},{6,4},{7,5},{8,10},{9,11},{10,... | collective-permute-start | bytes 393224 | tf_op jit(solution)/shard_map/ppermute | solution.py:48
  489.9 17.2 %collective-permute-start.132 = (f32[1088,128]{1,0:T(8,128)S(1)}, f32[1088,128]{1,0:T(8,128)S(1)}, u32[]{:S(2)}, u32[]{:S(2)}) collective-permute-start(f32[1088,128]{1,0:T(8,128)S(1)} %get-tuple-element.152), channel_id=1, source_target_pairs={{0,8},{1,9},{2,10},{3,11},{4,12},{5,13},{6,14},{7,15},{8,0},{9,1},... | collective-permute-start | bytes 1671176 | tf_op jit(solution)/shard_map/ppermute | solution.py:48
  491.3 27.0 %collective-permute-start.134 = (f32[1088,128]{1,0:T(8,128)S(1)}, f32[1088,128]{1,0:T(8,128)S(1)}, u32[]{:S(2)}, u32[]{:S(2)}) collective-permute-start(f32[1088,128]{1,0:T(8,128)S(1)} %get-tuple-element.152), channel_id=1, source_target_pairs={{0,24},{1,25},{2,26},{3,27},{4,28},{5,29},{6,30},{7,31},{8,16},{9,... | collective-permute-start | bytes 1671176 | tf_op jit(solution)/shard_map/ppermute | solution.py:48
  495.5 26.5 %collective-permute-start.107 = (f32[1088,128]{1,0:T(8,128)S(1)}, f32[1088,128]{1,0:T(8,128)S(1)}, u32[]{:S(2)}, u32[]{:S(2)}) collective-permute-start(f32[1088,128]{1,0:T(8,128)S(1)} %get-tuple-element.154), channel_id=1, source_target_pairs={{0,16},{1,17},{2,18},{3,19},{4,20},{5,21},{6,22},{7,23},{8,24},{9,... | collective-permute-start | bytes 1671176 | tf_op jit(solution)/shard_map/ppermute | solution.py:48
  496.9 32.6 %collective-permute-start.106 = (f32[1088,128]{1,0:T(8,128)S(1)}, f32[1088,128]{1,0:T(8,128)S(1)}, u32[]{:S(2)}, u32[]{:S(2)}) collective-permute-start(f32[1088,128]{1,0:T(8,128)S(1)} %get-tuple-element.154), channel_id=1, source_target_pairs={{0,8},{1,9},{2,10},{3,11},{4,12},{5,13},{6,14},{7,15},{8,0},{9,1},... | collective-permute-start | bytes 1671176 | tf_op jit(solution)/shard_map/ppermute | solution.py:48
  504.4 34.7 %collective-permute-start.108 = (f32[1088,128]{1,0:T(8,128)S(1)}, f32[1088,128]{1,0:T(8,128)S(1)}, u32[]{:S(2)}, u32[]{:S(2)}) collective-permute-start(f32[1088,128]{1,0:T(8,128)S(1)} %get-tuple-element.154), channel_id=1, source_target_pairs={{0,24},{1,25},{2,26},{3,27},{4,28},{5,29},{6,30},{7,31},{8,16},{9,... | collective-permute-start | bytes 1671176 | tf_op jit(solution)/shard_map/ppermute | solution.py:48
  518.4 31.4 %collective-permute-start.135 = (f32[4,1088,128]{2,1,0:T(8,128)S(1)}, f32[4,1088,128]{2,1,0:T(8,128)}, u32[]{:S(2)}, u32[]{:S(2)}) collective-permute-start(f32[4,1088,128]{2,1,0:T(8,128)S(1)} %pad_maximum_fusion.1.own_ref), channel_id=1, source_target_pairs={{0,4},{1,5},{2,6},{3,7},{4,0},{5,1},{6,2},{7,3},{8,12},{9,13},{10,... | collective-permute-start | bytes 6684680 | tf_op jit(solution)/shard_map/ppermute | solution.py:48
  540.6 17.6 %collective-permute-start.109 = (f32[4,1088,128]{2,1,0:T(8,128)}, f32[4,1088,128]{2,1,0:T(8,128)}, u32[]{:S(2)}, u32[]{:S(2)}) collective-permute-start(f32[4,1088,128]{2,1,0:T(8,128)} %pad_maximum_fusion.own_ref), channel_id=1, source_target_pairs={{0,4},{1,5},{2,6},{3,7},{4,0},{5,1},{6,2},{7,3},{8,12},{9,13},{10,... | collective-permute-start | bytes 6684680 | tf_op jit(solution)/shard_map/ppermute | solution.py:48
  (219 other events, 1778.0 us)

commit v3 on v2

v3 whole, which is shorter than its diff:
```python
import functools

import jax
import jax.numpy as jnp
from jax import lax
from jax.experimental import pallas as pl
from jax.experimental.pallas import tpu as pltpu
from jax.sharding import PartitionSpec as P

BLOCKS = 2
MAP = 7
MAPW = 8
TILE = 2
PIECES = 9
SLOTS = 2
IMG_ROWS = MAP * MAPW * SLOTS
EPS = 1e-05
CH = 512
BF = jnp.bfloat16
F32 = jnp.float32
VMEM_LIMIT = 16 * 1024 * 1024
AXES = ("wide", "narrow")
ROOM = 640 * 1024


class Grid:
    def __init__(self, wide, narrow):
        chips = wide // 2
        side = 1
        while side * side < chips:
            side *= 2
        self.y, self.x, self.c, self.z = chips // side, side, 2, narrow

    def index(self):
        wide = lax.axis_index("wide")
        core = wide % 2
        chip = wide // 2
        return chip // self.x, chip % self.x, core, lax.axis_index("narrow")

    def swap(self, value, dy=0, dx=0, dc=0, dz=0):
        pairs = []
        for y in range(self.y):
            for x in range(self.x):
                for c in range(self.c):
                    for z in range(self.z):
                        src = ((y * self.x + x) * 2 + c) * self.z + z
                        dst = (((y ^ dy) * self.x + (x ^ dx)) * 2 + (c ^ dc)) * self.z + (z ^ dz)
                        pairs.append((src, dst))
        return lax.ppermute(value, AXES, pairs)

    def plane(self, value):
        if self.y * self.x == 4:
            return lax.all_gather(value, "wide")
        groups = {}
        for y in range(self.y):
            for x in range(self.x):
                for c in range(2):
                    groups.setdefault((y // 2, x // 2), []).append((y * self.x + x) * 2 + c)
        return lax.all_gather(value, "wide", axis_index_groups=list(groups.values()))

    def phases(self):
        found = [[dict(dc=1)]]
        step = 1
        while step < max(self.x, self.y):
            group = []
            for dy in (0, step):
                for dx in (0, step):
                    if (dy or dx) and dy < self.y and dx < self.x:
                        group.append(dict(dy=dy, dx=dx))
            found.append(group)
            step *= 2
        self.far_groups = found[2:]
        found.append([dict(dz=k) for k in range(1, min(self.z, 4))])
        step = 4
        while step < self.z:
            found.append([dict(dz=step)])
            step *= 2
        return found

    def far(self):
        self.phases()
        return self.far_groups


class Bulk:
    def __init__(self, grid, room):
        self.grid, self.room = grid, room
        self.waiting = []
        self.flying = {"plane": [], "deep": [], "spare": []}
        self.late = []

    def move(self, value, step):
        return step(value) if callable(step) else self.grid.swap(value, **step)

    def add(self, flow):
        self.advance(flow, None)

    def advance(self, flow, value):
        while True:
            try:
                kind, pieces = flow.send(value)
            except StopIteration:
                return
            if kind != "core":
                self.waiting.append((flow, kind, pieces))
                return
            value = [self.move(v, step) for v, step in pieces]

    def load(self, pieces):
        used = {}
        for value, step in pieces:
            for name in () if callable(step) else step:
                used[name] = used.get(name, 0) + value.size * 4
        return used

    def open(self, kinds, arrays):
        used, chosen, rest = {}, [], []
        for item in self.waiting:
            if item[1] in kinds:
                load = self.load(item[2])
                if all(used.get(n, 0) + load[n] <= self.room for n in load):
                    for n in load:
                        used[n] = used.get(n, 0) + load[n]
                    chosen.append(item)
                    continue
                for n in load:
                    used[n] = max(used.get(n, 0), self.room)
            rest.append(item)
        self.waiting = rest
        if not chosen:
            return arrays
        values = [v for _, _, pieces in chosen for v, _ in pieces]
        tied = lax.optimization_barrier(tuple(arrays) + tuple(values))
        arrays, values = list(tied[: len(arrays)]), list(tied[len(arrays) :])
        for flow, kind, pieces in chosen:
            got = [self.move(values.pop(0), step) for _, step in pieces]
            self.flying[kind].append((flow, got))
        return arrays

    def close(self, kind, array):
        done = self.flying[kind]
        self.flying[kind] = []
        if kind == "deep":
            done = done + self.late
            self.late, self.flying["spare"] = self.flying["spare"], []
        if not done:
            return array
        values = [v for _, got in done for v in got]
        tied = lax.optimization_barrier((array,) + tuple(values))
        array, values = tied[0], list(tied[1:])
        for flow, got in done:
            self.advance(flow, [values.pop(0) for _ in got])
        return array

    def last(self, array):
        return self.close("deep", self.close("plane", array))

    def finish(self):
        while self.waiting or self.late or self.flying["spare"]:
            batch, self.waiting = self.waiting, []
            flown = self.late
            self.late, self.flying["spare"] = self.flying["spare"], []
            for flow, kind, pieces in batch:
                got = [self.move(v, step) for v, step in pieces]
                if kind == "spare":
                    self.flying["spare"].append((flow, got))
                else:
                    flown = flown + [(flow, got)]
            values = [v for _, got in flown for v in got]
            if len(values) > 1:
                values = lax.optimization_barrier(values)
            values = list(values)
            for flow, got in flown:
                self.advance(flow, [values.pop(0) for _ in got])


def exchange(grid, bulk, payload, join):
    groups = grid.phases()
    for number, group in enumerate(groups):
        if number == 1:
            payload = bulk.close("plane", payload)
        if number + 1 == len(groups):
            (payload,) = bulk.open(("plane",), [payload])
            payload = bulk.close("deep", payload)
        members = [payload] + [grid.swap(payload, **step) for step in group]
        if number + 1 < len(groups):
            payload = join(members)
    return bulk.open(("deep", "spare"), members)


def add_members(members):
    return sum(members[1:], members[0])


def join_moments(members):
    count = sum(m[2] for m in members)
    plain = sum(m[0] for m in members)
    mean = plain / count
    square = sum(m[1] for m in members)
    for m in members:
        gap = m[0] / jnp.maximum(m[2], 1.0) - mean
        square = square + m[2] * (gap * gap)
    return jnp.stack([plain, square, count])


def put_rows(ref, at, stream, value, first=0):
    base = stream * (ref.shape[1] // 2)
    for j in range(value.shape[1] // 128):
        ref[at, pl.ds(base + first + j, 1), :] = value[:, j * 128 : (j + 1) * 128]


def as_row(value):
    return jnp.concatenate([value[j : j + 1] for j in range(value.shape[0])], axis=1)


def put_statistics(members, out_ref):
    counts = [m[2] for m in members]
    sums = [m[0] for m in members]
    count = sum(counts[1:], counts[0])
    mean = sum(sums[1:], sums[0]) / count
    square = None
    for m, n, v in zip(members, counts, sums):
        gap = v / jnp.maximum(n, 1.0) - mean
        term = m[1] + n * (gap * gap)
        square = term if square is None else square + term
    rstd = lax.rsqrt(square / count + EPS)
    inv = 1.0 / count
    half = mean.shape[0] // 2
    for stream in range(2):
        at = slice(stream * half, (stream + 1) * half)
        out_ref[2 * stream : 2 * stream + 1, :] = as_row(mean[at])
        out_ref[2 * stream + 1 : 2 * stream + 2, :] = as_row(rstd[at])
        out_ref[4 + stream : 5 + stream, :] = as_row(inv[at])
    out_ref[6:8, :] = jnp.zeros((2, out_ref.shape[1]), F32)


def put_shares(members, mr_ref, share_ref, both_ref):
    half = members[0].shape[1] // 2
    for kind in range(2):
        total = members[0][kind]
        for m in members[1:]:
            total += m[kind]
        for stream in range(2):
            value = as_row(total[stream * half : (stream + 1) * half])
            share_ref[2 * stream + kind : 2 * stream + kind + 1, :] = value * mr_ref[4 + stream : 5 + stream, :]
        both_ref[kind : kind + 1, :] = as_row(total[:half] + total[half:])


def parts(rows):
    return ((0, 0, IMG_ROWS), (1, IMG_ROWS, rows))


def sigmoid(v):
    return 0.5 * jnp.tanh(0.5 * v) + 0.5


def slope(v):
    s = sigmoid(v)
    return s * (1.0 + v * (1.0 - s))


def local_moments(value, mask_ref, stats_ref, first):
    width = value.shape[1]
    for stream, lo, hi in parts(value.shape[0]):
        v = value[lo:hi]
        m = mask_ref[lo:hi, :]
        count = jnp.sum(m, axis=0, keepdims=True)
        plain = jnp.sum(v * m, axis=0, keepdims=True)
        gap = (v - plain / jnp.maximum(count, 1.0)) * m
        put_rows(stats_ref, 0, stream, plain, first)
        put_rows(stats_ref, 1, stream, jnp.sum(gap * gap, axis=0, keepdims=True), first)
        put_rows(stats_ref, 2, stream, jnp.broadcast_to(count, (1, width)), first)


def normed_of(value, mr_ref, stream):
    return (value - mr_ref[2 * stream : 2 * stream + 1, :]) * mr_ref[2 * stream + 1 : 2 * stream + 2, :]


def shifted(image_ref, tile_ref, dy, dx, tile_rows):
    start = 24 + 2 * MAPW * dy + 2 * dx
    image = image_ref[start : start + IMG_ROWS, :]
    start = 8 + TILE * dy + dx
    tile = tile_ref[start : start + tile_rows, :]
    if dy or dx:
        place = lax.broadcasted_iota(jnp.int32, (tile_rows, 1), 0)
        ty = (place // TILE) % TILE + dy
        tx = place % TILE + dx
        valid = (ty >= 0) & (ty < TILE) & (tx >= 0) & (tx < TILE)
        tile = jnp.where(valid, tile, 0.0)
    return image, tile


def fill_patches(value, image_ref, tile_ref, patch_ref, sign):
    rows = value.shape[0]
    tile_rows = rows - IMG_ROWS
    width = value.shape[1]
    image_ref[0:24, :] = jnp.zeros((24, width), F32)
    image_ref[24 + IMG_ROWS : 48 + IMG_ROWS, :] = jnp.zeros((24, width), F32)
    image_ref[24 : 24 + IMG_ROWS, :] = value[0:IMG_ROWS]
    tile_ref[0:8, :] = jnp.zeros((8, width), F32)
    tile_ref[8 + tile_rows : 16 + tile_rows, :] = jnp.zeros((8, width), F32)
    tile_ref[8 : 8 + tile_rows, :] = value[IMG_ROWS:]
    for tap in range(9):
        dy, dx = tap // 3 - 1, tap % 3 - 1
        image, tile = shifted(image_ref, tile_ref, sign * dy, sign * dx, tile_rows)
        patch_ref[tap, 0:IMG_ROWS, :] = image.astype(BF)
        patch_ref[tap, IMG_ROWS:rows, :] = tile.astype(BF)


def dot(a, b):
    return jnp.dot(a, b, preferred_element_type=F32)


def dot_nt(a, b):
    return lax.dot_general(a, b, (((1,), (1,)), ((), ())), preferred_element_type=F32)


def full(shape):
    zeros = (0,) * len(shape)
    return pl.BlockSpec(shape, lambda k: zeros)


def cols(rows):
    return pl.BlockSpec((rows, CH), lambda k: (0, k))


def smem():
    return pl.BlockSpec(memory_space=pltpu.SMEM)


def call(body, steps, in_specs, out_specs, out_shape, scratch=(), name=None, flops=0, transcendentals=0):
    return pl.pallas_call(
        body,
        grid=(steps,),
        in_specs=in_specs,
        out_specs=out_specs,
        out_shape=out_shape,
        scratch_shapes=list(scratch),
        compiler_params=pltpu.CompilerParams(
            vmem_limit_bytes=VMEM_LIMIT, dimension_semantics=("arbitrary",)
        ),
        cost_estimate=pl.CostEstimate(flops=0, bytes_accessed=0, transcendentals=0),
        name=name,
    )


def sds(shape, dtype=F32):
    return jax.ShapeDtypeStruct(shape, dtype)


def near(shape, dtype=F32):
    return pltpu.VMEM(shape, dtype)


def stay(value):
    return pltpu.with_memory_space_constraint(value, pltpu.VMEM)


def mid_rows(table_ref, block, place):
    at = 2 * block + place
    return table_ref.at[at : at + 1], table_ref.at[2 * BLOCKS + at : 2 * BLOCKS + at + 1]


def out_rows(table_ref, block):
    return table_ref.at[block : block + 1], table_ref.at[BLOCKS + block : BLOCKS + block + 1]


def rounded(value):
    return value.astype(BF).astype(F32)


def payload(width, kinds=3):
    return (kinds, 2 * width // 128, 128)


def reduce_first(x, w_reduce, mask):
    rows, d_in = x.shape
    mid = w_reduce.shape[2]

    def body(x_ref, w_ref, mask_ref, red_ref, stats_ref):
        k = pl.program_id(0)
        part = dot(x_ref[...], w_ref[0])

        @pl.when(k == 0)
        def _():
            red_ref[...] = part

        @pl.when(k > 0)
        def _():
            red_ref[...] += part

        @pl.when(k == pl.num_programs(0) - 1)
        def _():
            local_moments(red_ref[...], mask_ref, stats_ref, 0)

    return call(
        body,
        d_in // CH,
        [cols(rows), pl.BlockSpec((1, CH, mid), lambda k: (0, k, 0)), full((rows, 1))],
        [full((rows, mid)), full(payload(mid))],
        [near((rows, mid)), near(payload(mid))],
        name="reduce_first",
        flops=2 * rows * d_in * mid,
    )(x, w_reduce, mask)


def spatial_stage(number, red, members, table, mask, w9, select):
    rows, mid = red.shape
    size = len(members)

    def body(red_ref, table_ref, mask_ref, w_ref, select_ref, *refs):
        gain_ref, bias_ref = mid_rows(table_ref, number, 0)
        got, (mr_ref, hid_ref, out_ref, stats_ref, image, tile, patch) = refs[:size], refs[size:]
        k = pl.program_id(0)

        @pl.when(k == 0)
        def _():
            put_statistics(got, mr_ref)
            pieces = []
            for stream, lo, hi in parts(rows):
                z = normed_of(red_ref[lo:hi, :], mr_ref, stream) * gain_ref[...] + bias_ref[...]
                pieces.append(z * sigmoid(z) * mask_ref[lo:hi, :])
            hidden = jnp.concatenate(pieces, axis=0)
            fill_patches(hidden, image, tile, patch, 1)
            hid_ref[...] = dot(hidden.astype(BF), select_ref[...])
            out_ref[...] = jnp.zeros((rows, mid), F32)

        total = out_ref[...]
        for j in range(3):
            total += dot(patch[3 * k + j], w_ref[0, j])
        out_ref[...] = total

        @pl.when(k == 2)
        def _():
            local_moments(out_ref[...], mask_ref, stats_ref, 0)

    return call(
        body,
        3,
        [
            full((rows, mid)),
            full(table.shape),
            full((rows, 1)),
            pl.BlockSpec((1, 3, mid, mid), lambda k: (number, k, 0, 0)),
            full((mid, mid)),
        ]
        + [full(payload(mid))] * size,
        [
            full((8, mid)),
            full((rows, mid)),
            full((rows, mid)),
            full(payload(mid)),
        ],
        [
            near((8, mid)),
            near((rows, mid)),
            near((rows, mid)),
            near(payload(mid)),
        ],
        [
            pltpu.VMEM((IMG_ROWS + 48, mid), F32),
            pltpu.VMEM((rows - IMG_ROWS + 16, mid), F32),
            pltpu.VMEM((9, rows, mid), BF),
        ],
        name="spatial_stage",
        flops=2 * rows * 9 * mid * mid,
    )(red, table, mask, w9, select, *members)


def expand_stage(number, spa, members, table, mask, w_expand):
    rows, mid = spa.shape
    d_in = w_expand.shape[2]
    size = len(members)

    def body(spa_ref, table_ref, mask_ref, w_ref, *refs):
        gain_ref, bias_ref = mid_rows(table_ref, number, 1)
        got, (mr_ref, hid_ref, out_ref, stats_ref) = refs[:size], refs[size:]
        k = pl.program_id(0)

        @pl.when(k == 0)
        def _():
            put_statistics(got, mr_ref)
            for stream, lo, hi in parts(rows):
                z = normed_of(spa_ref[lo:hi, :], mr_ref, stream) * gain_ref[...] + bias_ref[...]
                hid_ref[lo:hi, :] = rounded(z * sigmoid(z) * mask_ref[lo:hi, :])

        value = dot(hid_ref[...].astype(BF), w_ref[0])
        out_ref[...] = value
        local_moments(value, mask_ref, stats_ref, k * (CH // 128))

    return call(
        body,
        d_in // CH,
        [
            full((rows, mid)),
            full(table.shape),
            full((rows, 1)),
            pl.BlockSpec((1, mid, CH), lambda k: (number, 0, k)),
        ]
        + [full(payload(mid))] * size,
        [full((8, mid)), full((rows, mid)), cols(rows), full(payload(d_in))],
        [near((8, mid)), near((rows, mid)), near((rows, d_in)), near(payload(d_in))],
        name="expand_stage",
        flops=2 * rows * d_in * mid,
    )(spa, table, mask, w_expand, *members)


def pick(ref, k, stream, row):
    return ref[2 * stream + row : 2 * stream + row + 1, pl.ds(pl.multiple_of(k * CH, CH), CH)]


def normed_at(value, mr_ref, k, stream):
    return (value - pick(mr_ref, k, stream, 0)) * pick(mr_ref, k, stream, 1)


def join_stage(number, exp, members, table, act, mask, w_reduce):
    rows, d_in = exp.shape
    mid = w_reduce.shape[2]
    size = len(members)

    def body(exp_ref, table_ref, act_ref, mask_ref, w_ref, *refs):
        gain_ref, bias_ref = out_rows(table_ref, number - 1)
        got, (mr_ref, out_ref, low_ref, red_ref, stats_ref) = refs[:size], refs[size:]
        k = pl.program_id(0)

        @pl.when(k == 0)
        def _():
            put_statistics(got, mr_ref)

        for stream, lo, hi in parts(rows):
            z = (
                normed_at(exp_ref[lo:hi, :], mr_ref, k, stream) * gain_ref[...]
                + bias_ref[...]
                + act_ref[lo:hi, :].astype(F32)
            )
            out = z * sigmoid(z) * mask_ref[lo:hi, :]
            out_ref[lo:hi, :] = out
            low_ref[lo:hi, :] = rounded(out)
        part = dot(low_ref[...].astype(BF), w_ref[0])

        @pl.when(k == 0)
        def _():
            red_ref[...] = part

        @pl.when(k > 0)
        def _():
            red_ref[...] += part

        @pl.when(k == pl.num_programs(0) - 1)
        def _():
            local_moments(red_ref[...], mask_ref, stats_ref, 0)

    return call(
        body,
        d_in // CH,
        [
            cols(rows),
            cols(table.shape[0]),
            cols(rows),
            full((rows, 1)),
            pl.BlockSpec((1, CH, mid), lambda k: (number, k, 0)),
        ]
        + [full(payload(d_in))] * size,
        [full((8, d_in)), cols(rows), cols(rows), full((rows, mid)), full(payload(mid))],
        [near((8, d_in)), near((rows, d_in)), near((rows, d_in)), near((rows, mid)), near(payload(mid))],
        name="join_stage",
        flops=2 * rows * d_in * mid,
        transcendentals=rows * d_in,
    )(exp, table, act, mask, w_reduce, *members)


def put_sums(stream, pre, normed, sums_ref, first=0):
    put_rows(sums_ref, 0, stream, jnp.sum(pre, axis=0, keepdims=True), first)
    put_rows(sums_ref, 1, stream, jnp.sum(pre * normed, axis=0, keepdims=True), first)


def turn_stage(number, exp, members, table, act, mask, grad):
    rows, d_in = exp.shape
    size = len(members)

    def body(exp_ref, table_ref, act_ref, mask_ref, grad_ref, *refs):
        gain_ref, bias_ref = out_rows(table_ref, number)
        got, (mr_ref, out_ref, pre_ref, sums_ref) = refs[:size], refs[size:]
        k = pl.program_id(0)

        @pl.when(k == 0)
        def _():
            put_statistics(got, mr_ref)

        for stream, lo, hi in parts(rows):
            n = normed_at(exp_ref[lo:hi, :], mr_ref, k, stream)
            z = n * gain_ref[...] + bias_ref[...] + act_ref[lo:hi, :].astype(F32)
            s = sigmoid(z)
            m = mask_ref[lo:hi, :]
            out_ref[lo:hi, :] = z * s * m
            pre = grad_ref[lo:hi, :].astype(F32) * m * (s * (1.0 + z * (1.0 - s)))
            pre_ref[lo:hi, :] = pre
            put_sums(stream, pre, n, sums_ref, k * (CH // 128))

    return call(
        body,
        d_in // CH,
        [cols(rows), cols(table.shape[0]), cols(rows), full((rows, 1)), cols(rows)]
        + [full(payload(d_in))] * size,
        [full((8, d_in)), cols(rows), cols(rows), full(payload(d_in, 2))],
        [near((8, d_in)), near((rows, d_in)), near((rows, d_in)), near(payload(d_in, 2))],
        name="turn_stage",
        flops=20 * rows * d_in,
        transcendentals=rows * d_in,
    )(exp, table, act, mask, grad, *members)


def norm_back(pre, normed, plain, cross, scale, mask):
    return mask * scale * (pre - plain - normed * cross)


def rows_of(ref, stream):
    return ref[2 * stream : 2 * stream + 1, :], ref[2 * stream + 1 : 2 * stream + 2, :]


def back_expand(number, me, pre3, exp, mr3, members, outer, mask, w_expand, spa, mr2, table):
    rows, d_in = exp.shape
    mid = spa.shape[1]
    half = d_in // 2
    size = len(members)

    def body(me_ref, pre3_ref, exp_ref, mr3_ref, outer_ref, mask_ref, w_ref, spa_ref, mr2_ref, table_ref, *refs):
        gain3_ref, _ = out_rows(outer_ref, number)
        gain2_ref, bias2_ref = mid_rows(table_ref, number, 1)
        got, (both_ref, keep_ref, send_ref, pre2_ref, sums_ref, share, grad) = refs[:size], refs[size:]
        k = pl.program_id(0)

        @pl.when(k == 0)
        def _():
            put_shares(got, mr3_ref, share, both_ref)

        for stream, lo, hi in parts(rows):
            n = normed_at(exp_ref[lo:hi, :], mr3_ref, k, stream)
            grad[lo:hi, :] = norm_back(
                pre3_ref[lo:hi, :],
                n,
                pick(share, k, stream, 0),
                pick(share, k, stream, 1),
                gain3_ref[...] * pick(mr3_ref, k, stream, 1),
                mask_ref[lo:hi, :],
            ).astype(BF)
        per_half = half // CH
        at = pl.ds(pl.multiple_of(lax.rem(k, per_half) * CH, CH), CH)
        mine = k // per_half == me_ref[0]

        @pl.when(mine)
        def _():
            keep_ref[:, at] = grad[...].astype(F32)

        @pl.when(jnp.logical_not(mine))
        def _():
            send_ref[:, at] = grad[...].astype(F32)

        part = dot_nt(grad[...], w_ref[0])

        @pl.when(k == 0)
        def _():
            pre2_ref[...] = part

        @pl.when(k > 0)
        def _():
            pre2_ref[...] += part

        @pl.when(k == pl.num_programs(0) - 1)
        def _():
            for stream, lo, hi in parts(rows):
                n2 = normed_of(spa_ref[lo:hi, :], mr2_ref, stream)
                z2 = n2 * gain2_ref[...] + bias2_ref[...]
                pre2 = pre2_ref[lo:hi, :] * mask_ref[lo:hi, :] * slope(z2)
                pre2_ref[lo:hi, :] = pre2
                put_sums(stream, pre2, n2, sums_ref)

    return call(
        body,
        d_in // CH,
        [
            smem(),
            cols(rows),
            cols(rows),
            full((8, d_in)),
            cols(outer.shape[0]),
            full((rows, 1)),
            pl.BlockSpec((1, mid, CH), lambda k: (number, 0, k)),
            full((rows, mid)),
            full((8, mid)),
            full(table.shape),
        ]
        + [full(payload(d_in, 2))] * size,
        [full((2, d_in)), full((rows, half)), full((rows, half)), full((rows, mid)), full(payload(mid, 2))],
        [near((2, d_in)), near((rows, half)), near((rows, half)), near((rows, mid)), near(payload(mid, 2))],
        [pltpu.VMEM((4, d_in), F32), pltpu.VMEM((rows, CH), BF)],
        name="back_expand",
        flops=2 * rows * d_in * mid,
    )(me, pre3, exp, mr3, outer, mask, w_expand, spa, mr2, table, *members)


def back_spatial(number, me, pre2, spa, mr2, members, table, mask, w9, red, mr1):
    rows, mid = spa.shape
    size = len(members)
    quarter = mid // 4

    def body(me_ref, pre2_ref, spa_ref, mr2_ref, table_ref, mask_ref, w_ref, red_ref, mr1_ref, *refs):
        gain2_ref, _ = mid_rows(table_ref, number, 1)
        gain1_ref, bias1_ref = mid_rows(table_ref, number, 0)
        got, rest = refs[:size], refs[size:]
        both_ref, gs0, gs1, gs2, gs3, pre1_ref, sums_ref, share, image, tile, patch = rest
        k = pl.program_id(0)

        @pl.when(k == 0)
        def _():
            put_shares(got, mr2_ref, share, both_ref)
            pieces = []
            for stream, lo, hi in parts(rows):
                n = normed_of(spa_ref[lo:hi, :], mr2_ref, stream)
                plain, cross = rows_of(share, stream)
                scale = gain2_ref[...] * mr2_ref[2 * stream + 1 : 2 * stream + 2, :]
                pieces.append(norm_back(pre2_ref[lo:hi, :], n, plain, cross, scale, mask_ref[lo:hi, :]))
            value = rounded(jnp.concatenate(pieces, axis=0))
            fill_patches(value, image, tile, patch, -1)
            pre1_ref[...] = value
            for m, ref in enumerate((gs0, gs1, gs2, gs3)):
                at = pl.ds(pl.multiple_of((me_ref[1] ^ m) * quarter, quarter), quarter)
                ref[...] = pre1_ref[:, at]
            pre1_ref[...] = jnp.zeros((rows, mid), F32)

        total = pre1_ref[...]
        for j in range(3):
            total += dot_nt(patch[3 * k + j], w_ref[0, j])
        pre1_ref[...] = total

        @pl.when(k == 2)
        def _():
            for stream, lo, hi in parts(rows):
                n1 = normed_of(red_ref[lo:hi, :], mr1_ref, stream)
                z1 = n1 * gain1_ref[...] + bias1_ref[...]
                pre1 = pre1_ref[lo:hi, :] * mask_ref[lo:hi, :] * slope(z1)
                pre1_ref[lo:hi, :] = pre1
                put_sums(stream, pre1, n1, sums_ref)

    return call(
        body,
        3,
        [
            smem(),
            full((rows, mid)),
            full((rows, mid)),
            full((8, mid)),
            full(table.shape),
            full((rows, 1)),
            pl.BlockSpec((1, 3, mid, mid), lambda k: (number, k, 0, 0)),
            full((rows, mid)),
            full((8, mid)),
        ]
        + [full(payload(mid, 2))] * size,
        [full((2, mid))] + [full((rows, quarter))] * 4 + [full((rows, mid)), full(payload(mid, 2))],
        [near((2, mid))] + [near((rows, quarter))] * 4 + [near((rows, mid)), near(payload(mid, 2))],
        [
            pltpu.VMEM((4, mid), F32),
            pltpu.VMEM((IMG_ROWS + 48, mid), F32),
            pltpu.VMEM((rows - IMG_ROWS + 16, mid), F32),
            pltpu.VMEM((9, rows, mid), BF),
        ],
        name="back_spatial",
        flops=2 * rows * 9 * mid * mid,
    )(me, pre2, spa, mr2, table, mask, w9, red, mr1, *members)


def back_reduce(number, pre1, red, mr1, members, table, mask, w_reduce, pre3, below):
    rows, mid = red.shape
    d_in = pre3.shape[1]
    size = len(members)

    def head(k, got, pre1_ref, red_ref, mr1_ref, table_ref, mask_ref, both_ref, gr_ref, share, low):
        gain1_ref, _ = mid_rows(table_ref, number, 0)

        @pl.when(k == 0)
        def _():
            put_shares(got, mr1_ref, share, both_ref)
            for stream, lo, hi in parts(rows):
                n = normed_of(red_ref[lo:hi, :], mr1_ref, stream)
                plain, cross = rows_of(share, stream)
                scale = gain1_ref[...] * mr1_ref[2 * stream + 1 : 2 * stream + 2, :]
                low[lo:hi, :] = norm_back(pre1_ref[lo:hi, :], n, plain, cross, scale, mask_ref[lo:hi, :]).astype(BF)
            gr_ref[...] = low[...].astype(F32)

    specs = [
        full((rows, mid)),
        full((rows, mid)),
        full((8, mid)),
        full(table.shape),
        full((rows, 1)),
        pl.BlockSpec((1, CH, mid), lambda k: (number, k, 0)),
        cols(rows),
    ]
    args = [pre1, red, mr1, table, mask, w_reduce, pre3]
    scratch = [pltpu.VMEM((4, mid), F32), pltpu.VMEM((rows, mid), BF)]
    if below is None:

        def body(pre1_ref, red_ref, mr1_ref, table_ref, mask_ref, w_ref, pre3_ref, *refs):
            got, (both_ref, gr_ref, out_ref, share, low) = refs[:size], refs[size:]
            k = pl.program_id(0)
            head(k, got, pre1_ref, red_ref, mr1_ref, table_ref, mask_ref, both_ref, gr_ref, share, low)
            out_ref[...] = pre3_ref[...] + dot_nt(low[...], w_ref[0])

        return call(
            body,
            d_in // CH,
            specs + [full(payload(mid, 2))] * size,
            [full((2, mid)), full((rows, mid)), cols(rows)],
            [near((2, mid)), near((rows, mid)), near((rows, d_in))],
            scratch,
            name="back_reduce_last",
            flops=2 * rows * d_in * mid,
        )(*args, *members)

    def body(pre1_ref, red_ref, mr1_ref, table_ref, mask_ref, w_ref, pre3_ref, exp_ref, mr3_ref, outer_ref, act_ref, *refs):
        gain3_ref, bias3_ref = out_rows(outer_ref, number - 1)
        got, (both_ref, gr_ref, out_ref, sums_ref, share, low) = refs[:size], refs[size:]
        k = pl.program_id(0)
        head(k, got, pre1_ref, red_ref, mr1_ref, table_ref, mask_ref, both_ref, gr_ref, share, low)
        grad = pre3_ref[...] + dot_nt(low[...], w_ref[0])
        for stream, lo, hi in parts(rows):
            n = normed_at(exp_ref[lo:hi, :], mr3_ref, k, stream)
            z = n * gain3_ref[...] + bias3_ref[...] + act_ref[lo:hi, :].astype(F32)
            pre = grad[lo:hi] * mask_ref[lo:hi, :] * slope(z)
            out_ref[lo:hi, :] = pre
            put_sums(stream, pre, n, sums_ref, k * (CH // 128))

    return call(
        body,
        d_in // CH,
        specs + [cols(rows), full((8, d_in)), cols(below[2].shape[0]), cols(rows)] + [full(payload(mid, 2))] * size,
        [full((2, mid)), full((rows, mid)), cols(rows), full(payload(d_in, 2))],
        [near((2, mid)), near((rows, mid)), near((rows, d_in)), near(payload(d_in, 2))],
        scratch,
        name="back_reduce",
        flops=2 * rows * d_in * mid,
        transcendentals=rows * d_in,
    )(*args, *below, *members)


def dot_tn(a, b):
    return lax.dot_general(a, b, (((0,), (0,)), ((), ())), preferred_element_type=F32)


def spot(index, size):
    place, bit = 0, 1
    while bit < size:
        place = place * 2 + (index // bit) % 2
        bit *= 2
    return place


def weight_expand(me, own, peer, keep, got, nz, plain):
    rows, mid = own.shape
    half = keep.shape[1]
    step = half // 4
    deep = mid // nz

    def body(me_ref, own_ref, peer_ref, keep_ref, got_ref, x_keep, x_send, y_keep, y_send):
        a = jnp.concatenate([own_ref[...].astype(BF), peer_ref[...].astype(BF)], axis=0)
        for m in range(4):
            at = pl.ds(pl.multiple_of((me_ref[3] ^ m) * step, step), step)
            b = jnp.concatenate([keep_ref[:, at].astype(BF), got_ref[:, at].astype(BF)], axis=0)
            value = dot_tn(a, b)
            x_ref = x_keep if m < 2 else x_send
            y_ref = y_keep if m % 2 == 0 else y_send
            for z in range(nz):
                place = z if plain else spot(me_ref[2] ^ z, nz)
                x_ref[m % 2, place] = value[z * deep : (z + 1) * deep, 0:128]
                y_ref[m // 2, place] = value[z * deep : (z + 1) * deep, 128:256]

    vmem = pl.BlockSpec(memory_space=pltpu.VMEM)
    return pl.pallas_call(
        body,
        in_specs=[smem()] + [vmem] * 4,
        out_specs=[vmem] * 4,
        out_shape=[sds((2, nz, deep, 128))] * 4,
        compiler_params=pltpu.CompilerParams(vmem_limit_bytes=VMEM_LIMIT),
        cost_estimate=pl.CostEstimate(flops=0, bytes_accessed=0, transcendentals=0),
        name="weight_expand",
    )(me, own, peer, keep, got)


def slice_outputs(nz, shape, plain):
    if plain:
        return [sds((nz,) + shape)]
    return [sds((nz // 2,) + shape)] * 2


def put_slices(me_ref, total, outs, nz, deep, plain, put):
    for p in range(nz):
        z = p if plain else me_ref[2] ^ spot(p, nz)
        rows = total[pl.ds(pl.multiple_of(z * deep, deep), deep), :]
        part, at = (0, p) if plain else divmod(p, nz // 2)
        put(outs[part], at, rows)


def weight_reduce(me, own, peer, keep, got, nz, plain):
    rows, width = own.shape
    mid = keep.shape[1]
    step = mid // 4
    deep = width // nz
    part = deep // 2

    def body(me_ref, own_ref, peer_ref, keep_ref, got_ref, x_keep, x_send, y_keep, y_send, total):
        b = jnp.concatenate([keep_ref[...].astype(BF), got_ref[...].astype(BF)], axis=0)
        for z in range(nz):
            at = slice(z * deep, (z + 1) * deep)
            a = jnp.concatenate([own_ref[:, at].astype(BF), peer_ref[:, at].astype(BF)], axis=0)
            total[...] = dot_tn(a, b)
            place = z if plain else spot(me_ref[2] ^ z, nz)
            for m in range(4):
                column = me_ref[1] ^ ((m % 2) * 2 + m // 2)
                value = total[:, pl.ds(pl.multiple_of(column * step, step), step)]
                (x_keep if m < 2 else x_send)[m % 2, place] = value[:part]
                (y_keep if m % 2 == 0 else y_send)[m // 2, place] = value[part:]

    vmem = pl.BlockSpec(memory_space=pltpu.VMEM)
    return pl.pallas_call(
        body,
        in_specs=[smem()] + [vmem] * 4,
        out_specs=[vmem] * 4,
        out_shape=[sds((2, nz, part, step))] * 4,
        scratch_shapes=[pltpu.VMEM((deep, mid), F32)],
        compiler_params=pltpu.CompilerParams(vmem_limit_bytes=VMEM_LIMIT),
        cost_estimate=pl.CostEstimate(flops=0, bytes_accessed=0, transcendentals=0),
        name="weight_reduce",
    )(me, own, peer, keep, got)


def weight_spatial(me, hidden, near, far, nz, plain):
    _, rows, mid = hidden.shape
    width = near.shape[2]
    half = mid // 2
    deep = half // nz
    tile_rows = rows - IMG_ROWS
    shapes = slice_outputs(nz, (9, deep, width), plain)

    def body(me_ref, hidden_ref, near_ref, far_ref, *refs):
        outs, (image, tile, left, patch, total) = refs[:-5], refs[-5:]
        k = pl.program_id(0)
        m = (k // 2) ^ me_ref[1]
        mine = lax.rem(k, 2) == me_ref[0]

        @pl.when(k == 0)
        def _():
            image[...] = jnp.zeros_like(image)
            tile[...] = jnp.zeros_like(tile)

        value = jnp.where(mine, near_ref[m], far_ref[m])
        image[24 : 24 + IMG_ROWS, :] = value[0:IMG_ROWS]
        tile[8 : 8 + tile_rows, :] = value[IMG_ROWS:rows]
        for tap in range(9):
            dy, dx = tap // 3 - 1, tap % 3 - 1
            part, rest = shifted(image, tile, -dy, -dx, tile_rows)
            patch[k, 0:IMG_ROWS, tap * width : (tap + 1) * width] = part.astype(BF)
            patch[k, IMG_ROWS:rows, tap * width : (tap + 1) * width] = rest.astype(BF)
        at = pl.ds(pl.multiple_of(jnp.where(mine, 0, half), half), half)
        left[k] = hidden_ref[0, :, at].astype(BF)

        @pl.when(k == 7)
        def _():
            a = left[...].reshape(8 * rows, half)
            total[...] = dot_tn(a, patch[...].reshape(8 * rows, 9 * width))

            def put(ref, at, value):
                for tap in range(9):
                    ref[at, tap] = value[:, tap * width : (tap + 1) * width]

            put_slices(me_ref, total, outs, nz, deep, plain, put)

    return call(
        body,
        8,
        [
            smem(),
            pl.BlockSpec((1, rows, mid), lambda k: (k, 0, 0)),
            full(near.shape),
            full(far.shape),
        ],
        [full(v.shape) for v in shapes],
        shapes,
        [
            pltpu.VMEM((IMG_ROWS + 48, width), F32),
            pltpu.VMEM((tile_rows + 16, width), F32),
            pltpu.VMEM((8, rows, half), BF),
            pltpu.VMEM((8, rows, 9 * width), BF),
            pltpu.VMEM((half, 9 * width), F32),
        ],
        name="weight_spatial",
        flops=16 * rows * 9 * half * width,
    )(me, hidden, near, far)


class Collect:
    def __init__(self, grid, me, spare):
        self.grid, self.me, self.spare = grid, me, spare

    def over_z(self, keep, send):
        step = 1
        while True:
            (got,) = yield "deep", [(send, dict(dz=step))]
            step *= 2
            if step == self.grid.z:
                return keep[0] + got[0]
            half = keep.shape[0] // 2
            keep, send = keep[:half] + got[:half], keep[half:] + got[half:]

    def scatter(self, value):
        return lax.psum_scatter(value, "narrow", scatter_dimension=0, tiled=True)[0]

    def by_halves(self, kernel, own, peer, keep, send, out, after=None):
        (got,) = yield "core", [(send, dict(dc=1))]
        if after is not None:
            got, _ = lax.optimization_barrier((got, after()[0]))
        x_keep, x_send, y_keep, y_send = kernel(self.me, own, peer, keep, got, self.grid.z, self.spare)
        got = yield "plane", [(x_send, dict(dx=1)), (y_send, dict(dy=1))]
        x_last, y_last = x_keep[1:] + got[0][1:], y_keep[1:] + got[1][1:]
        x_keep, y_keep = x_keep[:1] + got[0][:1], y_keep[:1] + got[1][:1]
        got = yield "plane", [(x_last, dict(dy=1)), (y_last, dict(dx=1))]
        if self.spare:
            value = jnp.concatenate([x_keep[0] + got[0][0], y_keep[0] + got[1][0]], axis=1)
            (piece,) = yield "spare", [(value, self.scatter)]
            out.append(piece)
            return
        half = self.grid.z // 2

        def side(at):
            return jnp.concatenate([x_keep[0, at] + got[0][0, at], y_keep[0, at] + got[1][0, at]], axis=1)

        piece = yield from self.over_z(side(slice(0, half)), side(slice(half, 2 * half)))
        out.append(piece)

    def by_rows(self, kernel, rows_of_plane, grad, out):
        got = yield "plane", [(grad[1], dict(dx=1)), (grad[2], dict(dy=1)), (grad[3], dict(dy=1, dx=1))]
        near = jnp.stack([grad[0]] + list(got))
        (far,) = yield "core", [(near, dict(dc=1))]
        result = kernel(self.me, rows_of_plane, near, far, self.grid.z, self.spare)
        self.marks = result
        if self.spare:
            (piece,) = yield "spare", [(result[0], self.scatter)]
            out.append(piece)
        else:
            piece = yield from self.over_z(*result)
            out.append(piece)

    def flat(self, pieces):
        flat = jnp.concatenate([p[0].reshape(-1, 128) for p in pieces], axis=0)
        for group in self.grid.far():
            flat = flat + sum(self.grid.swap(flat, **step) for step in group)
        return flat

    def gather(self, pieces, out):
        (got,) = yield "spare", [(self.flat(pieces), self.grid.plane)]
        out.append(got)

    def chips(self, flat):
        return [flat] + [self.grid.swap(flat, dy=m >> 1, dx=m & 1) for m in (1, 2, 3)]

    def cores(self, values):
        return values + [self.grid.swap(v, dc=1) for v in values]


def place_slices(me, number, gathered, shapes, before):
    (e_rows, d_in), (r_rows, mid), (s_rows, _) = shapes
    dims = ((BLOCKS, r_rows, mid), (BLOCKS, 9, s_rows, mid), (BLOCKS, e_rows, d_in))
    size = len(gathered)
    r_len, s_len = r_rows // 2, s_rows // 2

    def body(me_ref, *refs):
        got = refs[:size]
        outs, (red, spa, exp, sems, out_sems) = refs[-8:-5], refs[-5:]

        def aligned(value, unit):
            return value if isinstance(value, int) else pl.multiple_of(value, unit)

        copies = []
        for a in range(8):
            if size == 2:
                core, chip = a % 2, a // 2
                source, source_r = got[0].at[a], got[1].at[a]
            else:
                core = me_ref[0] if a < 4 else 1 - me_ref[0]
                chip = (a % 4) ^ me_ref[1]
                source, source_r = got[a], got[8 + a]
            column = core * 4 + (chip % 2) * 2 + chip // 2
            moves = []
            for t in range(2):
                at = aligned(column * 256 + t * 128, 128)
                moves.append((source.at[pl.ds(t * e_rows, e_rows), :], exp.at[:, pl.ds(at, 128)]))
            at = aligned(chip * 128, 128)
            row = aligned(core * r_len, r_len)
            moves.append((source_r, red.at[pl.ds(row, r_len), pl.ds(at, 128)]))
            row = aligned(core * s_len, s_len)
            for tap in range(9):
                moves.append(
                    (
                        source.at[pl.ds(2 * e_rows + tap * s_len, s_len), :],
                        spa.at[tap, pl.ds(row, s_len), pl.ds(at, 128)],
                    )
                )
            copies += [pltpu.make_async_copy(src, dst, sems.at[a, i]) for i, (src, dst) in enumerate(moves)]
        for copy in copies:
            copy.start()
        for copy in copies:
            copy.wait()
        copies = [
            pltpu.make_async_copy(src, dst.at[number], out_sems.at[i])
            for i, (src, dst) in enumerate(zip((red, spa, exp), outs))
        ]
        for copy in copies:
            copy.start()
        for copy in copies:
            copy.wait()

    anywhere = pl.BlockSpec(memory_space=pl.ANY)
    args = (me,) + tuple(gathered)
    aliases = {}
    if before is not None:
        aliases = {len(args) + i: i for i in range(3)}
        args = args + tuple(before)
    return pl.pallas_call(
        body,
        in_specs=[smem()] + [anywhere] * (len(args) - 1),
        out_specs=[anywhere] * 3,
        out_shape=[sds(d) for d in dims],
        scratch_shapes=[pltpu.VMEM(d[1:], F32) for d in dims]
        + [pltpu.SemaphoreType.DMA((8, 12)), pltpu.SemaphoreType.DMA((3,))],
        input_output_aliases=aliases,
        compiler_params=pltpu.CompilerParams(vmem_limit_bytes=VMEM_LIMIT),
        name="place_slices",
    )(*args)


def to_rows(image, tile, rows):
    width = image.shape[-1]
    image = jnp.transpose(image, (1, 2, 0, 3))
    image = jnp.pad(image, ((0, 0), (0, 1), (0, 0), (0, 0))).reshape(IMG_ROWS, width)
    tile = tile.reshape(-1, width)
    pad = jnp.zeros((rows - IMG_ROWS - tile.shape[0], width), tile.dtype)
    return jnp.concatenate([image, tile, pad], axis=0)


def from_rows(value, tiles):
    width = value.shape[1]
    image = value[:IMG_ROWS].reshape(MAP, MAPW, SLOTS, width)[:, :MAP]
    image = jnp.transpose(image, (2, 0, 1, 3))
    tile = value[IMG_ROWS : IMG_ROWS + tiles * 4].reshape(tiles, TILE, TILE, width)
    return image, tile


def row_mask(map_sizes, rows):
    row = jnp.arange(MAP)
    col = jnp.arange(MAPW)
    inside = (row[:, None, None] < map_sizes[None, None, :]) & (col[None, :, None] < map_sizes[None, None, :])
    image = inside.astype(F32).reshape(IMG_ROWS)
    tile = jnp.repeat((map_sizes > 0).astype(F32), PIECES * TILE * TILE)
    pad = jnp.zeros((rows - IMG_ROWS - tile.shape[0],), F32)
    return jnp.concatenate([image, tile, pad])[:, None]


def core_halves(value, core, nz):
    deep = value.shape[1] // (2 * nz)
    low = [value[:, 2 * z * deep : (2 * z + 1) * deep] for z in range(nz)]
    high = [value[:, (2 * z + 1) * deep : (2 * z + 2) * deep] for z in range(nz)]
    low, high = jnp.concatenate(low, axis=1), jnp.concatenate(high, axis=1)
    keep = jnp.where(core == 0, low, high).astype(F32)
    send = jnp.where(core == 0, high, low).astype(F32)
    return keep, send


def core_select(core, mid, nz):
    deep = mid // (2 * nz)
    at = jnp.arange(mid)
    side = at // (mid // 2)
    inner = at % (mid // 2)
    source = (inner // deep) * 2 * deep + (side ^ core) * deep + inner % deep
    return (jnp.arange(mid)[:, None] == source[None, :]).astype(BF)


def per_device(
    grid,
    images,
    tile_maps,
    map_sizes,
    w_reduce,
    w_spatial,
    w_expand,
    gain_mid,
    bias_mid,
    gain_out,
    bias_out,
    grad_images,
    grad_tiles,
):
    tiles = tile_maps.shape[0]
    rows = -(-(IMG_ROWS + tiles * TILE * TILE) // 16) * 16
    d_in, mid = w_reduce.shape[1:]
    nz = grid.z
    y, x, core, z = grid.index()
    chip = (y % 2) * 2 + x % 2
    turned = (x % 2) * 2 + y % 2
    me = jnp.stack([core, chip, z, turned]).astype(jnp.int32)
    mask = row_mask(map_sizes, rows)
    w9 = w_spatial.reshape(BLOCKS, 9, mid, mid)
    start = to_rows(images, tile_maps, rows)
    grad = to_rows(grad_images, grad_tiles, rows)
    select = core_select(core, mid, nz)
    collect = [Collect(grid, me, b > 0) for b in range(BLOCKS)]
    bulk = Bulk(grid, ROOM)

    table = stay(jnp.concatenate([gain_mid.reshape(-1, mid), bias_mid.reshape(-1, mid)]))
    outer = stay(jnp.concatenate([gain_out, bias_out]))
    w_reduce, w9, w_expand = stay(w_reduce), stay(w9), stay(w_expand)

    def moments(stats):
        return exchange(grid, bulk, stats, join_moments)

    def sums(value):
        return exchange(grid, bulk, value, add_members)

    acts, lows, reds, spas, exps = [start], [], [], [], []
    mr1, mr2, mr3, hid1, hid2 = [], [], [], [], []
    red, stats = reduce_first(start, w_reduce, mask)
    low = start
    for b in range(BLOCKS):
        reds.append(red)
        mr, hidden, spa, stats = spatial_stage(
            b, red, moments(stats), table, mask, w9, select
        )
        mr1.append(mr)
        hid1.append(pltpu.with_memory_space_constraint(grid.plane(hidden), pltpu.HBM))
        keep, send = core_halves(low, core, nz)
        peer = grid.swap(send, dc=1)
        stats, keep, peer = lax.optimization_barrier((stats, keep, peer))
        lows.append((keep, peer))
        spas.append(spa)
        mr, hidden, exp, stats = expand_stage(
            b, spa, moments(stats), table, mask, w_expand
        )
        mr2.append(mr)
        hid2.append((hidden, grid.swap(hidden, dc=1)))
        exps.append(exp)
        if b + 1 < BLOCKS:
            mr, out, low, red, stats = join_stage(
                b + 1, exp, moments(stats), outer, acts[b], mask, w_reduce
            )
            mr3.append(mr)
            acts.append(out)
    last = BLOCKS - 1
    mr, out, pre3, sums3 = turn_stage(
        last, exps[last], moments(stats), outer, acts[last], mask, grad
    )
    mr3.append(mr)

    both1, both2, both3 = [None] * BLOCKS, [None] * BLOCKS, [None] * BLOCKS
    shapes = ((mid // nz, d_in), (d_in // nz, mid), (mid // nz, mid))
    pieces = [([], [], []) for _ in range(BLOCKS)]
    whole = [[[], []] for _ in range(BLOCKS)]

    def then(flow, b):
        yield from flow
        part_e, part_r, part_s = pieces[b]
        if b > 0 and part_e and part_s and not started[b][0]:
            started[b][0] = True
            bulk.add(collect[b].gather((part_e, part_s), whole[b][0]))
        if b > 0 and part_r and not started[b][1]:
            started[b][1] = True
            bulk.add(collect[b].gather((part_r,), whole[b][1]))

    started = [[False, False] for _ in range(BLOCKS)]
    for b in reversed(range(BLOCKS)):
        both3[b], keep, send, pre2, sums2 = back_expand(
            b, me, pre3, exps[b], mr3[b], sums(sums3), outer, mask, w_expand,
            spas[b], mr2[b], table,
        )
        bulk.add(then(collect[b].by_halves(weight_expand, *hid2[b], keep, send, pieces[b][0]), b))
        both2[b], *gs, pre1, sums1 = back_spatial(
            b, me, pre2, spas[b], mr2[b], sums(sums2), table, mask, w9,
            reds[b], mr1[b],
        )
        bulk.add(then(collect[b].by_rows(weight_spatial, hid1[b], gs, pieces[b][2]), b))
        below = None
        if b > 0:
            below = (exps[b - 1], mr3[b - 1], outer, acts[b - 1])
        result = back_reduce(
            b, pre1, reds[b], mr1[b], sums(sums1), table, mask, w_reduce, pre3, below
        )
        both1[b] = result[0]
        gr = result[1]
        after = None
        if b == 0:
            gr = bulk.last(gr)
            after = lambda: collect[0].marks
        bulk.add(then(collect[b].by_halves(weight_reduce, *lows[b], gr, gr, pieces[b][1], after), b))
        if b > 0:
            pre3, sums3 = result[2], result[3]
        else:
            grad_in = result[2]

    bulk.finish()
    slices = None
    for b in reversed(range(BLOCKS)):
        part_e, part_r, part_s = pieces[b]
        if b > 0:
            gathered = whole[b][0] + whole[b][1]
        else:
            first = collect[b].chips(collect[b].flat((part_e, part_s)))
            second = collect[b].chips(collect[b].flat((part_r,)))
            slices, first = lax.optimization_barrier((slices, first))
            gathered = collect[b].cores(first) + collect[b].cores(second)
        slices = place_slices(me, b, gathered, shapes, slices)
    out_images, out_tiles = from_rows(out, tiles)
    in_images, in_tiles = from_rows(grad_in, tiles)
    g_reduce, g_spatial, g_expand = slices

    def pair(at):
        return jnp.stack([jnp.stack([both1[b][at], both2[b][at]]) for b in range(BLOCKS)])

    return (
        out_images,
        out_tiles,
        in_images,
        in_tiles,
        g_reduce,
        g_spatial.reshape(BLOCKS, 3, 3, mid // nz, mid),
        g_expand,
        pair(1),
        pair(0),
        jnp.stack([both3[b][1] for b in range(BLOCKS)]),
        jnp.stack([both3[b][0] for b in range(BLOCKS)]),
    )


def solution(mesh):
    both = ("wide", "narrow")
    batch = P(both, None, None, None)
    grid = Grid(mesh.shape["wide"], mesh.shape["narrow"])
    return jax.shard_map(
        functools.partial(per_device, grid),
        mesh=mesh,
        in_specs=(batch, batch, P(both), P(), P(), P(), P(), P(), P(), P(), batch, batch),
        out_specs=(
            batch,
            batch,
            batch,
            batch,
            P(None, "narrow", None),
            P(None, None, None, "narrow", None),
            P(None, "narrow", None),
            P(),
            P(),
            P(),
            P(),
        ),
        check_vma=False,
    )
```

time: 575 us -> 477 us (0.83); the launches traced: 567 us -> 476 us
  waiting for transfers between devices: 216 us -> 165 us
  Pallas kernels: 112 us -> 62 us
  between operations: 2.14 us -> 15.6 us
  local copies, waits for them, and re-layouts: 70.8 us -> 61.8 us
  other arithmetic: 21.3 us -> 30.1 us
    ppermute x136, waiting for transfers between devices: 216 us -> 161 us  [swap(): return lax.ppermute(value, AXES, pairs)]
    pallas_call x28 -> x16, Pallas kernels: 91.6 us -> 47 us  [the longest x2 12.2 us: weight_spatial(): call(body, 8, [smem(), pl.BlockSpec((1, rows, mid), lambda k: (k, 0, 0)),...]
    add x18 -> x33, other arithmetic: 5.51 us -> 15 us  [the longest x4 3.68 us: by_halves(): x_keep, y_keep = (x_keep[:1] + got[0][:1], y_keep[:1] + got[1][:1])]
    slice x28 -> x4, local copies, waits for them, and re-layouts: 8.02 us -> 0.02 us  [the longest x2 0.01 us: pair(): both2[b][at]]
    unnamed x264 -> x202, local copies, waits for them, and re-layouts: 41.9 us -> 44.1 us
  transfers between devices with their start and end apart: 136 -> 143, of which waited for: 92 -> 83; matrix products, arithmetic and copies ran while one was open for 7% -> 8% of each run, Pallas kernels for 8% -> 11%
where the time goes in v3:
time: 477 us; the launch traced here: 476 us
  waiting for transfers between devices  165 us (35%)
  starting transfers between devices  142 us (30%)
  Pallas kernels  62 us (13%)
  local copies, waits for them, and re-layouts  61.8 us (13%)
  other arithmetic  30.1 us (6%)
  between operations  15.6 us (3%)
    ppermute x136, waiting for transfers between devices, swap(): return lax.ppermute(value, AXES, pairs)  161 us
    ppermute x136, starting transfers between devices, swap(): return lax.ppermute(value, AXES, pairs)  141 us
    unnamed x202, local copies, waits for them, and re-layouts  44.1 us
    pallas_call x2, Pallas kernels, weight_spatial(): call(body, 8, [smem(), pl.BlockSpec((1, rows, mid), lambda k: (k, 0, 0)),...  12.2 us
    pallas_call x2, Pallas kernels, place_slices(): pl.pallas_call(body, in_specs=[smem()] + [anywhere] * (len(args) - 1), ou...  9.67 us
  transfers between devices with their start and end apart: 143, of which 83 were waited for; matrix products, arithmetic and copies ran while one was open for 8% of the time, Pallas kernels for 11%

profile of v3, /device:TPU:0, one launch (start us, length us, event | category | flops | bytes accessed | tf_op | source)
XLA Modules:
  0.0 475.9 jit_solution(5993504087527838471)
XLA Ops:
  14.6 2.2 copy-done.7
  20.4 3.9 collective-permute-start.3
  28.6 3.7 collective-permute-start.6
  34.1 2.7 collective-permute-done.5.refs_2_
  36.8 3.7 copy-done
  40.5 3.0 spatial_stage.2
  52.7 2.3 collective-permute-start.12
  56.8 2.2 copy-done.3
  62.2 2.5 collective-permute-start.18
  69.3 2.5 collective-permute-start.21
  77.4 2.5 join_stage.1
  89.0 2.4 collective-permute-start.26
  93.7 2.3 spatial_stage.3
  105.3 2.3 collective-permute-start.36
  112.5 2.2 copy-done.4
  123.1 3.0 collective-permute-done.40
  159.7 3.2 back_expand.2
  163.6 2.3 collective-permute-done.51
  182.0 3.7 copy-done.1
  185.7 3.5 back_spatial.2
  205.4 2.6 back_reduce.1
  213.3 3.3 collective-permute-done.71
  232.3 6.0 %weight_spatial.2 = f32[4,9,64,128]{3,2,1,0:T(8,128)S(1)} custom-call(s32[4]{0:T(128)S(1)} %pad_add_fusion.me_ref, f32[8,192,512]{2,1,0:T(8,128)} %bitcast.78, f32[4,192,128]{2,1,0:T(8,128)S(1)} %pad_maximum_fusion.8.near_ref, f32[4,192,128]{2,1,0:T(8,128)S(1)} %collective-permute-done.82.far_ref), custom_call_target="tpu_custom_call" | custom-call | tf_op jit(solution)/shard_map/weight_spatial/pallas_call | solution.py:978
  244.6 3.3 back_expand.3
  251.7 10.6 %collective-permute-done.84 = f32[2,4,128,128]{3,2,1,0:T(8,128)S(1)} collective-permute-done((f32[2,4,128,128]{3,2,1,0:T(8,128)S(1)}, f32[2,4,128,128]{3,2,1,0:T(8,128)S(1)}, u32[]{:S(2)}, u32[]{:S(2)}) %collective-permute-start.84) | collective-permute-done | bytes 524320 | tf_op jit(solution)/shard_map/ppermute | solution.py:49
  274.5 2.4 collective-permute-start.91
  280.1 3.7 copy-done.2
  283.8 3.5 back_spatial.3
  295.1 2.5 collective-permute-start.102
  304.0 2.6 reshape.192
  306.7 2.3 reshape.193
  317.1 2.2 copy-done.10
  319.4 2.2 back_reduce_last.1
  322.8 6.3 %collective-permute-done.107 = f32[192,128]{1,0:T(8,128)S(1)} collective-permute-done((f32[192,128]{1,0:T(8,128)S(1)}, f32[192,128]{1,0:T(8,128)S(1)}, u32[]{:S(2)}, u32[]{:S(2)}) %collective-permute-start.107) | collective-permute-done | bytes 98336 | tf_op jit(solution)/shard_map/ppermute | solution.py:49
  333.2 6.2 %weight_spatial.3 = (f32[2,9,64,128]{3,2,1,0:T(8,128)S(1)}, f32[2,9,64,128]{3,2,1,0:T(8,128)S(1)}) custom-call(s32[4]{0:T(128)S(1)} %pad_add_fusion.me_ref, f32[8,192,512]{2,1,0:T(8,128)} %bitcast.77, f32[4,192,128]{2,1,0:T(8,128)S(1)} %pad_maximum_fusion.9.near_ref, f32[4,192,128]{2,1,0:T(8,128)S(1)} %collective-permute-done.110.far_ref), custom_call_target="tpu_custom_call" | custom-call | tf_op jit(solution)/shard_map/weight_spatial/pallas_call | solution.py:978
  339.5 2.3 weight_reduce.3
  346.6 22.9 %collective-permute-done.103 = f32[1,4,128,128]{3,2,1,0:T(8,128)S(1)} collective-permute-done((f32[1,4,128,128]{3,2,1,0:T(8,128)S(1)}, f32[1,4,128,128]{3,2,1,0:T(8,128)S(1)}, u32[]{:S(2)}, u32[]{:S(2)}) %collective-permute-start.103) | collective-permute-done | bytes 262176 | tf_op jit(solution)/shard_map/ppermute | solution.py:49
  371.2 2.4 all-gather.11.cloned.1.call-done
  383.5 2.4 collective-permute-start.116
  387.1 5.1 %collective-permute-done.115 = f32[2,256,128]{2,1,0:T(8,128)} collective-permute-done((f32[2,256,128]{2,1,0:T(8,128)}, f32[2,256,128]{2,1,0:T(8,128)}, u32[]{:S(2)}, u32[]{:S(2)}) %collective-permute-start.115) | collective-permute-done | bytes 262176 | tf_op jit(solution)/shard_map/ppermute | solution.py:49
  392.3 14.5 %collective-permute-done.116 = f32[1,9,64,128]{3,2,1,0:T(8,128)} collective-permute-done((f32[1,9,64,128]{3,2,1,0:T(8,128)}, f32[1,9,64,128]{3,2,1,0:T(8,128)}, u32[]{:S(2)}, u32[]{:S(2)}) %collective-permute-start.116) | collective-permute-done | bytes 294944 | tf_op jit(solution)/shard_map/ppermute | solution.py:49
  410.6 2.5 collective-permute-start.119
  413.7 3.1 collective-permute-done.119
  420.6 2.3 collective-permute-start.128
  428.9 2.2 collective-permute-start.131
  432.1 17.9 %collective-permute-done.131.refs_11_ = f32[256,128]{1,0:T(8,128)} collective-permute-done((f32[256,128]{1,0:T(8,128)}, f32[256,128]{1,0:T(8,128)}, u32[]{:S(2)}, u32[]{:S(2)}) %collective-permute-start.131) | collective-permute-done | bytes 131104 | tf_op jit(solution)/shard_map/ppermute | solution.py:49
  454.1 4.3 place_slices.2
  463.6 5.4 %place_slices.3 = (f32[2,512,512]{2,1,0:T(8,128)}, f32[2,9,128,512]{3,2,1,0:T(8,128)}, f32[2,128,2048]{2,1,0:T(8,128)}) custom-call(s32[4]{0:T(128)S(1)} %pad_add_fusion.me_ref, f32[832,128]{1,0:T(8,128)} %pad_maximum_fusion.5.refs_0_, f32[832,128]{1,0:T(8,128)} %collective-permute-done.121.refs_1_, ...), custom_call_target="tpu_custom_call", output_to_operand_aliasing={{0}: (17, {}), {1}: (18, {}), {2}: (19, {})} | custom-call | tf_op jit(solution)/shard_map/place_slices/pallas_call | solution.py:1128
  (587 shorter events, 257.1 us)
Async XLA Ops:
  7.2 225.1 %all-gather.9.cloned.1.call-start = ((), (), s32[]{:S(2)}) async-start(), calls=%async_computation.6 | async-start | bytes 3538944 | tf_op jit(solution)/shard_map/all_gather | solution.py:53
  20.2 23.3 %collective-permute-start.7 = (f32[192,1024]{1,0:T(8,128)}, f32[192,1024]{1,0:T(8,128)}, u32[]{:S(2)}, u32[]{:S(2)}) collective-permute-start(f32[192,1024]{1,0:T(8,128)} %get-tuple-element.395), channel_id=1, source_target_pairs={{0,4},{1,5},{2,6},{3,7},{4,0},{5,1},{6,2},{7,3},{8,12},{9,13},{10,... | collective-permute-start | bytes 2359304 | tf_op jit(solution)/shard_map/ppermute | solution.py:49
  86.2 11.6 %collective-permute-start.29 = (f32[192,1024]{1,0:T(8,128)}, f32[192,1024]{1,0:T(8,128)}, u32[]{:S(2)}, u32[]{:S(2)}) collective-permute-start(f32[192,1024]{1,0:T(8,128)} %get-tuple-element.377), channel_id=1, source_target_pairs={{0,4},{1,5},{2,6},{3,7},{4,0},{5,1},{6,2},{7,3},{8,12},{9,13},{10,... | collective-permute-start | bytes 2359304 | tf_op jit(solution)/shard_map/ppermute | solution.py:49
  97.5 197.5 %reduce-scatter.6.cloned.1.call-start = ((), (), s32[]{:S(2)}) async-start(), calls=%async_computation.4 | async-start | bytes 655360 | tf_op jit(solution)/shard_map/reduce_scatter | solution.py:1016
  163.0 9.5 %collective-permute-start.56 = (f32[192,1024]{1,0:T(8,128)S(1)}, f32[192,1024]{1,0:T(8,128)S(1)}, u32[]{:S(2)}, u32[]{:S(2)}) collective-permute-start(f32[192,1024]{1,0:T(8,128)S(1)} %get-tuple-element.202), channel_id=1, source_target_pairs={{0,4},{1,5},{2,6},{3,7},{4,0},{5,1},{6,2},{7,3},{8,12},{9,13},{10,... | collective-permute-start | bytes 2359304 | tf_op jit(solution)/shard_map/ppermute | solution.py:49
  163.1 9.4 %collective-permute-start.55 = (f32[192,512]{1,0:T(8,128)S(1)}, f32[192,512]{1,0:T(8,128)S(1)}, u32[]{:S(2)}, u32[]{:S(2)}) collective-permute-start(f32[192,512]{1,0:T(8,128)S(1)} %copy-done.47), channel_id=1, source_target_pairs={{0,4},{1,5},{2,6},{3,7},{4,0},{5,1},{6,2},{7,3},{8,12},{9,13},{10,... | collective-permute-start | bytes 1179656 | tf_op jit(solution)/shard_map/ppermute | solution.py:49
  173.8 16.7 %collective-permute-start.61 = (f32[2,4,128,128]{3,2,1,0:T(8,128)S(1)}, f32[2,4,128,128]{3,2,1,0:T(8,128)S(1)}, u32[]{:S(2)}, u32[]{:S(2)}) collective-permute-start(f32[2,4,128,128]{3,2,1,0:T(8,128)S(1)} %get-tuple-element.209), channel_id=1, source_target_pairs={{0,8},{1,9},{2,10},{3,11},{4,12},{5,13},{6,14},{7,15},{8,0},{9,1},... | collective-permute-start | bytes 1572872 | tf_op jit(solution)/shard_map/ppermute | solution.py:49
  174.4 16.1 %collective-permute-start.62 = (f32[2,4,128,128]{3,2,1,0:T(8,128)S(1)}, f32[2,4,128,128]{3,2,1,0:T(8,128)S(1)}, u32[]{:S(2)}, u32[]{:S(2)}) collective-permute-start(f32[2,4,128,128]{3,2,1,0:T(8,128)S(1)} %get-tuple-element.210), channel_id=1, source_target_pairs={{0,16},{1,17},{2,18},{3,19},{4,20},{5,21},{6,22},{7,23},{8,24},{9,... | collective-permute-start | bytes 1572872 | tf_op jit(solution)/shard_map/ppermute | solution.py:49
  196.7 19.8 %collective-permute-start.73 = (f32[1,4,128,128]{3,2,1,0:T(8,128)S(1)}, f32[1,4,128,128]{3,2,1,0:T(8,128)S(1)}, u32[]{:S(2)}, u32[]{:S(2)}) collective-permute-start(f32[1,4,128,128]{3,2,1,0:T(8,128)S(1)} %slice_add_fusion.12), channel_id=1, source_target_pairs={{0,16},{1,17},{2,18},{3,19},{4,20},{5,21},{6,22},{7,23},{8,24},{9,... | collective-permute-start | bytes 786440 | tf_op jit(solution)/shard_map/ppermute | solution.py:49
  198.3 18.3 %collective-permute-start.74 = (f32[1,4,128,128]{3,2,1,0:T(8,128)S(1)}, f32[1,4,128,128]{3,2,1,0:T(8,128)S(1)}, u32[]{:S(2)}, u32[]{:S(2)}) collective-permute-start(f32[1,4,128,128]{3,2,1,0:T(8,128)S(1)} %slice_add_fusion.11), channel_id=1, source_target_pairs={{0,8},{1,9},{2,10},{3,11},{4,12},{5,13},{6,14},{7,15},{8,0},{9,1},... | collective-permute-start | bytes 786440 | tf_op jit(solution)/shard_map/ppermute | solution.py:49
  213.3 9.3 %collective-permute-start.78 = (f32[192,512]{1,0:T(8,128)S(1)}, f32[192,512]{1,0:T(8,128)S(1)}, u32[]{:S(2)}, u32[]{:S(2)}) collective-permute-start(f32[192,512]{1,0:T(8,128)S(1)} %get-tuple-element.231.keep_ref), channel_id=1, source_target_pairs={{0,4},{1,5},{2,6},{3,7},{4,0},{5,1},{6,2},{7,3},{8,12},{9,13},{10,... | collective-permute-start | bytes 1179656 | tf_op jit(solution)/shard_map/ppermute | solution.py:49
  220.2 12.1 %collective-permute-start.82 = (f32[4,192,128]{2,1,0:T(8,128)S(1)}, f32[4,192,128]{2,1,0:T(8,128)S(1)}, u32[]{:S(2)}, u32[]{:S(2)}) collective-permute-start(f32[4,192,128]{2,1,0:T(8,128)S(1)} %pad_maximum_fusion.8.near_ref), channel_id=1, source_target_pairs={{0,4},{1,5},{2,6},{3,7},{4,0},{5,1},{6,2},{7,3},{8,12},{9,13},{10,... | collective-permute-start | bytes 1179656 | tf_op jit(solution)/shard_map/ppermute | solution.py:49
  227.1 12.2 %collective-permute-start.81 = (f32[2,32,128]{2,1,0:T(8,128)S(1)}, f32[2,32,128]{2,1,0:T(8,128)S(1)}, u32[]{:S(2)}, u32[]{:S(2)}) collective-permute-start(f32[2,32,128]{2,1,0:T(8,128)S(1)} %add_add_fusion.1.refs_0_), channel_id=1, source_target_pairs={{0,3},{1,2},{2,1},{3,0},{4,7},{5,6},{6,5},{7,4},{8,11},{9,10},{10,... | collective-permute-start | bytes 98312 | tf_op jit(solution)/shard_map/ppermute | solution.py:49
  229.0 10.3 %collective-permute-start.80 = (f32[2,32,128]{2,1,0:T(8,128)S(1)}, f32[2,32,128]{2,1,0:T(8,128)S(1)}, u32[]{:S(2)}, u32[]{:S(2)}) collective-permute-start(f32[2,32,128]{2,1,0:T(8,128)S(1)} %add_add_fusion.1.refs_0_), channel_id=1, source_target_pairs={{0,2},{1,3},{2,0},{3,1},{4,6},{5,7},{6,4},{7,5},{8,10},{9,11},{10,... | collective-permute-start | bytes 98312 | tf_op jit(solution)/shard_map/ppermute | solution.py:49
  230.0 9.3 %collective-permute-start.79 = (f32[2,32,128]{2,1,0:T(8,128)S(1)}, f32[2,32,128]{2,1,0:T(8,128)S(1)}, u32[]{:S(2)}, u32[]{:S(2)}) collective-permute-start(f32[2,32,128]{2,1,0:T(8,128)S(1)} %add_add_fusion.1.refs_0_), channel_id=1, source_target_pairs={{0,1},{1,0},{2,3},{3,2},{4,5},{5,4},{6,7},{7,6},{8,9},{9,8},{10,11... | collective-permute-start | bytes 98312 | tf_op jit(solution)/shard_map/ppermute | solution.py:49
  239.4 55.7 %reduce-scatter.4.cloned.1.call-start = ((), (), s32[]{:S(2)}) async-start(), calls=%async_computation.3 | async-start | bytes 1474560 | tf_op jit(solution)/shard_map/reduce_scatter | solution.py:1016
  240.1 93.1 %all-gather.13.cloned.1.call-start = ((), (), s32[]{:S(2)}) async-start(), calls=%async_computation.8 | async-start | bytes 3538944 | tf_op jit(solution)/shard_map/all_gather | solution.py:53
  240.7 133.0 %all-gather.11.cloned.1.call-start = ((), (), s32[]{:S(2)}) async-start(), calls=%async_computation.7 | async-start | bytes 3833856 | tf_op jit(solution)/shard_map/all_gather | solution.py:53
  247.9 21.3 %collective-permute-start.90 = (f32[192,1024]{1,0:T(8,128)S(1)}, f32[192,1024]{1,0:T(8,128)S(1)}, u32[]{:S(2)}, u32[]{:S(2)}) collective-permute-start(f32[192,1024]{1,0:T(8,128)S(1)} %get-tuple-element.254), channel_id=1, source_target_pairs={{0,4},{1,5},{2,6},{3,7},{4,0},{5,1},{6,2},{7,3},{8,12},{9,13},{10,... | collective-permute-start | bytes 2359304 | tf_op jit(solution)/shard_map/ppermute | solution.py:49
  248.0 14.3 %collective-permute-start.84 = (f32[2,4,128,128]{3,2,1,0:T(8,128)S(1)}, f32[2,4,128,128]{3,2,1,0:T(8,128)S(1)}, u32[]{:S(2)}, u32[]{:S(2)}) collective-permute-start(f32[2,4,128,128]{3,2,1,0:T(8,128)S(1)} %copy-done.54), channel_id=1, source_target_pairs={{0,8},{1,9},{2,10},{3,11},{4,12},{5,13},{6,14},{7,15},{8,0},{9,1},... | collective-permute-start | bytes 1572872 | tf_op jit(solution)/shard_map/ppermute | solution.py:49
  249.5 14.0 %collective-permute-start.85 = (f32[2,4,128,128]{3,2,1,0:T(8,128)S(1)}, f32[2,4,128,128]{3,2,1,0:T(8,128)S(1)}, u32[]{:S(2)}, u32[]{:S(2)}) collective-permute-start(f32[2,4,128,128]{3,2,1,0:T(8,128)S(1)} %get-tuple-element.250), channel_id=1, source_target_pairs={{0,16},{1,17},{2,18},{3,19},{4,20},{5,21},{6,22},{7,23},{8,24},{9,... | collective-permute-start | bytes 1572872 | tf_op jit(solution)/shard_map/ppermute | solution.py:49
  250.0 19.2 %collective-permute-start.89 = (f32[192,512]{1,0:T(8,128)S(1)}, f32[192,512]{1,0:T(8,128)S(1)}, u32[]{:S(2)}, u32[]{:S(2)}) collective-permute-start(f32[192,512]{1,0:T(8,128)S(1)} %copy-done.45), channel_id=1, source_target_pairs={{0,4},{1,5},{2,6},{3,7},{4,0},{5,1},{6,2},{7,3},{8,12},{9,13},{10,... | collective-permute-start | bytes 1179656 | tf_op jit(solution)/shard_map/ppermute | solution.py:49
  270.5 18.7 %collective-permute-start.95 = (f32[2,4,128,128]{3,2,1,0:T(8,128)S(1)}, f32[2,4,128,128]{3,2,1,0:T(8,128)S(1)}, u32[]{:S(2)}, u32[]{:S(2)}) collective-permute-start(f32[2,4,128,128]{3,2,1,0:T(8,128)S(1)} %get-tuple-element.260), channel_id=1, source_target_pairs={{0,8},{1,9},{2,10},{3,11},{4,12},{5,13},{6,14},{7,15},{8,0},{9,1},... | collective-permute-start | bytes 1572872 | tf_op jit(solution)/shard_map/ppermute | solution.py:49
  272.0 17.2 %collective-permute-start.96 = (f32[2,4,128,128]{3,2,1,0:T(8,128)S(1)}, f32[2,4,128,128]{3,2,1,0:T(8,128)S(1)}, u32[]{:S(2)}, u32[]{:S(2)}) collective-permute-start(f32[2,4,128,128]{3,2,1,0:T(8,128)S(1)} %get-tuple-element.261), channel_id=1, source_target_pairs={{0,16},{1,17},{2,18},{3,19},{4,20},{5,21},{6,22},{7,23},{8,24},{9,... | collective-permute-start | bytes 1572872 | tf_op jit(solution)/shard_map/ppermute | solution.py:49
  302.1 111.6 %reduce-scatter.8.cloned.1.call-start = ((), (), s32[]{:S(2)}) async-start(), calls=%async_computation.5 | async-start | bytes 655360 | tf_op jit(solution)/shard_map/reduce_scatter | solution.py:1016
  311.2 19.3 %collective-permute-start.105 = (f32[1,4,128,128]{3,2,1,0:T(8,128)S(1)}, f32[1,4,128,128]{3,2,1,0:T(8,128)S(1)}, u32[]{:S(2)}, u32[]{:S(2)}) collective-permute-start(f32[1,4,128,128]{3,2,1,0:T(8,128)S(1)} %copy-done.81), channel_id=1, source_target_pairs={{0,16},{1,17},{2,18},{3,19},{4,20},{5,21},{6,22},{7,23},{8,24},{9,... | collective-permute-start | bytes 786440 | tf_op jit(solution)/shard_map/ppermute | solution.py:49
  312.3 18.2 %collective-permute-start.106 = (f32[1,4,128,128]{3,2,1,0:T(8,128)S(1)}, f32[1,4,128,128]{3,2,1,0:T(8,128)S(1)}, u32[]{:S(2)}, u32[]{:S(2)}) collective-permute-start(f32[1,4,128,128]{3,2,1,0:T(8,128)S(1)} %copy-done.82), channel_id=1, source_target_pairs={{0,8},{1,9},{2,10},{3,11},{4,12},{5,13},{6,14},{7,15},{8,0},{9,1},... | collective-permute-start | bytes 786440 | tf_op jit(solution)/shard_map/ppermute | solution.py:49
  313.5 15.5 %collective-permute-start.107 = (f32[192,128]{1,0:T(8,128)S(1)}, f32[192,128]{1,0:T(8,128)S(1)}, u32[]{:S(2)}, u32[]{:S(2)}) collective-permute-start(f32[192,128]{1,0:T(8,128)S(1)} %copy-done.56), channel_id=1, source_target_pairs={{0,8},{1,9},{2,10},{3,11},{4,12},{5,13},{6,14},{7,15},{8,0},{9,1},... | collective-permute-start | bytes 294920 | tf_op jit(solution)/shard_map/ppermute | solution.py:49
  314.4 14.7 %collective-permute-start.108 = (f32[192,128]{1,0:T(8,128)S(1)}, f32[192,128]{1,0:T(8,128)S(1)}, u32[]{:S(2)}, u32[]{:S(2)}) collective-permute-start(f32[192,128]{1,0:T(8,128)S(1)} %get-tuple-element.292), channel_id=1, source_target_pairs={{0,16},{1,17},{2,18},{3,19},{4,20},{5,21},{6,22},{7,23},{8,24},{9,... | collective-permute-start | bytes 294920 | tf_op jit(solution)/shard_map/ppermute | solution.py:49
  315.4 15.1 %collective-permute-start.109 = (f32[192,128]{1,0:T(8,128)S(1)}, f32[192,128]{1,0:T(8,128)S(1)}, u32[]{:S(2)}, u32[]{:S(2)}) collective-permute-start(f32[192,128]{1,0:T(8,128)S(1)} %get-tuple-element.293), channel_id=1, source_target_pairs={{0,24},{1,25},{2,26},{3,27},{4,28},{5,29},{6,30},{7,31},{8,16},{9,... | collective-permute-start | bytes 294920 | tf_op jit(solution)/shard_map/ppermute | solution.py:49
  330.6 8.8 %collective-permute-start.112 = (f32[192,512]{1,0:T(8,128)}, f32[192,512]{1,0:T(8,128)S(1)}, u32[]{:S(2)}, u32[]{:S(2)}) collective-permute-start(f32[192,512]{1,0:T(8,128)} %get-tuple-element.300.keep_ref), channel_id=1, source_target_pairs={{0,4},{1,5},{2,6},{3,7},{4,0},{5,1},{6,2},{7,3},{8,12},{9,13},{10,... | collective-permute-start | bytes 1179656 | tf_op jit(solution)/shard_map/ppermute | solution.py:49
  332.0 14.6 %collective-permute-start.104 = (f32[1,4,128,128]{3,2,1,0:T(8,128)}, f32[1,4,128,128]{3,2,1,0:T(8,128)}, u32[]{:S(2)}, u32[]{:S(2)}) collective-permute-start(f32[1,4,128,128]{3,2,1,0:T(8,128)} %get-tuple-element.392), channel_id=1, source_target_pairs={{0,8},{1,9},{2,10},{3,11},{4,12},{5,13},{6,14},{7,15},{8,0},{9,1},... | collective-permute-start | bytes 786440 | tf_op jit(solution)/shard_map/ppermute | solution.py:49
  341.8 27.8 %collective-permute-start.113 = (f32[2,4,128,128]{3,2,1,0:T(8,128)S(1)}, f32[2,4,128,128]{3,2,1,0:T(8,128)S(1)}, u32[]{:S(2)}, u32[]{:S(2)}) collective-permute-start(f32[2,4,128,128]{3,2,1,0:T(8,128)S(1)} %get-tuple-element.303), channel_id=1, source_target_pairs={{0,8},{1,9},{2,10},{3,11},{4,12},{5,13},{6,14},{7,15},{8,0},{9,1},... | collective-permute-start | bytes 1572872 | tf_op jit(solution)/shard_map/ppermute | solution.py:49
  342.8 26.8 %collective-permute-start.114 = (f32[2,4,128,128]{3,2,1,0:T(8,128)S(1)}, f32[2,4,128,128]{3,2,1,0:T(8,128)S(1)}, u32[]{:S(2)}, u32[]{:S(2)}) collective-permute-start(f32[2,4,128,128]{3,2,1,0:T(8,128)S(1)} %get-tuple-element.304), channel_id=1, source_target_pairs={{0,16},{1,17},{2,18},{3,19},{4,20},{5,21},{6,22},{7,23},{8,24},{9,... | collective-permute-start | bytes 1572872 | tf_op jit(solution)/shard_map/ppermute | solution.py:49
  343.8 27.4 %collective-permute-start.111 = (f32[2,9,64,128]{3,2,1,0:T(8,128)S(1)}, f32[2,9,64,128]{3,2,1,0:T(8,128)}, u32[]{:S(2)}, u32[]{:S(2)}) collective-permute-start(f32[2,9,64,128]{3,2,1,0:T(8,128)S(1)} %get-tuple-element.297), channel_id=1, source_target_pairs={{0,1},{1,0},{2,3},{3,2},{4,5},{5,4},{6,7},{7,6},{8,9},{9,8},{10,11... | collective-permute-start | bytes 1769480 | tf_op jit(solution)/shard_map/ppermute | solution.py:49
  344.9 24.7 %collective-permute-start.103 = (f32[1,4,128,128]{3,2,1,0:T(8,128)S(1)}, f32[1,4,128,128]{3,2,1,0:T(8,128)S(1)}, u32[]{:S(2)}, u32[]{:S(2)}) collective-permute-start(f32[1,4,128,128]{3,2,1,0:T(8,128)S(1)} %get-tuple-element.394), channel_id=1, source_target_pairs={{0,16},{1,17},{2,18},{3,19},{4,20},{5,21},{6,22},{7,23},{8,24},{9,... | collective-permute-start | bytes 786440 | tf_op jit(solution)/shard_map/ppermute | solution.py:49
  375.5 11.6 %collective-permute-start.118 = (f32[1,4,128,128]{3,2,1,0:T(8,128)}, f32[1,4,128,128]{3,2,1,0:T(8,128)}, u32[]{:S(2)}, u32[]{:S(2)}) collective-permute-start(f32[1,4,128,128]{3,2,1,0:T(8,128)} %get-tuple-element.390), channel_id=1, source_target_pairs={{0,8},{1,9},{2,10},{3,11},{4,12},{5,13},{6,14},{7,15},{8,0},{9,1},... | collective-permute-start | bytes 786440 | tf_op jit(solution)/shard_map/ppermute | solution.py:49
  377.9 9.2 %collective-permute-start.117 = (f32[1,4,128,128]{3,2,1,0:T(8,128)}, f32[1,4,128,128]{3,2,1,0:T(8,128)}, u32[]{:S(2)}, u32[]{:S(2)}) collective-permute-start(f32[1,4,128,128]{3,2,1,0:T(8,128)} %get-tuple-element.388), channel_id=1, source_target_pairs={{0,16},{1,17},{2,18},{3,19},{4,20},{5,21},{6,22},{7,23},{8,24},{9,... | collective-permute-start | bytes 786440 | tf_op jit(solution)/shard_map/ppermute | solution.py:49
  380.3 12.0 %collective-permute-start.115 = (f32[2,256,128]{2,1,0:T(8,128)}, f32[2,256,128]{2,1,0:T(8,128)}, u32[]{:S(2)}, u32[]{:S(2)}) collective-permute-start(f32[2,256,128]{2,1,0:T(8,128)} %pad_maximum_fusion.10), channel_id=1, source_target_pairs={{0,1},{1,0},{2,3},{3,2},{4,5},{5,4},{6,7},{7,6},{8,9},{9,8},{10,11... | collective-permute-start | bytes 786440 | tf_op jit(solution)/shard_map/ppermute | solution.py:49
  383.5 23.3 %collective-permute-start.116 = (f32[1,9,64,128]{3,2,1,0:T(8,128)}, f32[1,9,64,128]{3,2,1,0:T(8,128)}, u32[]{:S(2)}, u32[]{:S(2)}) collective-permute-start(f32[1,9,64,128]{3,2,1,0:T(8,128)} %slice_add_fusion), channel_id=1, source_target_pairs={{0,2},{1,3},{2,0},{3,1},{4,6},{5,7},{6,4},{7,5},{8,10},{9,11},{10,... | collective-permute-start | bytes 884744 | tf_op jit(solution)/shard_map/ppermute | solution.py:49
  386.8 66.1 %all-gather.15.cloned.1.call-start = ((), (), s32[]{:S(2)}) async-start(), calls=%async_computation.9 | async-start | bytes 1179648 | tf_op jit(solution)/shard_map/all_gather | solution.py:53
  408.9 8.1 %collective-permute-start.120 = (f32[2,256,128]{2,1,0:T(8,128)S(1)}, f32[2,256,128]{2,1,0:T(8,128)S(1)}, u32[]{:S(2)}, u32[]{:S(2)}) collective-permute-start(f32[2,256,128]{2,1,0:T(8,128)S(1)} %pad_maximum_fusion.11), channel_id=1, source_target_pairs={{0,1},{1,0},{2,3},{3,2},{4,5},{5,4},{6,7},{7,6},{8,9},{9,8},{10,11... | collective-permute-start | bytes 786440 | tf_op jit(solution)/shard_map/ppermute | solution.py:49
  424.7 28.1 %collective-permute-start.123 = (f32[832,128]{1,0:T(8,128)}, f32[832,128]{1,0:T(8,128)}, u32[]{:S(2)}, u32[]{:S(2)}) collective-permute-start(f32[832,128]{1,0:T(8,128)} %pad_maximum_fusion.5.refs_0_), channel_id=1, source_target_pairs={{0,24},{1,25},{2,26},{3,27},{4,28},{5,29},{6,30},{7,31},{8,16},{9,... | collective-permute-start | bytes 1277960 | tf_op jit(solution)/shard_map/ppermute | solution.py:49
  426.7 31.7 %collective-permute-start.122 = (f32[832,128]{1,0:T(8,128)}, f32[832,128]{1,0:T(8,128)}, u32[]{:S(2)}, u32[]{:S(2)}) collective-permute-start(f32[832,128]{1,0:T(8,128)} %pad_maximum_fusion.5.refs_0_), channel_id=1, source_target_pairs={{0,16},{1,17},{2,18},{3,19},{4,20},{5,21},{6,22},{7,23},{8,24},{9,... | collective-permute-start | bytes 1277960 | tf_op jit(solution)/shard_map/ppermute | solution.py:49
  426.8 32.2 %collective-permute-start.121 = (f32[832,128]{1,0:T(8,128)}, f32[832,128]{1,0:T(8,128)}, u32[]{:S(2)}, u32[]{:S(2)}) collective-permute-start(f32[832,128]{1,0:T(8,128)} %pad_maximum_fusion.5.refs_0_), channel_id=1, source_target_pairs={{0,8},{1,9},{2,10},{3,11},{4,12},{5,13},{6,14},{7,15},{8,0},{9,1},... | collective-permute-start | bytes 1277960 | tf_op jit(solution)/shard_map/ppermute | solution.py:49
  428.9 21.1 %collective-permute-start.131 = (f32[256,128]{1,0:T(8,128)}, f32[256,128]{1,0:T(8,128)}, u32[]{:S(2)}, u32[]{:S(2)}) collective-permute-start(f32[256,128]{1,0:T(8,128)} %fusion.6.refs_8_), channel_id=1, source_target_pairs={{0,24},{1,25},{2,26},{3,27},{4,28},{5,29},{6,30},{7,31},{8,16},{9,... | collective-permute-start | bytes 393224 | tf_op jit(solution)/shard_map/ppermute | solution.py:49
  431.1 21.0 %collective-permute-start.130 = (f32[256,128]{1,0:T(8,128)}, f32[256,128]{1,0:T(8,128)}, u32[]{:S(2)}, u32[]{:S(2)}) collective-permute-start(f32[256,128]{1,0:T(8,128)} %fusion.6.refs_8_), channel_id=1, source_target_pairs={{0,16},{1,17},{2,18},{3,19},{4,20},{5,21},{6,22},{7,23},{8,24},{9,... | collective-permute-start | bytes 393224 | tf_op jit(solution)/shard_map/ppermute | solution.py:49
  450.0 9.1 %collective-permute-start.132 = (f32[256,128]{1,0:T(8,128)}, f32[256,128]{1,0:T(8,128)}, u32[]{:S(2)}, u32[]{:S(2)}) collective-permute-start(f32[256,128]{1,0:T(8,128)} %fusion.6.refs_8_), channel_id=1, source_target_pairs={{0,4},{1,5},{2,6},{3,7},{4,0},{5,1},{6,2},{7,3},{8,12},{9,13},{10,... | collective-permute-start | bytes 393224 | tf_op jit(solution)/shard_map/ppermute | solution.py:49
  (196 other events, 1348.2 us)
Sparse Core Ops, SparseCore 0:
  97.6 33.8 all-gather.8
  239.5 20.2 reduce-scatter.5
  262.6 27.9 reduce-scatter.3
  292.4 37.7 all-gather.12
  331.9 41.6 all-gather.10
  386.9 22.7 reduce-scatter.7
  417.2 29.6 all-gather.14

commit v4 on v3

--- a/solution.py
+++ b/solution.py
@@ -86,13 +86,15 @@
     def __init__(self, grid, room):
         self.grid, self.room = grid, room
         self.waiting = []
-        self.flying = {"plane": [], "deep": [], "spare": []}
+        self.flying = {"plane": [], "tight": [], "deep": [], "spare": []}
         self.late = []
+        self.names = {}
 
     def move(self, value, step):
         return step(value) if callable(step) else self.grid.swap(value, **step)
 
-    def add(self, flow):
+    def add(self, name, flow):
+        self.names[flow] = name
         self.advance(flow, None)
 
     def advance(self, flow, value):
@@ -152,26 +154,50 @@
             self.advance(flow, [values.pop(0) for _ in got])
         return array
 
-    def last(self, array):
-        return self.close("deep", self.close("plane", array))
-
-    def finish(self):
-        while self.waiting or self.late or self.flying["spare"]:
-            batch, self.waiting = self.waiting, []
-            flown = self.late
-            self.late, self.flying["spare"] = self.flying["spare"], []
+    def last(self, array, first):
+        done = self.flying["plane"] + self.flying["deep"]
+        self.flying = {"plane": [], "tight": [], "deep": [], "spare": []}
+        values = [v for _, got in done for v in got]
+        tied = lax.optimization_barrier((array,) + tuple(values))
+        array, values = tied[0], list(tied[1:])
+        self.parked = []
+        for flow, got in done:
+            got = [values.pop(0) for _ in got]
+            if self.names[flow] in first:
+                self.advance(flow, got)
+            else:
+                self.parked.append((flow, got))
+        return array
+
+    def resume(self, after):
+        for flow, got in self.parked:
+            *got, _ = lax.optimization_barrier((*got, after))
+            self.advance(flow, got)
+
+    def hold(self, names, after):
+        held = [item for item in self.waiting if self.names[item[0]] in names]
+        if not held:
+            return
+        values = [v for _, _, pieces in held for v, _ in pieces]
+        *values, _ = lax.optimization_barrier((*values, after))
+        fresh = {}
+        for flow, kind, pieces in held:
+            fresh[flow] = (flow, kind, [(values.pop(0), step) for _, step in pieces])
+        self.waiting = [fresh.get(item[0], item) for item in self.waiting]
+
+    def run(self, names, kinds=("plane", "deep"), rounds=9, tie=None):
+        for _ in range(rounds):
+            batch = [i for i in self.waiting if self.names[i[0]] in names and i[1] in kinds]
+            if not batch:
+                return tie
+            self.waiting = [i for i in self.waiting if i not in batch]
             for flow, kind, pieces in batch:
                 got = [self.move(v, step) for v, step in pieces]
-                if kind == "spare":
-                    self.flying["spare"].append((flow, got))
-                else:
-                    flown = flown + [(flow, got)]
-            values = [v for _, got in flown for v in got]
-            if len(values) > 1:
-                values = lax.optimization_barrier(values)
-            values = list(values)
-            for flow, got in flown:
-                self.advance(flow, [values.pop(0) for _ in got])
+                if tie is not None:
+                    tied = lax.optimization_barrier((*got, *tie))
+                    got, tie = list(tied[: len(got)]), list(tied[len(got) :])
+                self.advance(flow, got)
+        return tie
 
 
 def exchange(grid, bulk, payload, join):
@@ -180,11 +206,12 @@
         if number == 1:
             payload = bulk.close("plane", payload)
         if number + 1 == len(groups):
-            (payload,) = bulk.open(("plane",), [payload])
+            (payload,) = bulk.open(("plane", "tight"), [payload])
             payload = bulk.close("deep", payload)
         members = [payload] + [grid.swap(payload, **step) for step in group]
         if number + 1 < len(groups):
             payload = join(members)
+    members[0] = bulk.close("tight", members[0])
     return bulk.open(("deep", "spare"), members)
 
 
@@ -352,6 +379,14 @@
     return pltpu.VMEM(shape, dtype)
 
 
+def far(shape, dtype=F32):
+    return pltpu.HBM(shape, dtype)
+
+
+def away(value):
+    return pltpu.with_memory_space_constraint(value, pltpu.HBM)
+
+
 def stay(value):
     return pltpu.with_memory_space_constraint(value, pltpu.VMEM)
 
@@ -410,7 +445,7 @@
 
     def body(red_ref, table_ref, mask_ref, w_ref, select_ref, *refs):
         gain_ref, bias_ref = mid_rows(table_ref, number, 0)
-        got, (mr_ref, hid_ref, out_ref, stats_ref, image, tile, patch) = refs[:size], refs[size:]
+        got, (mr_ref, keep_ref, send_ref, out_ref, stats_ref, image, tile, patch) = refs[:size], refs[size:]
         k = pl.program_id(0)
 
         @pl.when(k == 0)
@@ -422,7 +457,9 @@
                 pieces.append(z * sigmoid(z) * mask_ref[lo:hi, :])
             hidden = jnp.concatenate(pieces, axis=0)
             fill_patches(hidden, image, tile, patch, 1)
-            hid_ref[...] = dot(hidden.astype(BF), select_ref[...])
+            halves = dot(hidden.astype(BF), select_ref[...])
+            keep_ref[...] = halves[:, : mid // 2]
+            send_ref[...] = halves[:, mid // 2 :]
             out_ref[...] = jnp.zeros((rows, mid), F32)
 
         total = out_ref[...]
@@ -447,13 +484,15 @@
         + [full(payload(mid))] * size,
         [
             full((8, mid)),
-            full((rows, mid)),
+            full((rows, mid // 2)),
+            full((rows, mid // 2)),
             full((rows, mid)),
             full(payload(mid)),
         ],
         [
             near((8, mid)),
-            near((rows, mid)),
+            near((rows, mid // 2)),
+            near((rows, mid // 2)),
             near((rows, mid)),
             near(payload(mid)),
         ],
@@ -499,7 +538,7 @@
         ]
         + [full(payload(mid))] * size,
         [full((8, mid)), full((rows, mid)), cols(rows), full(payload(d_in))],
-        [near((8, mid)), near((rows, mid)), near((rows, d_in)), near(payload(d_in))],
+        [near((8, mid)), near((rows, mid)), far((rows, d_in)), near(payload(d_in))],
         name="expand_stage",
         flops=2 * rows * d_in * mid,
     )(spa, table, mask, w_expand, *members)
@@ -562,25 +601,33 @@
         ]
         + [full(payload(d_in))] * size,
         [full((8, d_in)), cols(rows), cols(rows), full((rows, mid)), full(payload(mid))],
-        [near((8, d_in)), near((rows, d_in)), near((rows, d_in)), near((rows, mid)), near(payload(mid))],
+        [near((8, d_in)), far((rows, d_in)), far((rows, d_in)), near((rows, mid)), near(payload(mid))],
         name="join_stage",
         flops=2 * rows * d_in * mid,
         transcendentals=rows * d_in,
     )(exp, table, act, mask, w_reduce, *members)
 
 
+def put_places(value, image_ref, tile_ref):
+    row = MAP * SLOTS
+    for p in range(MAP):
+        image_ref[p * row : (p + 1) * row, :] = value[p * MAPW * SLOTS : p * MAPW * SLOTS + row]
+    tile_ref[...] = value[IMG_ROWS : IMG_ROWS + tile_ref.shape[0]]
+
+
 def put_sums(stream, pre, normed, sums_ref, first=0):
     put_rows(sums_ref, 0, stream, jnp.sum(pre, axis=0, keepdims=True), first)
     put_rows(sums_ref, 1, stream, jnp.sum(pre * normed, axis=0, keepdims=True), first)
 
 
-def turn_stage(number, exp, members, table, act, mask, grad):
+def turn_stage(number, exp, members, table, act, mask, grad, tile_rows):
     rows, d_in = exp.shape
     size = len(members)
 
     def body(exp_ref, table_ref, act_ref, mask_ref, grad_ref, *refs):
         gain_ref, bias_ref = out_rows(table_ref, number)
-        got, (mr_ref, out_ref, pre_ref, sums_ref) = refs[:size], refs[size:]
+        got, (mr_ref, image_ref, tile_ref, pre_ref, sums_ref) = refs[:size], refs[size:]
+        outs = []
         k = pl.program_id(0)
 
         @pl.when(k == 0)
@@ -592,18 +639,25 @@
             z = n * gain_ref[...] + bias_ref[...] + act_ref[lo:hi, :].astype(F32)
             s = sigmoid(z)
             m = mask_ref[lo:hi, :]
-            out_ref[lo:hi, :] = z * s * m
+            outs.append(z * s * m)
             pre = grad_ref[lo:hi, :].astype(F32) * m * (s * (1.0 + z * (1.0 - s)))
             pre_ref[lo:hi, :] = pre
             put_sums(stream, pre, n, sums_ref, k * (CH // 128))
+        put_places(jnp.concatenate(outs, axis=0), image_ref, tile_ref)
 
     return call(
         body,
         d_in // CH,
         [cols(rows), cols(table.shape[0]), cols(rows), full((rows, 1)), cols(rows)]
         + [full(payload(d_in))] * size,
-        [full((8, d_in)), cols(rows), cols(rows), full(payload(d_in, 2))],
-        [near((8, d_in)), near((rows, d_in)), near((rows, d_in)), near(payload(d_in, 2))],
+        [full((8, d_in)), cols(MAP * MAP * SLOTS), cols(tile_rows), cols(rows), full(payload(d_in, 2))],
+        [
+            near((8, d_in)),
+            far((MAP * MAP * SLOTS, d_in)),
+            far((tile_rows, d_in)),
+            far((rows, d_in)),
+            near(payload(d_in, 2)),
+        ],
         name="turn_stage",
         flops=20 * rows * d_in,
         transcendentals=rows * d_in,
@@ -770,7 +824,7 @@
     )(me, pre2, spa, mr2, table, mask, w9, red, mr1, *members)
 
 
-def back_reduce(number, pre1, red, mr1, members, table, mask, w_reduce, pre3, below):
+def back_reduce(number, pre1, red, mr1, members, table, mask, w_reduce, pre3, below, tile_rows):
     rows, mid = red.shape
     d_in = pre3.shape[1]
     size = len(members)
@@ -802,17 +856,17 @@
     if below is None:
 
         def body(pre1_ref, red_ref, mr1_ref, table_ref, mask_ref, w_ref, pre3_ref, *refs):
-            got, (both_ref, gr_ref, out_ref, share, low) = refs[:size], refs[size:]
+            got, (both_ref, gr_ref, image_ref, tile_ref, share, low) = refs[:size], refs[size:]
             k = pl.program_id(0)
             head(k, got, pre1_ref, red_ref, mr1_ref, table_ref, mask_ref, both_ref, gr_ref, share, low)
-            out_ref[...] = pre3_ref[...] + dot_nt(low[...], w_ref[0])
+            put_places(pre3_ref[...] + dot_nt(low[...], w_ref[0]), image_ref, tile_ref)
 
         return call(
             body,
             d_in // CH,
             specs + [full(payload(mid, 2))] * size,
-            [full((2, mid)), full((rows, mid)), cols(rows)],
-            [near((2, mid)), near((rows, mid)), near((rows, d_in))],
+            [full((2, mid)), full((rows, mid)), cols(MAP * MAP * SLOTS), cols(tile_rows)],
+            [near((2, mid)), near((rows, mid)), far((MAP * MAP * SLOTS, d_in)), far((tile_rows, d_in))],
             scratch,
             name="back_reduce_last",
             flops=2 * rows * d_in * mid,
@@ -836,7 +890,7 @@
         d_in // CH,
         specs + [cols(rows), full((8, d_in)), cols(below[2].shape[0]), cols(rows)] + [full(payload(mid, 2))] * size,
         [full((2, mid)), full((rows, mid)), cols(rows), full(payload(d_in, 2))],
-        [near((2, mid)), near((rows, mid)), near((rows, d_in)), near(payload(d_in, 2))],
+        [near((2, mid)), near((rows, mid)), far((rows, d_in)), near(payload(d_in, 2))],
         scratch,
         name="back_reduce",
         flops=2 * rows * d_in * mid,
@@ -856,10 +910,23 @@
     return place
 
 
-def weight_expand(me, own, peer, keep, got, nz, plain):
+def weight_halves(body, args, shape, scratch, flops, name):
+    vmem = pl.BlockSpec(memory_space=pltpu.VMEM)
+    return pl.pallas_call(
+        body,
+        in_specs=[smem()] + [vmem] * 4,
+        out_specs=[vmem] * 4,
+        out_shape=[sds(shape)] * 4,
+        scratch_shapes=list(scratch),
+        compiler_params=pltpu.CompilerParams(vmem_limit_bytes=VMEM_LIMIT),
+        cost_estimate=pl.CostEstimate(flops=0, bytes_accessed=0, transcendentals=0),
+        name=name,
+    )(*args)
+
+
+def weight_expand(me, own, peer, keep, got, nz):
     rows, mid = own.shape
-    half = keep.shape[1]
-    step = half // 4
+    step = keep.shape[1] // 4
     deep = mid // nz
 
     def body(me_ref, own_ref, peer_ref, keep_ref, got_ref, x_keep, x_send, y_keep, y_send):
@@ -871,37 +938,14 @@
             x_ref = x_keep if m < 2 else x_send
             y_ref = y_keep if m % 2 == 0 else y_send
             for z in range(nz):
-                place = z if plain else spot(me_ref[2] ^ z, nz)
+                place = spot(me_ref[2] ^ z, nz)
                 x_ref[m % 2, place] = value[z * deep : (z + 1) * deep, 0:128]
                 y_ref[m // 2, place] = value[z * deep : (z + 1) * deep, 128:256]
 
-    vmem = pl.BlockSpec(memory_space=pltpu.VMEM)
-    return pl.pallas_call(
-        body,
-        in_specs=[smem()] + [vmem] * 4,
-        out_specs=[vmem] * 4,
-        out_shape=[sds((2, nz, deep, 128))] * 4,
-        compiler_params=pltpu.CompilerParams(vmem_limit_bytes=VMEM_LIMIT),
-        cost_estimate=pl.CostEstimate(flops=0, bytes_accessed=0, transcendentals=0),
-        name="weight_expand",
-    )(me, own, peer, keep, got)
-
-
-def slice_outputs(nz, shape, plain):
-    if plain:
-        return [sds((nz,) + shape)]
-    return [sds((nz // 2,) + shape)] * 2
-
-
-def put_slices(me_ref, total, outs, nz, deep, plain, put):
-    for p in range(nz):
-        z = p if plain else me_ref[2] ^ spot(p, nz)
-        rows = total[pl.ds(pl.multiple_of(z * deep, deep), deep), :]
-        part, at = (0, p) if plain else divmod(p, nz // 2)
-        put(outs[part], at, rows)
-
-
-def weight_reduce(me, own, peer, keep, got, nz, plain):
+    return weight_halves(body, (me, own, peer, keep, got), (2, nz, deep, 128), (), 0, "weight_expand")
+
+
+def weight_reduce(me, own, peer, keep, got, nz):
     rows, width = own.shape
     mid = keep.shape[1]
     step = mid // 4
@@ -914,93 +958,70 @@
             at = slice(z * deep, (z + 1) * deep)
             a = jnp.concatenate([own_ref[:, at].astype(BF), peer_ref[:, at].astype(BF)], axis=0)
             total[...] = dot_tn(a, b)
-            place = z if plain else spot(me_ref[2] ^ z, nz)
+            place = spot(me_ref[2] ^ z, nz)
             for m in range(4):
                 column = me_ref[1] ^ ((m % 2) * 2 + m // 2)
                 value = total[:, pl.ds(pl.multiple_of(column * step, step), step)]
                 (x_keep if m < 2 else x_send)[m % 2, place] = value[:part]
                 (y_keep if m % 2 == 0 else y_send)[m // 2, place] = value[part:]
 
+    return weight_halves(
+        body, (me, own, peer, keep, got), (2, nz, part, step), [pltpu.VMEM((deep, mid), F32)], 0, "weight_reduce"
+    )
+
+
+def weight_spatial(me, hidden, near, far, nz):
+    both, half = hidden[0].shape
+    rows = both // 2
+    width = near[0].shape[1]
+    deep = half // nz
+    tile_rows = rows - IMG_ROWS
+
+    def body(me_ref, h0, h1, h2, h3, n0, n1, n2, n3, far_ref, keep_ref, send_ref, image, tile, left, patch, total):
+        image[...] = jnp.zeros_like(image)
+        tile[...] = jnp.zeros_like(tile)
+        for m, (h_ref, n_ref) in enumerate(((h0, n0), (h1, n1), (h2, n2), (h3, n3))):
+            left[m * both : (m + 1) * both, :] = h_ref[...].astype(BF)
+            for core in range(2):
+                value = n_ref[...] if core == 0 else far_ref[m]
+                at = m * both + core * rows
+                image[24 : 24 + IMG_ROWS, :] = value[0:IMG_ROWS]
+                tile[8 : 8 + tile_rows, :] = value[IMG_ROWS:rows]
+                for tap in range(9):
+                    dy, dx = tap // 3 - 1, tap % 3 - 1
+                    part, rest = shifted(image, tile, -dy, -dx, tile_rows)
+                    patch[at : at + IMG_ROWS, tap * width : (tap + 1) * width] = part.astype(BF)
+                    patch[at + IMG_ROWS : at + rows, tap * width : (tap + 1) * width] = rest.astype(BF)
+        total[...] = dot_tn(left[...], patch[...])
+        for p in range(nz):
+            z = me_ref[2] ^ spot(p, nz)
+            value = total[pl.ds(pl.multiple_of(z * deep, deep), deep), :]
+            ref, at = (keep_ref, p) if p < nz // 2 else (send_ref, p - nz // 2)
+            for tap in range(9):
+                ref[at, tap] = value[:, tap * width : (tap + 1) * width]
+
     vmem = pl.BlockSpec(memory_space=pltpu.VMEM)
     return pl.pallas_call(
         body,
-        in_specs=[smem()] + [vmem] * 4,
-        out_specs=[vmem] * 4,
-        out_shape=[sds((2, nz, part, step))] * 4,
-        scratch_shapes=[pltpu.VMEM((deep, mid), F32)],
+        in_specs=[smem()] + [vmem] * 9,
+        out_specs=[vmem] * 2,
+        out_shape=[sds((nz // 2, 9, deep, width))] * 2,
+        scratch_shapes=[
+            pltpu.VMEM((IMG_ROWS + 48, width), F32),
+            pltpu.VMEM((tile_rows + 16, width), F32),
+            pltpu.VMEM((4 * both, half), BF),
+            pltpu.VMEM((4 * both, 9 * width), BF),
+            pltpu.VMEM((half, 9 * width), F32),
+        ],
         compiler_params=pltpu.CompilerParams(vmem_limit_bytes=VMEM_LIMIT),
         cost_estimate=pl.CostEstimate(flops=0, bytes_accessed=0, transcendentals=0),
-        name="weight_reduce",
-    )(me, own, peer, keep, got)
-
-
-def weight_spatial(me, hidden, near, far, nz, plain):
-    _, rows, mid = hidden.shape
-    width = near.shape[2]
-    half = mid // 2
-    deep = half // nz
-    tile_rows = rows - IMG_ROWS
-    shapes = slice_outputs(nz, (9, deep, width), plain)
-
-    def body(me_ref, hidden_ref, near_ref, far_ref, *refs):
-        outs, (image, tile, left, patch, total) = refs[:-5], refs[-5:]
-        k = pl.program_id(0)
-        m = (k // 2) ^ me_ref[1]
-        mine = lax.rem(k, 2) == me_ref[0]
-
-        @pl.when(k == 0)
-        def _():
-            image[...] = jnp.zeros_like(image)
-            tile[...] = jnp.zeros_like(tile)
-
-        value = jnp.where(mine, near_ref[m], far_ref[m])
-        image[24 : 24 + IMG_ROWS, :] = value[0:IMG_ROWS]
-        tile[8 : 8 + tile_rows, :] = value[IMG_ROWS:rows]
-        for tap in range(9):
-            dy, dx = tap // 3 - 1, tap % 3 - 1
-            part, rest = shifted(image, tile, -dy, -dx, tile_rows)
-            patch[k, 0:IMG_ROWS, tap * width : (tap + 1) * width] = part.astype(BF)
-            patch[k, IMG_ROWS:rows, tap * width : (tap + 1) * width] = rest.astype(BF)
-        at = pl.ds(pl.multiple_of(jnp.where(mine, 0, half), half), half)
-        left[k] = hidden_ref[0, :, at].astype(BF)
-
-        @pl.when(k == 7)
-        def _():
-            a = left[...].reshape(8 * rows, half)
-            total[...] = dot_tn(a, patch[...].reshape(8 * rows, 9 * width))
-
-            def put(ref, at, value):
-                for tap in range(9):
-                    ref[at, tap] = value[:, tap * width : (tap + 1) * width]
-
-            put_slices(me_ref, total, outs, nz, deep, plain, put)
-
-    return call(
-        body,
-        8,
-        [
-            smem(),
-            pl.BlockSpec((1, rows, mid), lambda k: (k, 0, 0)),
-            full(near.shape),
-            full(far.shape),
-        ],
-        [full(v.shape) for v in shapes],
-        shapes,
-        [
-            pltpu.VMEM((IMG_ROWS + 48, width), F32),
-            pltpu.VMEM((tile_rows + 16, width), F32),
-            pltpu.VMEM((8, rows, half), BF),
-            pltpu.VMEM((8, rows, 9 * width), BF),
-            pltpu.VMEM((half, 9 * width), F32),
-        ],
         name="weight_spatial",
-        flops=16 * rows * 9 * half * width,
-    )(me, hidden, near, far)
+    )(me, *hidden, *near, far)
 
 
 class Collect:
-    def __init__(self, grid, me, spare):
-        self.grid, self.me, self.spare = grid, me, spare
+    def __init__(self, grid, me):
+        self.grid, self.me, self.marks = grid, me, None
 
     def over_z(self, keep, send):
         step = 1
@@ -1012,23 +1033,26 @@
             half = keep.shape[0] // 2
             keep, send = keep[:half] + got[:half], keep[half:] + got[half:]
 
-    def scatter(self, value):
-        return lax.psum_scatter(value, "narrow", scatter_dimension=0, tiled=True)[0]
+    def chips(self, pieces, out):
+        flat = jnp.concatenate([p.reshape(-1, 128) for p in pieces])
+        for group in self.grid.far():
+            flat = flat + sum(self.grid.swap(flat, **step) for step in group)
+        got = yield "plane", [(flat, dict(dx=1)), (flat, dict(dy=1)), (flat, dict(dy=1, dx=1))]
+        out.extend([flat] + list(lax.optimization_barrier(tuple(got))))
 
     def by_halves(self, kernel, own, peer, keep, send, out, after=None):
         (got,) = yield "core", [(send, dict(dc=1))]
+        if after:
+            got, _ = lax.optimization_barrier((got, after[0]))
+        x_keep, x_send, y_keep, y_send = kernel(self.me, own, peer, keep, got, self.grid.z)
+        got = yield "plane", [(x_send, dict(dx=1)), (y_send, dict(dy=1))]
         if after is not None:
-            got, _ = lax.optimization_barrier((got, after()[0]))
-        x_keep, x_send, y_keep, y_send = kernel(self.me, own, peer, keep, got, self.grid.z, self.spare)
-        got = yield "plane", [(x_send, dict(dx=1)), (y_send, dict(dy=1))]
+            after.append(got[0])
         x_last, y_last = x_keep[1:] + got[0][1:], y_keep[1:] + got[1][1:]
         x_keep, y_keep = x_keep[:1] + got[0][:1], y_keep[:1] + got[1][:1]
         got = yield "plane", [(x_last, dict(dy=1)), (y_last, dict(dx=1))]
-        if self.spare:
-            value = jnp.concatenate([x_keep[0] + got[0][0], y_keep[0] + got[1][0]], axis=1)
-            (piece,) = yield "spare", [(value, self.scatter)]
-            out.append(piece)
-            return
+        if after is not None:
+            after.append(got[0])
         half = self.grid.z // 2
 
         def side(at):
@@ -1037,105 +1061,79 @@
         piece = yield from self.over_z(side(slice(0, half)), side(slice(half, 2 * half)))
         out.append(piece)
 
-    def by_rows(self, kernel, rows_of_plane, grad, out):
-        got = yield "plane", [(grad[1], dict(dx=1)), (grad[2], dict(dy=1)), (grad[3], dict(dy=1, dx=1))]
-        near = jnp.stack([grad[0]] + list(got))
-        (far,) = yield "core", [(near, dict(dc=1))]
-        result = kernel(self.me, rows_of_plane, near, far, self.grid.z, self.spare)
-        self.marks = result
-        if self.spare:
-            (piece,) = yield "spare", [(result[0], self.scatter)]
-            out.append(piece)
-        else:
-            piece = yield from self.over_z(*result)
-            out.append(piece)
-
-    def flat(self, pieces):
-        flat = jnp.concatenate([p[0].reshape(-1, 128) for p in pieces], axis=0)
-        for group in self.grid.far():
-            flat = flat + sum(self.grid.swap(flat, **step) for step in group)
-        return flat
-
-    def gather(self, pieces, out):
-        (got,) = yield "spare", [(self.flat(pieces), self.grid.plane)]
-        out.append(got)
-
-    def chips(self, flat):
-        return [flat] + [self.grid.swap(flat, dy=m >> 1, dx=m & 1) for m in (1, 2, 3)]
-
-    def cores(self, values):
-        return values + [self.grid.swap(v, dc=1) for v in values]
-
-
-def place_slices(me, number, gathered, shapes, before):
+    def by_rows(self, hidden, grad, out, after=None):
+        got = yield "tight", [(grad[1], dict(dx=1)), (grad[2], dict(dy=1)), (grad[3], dict(dy=1, dx=1))]
+        near = [grad[0]] + list(got)
+        (far,) = yield "core", [(jnp.stack(near), dict(dc=1))]
+        keep, send = weight_spatial(self.me, hidden, near, far, self.grid.z)
+        if after is not None:
+            after.append(keep)
+        piece = yield from self.over_z(keep, send)
+        out.append(piece)
+
+    def hidden(self, keep, send, out):
+        (got,) = yield "core", [(send, dict(dc=1))]
+        value = jnp.concatenate([keep, got], axis=0)
+        got = yield "plane", [(value, dict(dx=1)), (value, dict(dy=1))]
+        (last,) = yield "tight", [(value, dict(dy=1, dx=1))]
+        out.extend([value, got[0], got[1], last])
+
+
+def place_slices(me, gathered, shapes):
     (e_rows, d_in), (r_rows, mid), (s_rows, _) = shapes
     dims = ((BLOCKS, r_rows, mid), (BLOCKS, 9, s_rows, mid), (BLOCKS, e_rows, d_in))
-    size = len(gathered)
+    size = 8 * BLOCKS
     r_len, s_len = r_rows // 2, s_rows // 2
 
     def body(me_ref, *refs):
         got = refs[:size]
         outs, (red, spa, exp, sems, out_sems) = refs[-8:-5], refs[-5:]
-
-        def aligned(value, unit):
-            return value if isinstance(value, int) else pl.multiple_of(value, unit)
-
-        copies = []
-        for a in range(8):
-            if size == 2:
-                core, chip = a % 2, a // 2
-                source, source_r = got[0].at[a], got[1].at[a]
-            else:
+        copies = [[] for _ in range(BLOCKS)]
+        for b in range(BLOCKS):
+            for a in range(8):
                 core = me_ref[0] if a < 4 else 1 - me_ref[0]
                 chip = (a % 4) ^ me_ref[1]
-                source, source_r = got[a], got[8 + a]
-            column = core * 4 + (chip % 2) * 2 + chip // 2
-            moves = []
-            for t in range(2):
-                at = aligned(column * 256 + t * 128, 128)
-                moves.append((source.at[pl.ds(t * e_rows, e_rows), :], exp.at[:, pl.ds(at, 128)]))
-            at = aligned(chip * 128, 128)
-            row = aligned(core * r_len, r_len)
-            moves.append((source_r, red.at[pl.ds(row, r_len), pl.ds(at, 128)]))
-            row = aligned(core * s_len, s_len)
-            for tap in range(9):
-                moves.append(
-                    (
-                        source.at[pl.ds(2 * e_rows + tap * s_len, s_len), :],
-                        spa.at[tap, pl.ds(row, s_len), pl.ds(at, 128)],
-                    )
-                )
-            copies += [pltpu.make_async_copy(src, dst, sems.at[a, i]) for i, (src, dst) in enumerate(moves)]
-        for copy in copies:
+                source = got[8 * b + a]
+                column = core * 4 + (chip % 2) * 2 + chip // 2
+                moves = []
+                for t in range(2):
+                    at = pl.multiple_of(column * 256 + t * 128, 128)
+                    moves.append((source.at[pl.ds(t * e_rows, e_rows), :], exp.at[b, :, pl.ds(at, 128)]))
+                at = pl.multiple_of(chip * 128, 128)
+                row = pl.multiple_of(core * r_len, r_len)
+                start = 2 * e_rows
+                moves.append((source.at[pl.ds(start, r_len), :], red.at[b, pl.ds(row, r_len), pl.ds(at, 128)]))
+                row = pl.multiple_of(core * s_len, s_len)
+                start = 2 * e_rows + r_len
+                taps = source.at[pl.ds(start, 9 * s_len), :].reshape(9, s_len, 128)
+                moves.append((taps, spa.at[b, :, pl.ds(row, s_len), pl.ds(at, 128)]))
+                copies[b] += [
+                    pltpu.make_async_copy(src, dst, sems.at[b, a, i]) for i, (src, dst) in enumerate(moves)
+                ]
+        last = []
+        for copy in copies[0] + copies[1]:
             copy.start()
-        for copy in copies:
+        for b in range(BLOCKS):
+            for copy in copies[b]:
+                copy.wait()
+            for i, (src, dst) in enumerate(zip((red, spa, exp), outs)):
+                copy = pltpu.make_async_copy(src.at[b], dst.at[b], out_sems.at[b, i])
+                copy.start()
+                last.append(copy)
+        for copy in last:
             copy.wait()
-        copies = [
-            pltpu.make_async_copy(src, dst.at[number], out_sems.at[i])
-            for i, (src, dst) in enumerate(zip((red, spa, exp), outs))
-        ]
-        for copy in copies:
-            copy.start()
-        for copy in copies:
-            copy.wait()
 
     anywhere = pl.BlockSpec(memory_space=pl.ANY)
-    args = (me,) + tuple(gathered)
-    aliases = {}
-    if before is not None:
-        aliases = {len(args) + i: i for i in range(3)}
-        args = args + tuple(before)
     return pl.pallas_call(
         body,
-        in_specs=[smem()] + [anywhere] * (len(args) - 1),
+        in_specs=[smem()] + [anywhere] * size,
         out_specs=[anywhere] * 3,
         out_shape=[sds(d) for d in dims],
-        scratch_shapes=[pltpu.VMEM(d[1:], F32) for d in dims]
-        + [pltpu.SemaphoreType.DMA((8, 12)), pltpu.SemaphoreType.DMA((3,))],
-        input_output_aliases=aliases,
+        scratch_shapes=[pltpu.VMEM(d, F32) for d in dims]
+        + [pltpu.SemaphoreType.DMA((BLOCKS, 8, 4)), pltpu.SemaphoreType.DMA((BLOCKS, 3))],
         compiler_params=pltpu.CompilerParams(vmem_limit_bytes=VMEM_LIMIT),
         name="place_slices",
-    )(*args)
+    )(me, *gathered)
 
 
 def to_rows(image, tile, rows):
@@ -1147,12 +1145,10 @@
     return jnp.concatenate([image, tile, pad], axis=0)
 
 
-def from_rows(value, tiles):
-    width = value.shape[1]
-    image = value[:IMG_ROWS].reshape(MAP, MAPW, SLOTS, width)[:, :MAP]
-    image = jnp.transpose(image, (2, 0, 1, 3))
-    tile = value[IMG_ROWS : IMG_ROWS + tiles * 4].reshape(tiles, TILE, TILE, width)
-    return image, tile
+def from_rows(image, tile):
+    width = image.shape[1]
+    image = jnp.transpose(image.reshape(MAP, MAP, SLOTS, width), (2, 0, 1, 3))
+    return image, tile.reshape(-1, TILE, TILE, width)
 
 
 def row_mask(map_sizes, rows):
@@ -1212,12 +1208,12 @@
     start = to_rows(images, tile_maps, rows)
     grad = to_rows(grad_images, grad_tiles, rows)
     select = core_select(core, mid, nz)
-    collect = [Collect(grid, me, b > 0) for b in range(BLOCKS)]
+    collect = Collect(grid, me)
     bulk = Bulk(grid, ROOM)
 
     table = stay(jnp.concatenate([gain_mid.reshape(-1, mid), bias_mid.reshape(-1, mid)]))
     outer = stay(jnp.concatenate([gain_out, bias_out]))
-    w_reduce, w9, w_expand = stay(w_reduce), stay(w9), stay(w_expand)
+    w_reduce, w9, w_expand = (pltpu.with_memory_space_constraint(w, pltpu.HBM) for w in (w_reduce, w9, w_expand))
 
     def moments(stats):
         return exchange(grid, bulk, stats, join_moments)
@@ -1231,11 +1227,12 @@
     low = start
     for b in range(BLOCKS):
         reds.append(red)
-        mr, hidden, spa, stats = spatial_stage(
+        mr, keep, send, spa, stats = spatial_stage(
             b, red, moments(stats), table, mask, w9, select
         )
         mr1.append(mr)
-        hid1.append(pltpu.with_memory_space_constraint(grid.plane(hidden), pltpu.HBM))
+        hid1.append([])
+        bulk.add(("h", b), collect.hidden(keep, send, hid1[b]))
         keep, send = core_halves(low, core, nz)
         peer = grid.swap(send, dc=1)
         stats, keep, peer = lax.optimization_barrier((stats, keep, peer))
@@ -1246,78 +1243,85 @@
         )
         mr2.append(mr)
         hid2.append((hidden, grid.swap(hidden, dc=1)))
+        exp = away(exp)
         exps.append(exp)
         if b + 1 < BLOCKS:
             mr, out, low, red, stats = join_stage(
                 b + 1, exp, moments(stats), outer, acts[b], mask, w_reduce
             )
             mr3.append(mr)
-            acts.append(out)
+            acts.append(away(out))
     last = BLOCKS - 1
-    mr, out, pre3, sums3 = turn_stage(
-        last, exps[last], moments(stats), outer, acts[last], mask, grad
+    mr, *out, pre3, sums3 = turn_stage(
+        last, exps[last], moments(stats), outer, acts[last], mask, grad, tiles * TILE * TILE
     )
     mr3.append(mr)
+    pre3 = away(pre3)
 
     both1, both2, both3 = [None] * BLOCKS, [None] * BLOCKS, [None] * BLOCKS
     shapes = ((mid // nz, d_in), (d_in // nz, mid), (mid // nz, mid))
     pieces = [([], [], []) for _ in range(BLOCKS)]
-    whole = [[[], []] for _ in range(BLOCKS)]
-
-    def then(flow, b):
-        yield from flow
-        part_e, part_r, part_s = pieces[b]
-        if b > 0 and part_e and part_s and not started[b][0]:
-            started[b][0] = True
-            bulk.add(collect[b].gather((part_e, part_s), whole[b][0]))
-        if b > 0 and part_r and not started[b][1]:
-            started[b][1] = True
-            bulk.add(collect[b].gather((part_r,), whole[b][1]))
-
-    started = [[False, False] for _ in range(BLOCKS)]
+    after = []
     for b in reversed(range(BLOCKS)):
         both3[b], keep, send, pre2, sums2 = back_expand(
             b, me, pre3, exps[b], mr3[b], sums(sums3), outer, mask, w_expand,
             spas[b], mr2[b], table,
         )
-        bulk.add(then(collect[b].by_halves(weight_expand, *hid2[b], keep, send, pieces[b][0]), b))
+        bulk.add(("e", b), collect.by_halves(weight_expand, *hid2[b], keep, send, pieces[b][0]))
         both2[b], *gs, pre1, sums1 = back_spatial(
             b, me, pre2, spas[b], mr2[b], sums(sums2), table, mask, w9,
             reds[b], mr1[b],
         )
-        bulk.add(then(collect[b].by_rows(weight_spatial, hid1[b], gs, pieces[b][2]), b))
+        bulk.add(("s", b), collect.by_rows(hid1[b], gs, pieces[b][2], after if b == 0 else None))
         below = None
         if b > 0:
             below = (exps[b - 1], mr3[b - 1], outer, acts[b - 1])
         result = back_reduce(
-            b, pre1, reds[b], mr1[b], sums(sums1), table, mask, w_reduce, pre3, below
+            b, pre1, reds[b], mr1[b], sums(sums1), table, mask, w_reduce, pre3, below, tiles * TILE * TILE
         )
         both1[b] = result[0]
         gr = result[1]
-        after = None
-        if b == 0:
-            gr = bulk.last(gr)
-            after = lambda: collect[0].marks
-        bulk.add(then(collect[b].by_halves(weight_reduce, *lows[b], gr, gr, pieces[b][1], after), b))
+        reduce_flow = collect.by_halves(
+            weight_reduce, *lows[b], gr, gr, pieces[b][1], after if b == 0 else None
+        )
         if b > 0:
-            pre3, sums3 = result[2], result[3]
+            bulk.add(("r", b), reduce_flow)
+        if b > 0:
+            pre3, sums3 = away(result[2]), result[3]
         else:
-            grad_in = result[2]
-
-    bulk.finish()
-    slices = None
-    for b in reversed(range(BLOCKS)):
-        part_e, part_r, part_s = pieces[b]
-        if b > 0:
-            gathered = whole[b][0] + whole[b][1]
-        else:
-            first = collect[b].chips(collect[b].flat((part_e, part_s)))
-            second = collect[b].chips(collect[b].flat((part_r,)))
-            slices, first = lax.optimization_barrier((slices, first))
-            gathered = collect[b].cores(first) + collect[b].cores(second)
-        slices = place_slices(me, b, gathered, shapes, slices)
-    out_images, out_tiles = from_rows(out, tiles)
-    in_images, in_tiles = from_rows(grad_in, tiles)
+            grad_in = list(result[2:4])
+
+    grad_in[0] = bulk.last(grad_in[0], [("s", 0)])
+    bulk.add(("r", 0), reduce_flow)
+    bulk.run([("r", 0)], ("plane",), 1)
+    bulk.resume(after[1])
+    later = [(n, b) for b in range(1, BLOCKS) for n in "ers"]
+    every = later + [("e", 0)]
+    bulk.hold(every, after[1])
+    bulk.run([("s", 0)])
+    bulk.run(every, ("deep",))
+    bulk.run([("r", 0)], ("plane",))
+    views = []
+    for value in (*out, *grad_in):
+        value, _ = lax.optimization_barrier((value, after[2]))
+        views.append(value)
+    views = from_rows(*views[:2]) + from_rows(*views[2:])
+    bulk.run(every)
+    gathered = [[] for _ in range(BLOCKS)]
+    for b in range(1, BLOCKS):
+        bulk.add(("g", b), collect.chips([p[0] for p in pieces[b]], gathered[b]))
+        bulk.hold([("g", b)], after[2])
+        bulk.run([("g", b)])
+    bulk.run([("r", 0)])
+    bulk.add(("g", 0), collect.chips([p[0] for p in pieces[0]], gathered[0]))
+    bulk.run([("g", 0)])
+    *views, gathered[0][1] = lax.optimization_barrier((*views, gathered[0][1]))
+    final = []
+    for b in range(BLOCKS):
+        final += gathered[b] + [grid.swap(v, dc=1) for v in gathered[b]]
+    final = [pltpu.with_memory_space_constraint(v, pltpu.HBM) for v in final]
+    slices = place_slices(me, final, shapes)
+    out_images, out_tiles, in_images, in_tiles = views
     g_reduce, g_spatial, g_expand = slices
 
     def pair(at):

time: 477 us -> 421 us (0.88)
  local copies, waits for them, and re-layouts: 61.8 us -> 15.7 us
  other arithmetic: 30.1 us -> 11.2 us
  Pallas kernels: 62 us -> 79.3 us
  between operations: 15.6 us -> 2.01 us
  starting transfers between devices: 142 us -> 154 us
  waiting for transfers between devices: 165 us -> 157 us
    unnamed x202 -> x86, local copies, waits for them, and re-layouts: 44.1 us -> 4.06 us
    ppermute x136 -> x150, starting transfers between devices: 141 us -> 154 us  [swap(): return lax.ppermute(value, AXES, pairs)]
    pallas_call x8 -> x7, Pallas kernels: 28.8 us -> 18.3 us  [the longest x1 7.76 us: place_slices(): pl.pallas_call(body, in_specs=[smem()] + [anywhere] * size, out_specs=[an...]
    pallas_call x2, Pallas kernels: 3.65 us -> 8.8 us  [expand_stage(): call(body, d_in // CH, [full((rows, mid)), full(table.shape), full((rows,...]
    ppermute x136 -> x150, waiting for transfers between devices: 161 us -> 157 us  [swap(): return lax.ppermute(value, AXES, pairs)]
  transfers between devices with their start and end apart: 143 -> 150, of which waited for: 83 -> 92; matrix products, arithmetic and copies ran while one was open for 8% -> 3% of each run, Pallas kernels for 11% -> 11%
where the time goes in v4:
time: 421 us; the launch traced here: 419 us
  waiting for transfers between devices  157 us (37%)
  starting transfers between devices  154 us (37%)
  Pallas kernels  79.3 us (19%)
  local copies, waits for them, and re-layouts  15.7 us (4%)
  other arithmetic  11.2 us (3%)
    ppermute x150, waiting for transfers between devices, swap(): return lax.ppermute(value, AXES, pairs)  157 us
    ppermute x150, starting transfers between devices, swap(): return lax.ppermute(value, AXES, pairs)  154 us
    pallas_call x2, Pallas kernels, back_spatial(): call(body, 3, [smem(), full((rows, mid)), full((rows, mid)), full((8, mid...  10.5 us
    pallas_call x2, Pallas kernels, back_expand(): call(body, d_in // CH, [smem(), cols(rows), cols(rows), full((8, d_in)),...  9.39 us
    pallas_call x2, Pallas kernels, spatial_stage(): call(body, 3, [full((rows, mid)), full(table.shape), full((rows, 1)), pl....  9.26 us
    pallas_call x2, Pallas kernels, expand_stage(): call(body, d_in // CH, [full((rows, mid)), full(table.shape), full((rows,...  8.8 us
  transfers between devices with their start and end apart: 150, of which 92 were waited for; matrix products, arithmetic and copies ran while one was open for 3% of the time, Pallas kernels for 11%

profile of v4, /device:TPU:0, one launch (start us, length us, event | category | flops | bytes accessed | tf_op | source)
XLA Modules:
  0.0 419.2 jit_solution(10960073242588544790)
XLA Ops:
  8.0 3.3 reduce_first.1
  13.3 4.0 collective-permute-start.3
  19.0 2.0 collective-permute-done.2
  21.5 3.7 collective-permute-start.6
  27.1 2.7 collective-permute-done.5.refs_2_
  29.8 4.6 %spatial_stage.2 = (f32[8,512]{1,0:T(8,128)S(1)}, f32[192,256]{1,0:T(8,128)S(1)}, f32[192,256]{1,0:T(8,128)S(1)}, f32[192,512]{1,0:T(8,128)S(1)}, f32[3,8,128]{2,1,0:T(8,128)S(1)}) custom-call(f32[192,512]{1,0:T(8,128)S(1)} %get-tuple-element.219.red_ref, f32[8,512]{1,0:T(8,128)S(1)} %pad_maximum_fusion.21.table_ref, f32[192,1]{1,0:T(8,128)S(1)} %copy.23.mask_ref, ...), custom_call_target="tpu_custom_call" | custom-call | tf_op jit(solution)/shard_map/spatial_stage/pallas_call | solution.py:474
  43.9 2.3 collective-permute-start.13
  49.3 4.4 %expand_stage.2 = (f32[8,512]{1,0:T(8,128)S(1)}, f32[192,512]{1,0:T(8,128)S(1)}, f32[192,2048]{1,0:T(8,128)}, f32[3,32,128]{2,1,0:T(8,128)S(1)}) custom-call(f32[192,512]{1,0:T(8,128)S(1)} %get-tuple-element.221.spa_ref, f32[8,512]{1,0:T(8,128)S(1)} %pad_maximum_fusion.21.table_ref, f32[192,1]{1,0:T(8,128)S(1)} %copy.23.mask_ref, ...), custom_call_target="tpu_custom_call" | custom-call | tf_op jit(solution)/shard_map/expand_stage/pallas_call | solution.py:530
  62.6 2.3 collective-permute-start.22
  66.6 2.6 collective-permute-start.23
  69.3 3.1 collective-permute-done.22.h3
  73.2 5.3 %join_stage.1 = (f32[8,2048]{1,0:T(8,128)S(1)}, f32[192,2048]{1,0:T(8,128)}, f32[192,2048]{1,0:T(8,128)}, f32[192,512]{1,0:T(8,128)S(1)}, f32[3,8,128]{2,1,0:T(8,128)S(1)}) custom-call(f32[192,2048]{1,0:T(8,128)} %get-tuple-element.227.exp_ref, f32[4,2048]{1,0:T(4,128)S(1)} %pad_maximum_fusion.20.table_ref.outer_ref, ...), custom_call_target="tpu_custom_call" | custom-call | tf_op jit(solution)/shard_map/join_stage/pallas_call | solution.py:592
  83.4 2.3 collective-permute-start.29
  93.3 2.1 collective-permute-start.30
  97.0 4.6 %spatial_stage.3 = (f32[8,512]{1,0:T(8,128)S(1)}, f32[192,256]{1,0:T(8,128)S(1)}, f32[192,256]{1,0:T(8,128)S(1)}, f32[192,512]{1,0:T(8,128)S(1)}, f32[3,8,128]{2,1,0:T(8,128)S(1)}) custom-call(f32[192,512]{1,0:T(8,128)S(1)} %get-tuple-element.235.red_ref, f32[8,512]{1,0:T(8,128)S(1)} %pad_maximum_fusion.21.table_ref, f32[192,1]{1,0:T(8,128)S(1)} %copy.23.mask_ref, ...), custom_call_target="tpu_custom_call" | custom-call | tf_op jit(solution)/shard_map/spatial_stage/pallas_call | solution.py:474
  112.0 2.2 collective-permute-start.39
  116.0 4.4 %expand_stage.3 = (f32[8,512]{1,0:T(8,128)S(1)}, f32[192,512]{1,0:T(8,128)S(1)}, f32[192,2048]{1,0:T(8,128)}, f32[3,32,128]{2,1,0:T(8,128)S(1)}) custom-call(f32[192,512]{1,0:T(8,128)S(1)} %get-tuple-element.237.spa_ref, f32[8,512]{1,0:T(8,128)S(1)} %pad_maximum_fusion.21.table_ref, f32[192,1]{1,0:T(8,128)S(1)} %copy.23.mask_ref, ...), custom_call_target="tpu_custom_call" | custom-call | tf_op jit(solution)/shard_map/expand_stage/pallas_call | solution.py:530
  136.1 4.7 %collective-permute-done.48.h3 = f32[384,256]{1,0:T(8,128)S(1)} collective-permute-done((f32[384,256]{1,0:T(8,128)S(1)}, f32[384,256]{1,0:T(8,128)S(1)}, u32[]{:S(2)}, u32[]{:S(2)}) %collective-permute-start.48) | collective-permute-done | bytes 393248 | tf_op jit(solution)/shard_map/ppermute | solution.py:49
  141.6 4.7 %turn_stage.1 = (f32[8,2048]{1,0:T(8,128)S(1)}, f32[98,2048]{1,0:T(8,128)}, f32[72,2048]{1,0:T(8,128)}, f32[192,2048]{1,0:T(8,128)}, f32[2,32,128]{2,1,0:T(8,128)S(1)}) custom-call(f32[192,2048]{1,0:T(8,128)} %get-tuple-element.244.exp_ref, f32[4,2048]{1,0:T(4,128)S(1)} %pad_maximum_fusion.20.table_ref.outer_ref, f32[192,2048]{1,0:T(8,128)} %get-tuple-element.245.act_ref, ...), custom_call_target="tpu_custom_call" | custom-call | tf_op jit(solution)/shard_map/turn_stage/pallas_call | solution.py:648
  154.0 3.1 collective-permute-start.58
  159.8 2.3 collective-permute-done.57.refs_2_
  162.0 4.8 %back_expand.2 = (f32[2,2048]{1,0:T(2,128)S(1)}, f32[192,1024]{1,0:T(8,128)S(1)}, f32[192,1024]{1,0:T(8,128)S(1)}, f32[192,512]{1,0:T(8,128)S(1)}, f32[2,8,128]{2,1,0:T(8,128)S(1)}) custom-call(s32[4]{0:T(128)S(1)} %pad_add_fusion.me_ref, f32[192,2048]{1,0:T(8,128)} %get-tuple-element.256.pre3_ref, f32[192,2048]{1,0:T(8,128)} %get-tuple-element.244.exp_ref, ...), custom_call_target="tpu_custom_call" | custom-call | tf_op jit(solution)/shard_map/back_expand/pallas_call | solution.py:732
  167.5 2.3 collective-permute-done.59
  185.8 5.1 %back_spatial.2 = (f32[2,512]{1,0:T(2,128)S(1)}, f32[192,128]{1,0:T(8,128)S(1)}, f32[192,128]{1,0:T(8,128)S(1)}, f32[192,128]{1,0:T(8,128)S(1)}, f32[192,128]{1,...) custom-call(s32[4]{0:T(128)S(1)} %pad_add_fusion.me_ref, f32[192,512]{1,0:T(8,128)S(1)} %get-tuple-element.260.pre2_ref, ...), custom_call_target="tpu_custom_call" | custom-call | tf_op jit(solution)/shard_map/back_spatial/pallas_call | solution.py:799
  212.3 2.2 weight_spatial.2
  214.6 5.3 %back_reduce.1 = (f32[2,512]{1,0:T(2,128)S(1)}, f32[192,512]{1,0:T(8,128)S(1)}, f32[192,2048]{1,0:T(8,128)}, f32[2,32,128]{2,1,0:T(8,128)S(1)}) custom-call(f32[192,512]{1,0:T(8,128)S(1)} %get-tuple-element.269.pre1_ref, f32[192,512]{1,0:T(8,128)S(1)} %get-tuple-element.235.red_ref, f32[8,512]{1,0:T(8,128)S(1)} %get-tuple-element.261.mr1_ref, ...), custom_call_target="tpu_custom_call" | custom-call | tf_op jit(solution)/shard_map/back_reduce/pallas_call | solution.py:888
  229.9 5.8 %collective-permute-done.88 = f32[2,9,64,128]{3,2,1,0:T(8,128)S(1)} collective-permute-done((f32[2,9,64,128]{3,2,1,0:T(8,128)S(1)}, f32[2,9,64,128]{3,2,1,0:T(8,128)S(1)}, u32[]{:S(2)}, u32[]{:S(2)}) %collective-permute-start.88) | collective-permute-done | bytes 589856 | tf_op jit(solution)/shard_map/ppermute | solution.py:49
  242.8 4.6 %back_expand.3 = (f32[2,2048]{1,0:T(2,128)S(1)}, f32[192,1024]{1,0:T(8,128)S(1)}, f32[192,1024]{1,0:T(8,128)S(1)}, f32[192,512]{1,0:T(8,128)S(1)}, f32[2,8,128]{2,1,0:T(8,128)S(1)}) custom-call(s32[4]{0:T(128)S(1)} %pad_add_fusion.me_ref, f32[192,2048]{1,0:T(8,128)} %get-tuple-element.299.pre3_ref, f32[192,2048]{1,0:T(8,128)} %get-tuple-element.227.exp_ref, ...), custom_call_target="tpu_custom_call" | custom-call | tf_op jit(solution)/shard_map/back_expand/pallas_call | solution.py:732
  253.2 8.6 %collective-permute-done.93 = f32[2,4,128,128]{3,2,1,0:T(8,128)S(1)} collective-permute-done((f32[2,4,128,128]{3,2,1,0:T(8,128)S(1)}, f32[2,4,128,128]{3,2,1,0:T(8,128)S(1)}, u32[]{:S(2)}, u32[]{:S(2)}) %collective-permute-start.93) | collective-permute-done | bytes 524320 | tf_op jit(solution)/shard_map/ppermute | solution.py:49
  265.0 2.2 collective-permute-done.97
  280.9 5.4 %back_spatial.3 = (f32[2,512]{1,0:T(2,128)S(1)}, f32[192,128]{1,0:T(8,128)S(1)}, f32[192,128]{1,0:T(8,128)S(1)}, f32[192,128]{1,0:T(8,128)S(1)}, f32[192,128]{1,...) custom-call(s32[4]{0:T(128)S(1)} %pad_add_fusion.me_ref, f32[192,512]{1,0:T(8,128)S(1)} %get-tuple-element.321.pre2_ref, ...), custom_call_target="tpu_custom_call" | custom-call | tf_op jit(solution)/shard_map/back_spatial/pallas_call | solution.py:799
  291.1 2.1 collective-permute-start.111
  297.4 2.2 collective-permute-done.111
  301.5 2.1 collective-permute-start.117
  306.0 2.2 weight_spatial.3
  311.8 4.6 %back_reduce_last.1 = (f32[2,512]{1,0:T(2,128)S(1)}, f32[192,512]{1,0:T(8,128)S(1)}, f32[98,2048]{1,0:T(8,128)}, f32[72,2048]{1,0:T(8,128)}) custom-call(f32[192,512]{1,0:T(8,128)S(1)} %get-tuple-element.341.pre1_ref, f32[192,512]{1,0:T(8,128)S(1)} %get-tuple-element.219.red_ref, f32[8,512]{1,0:T(8,128)S(1)} %get-tuple-element.322.mr1_ref, ...), custom_call_target="tpu_custom_call" | custom-call | tf_op jit(solution)/shard_map/back_reduce_last/pallas_call | solution.py:864
  318.1 2.1 weight_reduce.3
  321.0 2.1 collective-permute-done.124
  325.6 12.2 %collective-permute-done.133 = f32[1,9,64,128]{3,2,1,0:T(8,128)S(1)} collective-permute-done((f32[1,9,64,128]{3,2,1,0:T(8,128)S(1)}, f32[1,9,64,128]{3,2,1,0:T(8,128)S(1)}, u32[]{:S(2)}, u32[]{:S(2)}) %collective-permute-start.133) | collective-permute-done | bytes 294944 | tf_op jit(solution)/shard_map/ppermute | solution.py:49
  342.3 4.8 %collective-permute-done.121 = f32[1,4,128,128]{3,2,1,0:T(8,128)S(1)} collective-permute-done((f32[1,4,128,128]{3,2,1,0:T(8,128)S(1)}, f32[1,4,128,128]{3,2,1,0:T(8,128)S(1)}, u32[]{:S(2)}, u32[]{:S(2)}) %collective-permute-start.121) | collective-permute-done | bytes 262176 | tf_op jit(solution)/shard_map/ppermute | solution.py:49
  353.1 4.8 %collective-permute-done.142 = f32[1,256,128]{2,1,0:T(8,128)S(1)} collective-permute-done((f32[1,256,128]{2,1,0:T(8,128)S(1)}, f32[1,256,128]{2,1,0:T(8,128)S(1)}, u32[]{:S(2)}, u32[]{:S(2)}) %collective-permute-start.142) | collective-permute-done | bytes 131104 | tf_op jit(solution)/shard_map/ppermute | solution.py:49
  361.6 3.4 collective-permute-start.132
  365.7 7.5 %collective-permute-done.132 = f32[1,256,128]{2,1,0:T(8,128)S(1)} collective-permute-done((f32[1,256,128]{2,1,0:T(8,128)S(1)}, f32[1,256,128]{2,1,0:T(8,128)S(1)}, u32[]{:S(2)}, u32[]{:S(2)}) %collective-permute-start.132) | collective-permute-done | bytes 131104 | tf_op jit(solution)/shard_map/ppermute | solution.py:49
  376.9 15.3 %collective-permute-done.144.refs_10_ = f32[1088,128]{1,0:T(8,128)S(1)} collective-permute-done((f32[1088,128]{1,0:T(8,128)S(1)}, f32[1088,128]{1,0:T(8,128)S(1)}, u32[]{:S(2)}, u32[]{:S(2)}) %collective-permute-start.144) | collective-permute-done | bytes 557088 | tf_op jit(solution)/shard_map/ppermute | solution.py:49
  392.4 2.9 collective-permute-done.136.refs_3_
  397.8 2.3 reshape.200
  402.8 2.2 collective-permute-done.135.refs_2_
  411.2 7.8 %place_slices.1 = (f32[2,512,512]{2,1,0:T(8,128)}, f32[2,9,128,512]{3,2,1,0:T(8,128)}, f32[2,128,2048]{2,1,0:T(8,128)}) custom-call(s32[4]{0:T(128)S(1)} %pad_add_fusion.me_ref, f32[1088,128]{1,0:T(8,128)} %copy-done.22, f32[1088,128]{1,0:T(8,128)} %collective-permute-done.134.refs_1_, f32[1088,128]{1,0:T(8,128)} %collective-permute-done.135.refs_2_, ...), custom_call_target="tpu_custom_call" | custom-call | tf_op jit(solution)/shard_map/place_slices/pallas_call | solution.py:1127
  (479 shorter events, 219.9 us)
Async XLA Ops:
  13.2 21.3 %collective-permute-start.7 = (f32[192,1024]{1,0:T(8,128)}, f32[192,1024]{1,0:T(8,128)}, u32[]{:S(2)}, u32[]{:S(2)}) collective-permute-start(f32[192,1024]{1,0:T(8,128)} %get-tuple-element.489), channel_id=1, source_target_pairs={{0,4},{1,5},{2,6},{3,7},{4,0},{5,1},{6,2},{7,3},{8,12},{9,13},{10,... | collective-permute-start | bytes 2359304 | tf_op jit(solution)/shard_map/ppermute | solution.py:49
  46.2 9.5 %collective-permute-start.17 = (f32[384,256]{1,0:T(8,128)S(1)}, f32[384,256]{1,0:T(8,128)S(1)}, u32[]{:S(2)}, u32[]{:S(2)}) collective-permute-start(f32[384,256]{1,0:T(8,128)S(1)} %constant_dynamic-update-slice_fusion.h0), channel_id=1, source_target_pairs={{0,8},{1,9},{2,10},{3,11},{4,12},{5,13},{6,14},{7,15},{8,0},{9,1},... | collective-permute-start | bytes 1179656 | tf_op jit(solution)/shard_map/ppermute | solution.py:49
  47.7 8.4 %collective-permute-start.18 = (f32[384,256]{1,0:T(8,128)S(1)}, f32[384,256]{1,0:T(8,128)S(1)}, u32[]{:S(2)}, u32[]{:S(2)}) collective-permute-start(f32[384,256]{1,0:T(8,128)S(1)} %constant_dynamic-update-slice_fusion.h0), channel_id=1, source_target_pairs={{0,16},{1,17},{2,18},{3,19},{4,20},{5,21},{6,22},{7,23},{8,24},{9,... | collective-permute-start | bytes 1179656 | tf_op jit(solution)/shard_map/ppermute | solution.py:49
  62.6 9.8 %collective-permute-start.22 = (f32[384,256]{1,0:T(8,128)S(1)}, f32[384,256]{1,0:T(8,128)S(1)}, u32[]{:S(2)}, u32[]{:S(2)}) collective-permute-start(f32[384,256]{1,0:T(8,128)S(1)} %constant_dynamic-update-slice_fusion.h0), channel_id=1, source_target_pairs={{0,24},{1,25},{2,26},{3,27},{4,28},{5,29},{6,30},{7,31},{8,16},{9,... | collective-permute-start | bytes 1179656 | tf_op jit(solution)/shard_map/ppermute | solution.py:49
  81.1 20.7 %collective-permute-start.33 = (f32[192,1024]{1,0:T(8,128)S(1)}, f32[192,1024]{1,0:T(8,128)S(1)}, u32[]{:S(2)}, u32[]{:S(2)}) collective-permute-start(f32[192,1024]{1,0:T(8,128)S(1)} %get-tuple-element.463), channel_id=1, source_target_pairs={{0,4},{1,5},{2,6},{3,7},{4,0},{5,1},{6,2},{7,3},{8,12},{9,13},{10,... | collective-permute-start | bytes 2359304 | tf_op jit(solution)/shard_map/ppermute | solution.py:49
  114.2 8.7 %collective-permute-start.43 = (f32[384,256]{1,0:T(8,128)S(1)}, f32[384,256]{1,0:T(8,128)S(1)}, u32[]{:S(2)}, u32[]{:S(2)}) collective-permute-start(f32[384,256]{1,0:T(8,128)S(1)} %constant_dynamic-update-slice_fusion.2.h0), channel_id=1, source_target_pairs={{0,8},{1,9},{2,10},{3,11},{4,12},{5,13},{6,14},{7,15},{8,0},{9,1},... | collective-permute-start | bytes 1179656 | tf_op jit(solution)/shard_map/ppermute | solution.py:49
  114.9 8.7 %collective-permute-start.44 = (f32[384,256]{1,0:T(8,128)S(1)}, f32[384,256]{1,0:T(8,128)S(1)}, u32[]{:S(2)}, u32[]{:S(2)}) collective-permute-start(f32[384,256]{1,0:T(8,128)S(1)} %constant_dynamic-update-slice_fusion.2.h0), channel_id=1, source_target_pairs={{0,16},{1,17},{2,18},{3,19},{4,20},{5,21},{6,22},{7,23},{8,24},{9,... | collective-permute-start | bytes 1179656 | tf_op jit(solution)/shard_map/ppermute | solution.py:49
  130.3 10.6 %collective-permute-start.48 = (f32[384,256]{1,0:T(8,128)S(1)}, f32[384,256]{1,0:T(8,128)S(1)}, u32[]{:S(2)}, u32[]{:S(2)}) collective-permute-start(f32[384,256]{1,0:T(8,128)S(1)} %constant_dynamic-update-slice_fusion.2.h0), channel_id=1, source_target_pairs={{0,24},{1,25},{2,26},{3,27},{4,28},{5,29},{6,30},{7,31},{8,16},{9,... | collective-permute-start | bytes 1179656 | tf_op jit(solution)/shard_map/ppermute | solution.py:49
  131.7 9.8 %collective-permute-start.51 = (f32[3,32,128]{2,1,0:T(8,128)S(1)}, f32[3,32,128]{2,1,0:T(8,128)S(1)}, u32[]{:S(2)}, u32[]{:S(2)}) collective-permute-start(f32[3,32,128]{2,1,0:T(8,128)S(1)} %pad_maximum_fusion.19.refs_0_), channel_id=1, source_target_pairs={{0,3},{1,2},{2,1},{3,0},{4,7},{5,6},{6,5},{7,4},{8,11},{9,10},{10,... | collective-permute-start | bytes 147464 | tf_op jit(solution)/shard_map/ppermute | solution.py:49
  166.8 8.8 %collective-permute-start.64 = (f32[192,1024]{1,0:T(8,128)S(1)}, f32[192,1024]{1,0:T(8,128)S(1)}, u32[]{:S(2)}, u32[]{:S(2)}) collective-permute-start(f32[192,1024]{1,0:T(8,128)S(1)} %get-tuple-element.265), channel_id=1, source_target_pairs={{0,4},{1,5},{2,6},{3,7},{4,0},{5,1},{6,2},{7,3},{8,12},{9,13},{10,... | collective-permute-start | bytes 2359304 | tf_op jit(solution)/shard_map/ppermute | solution.py:49
  166.9 8.7 %collective-permute-start.63 = (f32[192,512]{1,0:T(8,128)S(1)}, f32[192,512]{1,0:T(8,128)S(1)}, u32[]{:S(2)}, u32[]{:S(2)}) collective-permute-start(f32[192,512]{1,0:T(8,128)S(1)} %copy-done.20), channel_id=1, source_target_pairs={{0,4},{1,5},{2,6},{3,7},{4,0},{5,1},{6,2},{7,3},{8,12},{9,13},{10,... | collective-permute-start | bytes 1179656 | tf_op jit(solution)/shard_map/ppermute | solution.py:49
  177.0 15.2 %collective-permute-start.69 = (f32[2,4,128,128]{3,2,1,0:T(8,128)S(1)}, f32[2,4,128,128]{3,2,1,0:T(8,128)S(1)}, u32[]{:S(2)}, u32[]{:S(2)}) collective-permute-start(f32[2,4,128,128]{3,2,1,0:T(8,128)S(1)} %get-tuple-element.272), channel_id=1, source_target_pairs={{0,8},{1,9},{2,10},{3,11},{4,12},{5,13},{6,14},{7,15},{8,0},{9,1},... | collective-permute-start | bytes 1572872 | tf_op jit(solution)/shard_map/ppermute | solution.py:49
  178.3 13.9 %collective-permute-start.70 = (f32[2,4,128,128]{3,2,1,0:T(8,128)S(1)}, f32[2,4,128,128]{3,2,1,0:T(8,128)S(1)}, u32[]{:S(2)}, u32[]{:S(2)}) collective-permute-start(f32[2,4,128,128]{3,2,1,0:T(8,128)S(1)} %get-tuple-element.273), channel_id=1, source_target_pairs={{0,16},{1,17},{2,18},{3,19},{4,20},{5,21},{6,22},{7,23},{8,24},{9,... | collective-permute-start | bytes 1572872 | tf_op jit(solution)/shard_map/ppermute | solution.py:49
  205.8 15.9 %collective-permute-start.82 = (f32[1,4,128,128]{3,2,1,0:T(8,128)S(1)}, f32[1,4,128,128]{3,2,1,0:T(8,128)S(1)}, u32[]{:S(2)}, u32[]{:S(2)}) collective-permute-start(f32[1,4,128,128]{3,2,1,0:T(8,128)S(1)} %get-tuple-element.302), channel_id=1, source_target_pairs={{0,16},{1,17},{2,18},{3,19},{4,20},{5,21},{6,22},{7,23},{8,24},{9,... | collective-permute-start | bytes 786440 | tf_op jit(solution)/shard_map/ppermute | solution.py:49
  207.1 14.7 %collective-permute-start.83 = (f32[1,4,128,128]{3,2,1,0:T(8,128)S(1)}, f32[1,4,128,128]{3,2,1,0:T(8,128)S(1)}, u32[]{:S(2)}, u32[]{:S(2)}) collective-permute-start(f32[1,4,128,128]{3,2,1,0:T(8,128)S(1)} %get-tuple-element.303), channel_id=1, source_target_pairs={{0,8},{1,9},{2,10},{3,11},{4,12},{5,13},{6,14},{7,15},{8,0},{9,1},... | collective-permute-start | bytes 786440 | tf_op jit(solution)/shard_map/ppermute | solution.py:49
  219.8 8.6 %collective-permute-start.87 = (f32[192,512]{1,0:T(8,128)S(1)}, f32[192,512]{1,0:T(8,128)S(1)}, u32[]{:S(2)}, u32[]{:S(2)}) collective-permute-start(f32[192,512]{1,0:T(8,128)S(1)} %get-tuple-element.307.keep_ref), channel_id=1, source_target_pairs={{0,4},{1,5},{2,6},{3,7},{4,0},{5,1},{6,2},{7,3},{8,12},{9,13},{10,... | collective-permute-start | bytes 1179656 | tf_op jit(solution)/shard_map/ppermute | solution.py:49
  220.3 15.3 %collective-permute-start.88 = (f32[2,9,64,128]{3,2,1,0:T(8,128)S(1)}, f32[2,9,64,128]{3,2,1,0:T(8,128)S(1)}, u32[]{:S(2)}, u32[]{:S(2)}) collective-permute-start(f32[2,9,64,128]{3,2,1,0:T(8,128)S(1)} %get-tuple-element.311), channel_id=1, source_target_pairs={{0,1},{1,0},{2,3},{3,2},{4,5},{5,4},{6,7},{7,6},{8,9},{9,8},{10,11... | collective-permute-start | bytes 1769480 | tf_op jit(solution)/shard_map/ppermute | solution.py:49
  247.4 23.5 %collective-permute-start.99 = (f32[192,1024]{1,0:T(8,128)S(1)}, f32[192,1024]{1,0:T(8,128)S(1)}, u32[]{:S(2)}, u32[]{:S(2)}) collective-permute-start(f32[192,1024]{1,0:T(8,128)S(1)} %get-tuple-element.329), channel_id=1, source_target_pairs={{0,4},{1,5},{2,6},{3,7},{4,0},{5,1},{6,2},{7,3},{8,12},{9,13},{10,... | collective-permute-start | bytes 2359304 | tf_op jit(solution)/shard_map/ppermute | solution.py:49
  247.5 14.3 %collective-permute-start.93 = (f32[2,4,128,128]{3,2,1,0:T(8,128)S(1)}, f32[2,4,128,128]{3,2,1,0:T(8,128)S(1)}, u32[]{:S(2)}, u32[]{:S(2)}) collective-permute-start(f32[2,4,128,128]{3,2,1,0:T(8,128)S(1)} %get-tuple-element.324), channel_id=1, source_target_pairs={{0,8},{1,9},{2,10},{3,11},{4,12},{5,13},{6,14},{7,15},{8,0},{9,1},... | collective-permute-start | bytes 1572872 | tf_op jit(solution)/shard_map/ppermute | solution.py:49
  248.7 14.0 %collective-permute-start.94 = (f32[2,4,128,128]{3,2,1,0:T(8,128)S(1)}, f32[2,4,128,128]{3,2,1,0:T(8,128)S(1)}, u32[]{:S(2)}, u32[]{:S(2)}) collective-permute-start(f32[2,4,128,128]{3,2,1,0:T(8,128)S(1)} %get-tuple-element.325), channel_id=1, source_target_pairs={{0,16},{1,17},{2,18},{3,19},{4,20},{5,21},{6,22},{7,23},{8,24},{9,... | collective-permute-start | bytes 1572872 | tf_op jit(solution)/shard_map/ppermute | solution.py:49
  249.7 21.2 %collective-permute-start.98 = (f32[192,512]{1,0:T(8,128)S(1)}, f32[192,512]{1,0:T(8,128)S(1)}, u32[]{:S(2)}, u32[]{:S(2)}) collective-permute-start(f32[192,512]{1,0:T(8,128)S(1)} %copy-done.12), channel_id=1, source_target_pairs={{0,4},{1,5},{2,6},{3,7},{4,0},{5,1},{6,2},{7,3},{8,12},{9,13},{10,... | collective-permute-start | bytes 1179656 | tf_op jit(solution)/shard_map/ppermute | solution.py:49
  251.5 23.0 %collective-permute-start.101 = (f32[1,9,64,128]{3,2,1,0:T(8,128)S(1)}, f32[1,9,64,128]{3,2,1,0:T(8,128)S(1)}, u32[]{:S(2)}, u32[]{:S(2)}) collective-permute-start(f32[1,9,64,128]{3,2,1,0:T(8,128)S(1)} %slice_add_fusion.1), channel_id=1, source_target_pairs={{0,2},{1,3},{2,0},{3,1},{4,6},{5,7},{6,4},{7,5},{8,10},{9,11},{10,... | collective-permute-start | bytes 884744 | tf_op jit(solution)/shard_map/ppermute | solution.py:49
  272.2 15.2 %collective-permute-start.106 = (f32[2,4,128,128]{3,2,1,0:T(8,128)S(1)}, f32[2,4,128,128]{3,2,1,0:T(8,128)S(1)}, u32[]{:S(2)}, u32[]{:S(2)}) collective-permute-start(f32[2,4,128,128]{3,2,1,0:T(8,128)S(1)} %get-tuple-element.343), channel_id=1, source_target_pairs={{0,8},{1,9},{2,10},{3,11},{4,12},{5,13},{6,14},{7,15},{8,0},{9,1},... | collective-permute-start | bytes 1572872 | tf_op jit(solution)/shard_map/ppermute | solution.py:49
  273.2 14.3 %collective-permute-start.107 = (f32[2,4,128,128]{3,2,1,0:T(8,128)S(1)}, f32[2,4,128,128]{3,2,1,0:T(8,128)S(1)}, u32[]{:S(2)}, u32[]{:S(2)}) collective-permute-start(f32[2,4,128,128]{3,2,1,0:T(8,128)S(1)} %get-tuple-element.344), channel_id=1, source_target_pairs={{0,16},{1,17},{2,18},{3,19},{4,20},{5,21},{6,22},{7,23},{8,24},{9,... | collective-permute-start | bytes 1572872 | tf_op jit(solution)/shard_map/ppermute | solution.py:49
  291.1 8.5 %collective-permute-start.111 = (f32[1,256,128]{2,1,0:T(8,128)S(1)}, f32[1,256,128]{2,1,0:T(8,128)S(1)}, u32[]{:S(2)}, u32[]{:S(2)}) collective-permute-start(f32[1,256,128]{2,1,0:T(8,128)S(1)} %fusion.16), channel_id=1, source_target_pairs={{0,2},{1,3},{2,0},{3,1},{4,6},{5,7},{6,4},{7,5},{8,10},{9,11},{10,... | collective-permute-start | bytes 393224 | tf_op jit(solution)/shard_map/ppermute | solution.py:49
  308.4 14.8 %collective-permute-start.124 = (f32[2,9,64,128]{3,2,1,0:T(8,128)S(1)}, f32[2,9,64,128]{3,2,1,0:T(8,128)S(1)}, u32[]{:S(2)}, u32[]{:S(2)}) collective-permute-start(f32[2,9,64,128]{3,2,1,0:T(8,128)S(1)} %get-tuple-element.383), channel_id=1, source_target_pairs={{0,1},{1,0},{2,3},{3,2},{4,5},{5,4},{6,7},{7,6},{8,9},{9,8},{10,11... | collective-permute-start | bytes 1769480 | tf_op jit(solution)/shard_map/ppermute | solution.py:49
  309.6 11.4 %collective-permute-start.122 = (f32[1,4,128,128]{3,2,1,0:T(8,128)S(1)}, f32[1,4,128,128]{3,2,1,0:T(8,128)S(1)}, u32[]{:S(2)}, u32[]{:S(2)}) collective-permute-start(f32[1,4,128,128]{3,2,1,0:T(8,128)S(1)} %get-tuple-element.381), channel_id=1, source_target_pairs={{0,16},{1,17},{2,18},{3,19},{4,20},{5,21},{6,22},{7,23},{8,24},{9,... | collective-permute-start | bytes 786440 | tf_op jit(solution)/shard_map/ppermute | solution.py:49
  310.5 10.5 %collective-permute-start.123 = (f32[1,4,128,128]{3,2,1,0:T(8,128)S(1)}, f32[1,4,128,128]{3,2,1,0:T(8,128)S(1)}, u32[]{:S(2)}, u32[]{:S(2)}) collective-permute-start(f32[1,4,128,128]{3,2,1,0:T(8,128)S(1)} %get-tuple-element.382), channel_id=1, source_target_pairs={{0,8},{1,9},{2,10},{3,11},{4,12},{5,13},{6,14},{7,15},{8,0},{9,1},... | collective-permute-start | bytes 786440 | tf_op jit(solution)/shard_map/ppermute | solution.py:49
  320.2 17.6 %collective-permute-start.120 = (f32[2,4,128,128]{3,2,1,0:T(8,128)S(1)}, f32[2,4,128,128]{3,2,1,0:T(8,128)S(1)}, u32[]{:S(2)}, u32[]{:S(2)}) collective-permute-start(f32[2,4,128,128]{3,2,1,0:T(8,128)S(1)} %get-tuple-element.376), channel_id=1, source_target_pairs={{0,8},{1,9},{2,10},{3,11},{4,12},{5,13},{6,14},{7,15},{8,0},{9,1},... | collective-permute-start | bytes 1572872 | tf_op jit(solution)/shard_map/ppermute | solution.py:49
  323.2 14.6 %collective-permute-start.133 = (f32[1,9,64,128]{3,2,1,0:T(8,128)S(1)}, f32[1,9,64,128]{3,2,1,0:T(8,128)S(1)}, u32[]{:S(2)}, u32[]{:S(2)}) collective-permute-start(f32[1,9,64,128]{3,2,1,0:T(8,128)S(1)} %slice_add_fusion), channel_id=1, source_target_pairs={{0,2},{1,3},{2,0},{3,1},{4,6},{5,7},{6,4},{7,5},{8,10},{9,11},{10,... | collective-permute-start | bytes 884744 | tf_op jit(solution)/shard_map/ppermute | solution.py:49
  324.6 14.2 %collective-permute-start.129 = (f32[2,4,128,128]{3,2,1,0:T(8,128)S(1)}, f32[2,4,128,128]{3,2,1,0:T(8,128)S(1)}, u32[]{:S(2)}, u32[]{:S(2)}) collective-permute-start(f32[2,4,128,128]{3,2,1,0:T(8,128)S(1)} %get-tuple-element.399), channel_id=1, source_target_pairs={{0,16},{1,17},{2,18},{3,19},{4,20},{5,21},{6,22},{7,23},{8,24},{9,... | collective-permute-start | bytes 1572872 | tf_op jit(solution)/shard_map/ppermute | solution.py:49
  337.9 9.2 %collective-permute-start.121 = (f32[1,4,128,128]{3,2,1,0:T(8,128)S(1)}, f32[1,4,128,128]{3,2,1,0:T(8,128)S(1)}, u32[]{:S(2)}, u32[]{:S(2)}) collective-permute-start(f32[1,4,128,128]{3,2,1,0:T(8,128)S(1)} %get-tuple-element.482), channel_id=1, source_target_pairs={{0,16},{1,17},{2,18},{3,19},{4,20},{5,21},{6,22},{7,23},{8,24},{9,... | collective-permute-start | bytes 786440 | tf_op jit(solution)/shard_map/ppermute | solution.py:49
  338.9 9.3 %collective-permute-start.130 = (f32[1,4,128,128]{3,2,1,0:T(8,128)S(1)}, f32[1,4,128,128]{3,2,1,0:T(8,128)S(1)}, u32[]{:S(2)}, u32[]{:S(2)}) collective-permute-start(f32[1,4,128,128]{3,2,1,0:T(8,128)S(1)} %get-tuple-element.484), channel_id=1, source_target_pairs={{0,8},{1,9},{2,10},{3,11},{4,12},{5,13},{6,14},{7,15},{8,0},{9,1},... | collective-permute-start | bytes 786440 | tf_op jit(solution)/shard_map/ppermute | solution.py:49
  340.2 11.6 %collective-permute-start.125 = (f32[1,4,128,128]{3,2,1,0:T(8,128)S(1)}, f32[1,4,128,128]{3,2,1,0:T(8,128)S(1)}, u32[]{:S(2)}, u32[]{:S(2)}) collective-permute-start(f32[1,4,128,128]{3,2,1,0:T(8,128)S(1)} %get-tuple-element.396), channel_id=1, source_target_pairs={{0,16},{1,17},{2,18},{3,19},{4,20},{5,21},{6,22},{7,23},{8,24},{9,... | collective-permute-start | bytes 786440 | tf_op jit(solution)/shard_map/ppermute | solution.py:49
  341.5 11.1 %collective-permute-start.126 = (f32[1,4,128,128]{3,2,1,0:T(8,128)S(1)}, f32[1,4,128,128]{3,2,1,0:T(8,128)S(1)}, u32[]{:S(2)}, u32[]{:S(2)}) collective-permute-start(f32[1,4,128,128]{3,2,1,0:T(8,128)S(1)} %get-tuple-element.397), channel_id=1, source_target_pairs={{0,8},{1,9},{2,10},{3,11},{4,12},{5,13},{6,14},{7,15},{8,0},{9,1},... | collective-permute-start | bytes 786440 | tf_op jit(solution)/shard_map/ppermute | solution.py:49
  348.2 13.3 %collective-permute-start.131 = (f32[2,256,128]{2,1,0:T(8,128)S(1)}, f32[2,256,128]{2,1,0:T(8,128)S(1)}, u32[]{:S(2)}, u32[]{:S(2)}) collective-permute-start(f32[2,256,128]{2,1,0:T(8,128)S(1)} %pad_maximum_fusion.11), channel_id=1, source_target_pairs={{0,1},{1,0},{2,3},{3,2},{4,5},{5,4},{6,7},{7,6},{8,9},{9,8},{10,11... | collective-permute-start | bytes 786440 | tf_op jit(solution)/shard_map/ppermute | solution.py:49
  352.6 12.4 %collective-permute-start.127 = (f32[2,256,128]{2,1,0:T(8,128)S(1)}, f32[2,256,128]{2,1,0:T(8,128)S(1)}, u32[]{:S(2)}, u32[]{:S(2)}) collective-permute-start(f32[2,256,128]{2,1,0:T(8,128)S(1)} %pad_maximum_fusion.10), channel_id=1, source_target_pairs={{0,1},{1,0},{2,3},{3,2},{4,5},{5,4},{6,7},{7,6},{8,9},{9,8},{10,11... | collective-permute-start | bytes 786440 | tf_op jit(solution)/shard_map/ppermute | solution.py:49
  358.0 18.5 %collective-permute-start.143 = (f32[1088,128]{1,0:T(8,128)S(1)}, f32[1088,128]{1,0:T(8,128)}, u32[]{:S(2)}, u32[]{:S(2)}) collective-permute-start(f32[1088,128]{1,0:T(8,128)S(1)} %pad_maximum_fusion.3.refs_8_), channel_id=1, source_target_pairs={{0,8},{1,9},{2,10},{3,11},{4,12},{5,13},{6,14},{7,15},{8,0},{9,1},... | collective-permute-start | bytes 1671176 | tf_op jit(solution)/shard_map/ppermute | solution.py:49
  359.2 33.1 %collective-permute-start.144 = (f32[1088,128]{1,0:T(8,128)S(1)}, f32[1088,128]{1,0:T(8,128)S(1)}, u32[]{:S(2)}, u32[]{:S(2)}) collective-permute-start(f32[1088,128]{1,0:T(8,128)S(1)} %pad_maximum_fusion.3.refs_8_), channel_id=1, source_target_pairs={{0,16},{1,17},{2,18},{3,19},{4,20},{5,21},{6,22},{7,23},{8,24},{9,... | collective-permute-start | bytes 1671176 | tf_op jit(solution)/shard_map/ppermute | solution.py:49
  360.4 31.9 %collective-permute-start.145 = (f32[1088,128]{1,0:T(8,128)S(1)}, f32[1088,128]{1,0:T(8,128)S(1)}, u32[]{:S(2)}, u32[]{:S(2)}) collective-permute-start(f32[1088,128]{1,0:T(8,128)S(1)} %pad_maximum_fusion.3.refs_8_), channel_id=1, source_target_pairs={{0,24},{1,25},{2,26},{3,27},{4,28},{5,29},{6,30},{7,31},{8,16},{9,... | collective-permute-start | bytes 1671176 | tf_op jit(solution)/shard_map/ppermute | solution.py:49
  361.6 11.7 %collective-permute-start.132 = (f32[1,256,128]{2,1,0:T(8,128)S(1)}, f32[1,256,128]{2,1,0:T(8,128)S(1)}, u32[]{:S(2)}, u32[]{:S(2)}) collective-permute-start(f32[1,256,128]{2,1,0:T(8,128)S(1)} %slice_add_fusion.21), channel_id=1, source_target_pairs={{0,2},{1,3},{2,0},{3,1},{4,6},{5,7},{6,4},{7,5},{8,10},{9,11},{10,... | collective-permute-start | bytes 393224 | tf_op jit(solution)/shard_map/ppermute | solution.py:49
  365.0 9.6 %collective-permute-start.128 = (f32[1,256,128]{2,1,0:T(8,128)S(1)}, f32[1,256,128]{2,1,0:T(8,128)S(1)}, u32[]{:S(2)}, u32[]{:S(2)}) collective-permute-start(f32[1,256,128]{2,1,0:T(8,128)S(1)} %slice_add_fusion.26), channel_id=1, source_target_pairs={{0,2},{1,3},{2,0},{3,1},{4,6},{5,7},{6,4},{7,5},{8,10},{9,11},{10,... | collective-permute-start | bytes 393224 | tf_op jit(solution)/shard_map/ppermute | solution.py:49
  374.8 20.6 %collective-permute-start.136 = (f32[1088,128]{1,0:T(8,128)S(1)}, f32[1088,128]{1,0:T(8,128)}, u32[]{:S(2)}, u32[]{:S(2)}) collective-permute-start(f32[1088,128]{1,0:T(8,128)S(1)} %pad_maximum_fusion.2.refs_0_), channel_id=1, source_target_pairs={{0,24},{1,25},{2,26},{3,27},{4,28},{5,29},{6,30},{7,31},{8,16},{9,... | collective-permute-start | bytes 1671176 | tf_op jit(solution)/shard_map/ppermute | solution.py:49
  376.3 29.2 %collective-permute-start.146 = (f32[1088,128]{1,0:T(8,128)S(1)}, f32[1088,128]{1,0:T(8,128)}, u32[]{:S(2)}, u32[]{:S(2)}) collective-permute-start(f32[1088,128]{1,0:T(8,128)S(1)} %pad_maximum_fusion.3.refs_8_), channel_id=1, source_target_pairs={{0,4},{1,5},{2,6},{3,7},{4,0},{5,1},{6,2},{7,3},{8,12},{9,13},{10,... | collective-permute-start | bytes 1671176 | tf_op jit(solution)/shard_map/ppermute | solution.py:49
  376.4 29.2 %collective-permute-start.137 = (f32[1088,128]{1,0:T(8,128)S(1)}, f32[1088,128]{1,0:T(8,128)}, u32[]{:S(2)}, u32[]{:S(2)}) collective-permute-start(f32[1088,128]{1,0:T(8,128)S(1)} %pad_maximum_fusion.2.refs_0_), channel_id=1, source_target_pairs={{0,4},{1,5},{2,6},{3,7},{4,0},{5,1},{6,2},{7,3},{8,12},{9,13},{10,... | collective-permute-start | bytes 1671176 | tf_op jit(solution)/shard_map/ppermute | solution.py:49
  392.2 12.8 %collective-permute-start.135 = (f32[1088,128]{1,0:T(8,128)S(1)}, f32[1088,128]{1,0:T(8,128)}, u32[]{:S(2)}, u32[]{:S(2)}) collective-permute-start(f32[1088,128]{1,0:T(8,128)S(1)} %pad_maximum_fusion.2.refs_0_), channel_id=1, source_target_pairs={{0,16},{1,17},{2,18},{3,19},{4,20},{5,21},{6,22},{7,23},{8,24},{9,... | collective-permute-start | bytes 1671176 | tf_op jit(solution)/shard_map/ppermute | solution.py:49
  392.2 12.8 %collective-permute-start.134 = (f32[1088,128]{1,0:T(8,128)S(1)}, f32[1088,128]{1,0:T(8,128)}, u32[]{:S(2)}, u32[]{:S(2)}) collective-permute-start(f32[1088,128]{1,0:T(8,128)S(1)} %pad_maximum_fusion.2.refs_0_), channel_id=1, source_target_pairs={{0,8},{1,9},{2,10},{3,11},{4,12},{5,13},{6,14},{7,15},{8,0},{9,1},... | collective-permute-start | bytes 1671176 | tf_op jit(solution)/shard_map/ppermute | solution.py:49
  395.4 10.7 %collective-permute-start.147 = (f32[1088,128]{1,0:T(8,128)}, f32[1088,128]{1,0:T(8,128)}, u32[]{:S(2)}, u32[]{:S(2)}) collective-permute-start(f32[1088,128]{1,0:T(8,128)} %collective-permute-done.143.refs_9_), channel_id=1, source_target_pairs={{0,4},{1,5},{2,6},{3,7},{4,0},{5,1},{6,2},{7,3},{8,12},{9,13},{10,... | collective-permute-start | bytes 1671176 | tf_op jit(solution)/shard_map/ppermute | solution.py:49
  (144 other events, 921.0 us)

commit v5 on v4

--- a/solution.py
+++ b/solution.py
@@ -169,8 +169,12 @@
                 self.parked.append((flow, got))
         return array
 
-    def resume(self, after):
-        for flow, got in self.parked:
+    def resume(self, names, after):
+        parked, self.parked = self.parked, []
+        for flow, got in parked:
+            if self.names[flow] not in names:
+                self.parked.append((flow, got))
+                continue
             *got, _ = lax.optimization_barrier((*got, after))
             self.advance(flow, got)
 
@@ -977,11 +981,14 @@
     deep = half // nz
     tile_rows = rows - IMG_ROWS
 
-    def body(me_ref, h0, h1, h2, h3, n0, n1, n2, n3, far_ref, keep_ref, send_ref, image, tile, left, patch, total):
+    def body(me_ref, h0, h1, h2, h3, h4, n0, n1, n2, n3, far_ref, keep_ref, send_ref, image, tile, left, patch, total):
         image[...] = jnp.zeros_like(image)
         tile[...] = jnp.zeros_like(tile)
-        for m, (h_ref, n_ref) in enumerate(((h0, n0), (h1, n1), (h2, n2), (h3, n3))):
-            left[m * both : (m + 1) * both, :] = h_ref[...].astype(BF)
+        for m, ref in enumerate((h0, h1, h2)):
+            left[m * both : (m + 1) * both, :] = ref[...].astype(BF)
+        left[3 * both : 3 * both + rows, :] = h3[...].astype(BF)
+        left[3 * both + rows :, :] = h4[...].astype(BF)
+        for m, n_ref in enumerate((n0, n1, n2, n3)):
             for core in range(2):
                 value = n_ref[...] if core == 0 else far_ref[m]
                 at = m * both + core * rows
@@ -1003,7 +1010,7 @@
     vmem = pl.BlockSpec(memory_space=pltpu.VMEM)
     return pl.pallas_call(
         body,
-        in_specs=[smem()] + [vmem] * 9,
+        in_specs=[smem()] + [vmem] * 10,
         out_specs=[vmem] * 2,
         out_shape=[sds((nz // 2, 9, deep, width))] * 2,
         scratch_shapes=[
@@ -1023,12 +1030,14 @@
     def __init__(self, grid, me):
         self.grid, self.me, self.marks = grid, me, None
 
-    def over_z(self, keep, send):
+    def over_z(self, keep, send, gate=None):
         step = 1
         while True:
             (got,) = yield "deep", [(send, dict(dz=step))]
             step *= 2
             if step == self.grid.z:
+                if gate:
+                    got, _ = lax.optimization_barrier((got, gate[2]))
                 return keep[0] + got[0]
             half = keep.shape[0] // 2
             keep, send = keep[:half] + got[:half], keep[half:] + got[half:]
@@ -1040,12 +1049,14 @@
         got = yield "plane", [(flat, dict(dx=1)), (flat, dict(dy=1)), (flat, dict(dy=1, dx=1))]
         out.extend([flat] + list(lax.optimization_barrier(tuple(got))))
 
-    def by_halves(self, kernel, own, peer, keep, send, out, after=None):
+    def by_halves(self, kernel, own, peer, keep, send, out, after=None, gate=None):
         (got,) = yield "core", [(send, dict(dc=1))]
         if after:
             got, _ = lax.optimization_barrier((got, after[0]))
         x_keep, x_send, y_keep, y_send = kernel(self.me, own, peer, keep, got, self.grid.z)
+        self.begun = x_keep
         got = yield "plane", [(x_send, dict(dx=1)), (y_send, dict(dy=1))]
+        got = lax.optimization_barrier(tuple(got))
         if after is not None:
             after.append(got[0])
         x_last, y_last = x_keep[1:] + got[0][1:], y_keep[1:] + got[1][1:]
@@ -1058,7 +1069,7 @@
         def side(at):
             return jnp.concatenate([x_keep[0, at] + got[0][0, at], y_keep[0, at] + got[1][0, at]], axis=1)
 
-        piece = yield from self.over_z(side(slice(0, half)), side(slice(half, 2 * half)))
+        piece = yield from self.over_z(side(slice(0, half)), side(slice(half, 2 * half)), gate)
         out.append(piece)
 
     def by_rows(self, hidden, grad, out, after=None):
@@ -1068,15 +1079,16 @@
         keep, send = weight_spatial(self.me, hidden, near, far, self.grid.z)
         if after is not None:
             after.append(keep)
-        piece = yield from self.over_z(keep, send)
+        piece = yield from self.over_z(keep, send, after)
         out.append(piece)
 
     def hidden(self, keep, send, out):
         (got,) = yield "core", [(send, dict(dc=1))]
         value = jnp.concatenate([keep, got], axis=0)
         got = yield "plane", [(value, dict(dx=1)), (value, dict(dy=1))]
-        (last,) = yield "tight", [(value, dict(dy=1, dx=1))]
-        out.extend([value, got[0], got[1], last])
+        rows = keep.shape[0]
+        last = yield "tight", [(got[0][:rows], dict(dy=1)), (got[1][rows:], dict(dx=1))]
+        out.extend([value, got[0], got[1], last[0], last[1]])
 
 
 def place_slices(me, gathered, shapes):
@@ -1282,7 +1294,7 @@
         both1[b] = result[0]
         gr = result[1]
         reduce_flow = collect.by_halves(
-            weight_reduce, *lows[b], gr, gr, pieces[b][1], after if b == 0 else None
+            weight_reduce, *lows[b], gr, gr, pieces[b][1], after if b == 0 else None, after if b else None
         )
         if b > 0:
             bulk.add(("r", b), reduce_flow)
@@ -1293,14 +1305,16 @@
 
     grad_in[0] = bulk.last(grad_in[0], [("s", 0)])
     bulk.add(("r", 0), reduce_flow)
-    bulk.run([("r", 0)], ("plane",), 1)
-    bulk.resume(after[1])
     later = [(n, b) for b in range(1, BLOCKS) for n in "ers"]
     every = later + [("e", 0)]
-    bulk.hold(every, after[1])
+    bulk.hold(later, collect.begun)
+    bulk.resume(later, collect.begun)
+    bulk.run([("r", 0)], ("plane",), 1)
+    bulk.resume([("e", 0)], after[1])
+    bulk.hold([("e", 0)], after[1])
+    bulk.run([("r", 0)], ("plane",))
     bulk.run([("s", 0)])
     bulk.run(every, ("deep",))
-    bulk.run([("r", 0)], ("plane",))
     views = []
     for value in (*out, *grad_in):
         value, _ = lax.optimization_barrier((value, after[2]))

time: 421 us -> 413 us (0.981)
  waiting for transfers between devices: 157 us -> 143 us
  starting transfers between devices: 154 us -> 161 us
    ppermute x150 -> x152, waiting for transfers between devices: 157 us -> 143 us  [swap(): return lax.ppermute(value, AXES, pairs)]
    ppermute x150 -> x152, starting transfers between devices: 154 us -> 161 us  [swap(): return lax.ppermute(value, AXES, pairs)]
  transfers between devices with their start and end apart: 150 -> 152, of which waited for: 92 -> 90; matrix products, arithmetic and copies ran while one was open for 3% -> 3% of each run, Pallas kernels for 11% -> 12%
where the time goes in v5:
time: 413 us; the launch traced here: 412 us
  starting transfers between devices  161 us (39%)
  waiting for transfers between devices  143 us (35%)
  Pallas kernels  79.2 us (19%)
  local copies, waits for them, and re-layouts  15.4 us (4%)
  other arithmetic  11.2 us (3%)
    ppermute x152, starting transfers between devices, swap(): return lax.ppermute(value, AXES, pairs)  161 us
    ppermute x152, waiting for transfers between devices, swap(): return lax.ppermute(value, AXES, pairs)  143 us
    pallas_call x2, Pallas kernels, back_spatial(): call(body, 3, [smem(), full((rows, mid)), full((rows, mid)), full((8, mid...  10.5 us
    pallas_call x2, Pallas kernels, back_expand(): call(body, d_in // CH, [smem(), cols(rows), cols(rows), full((8, d_in)),...  9.39 us
    pallas_call x2, Pallas kernels, spatial_stage(): call(body, 3, [full((rows, mid)), full(table.shape), full((rows, 1)), pl....  9.25 us
    pallas_call x2, Pallas kernels, expand_stage(): call(body, d_in // CH, [full((rows, mid)), full(table.shape), full((rows,...  8.72 us
  transfers between devices with their start and end apart: 152, of which 90 were waited for; matrix products, arithmetic and copies ran while one was open for 3% of the time, Pallas kernels for 12%

profile of v5, /device:TPU:0, one launch (start us, length us, event | category | flops | bytes accessed | tf_op | source)
XLA Modules:
  0.0 412.0 jit_solution(14902221806494887943)
XLA Ops:
  8.0 3.3 reduce_first.1
  13.4 4.0 collective-permute-start.3
  21.6 3.7 collective-permute-start.6
  27.1 2.7 collective-permute-done.5.refs_2_
  29.8 4.6 %spatial_stage.2 = (f32[8,512]{1,0:T(8,128)S(1)}, f32[192,256]{1,0:T(8,128)S(1)}, f32[192,256]{1,0:T(8,128)S(1)}, f32[192,512]{1,0:T(8,128)S(1)}, f32[3,8,128]{2,1,0:T(8,128)S(1)}) custom-call(f32[192,512]{1,0:T(8,128)S(1)} %get-tuple-element.232.red_ref, f32[8,512]{1,0:T(8,128)S(1)} %pad_maximum_fusion.21.table_ref, f32[192,1]{1,0:T(8,128)S(1)} %copy.23.mask_ref, ...), custom_call_target="tpu_custom_call" | custom-call | tf_op jit(solution)/shard_map/spatial_stage/pallas_call | solution.py:478
  44.0 2.3 collective-permute-start.13
  49.3 4.4 %expand_stage.2 = (f32[8,512]{1,0:T(8,128)S(1)}, f32[192,512]{1,0:T(8,128)S(1)}, f32[192,2048]{1,0:T(8,128)}, f32[3,32,128]{2,1,0:T(8,128)S(1)}) custom-call(f32[192,512]{1,0:T(8,128)S(1)} %get-tuple-element.234.spa_ref, f32[8,512]{1,0:T(8,128)S(1)} %pad_maximum_fusion.21.table_ref, f32[192,1]{1,0:T(8,128)S(1)} %copy.23.mask_ref, ...), custom_call_target="tpu_custom_call" | custom-call | tf_op jit(solution)/shard_map/expand_stage/pallas_call | solution.py:534
  64.4 2.6 collective-permute-start.24
  69.9 2.9 collective-permute-done.22.h3
  75.0 5.3 %join_stage.1 = (f32[8,2048]{1,0:T(8,128)S(1)}, f32[192,2048]{1,0:T(8,128)}, f32[192,2048]{1,0:T(8,128)}, f32[192,512]{1,0:T(8,128)S(1)}, f32[3,8,128]{2,1,0:T(8,128)S(1)}) custom-call(f32[192,2048]{1,0:T(8,128)} %get-tuple-element.240.exp_ref, f32[4,2048]{1,0:T(4,128)S(1)} %pad_maximum_fusion.20.table_ref.outer_ref, ...), custom_call_target="tpu_custom_call" | custom-call | tf_op jit(solution)/shard_map/join_stage/pallas_call | solution.py:596
  93.2 2.9 collective-permute-start.31
  97.9 4.6 %spatial_stage.3 = (f32[8,512]{1,0:T(8,128)S(1)}, f32[192,256]{1,0:T(8,128)S(1)}, f32[192,256]{1,0:T(8,128)S(1)}, f32[192,512]{1,0:T(8,128)S(1)}, f32[3,8,128]{2,1,0:T(8,128)S(1)}) custom-call(f32[192,512]{1,0:T(8,128)S(1)} %get-tuple-element.251.red_ref, f32[8,512]{1,0:T(8,128)S(1)} %pad_maximum_fusion.21.table_ref, f32[192,1]{1,0:T(8,128)S(1)} %copy.23.mask_ref, ...), custom_call_target="tpu_custom_call" | custom-call | tf_op jit(solution)/shard_map/spatial_stage/pallas_call | solution.py:478
  110.1 2.3 collective-permute-start.42
  117.2 4.4 %expand_stage.3 = (f32[8,512]{1,0:T(8,128)S(1)}, f32[192,512]{1,0:T(8,128)S(1)}, f32[192,2048]{1,0:T(8,128)}, f32[3,32,128]{2,1,0:T(8,128)S(1)}) custom-call(f32[192,512]{1,0:T(8,128)S(1)} %get-tuple-element.253.spa_ref, f32[8,512]{1,0:T(8,128)S(1)} %pad_maximum_fusion.21.table_ref, f32[192,1]{1,0:T(8,128)S(1)} %copy.23.mask_ref, ...), custom_call_target="tpu_custom_call" | custom-call | tf_op jit(solution)/shard_map/expand_stage/pallas_call | solution.py:534
  132.4 2.2 collective-permute-start.53
  139.6 4.7 %turn_stage.1 = (f32[8,2048]{1,0:T(8,128)S(1)}, f32[98,2048]{1,0:T(8,128)}, f32[72,2048]{1,0:T(8,128)}, f32[192,2048]{1,0:T(8,128)}, f32[2,32,128]{2,1,0:T(8,128)S(1)}) custom-call(f32[192,2048]{1,0:T(8,128)} %get-tuple-element.260.exp_ref, f32[4,2048]{1,0:T(4,128)S(1)} %pad_maximum_fusion.20.table_ref.outer_ref, f32[192,2048]{1,0:T(8,128)} %get-tuple-element.261.act_ref, ...), custom_call_target="tpu_custom_call" | custom-call | tf_op jit(solution)/shard_map/turn_stage/pallas_call | solution.py:652
  145.5 2.2 collective-permute-start.57
  152.9 2.1 collective-permute-start.60
  160.1 4.8 %back_expand.2 = (f32[2,2048]{1,0:T(2,128)S(1)}, f32[192,1024]{1,0:T(8,128)S(1)}, f32[192,1024]{1,0:T(8,128)S(1)}, f32[192,512]{1,0:T(8,128)S(1)}, f32[2,8,128]{2,1,0:T(8,128)S(1)}) custom-call(s32[4]{0:T(128)S(1)} %pad_add_fusion.me_ref, f32[192,2048]{1,0:T(8,128)} %get-tuple-element.275.pre3_ref, f32[192,2048]{1,0:T(8,128)} %get-tuple-element.260.exp_ref, ...), custom_call_target="tpu_custom_call" | custom-call | tf_op jit(solution)/shard_map/back_expand/pallas_call | solution.py:736
  165.6 2.3 collective-permute-done.61
  167.8 2.0 collective-permute-start.64
  184.5 5.1 %back_spatial.2 = (f32[2,512]{1,0:T(2,128)S(1)}, f32[192,128]{1,0:T(8,128)S(1)}, f32[192,128]{1,0:T(8,128)S(1)}, f32[192,128]{1,0:T(8,128)S(1)}, f32[192,128]{1,...) custom-call(s32[4]{0:T(128)S(1)} %pad_add_fusion.me_ref, f32[192,512]{1,0:T(8,128)S(1)} %get-tuple-element.279.pre2_ref, ...), custom_call_target="tpu_custom_call" | custom-call | tf_op jit(solution)/shard_map/back_spatial/pallas_call | solution.py:803
  211.2 2.2 weight_spatial.2
  213.5 5.3 %back_reduce.1 = (f32[2,512]{1,0:T(2,128)S(1)}, f32[192,512]{1,0:T(8,128)S(1)}, f32[192,2048]{1,0:T(8,128)}, f32[2,32,128]{2,1,0:T(8,128)S(1)}) custom-call(f32[192,512]{1,0:T(8,128)S(1)} %get-tuple-element.288.pre1_ref, f32[192,512]{1,0:T(8,128)S(1)} %get-tuple-element.251.red_ref, f32[8,512]{1,0:T(8,128)S(1)} %get-tuple-element.280.mr1_ref, ...), custom_call_target="tpu_custom_call" | custom-call | tf_op jit(solution)/shard_map/back_reduce/pallas_call | solution.py:892
  228.7 5.9 %collective-permute-done.90 = f32[2,9,64,128]{3,2,1,0:T(8,128)S(1)} collective-permute-done((f32[2,9,64,128]{3,2,1,0:T(8,128)S(1)}, f32[2,9,64,128]{3,2,1,0:T(8,128)S(1)}, u32[]{:S(2)}, u32[]{:S(2)}) %collective-permute-start.90) | collective-permute-done | bytes 589856 | tf_op jit(solution)/shard_map/ppermute | solution.py:49
  241.7 4.6 %back_expand.3 = (f32[2,2048]{1,0:T(2,128)S(1)}, f32[192,1024]{1,0:T(8,128)S(1)}, f32[192,1024]{1,0:T(8,128)S(1)}, f32[192,512]{1,0:T(8,128)S(1)}, f32[2,8,128]{2,1,0:T(8,128)S(1)}) custom-call(s32[4]{0:T(128)S(1)} %pad_add_fusion.me_ref, f32[192,2048]{1,0:T(8,128)} %get-tuple-element.319.pre3_ref, f32[192,2048]{1,0:T(8,128)} %get-tuple-element.240.exp_ref, ...), custom_call_target="tpu_custom_call" | custom-call | tf_op jit(solution)/shard_map/back_expand/pallas_call | solution.py:736
  251.3 9.4 %collective-permute-done.95 = f32[2,4,128,128]{3,2,1,0:T(8,128)S(1)} collective-permute-done((f32[2,4,128,128]{3,2,1,0:T(8,128)S(1)}, f32[2,4,128,128]{3,2,1,0:T(8,128)S(1)}, u32[]{:S(2)}, u32[]{:S(2)}) %collective-permute-start.95) | collective-permute-done | bytes 524320 | tf_op jit(solution)/shard_map/ppermute | solution.py:49
  263.9 2.1 collective-permute-done.99
  279.9 5.4 %back_spatial.3 = (f32[2,512]{1,0:T(2,128)S(1)}, f32[192,128]{1,0:T(8,128)S(1)}, f32[192,128]{1,0:T(8,128)S(1)}, f32[192,128]{1,0:T(8,128)S(1)}, f32[192,128]{1,...) custom-call(s32[4]{0:T(128)S(1)} %pad_add_fusion.me_ref, f32[192,512]{1,0:T(8,128)S(1)} %get-tuple-element.341.pre2_ref, ...), custom_call_target="tpu_custom_call" | custom-call | tf_op jit(solution)/shard_map/back_spatial/pallas_call | solution.py:803
  290.1 2.1 collective-permute-start.113
  296.2 2.4 collective-permute-done.113
  304.6 2.2 weight_spatial.3
  310.7 4.6 %back_reduce_last.1 = (f32[2,512]{1,0:T(2,128)S(1)}, f32[192,512]{1,0:T(8,128)S(1)}, f32[98,2048]{1,0:T(8,128)}, f32[72,2048]{1,0:T(8,128)}) custom-call(f32[192,512]{1,0:T(8,128)S(1)} %get-tuple-element.361.pre1_ref, f32[192,512]{1,0:T(8,128)S(1)} %get-tuple-element.232.red_ref, f32[8,512]{1,0:T(8,128)S(1)} %get-tuple-element.342.mr1_ref, ...), custom_call_target="tpu_custom_call" | custom-call | tf_op jit(solution)/shard_map/back_reduce_last/pallas_call | solution.py:868
  317.0 2.1 weight_reduce.3
  324.6 9.1 %collective-permute-done.143 = f32[2,256,128]{2,1,0:T(8,128)S(1)} collective-permute-done((f32[2,256,128]{2,1,0:T(8,128)S(1)}, f32[2,256,128]{2,1,0:T(8,128)S(1)}, u32[]{:S(2)}, u32[]{:S(2)}) %collective-permute-start.143) | collective-permute-done | bytes 262176 | tf_op jit(solution)/shard_map/ppermute | solution.py:49
  337.5 3.5 collective-permute-done.128
  342.0 2.6 collective-permute-done.129
  344.7 2.2 collective-permute-start.130
  347.6 2.1 collective-permute-start.133
  354.5 2.1 collective-permute-start.131
  356.6 2.3 collective-permute-done.133
  358.9 2.3 collective-permute-start.134
  362.4 3.9 collective-permute-done.134
  366.3 2.0 collective-permute-start.138
  369.0 13.9 %collective-permute-done.146.refs_10_ = f32[1088,128]{1,0:T(8,128)S(1)} collective-permute-done((f32[1088,128]{1,0:T(8,128)S(1)}, f32[1088,128]{1,0:T(8,128)S(1)}, u32[]{:S(2)}, u32[]{:S(2)}) %collective-permute-start.146) | collective-permute-done | bytes 557088 | tf_op jit(solution)/shard_map/ppermute | solution.py:49
  383.9 5.9 %collective-permute-done.138.refs_3_ = f32[1088,128]{1,0:T(8,128)} collective-permute-done((f32[1088,128]{1,0:T(8,128)S(1)}, f32[1088,128]{1,0:T(8,128)}, u32[]{:S(2)}, u32[]{:S(2)}) %collective-permute-start.138) | collective-permute-done | bytes 557088 | tf_op jit(solution)/shard_map/ppermute | solution.py:49
  392.3 2.3 reshape.200
  404.1 7.8 %place_slices.1 = (f32[2,512,512]{2,1,0:T(8,128)}, f32[2,9,128,512]{3,2,1,0:T(8,128)}, f32[2,128,2048]{2,1,0:T(8,128)}) custom-call(s32[4]{0:T(128)S(1)} %pad_add_fusion.me_ref, f32[1088,128]{1,0:T(8,128)} %copy-done.26, f32[1088,128]{1,0:T(8,128)} %collective-permute-done.136.refs_1_, f32[1088,128]{1,0:T(8,128)} %collective-permute-done.137.refs_2_, ...), custom_call_target="tpu_custom_call" | custom-call | tf_op jit(solution)/shard_map/place_slices/pallas_call | solution.py:1139
  (491 shorter events, 224.7 us)
Async XLA Ops:
  13.3 21.3 %collective-permute-start.7 = (f32[192,1024]{1,0:T(8,128)}, f32[192,1024]{1,0:T(8,128)}, u32[]{:S(2)}, u32[]{:S(2)}) collective-permute-start(f32[192,1024]{1,0:T(8,128)} %get-tuple-element.515), channel_id=1, source_target_pairs={{0,4},{1,5},{2,6},{3,7},{4,0},{5,1},{6,2},{7,3},{8,12},{9,13},{10,... | collective-permute-start | bytes 2359304 | tf_op jit(solution)/shard_map/ppermute | solution.py:49
  41.8 7.5 %collective-permute-start.15 = (f32[3,8,128]{2,1,0:T(8,128)S(1)}, f32[3,8,128]{2,1,0:T(8,128)S(1)}, u32[]{:S(2)}, u32[]{:S(2)}) collective-permute-start(f32[3,8,128]{2,1,0:T(8,128)S(1)} %pad_maximum_fusion.27.refs_0_), channel_id=1, source_target_pairs={{0,3},{1,2},{2,1},{3,0},{4,7},{5,6},{6,5},{7,4},{8,11},{9,10},{10,... | collective-permute-start | bytes 36872 | tf_op jit(solution)/shard_map/ppermute | solution.py:49
  46.3 9.0 %collective-permute-start.17 = (f32[384,256]{1,0:T(8,128)S(1)}, f32[384,256]{1,0:T(8,128)S(1)}, u32[]{:S(2)}, u32[]{:S(2)}) collective-permute-start(f32[384,256]{1,0:T(8,128)S(1)} %constant_dynamic-update-slice_fusion.h0), channel_id=1, source_target_pairs={{0,8},{1,9},{2,10},{3,11},{4,12},{5,13},{6,14},{7,15},{8,0},{9,1},... | collective-permute-start | bytes 1179656 | tf_op jit(solution)/shard_map/ppermute | solution.py:49
  47.7 8.4 %collective-permute-start.18 = (f32[384,256]{1,0:T(8,128)S(1)}, f32[384,256]{1,0:T(8,128)S(1)}, u32[]{:S(2)}, u32[]{:S(2)}) collective-permute-start(f32[384,256]{1,0:T(8,128)S(1)} %constant_dynamic-update-slice_fusion.h0), channel_id=1, source_target_pairs={{0,16},{1,17},{2,18},{3,19},{4,20},{5,21},{6,22},{7,23},{8,24},{9,... | collective-permute-start | bytes 1179656 | tf_op jit(solution)/shard_map/ppermute | solution.py:49
  62.6 12.3 %collective-permute-start.26 = (f32[3,32,128]{2,1,0:T(8,128)S(1)}, f32[3,32,128]{2,1,0:T(8,128)S(1)}, u32[]{:S(2)}, u32[]{:S(2)}) collective-permute-start(f32[3,32,128]{2,1,0:T(8,128)S(1)} %pad_maximum_fusion.17.refs_0_), channel_id=1, source_target_pairs={{0,3},{1,2},{2,1},{3,0},{4,7},{5,6},{6,5},{7,4},{8,11},{9,10},{10,... | collective-permute-start | bytes 147464 | tf_op jit(solution)/shard_map/ppermute | solution.py:49
  64.1 10.8 %collective-permute-start.25 = (f32[3,32,128]{2,1,0:T(8,128)S(1)}, f32[3,32,128]{2,1,0:T(8,128)S(1)}, u32[]{:S(2)}, u32[]{:S(2)}) collective-permute-start(f32[3,32,128]{2,1,0:T(8,128)S(1)} %pad_maximum_fusion.17.refs_0_), channel_id=1, source_target_pairs={{0,2},{1,3},{2,0},{3,1},{4,6},{5,7},{6,4},{7,5},{8,10},{9,11},{10,... | collective-permute-start | bytes 147464 | tf_op jit(solution)/shard_map/ppermute | solution.py:49
  64.4 10.5 %collective-permute-start.24 = (f32[3,32,128]{2,1,0:T(8,128)S(1)}, f32[3,32,128]{2,1,0:T(8,128)S(1)}, u32[]{:S(2)}, u32[]{:S(2)}) collective-permute-start(f32[3,32,128]{2,1,0:T(8,128)S(1)} %pad_maximum_fusion.17.refs_0_), channel_id=1, source_target_pairs={{0,1},{1,0},{2,3},{3,2},{4,5},{5,4},{6,7},{7,6},{8,9},{9,8},{10,11... | collective-permute-start | bytes 147464 | tf_op jit(solution)/shard_map/ppermute | solution.py:49
  82.8 19.8 %collective-permute-start.34 = (f32[192,1024]{1,0:T(8,128)S(1)}, f32[192,1024]{1,0:T(8,128)S(1)}, u32[]{:S(2)}, u32[]{:S(2)}) collective-permute-start(f32[192,1024]{1,0:T(8,128)S(1)} %get-tuple-element.489), channel_id=1, source_target_pairs={{0,4},{1,5},{2,6},{3,7},{4,0},{5,1},{6,2},{7,3},{8,12},{9,13},{10,... | collective-permute-start | bytes 2359304 | tf_op jit(solution)/shard_map/ppermute | solution.py:49
  114.6 9.0 %collective-permute-start.44 = (f32[384,256]{1,0:T(8,128)S(1)}, f32[384,256]{1,0:T(8,128)S(1)}, u32[]{:S(2)}, u32[]{:S(2)}) collective-permute-start(f32[384,256]{1,0:T(8,128)S(1)} %constant_dynamic-update-slice_fusion.2.h0), channel_id=1, source_target_pairs={{0,8},{1,9},{2,10},{3,11},{4,12},{5,13},{6,14},{7,15},{8,0},{9,1},... | collective-permute-start | bytes 1179656 | tf_op jit(solution)/shard_map/ppermute | solution.py:49
  115.8 8.4 %collective-permute-start.45 = (f32[384,256]{1,0:T(8,128)S(1)}, f32[384,256]{1,0:T(8,128)S(1)}, u32[]{:S(2)}, u32[]{:S(2)}) collective-permute-start(f32[384,256]{1,0:T(8,128)S(1)} %constant_dynamic-update-slice_fusion.2.h0), channel_id=1, source_target_pairs={{0,16},{1,17},{2,18},{3,19},{4,20},{5,21},{6,22},{7,23},{8,24},{9,... | collective-permute-start | bytes 1179656 | tf_op jit(solution)/shard_map/ppermute | solution.py:49
  164.9 9.1 %collective-permute-start.66 = (f32[192,1024]{1,0:T(8,128)S(1)}, f32[192,1024]{1,0:T(8,128)S(1)}, u32[]{:S(2)}, u32[]{:S(2)}) collective-permute-start(f32[192,1024]{1,0:T(8,128)S(1)} %get-tuple-element.284), channel_id=1, source_target_pairs={{0,4},{1,5},{2,6},{3,7},{4,0},{5,1},{6,2},{7,3},{8,12},{9,13},{10,... | collective-permute-start | bytes 2359304 | tf_op jit(solution)/shard_map/ppermute | solution.py:49
  165.0 9.0 %collective-permute-start.65 = (f32[192,512]{1,0:T(8,128)S(1)}, f32[192,512]{1,0:T(8,128)S(1)}, u32[]{:S(2)}, u32[]{:S(2)}) collective-permute-start(f32[192,512]{1,0:T(8,128)S(1)} %copy-done.16), channel_id=1, source_target_pairs={{0,4},{1,5},{2,6},{3,7},{4,0},{5,1},{6,2},{7,3},{8,12},{9,13},{10,... | collective-permute-start | bytes 1179656 | tf_op jit(solution)/shard_map/ppermute | solution.py:49
  175.3 15.6 %collective-permute-start.71 = (f32[2,4,128,128]{3,2,1,0:T(8,128)S(1)}, f32[2,4,128,128]{3,2,1,0:T(8,128)S(1)}, u32[]{:S(2)}, u32[]{:S(2)}) collective-permute-start(f32[2,4,128,128]{3,2,1,0:T(8,128)S(1)} %get-tuple-element.291), channel_id=1, source_target_pairs={{0,8},{1,9},{2,10},{3,11},{4,12},{5,13},{6,14},{7,15},{8,0},{9,1},... | collective-permute-start | bytes 1572872 | tf_op jit(solution)/shard_map/ppermute | solution.py:49
  176.4 14.5 %collective-permute-start.72 = (f32[2,4,128,128]{3,2,1,0:T(8,128)S(1)}, f32[2,4,128,128]{3,2,1,0:T(8,128)S(1)}, u32[]{:S(2)}, u32[]{:S(2)}) collective-permute-start(f32[2,4,128,128]{3,2,1,0:T(8,128)S(1)} %get-tuple-element.292), channel_id=1, source_target_pairs={{0,16},{1,17},{2,18},{3,19},{4,20},{5,21},{6,22},{7,23},{8,24},{9,... | collective-permute-start | bytes 1572872 | tf_op jit(solution)/shard_map/ppermute | solution.py:49
  204.2 16.5 %collective-permute-start.84 = (f32[1,4,128,128]{3,2,1,0:T(8,128)S(1)}, f32[1,4,128,128]{3,2,1,0:T(8,128)S(1)}, u32[]{:S(2)}, u32[]{:S(2)}) collective-permute-start(f32[1,4,128,128]{3,2,1,0:T(8,128)S(1)} %get-tuple-element.322), channel_id=1, source_target_pairs={{0,16},{1,17},{2,18},{3,19},{4,20},{5,21},{6,22},{7,23},{8,24},{9,... | collective-permute-start | bytes 786440 | tf_op jit(solution)/shard_map/ppermute | solution.py:49
  205.9 14.8 %collective-permute-start.85 = (f32[1,4,128,128]{3,2,1,0:T(8,128)S(1)}, f32[1,4,128,128]{3,2,1,0:T(8,128)S(1)}, u32[]{:S(2)}, u32[]{:S(2)}) collective-permute-start(f32[1,4,128,128]{3,2,1,0:T(8,128)S(1)} %get-tuple-element.323), channel_id=1, source_target_pairs={{0,8},{1,9},{2,10},{3,11},{4,12},{5,13},{6,14},{7,15},{8,0},{9,1},... | collective-permute-start | bytes 786440 | tf_op jit(solution)/shard_map/ppermute | solution.py:49
  218.8 8.4 %collective-permute-start.89 = (f32[192,512]{1,0:T(8,128)S(1)}, f32[192,512]{1,0:T(8,128)S(1)}, u32[]{:S(2)}, u32[]{:S(2)}) collective-permute-start(f32[192,512]{1,0:T(8,128)S(1)} %get-tuple-element.327.keep_ref), channel_id=1, source_target_pairs={{0,4},{1,5},{2,6},{3,7},{4,0},{5,1},{6,2},{7,3},{8,12},{9,13},{10,... | collective-permute-start | bytes 1179656 | tf_op jit(solution)/shard_map/ppermute | solution.py:49
  219.3 15.3 %collective-permute-start.90 = (f32[2,9,64,128]{3,2,1,0:T(8,128)S(1)}, f32[2,9,64,128]{3,2,1,0:T(8,128)S(1)}, u32[]{:S(2)}, u32[]{:S(2)}) collective-permute-start(f32[2,9,64,128]{3,2,1,0:T(8,128)S(1)} %get-tuple-element.331), channel_id=1, source_target_pairs={{0,1},{1,0},{2,3},{3,2},{4,5},{5,4},{6,7},{7,6},{8,9},{9,8},{10,11... | collective-permute-start | bytes 1769480 | tf_op jit(solution)/shard_map/ppermute | solution.py:49
  246.3 23.4 %collective-permute-start.101 = (f32[192,1024]{1,0:T(8,128)S(1)}, f32[192,1024]{1,0:T(8,128)S(1)}, u32[]{:S(2)}, u32[]{:S(2)}) collective-permute-start(f32[192,1024]{1,0:T(8,128)S(1)} %get-tuple-element.349), channel_id=1, source_target_pairs={{0,4},{1,5},{2,6},{3,7},{4,0},{5,1},{6,2},{7,3},{8,12},{9,13},{10,... | collective-permute-start | bytes 2359304 | tf_op jit(solution)/shard_map/ppermute | solution.py:49
  246.4 14.3 %collective-permute-start.95 = (f32[2,4,128,128]{3,2,1,0:T(8,128)S(1)}, f32[2,4,128,128]{3,2,1,0:T(8,128)S(1)}, u32[]{:S(2)}, u32[]{:S(2)}) collective-permute-start(f32[2,4,128,128]{3,2,1,0:T(8,128)S(1)} %get-tuple-element.344), channel_id=1, source_target_pairs={{0,8},{1,9},{2,10},{3,11},{4,12},{5,13},{6,14},{7,15},{8,0},{9,1},... | collective-permute-start | bytes 1572872 | tf_op jit(solution)/shard_map/ppermute | solution.py:49
  247.5 14.0 %collective-permute-start.96 = (f32[2,4,128,128]{3,2,1,0:T(8,128)S(1)}, f32[2,4,128,128]{3,2,1,0:T(8,128)S(1)}, u32[]{:S(2)}, u32[]{:S(2)}) collective-permute-start(f32[2,4,128,128]{3,2,1,0:T(8,128)S(1)} %get-tuple-element.345), channel_id=1, source_target_pairs={{0,16},{1,17},{2,18},{3,19},{4,20},{5,21},{6,22},{7,23},{8,24},{9,... | collective-permute-start | bytes 1572872 | tf_op jit(solution)/shard_map/ppermute | solution.py:49
  247.9 21.8 %collective-permute-start.100 = (f32[192,512]{1,0:T(8,128)S(1)}, f32[192,512]{1,0:T(8,128)S(1)}, u32[]{:S(2)}, u32[]{:S(2)}) collective-permute-start(f32[192,512]{1,0:T(8,128)S(1)} %copy-done.14), channel_id=1, source_target_pairs={{0,4},{1,5},{2,6},{3,7},{4,0},{5,1},{6,2},{7,3},{8,12},{9,13},{10,... | collective-permute-start | bytes 1179656 | tf_op jit(solution)/shard_map/ppermute | solution.py:49
  249.6 23.8 %collective-permute-start.103 = (f32[1,9,64,128]{3,2,1,0:T(8,128)S(1)}, f32[1,9,64,128]{3,2,1,0:T(8,128)S(1)}, u32[]{:S(2)}, u32[]{:S(2)}) collective-permute-start(f32[1,9,64,128]{3,2,1,0:T(8,128)S(1)} %slice_add_fusion.1), channel_id=1, source_target_pairs={{0,2},{1,3},{2,0},{3,1},{4,6},{5,7},{6,4},{7,5},{8,10},{9,11},{10,... | collective-permute-start | bytes 884744 | tf_op jit(solution)/shard_map/ppermute | solution.py:49
  271.1 15.4 %collective-permute-start.108 = (f32[2,4,128,128]{3,2,1,0:T(8,128)S(1)}, f32[2,4,128,128]{3,2,1,0:T(8,128)S(1)}, u32[]{:S(2)}, u32[]{:S(2)}) collective-permute-start(f32[2,4,128,128]{3,2,1,0:T(8,128)S(1)} %get-tuple-element.363), channel_id=1, source_target_pairs={{0,8},{1,9},{2,10},{3,11},{4,12},{5,13},{6,14},{7,15},{8,0},{9,1},... | collective-permute-start | bytes 1572872 | tf_op jit(solution)/shard_map/ppermute | solution.py:49
  272.2 14.3 %collective-permute-start.109 = (f32[2,4,128,128]{3,2,1,0:T(8,128)S(1)}, f32[2,4,128,128]{3,2,1,0:T(8,128)S(1)}, u32[]{:S(2)}, u32[]{:S(2)}) collective-permute-start(f32[2,4,128,128]{3,2,1,0:T(8,128)S(1)} %get-tuple-element.364), channel_id=1, source_target_pairs={{0,16},{1,17},{2,18},{3,19},{4,20},{5,21},{6,22},{7,23},{8,24},{9,... | collective-permute-start | bytes 1572872 | tf_op jit(solution)/shard_map/ppermute | solution.py:49
  290.1 8.5 %collective-permute-start.113 = (f32[1,256,128]{2,1,0:T(8,128)S(1)}, f32[1,256,128]{2,1,0:T(8,128)S(1)}, u32[]{:S(2)}, u32[]{:S(2)}) collective-permute-start(f32[1,256,128]{2,1,0:T(8,128)S(1)} %fusion.16), channel_id=1, source_target_pairs={{0,2},{1,3},{2,0},{3,1},{4,6},{5,7},{6,4},{7,5},{8,10},{9,11},{10,... | collective-permute-start | bytes 393224 | tf_op jit(solution)/shard_map/ppermute | solution.py:49
  306.9 14.9 %collective-permute-start.127 = (f32[2,9,64,128]{3,2,1,0:T(8,128)S(1)}, f32[2,9,64,128]{3,2,1,0:T(8,128)S(1)}, u32[]{:S(2)}, u32[]{:S(2)}) collective-permute-start(f32[2,9,64,128]{3,2,1,0:T(8,128)S(1)} %get-tuple-element.406), channel_id=1, source_target_pairs={{0,1},{1,0},{2,3},{3,2},{4,5},{5,4},{6,7},{7,6},{8,9},{9,8},{10,11... | collective-permute-start | bytes 1769480 | tf_op jit(solution)/shard_map/ppermute | solution.py:49
  308.3 12.6 %collective-permute-start.125 = (f32[1,4,128,128]{3,2,1,0:T(8,128)S(1)}, f32[1,4,128,128]{3,2,1,0:T(8,128)S(1)}, u32[]{:S(2)}, u32[]{:S(2)}) collective-permute-start(f32[1,4,128,128]{3,2,1,0:T(8,128)S(1)} %get-tuple-element.404), channel_id=1, source_target_pairs={{0,16},{1,17},{2,18},{3,19},{4,20},{5,21},{6,22},{7,23},{8,24},{9,... | collective-permute-start | bytes 786440 | tf_op jit(solution)/shard_map/ppermute | solution.py:49
  309.6 11.2 %collective-permute-start.126 = (f32[1,4,128,128]{3,2,1,0:T(8,128)S(1)}, f32[1,4,128,128]{3,2,1,0:T(8,128)S(1)}, u32[]{:S(2)}, u32[]{:S(2)}) collective-permute-start(f32[1,4,128,128]{3,2,1,0:T(8,128)S(1)} %get-tuple-element.405), channel_id=1, source_target_pairs={{0,8},{1,9},{2,10},{3,11},{4,12},{5,13},{6,14},{7,15},{8,0},{9,1},... | collective-permute-start | bytes 786440 | tf_op jit(solution)/shard_map/ppermute | solution.py:49
  319.0 14.8 %collective-permute-start.122 = (f32[2,4,128,128]{3,2,1,0:T(8,128)S(1)}, f32[2,4,128,128]{3,2,1,0:T(8,128)S(1)}, u32[]{:S(2)}, u32[]{:S(2)}) collective-permute-start(f32[2,4,128,128]{3,2,1,0:T(8,128)S(1)} %get-tuple-element.397), channel_id=1, source_target_pairs={{0,8},{1,9},{2,10},{3,11},{4,12},{5,13},{6,14},{7,15},{8,0},{9,1},... | collective-permute-start | bytes 1572872 | tf_op jit(solution)/shard_map/ppermute | solution.py:49
  320.1 13.8 %collective-permute-start.123 = (f32[2,4,128,128]{3,2,1,0:T(8,128)S(1)}, f32[2,4,128,128]{3,2,1,0:T(8,128)S(1)}, u32[]{:S(2)}, u32[]{:S(2)}) collective-permute-start(f32[2,4,128,128]{3,2,1,0:T(8,128)S(1)} %get-tuple-element.398), channel_id=1, source_target_pairs={{0,16},{1,17},{2,18},{3,19},{4,20},{5,21},{6,22},{7,23},{8,24},{9,... | collective-permute-start | bytes 1572872 | tf_op jit(solution)/shard_map/ppermute | solution.py:49
  321.9 11.9 %collective-permute-start.143 = (f32[2,256,128]{2,1,0:T(8,128)S(1)}, f32[2,256,128]{2,1,0:T(8,128)S(1)}, u32[]{:S(2)}, u32[]{:S(2)}) collective-permute-start(f32[2,256,128]{2,1,0:T(8,128)S(1)} %pad_maximum_fusion.11), channel_id=1, source_target_pairs={{0,1},{1,0},{2,3},{3,2},{4,5},{5,4},{6,7},{7,6},{8,9},{9,8},{10,11... | collective-permute-start | bytes 786440 | tf_op jit(solution)/shard_map/ppermute | solution.py:49
  322.8 27.0 %collective-permute-start.135 = (f32[1,9,64,128]{3,2,1,0:T(8,128)S(1)}, f32[1,9,64,128]{3,2,1,0:T(8,128)S(1)}, u32[]{:S(2)}, u32[]{:S(2)}) collective-permute-start(f32[1,9,64,128]{3,2,1,0:T(8,128)S(1)} %slice_add_fusion), channel_id=1, source_target_pairs={{0,2},{1,3},{2,0},{3,1},{4,6},{5,7},{6,4},{7,5},{8,10},{9,11},{10,... | collective-permute-start | bytes 884744 | tf_op jit(solution)/shard_map/ppermute | solution.py:49
  333.8 15.9 %collective-permute-start.144 = (f32[1,256,128]{2,1,0:T(8,128)S(1)}, f32[1,256,128]{2,1,0:T(8,128)S(1)}, u32[]{:S(2)}, u32[]{:S(2)}) collective-permute-start(f32[1,256,128]{2,1,0:T(8,128)S(1)} %slice_add_fusion.18), channel_id=1, source_target_pairs={{0,2},{1,3},{2,0},{3,1},{4,6},{5,7},{6,4},{7,5},{8,10},{9,11},{10,... | collective-permute-start | bytes 393224 | tf_op jit(solution)/shard_map/ppermute | solution.py:49
  335.3 9.3 %collective-permute-start.129 = (f32[1,4,128,128]{3,2,1,0:T(8,128)S(1)}, f32[1,4,128,128]{3,2,1,0:T(8,128)S(1)}, u32[]{:S(2)}, u32[]{:S(2)}) collective-permute-start(f32[1,4,128,128]{3,2,1,0:T(8,128)S(1)} %get-tuple-element.418), channel_id=1, source_target_pairs={{0,8},{1,9},{2,10},{3,11},{4,12},{5,13},{6,14},{7,15},{8,0},{9,1},... | collective-permute-start | bytes 786440 | tf_op jit(solution)/shard_map/ppermute | solution.py:49
  336.4 11.0 %collective-permute-start.132 = (f32[1,4,128,128]{3,2,1,0:T(8,128)S(1)}, f32[1,4,128,128]{3,2,1,0:T(8,128)S(1)}, u32[]{:S(2)}, u32[]{:S(2)}) collective-permute-start(f32[1,4,128,128]{3,2,1,0:T(8,128)S(1)} %get-tuple-element.510), channel_id=1, source_target_pairs={{0,8},{1,9},{2,10},{3,11},{4,12},{5,13},{6,14},{7,15},{8,0},{9,1},... | collective-permute-start | bytes 786440 | tf_op jit(solution)/shard_map/ppermute | solution.py:49
  344.7 9.8 %collective-permute-start.130 = (f32[2,256,128]{2,1,0:T(8,128)S(1)}, f32[2,256,128]{2,1,0:T(8,128)S(1)}, u32[]{:S(2)}, u32[]{:S(2)}) collective-permute-start(f32[2,256,128]{2,1,0:T(8,128)S(1)} %pad_maximum_fusion.9), channel_id=1, source_target_pairs={{0,1},{1,0},{2,3},{3,2},{4,5},{5,4},{6,7},{7,6},{8,9},{9,8},{10,11... | collective-permute-start | bytes 786440 | tf_op jit(solution)/shard_map/ppermute | solution.py:49
  347.6 11.3 %collective-permute-start.133 = (f32[2,256,128]{2,1,0:T(8,128)S(1)}, f32[2,256,128]{2,1,0:T(8,128)S(1)}, u32[]{:S(2)}, u32[]{:S(2)}) collective-permute-start(f32[2,256,128]{2,1,0:T(8,128)S(1)} %pad_maximum_fusion.10), channel_id=1, source_target_pairs={{0,1},{1,0},{2,3},{3,2},{4,5},{5,4},{6,7},{7,6},{8,9},{9,8},{10,11... | collective-permute-start | bytes 786440 | tf_op jit(solution)/shard_map/ppermute | solution.py:49
  349.9 18.6 %collective-permute-start.145 = (f32[1088,128]{1,0:T(8,128)S(1)}, f32[1088,128]{1,0:T(8,128)}, u32[]{:S(2)}, u32[]{:S(2)}) collective-permute-start(f32[1088,128]{1,0:T(8,128)S(1)} %pad_maximum_fusion.3.refs_8_), channel_id=1, source_target_pairs={{0,8},{1,9},{2,10},{3,11},{4,12},{5,13},{6,14},{7,15},{8,0},{9,1},... | collective-permute-start | bytes 1671176 | tf_op jit(solution)/shard_map/ppermute | solution.py:49
  351.0 31.9 %collective-permute-start.146 = (f32[1088,128]{1,0:T(8,128)S(1)}, f32[1088,128]{1,0:T(8,128)S(1)}, u32[]{:S(2)}, u32[]{:S(2)}) collective-permute-start(f32[1088,128]{1,0:T(8,128)S(1)} %pad_maximum_fusion.3.refs_8_), channel_id=1, source_target_pairs={{0,16},{1,17},{2,18},{3,19},{4,20},{5,21},{6,22},{7,23},{8,24},{9,... | collective-permute-start | bytes 1671176 | tf_op jit(solution)/shard_map/ppermute | solution.py:49
  351.8 31.0 %collective-permute-start.147 = (f32[1088,128]{1,0:T(8,128)S(1)}, f32[1088,128]{1,0:T(8,128)}, u32[]{:S(2)}, u32[]{:S(2)}) collective-permute-start(f32[1088,128]{1,0:T(8,128)S(1)} %pad_maximum_fusion.3.refs_8_), channel_id=1, source_target_pairs={{0,24},{1,25},{2,26},{3,27},{4,28},{5,29},{6,30},{7,31},{8,16},{9,... | collective-permute-start | bytes 1671176 | tf_op jit(solution)/shard_map/ppermute | solution.py:49
  354.5 7.9 %collective-permute-start.131 = (f32[1,256,128]{2,1,0:T(8,128)S(1)}, f32[1,256,128]{2,1,0:T(8,128)S(1)}, u32[]{:S(2)}, u32[]{:S(2)}) collective-permute-start(f32[1,256,128]{2,1,0:T(8,128)S(1)} %slice_add_fusion.28), channel_id=1, source_target_pairs={{0,2},{1,3},{2,0},{3,1},{4,6},{5,7},{6,4},{7,5},{8,10},{9,11},{10,... | collective-permute-start | bytes 393224 | tf_op jit(solution)/shard_map/ppermute | solution.py:49
  366.3 23.5 %collective-permute-start.138 = (f32[1088,128]{1,0:T(8,128)S(1)}, f32[1088,128]{1,0:T(8,128)}, u32[]{:S(2)}, u32[]{:S(2)}) collective-permute-start(f32[1088,128]{1,0:T(8,128)S(1)} %pad_maximum_fusion.2.refs_0_), channel_id=1, source_target_pairs={{0,24},{1,25},{2,26},{3,27},{4,28},{5,29},{6,30},{7,31},{8,16},{9,... | collective-permute-start | bytes 1671176 | tf_op jit(solution)/shard_map/ppermute | solution.py:49
  368.4 30.0 %collective-permute-start.148 = (f32[1088,128]{1,0:T(8,128)S(1)}, f32[1088,128]{1,0:T(8,128)}, u32[]{:S(2)}, u32[]{:S(2)}) collective-permute-start(f32[1088,128]{1,0:T(8,128)S(1)} %pad_maximum_fusion.3.refs_8_), channel_id=1, source_target_pairs={{0,4},{1,5},{2,6},{3,7},{4,0},{5,1},{6,2},{7,3},{8,12},{9,13},{10,... | collective-permute-start | bytes 1671176 | tf_op jit(solution)/shard_map/ppermute | solution.py:49
  368.5 30.0 %collective-permute-start.139 = (f32[1088,128]{1,0:T(8,128)S(1)}, f32[1088,128]{1,0:T(8,128)}, u32[]{:S(2)}, u32[]{:S(2)}) collective-permute-start(f32[1088,128]{1,0:T(8,128)S(1)} %pad_maximum_fusion.2.refs_0_), channel_id=1, source_target_pairs={{0,4},{1,5},{2,6},{3,7},{4,0},{5,1},{6,2},{7,3},{8,12},{9,13},{10,... | collective-permute-start | bytes 1671176 | tf_op jit(solution)/shard_map/ppermute | solution.py:49
  382.8 15.1 %collective-permute-start.137 = (f32[1088,128]{1,0:T(8,128)S(1)}, f32[1088,128]{1,0:T(8,128)}, u32[]{:S(2)}, u32[]{:S(2)}) collective-permute-start(f32[1088,128]{1,0:T(8,128)S(1)} %pad_maximum_fusion.2.refs_0_), channel_id=1, source_target_pairs={{0,16},{1,17},{2,18},{3,19},{4,20},{5,21},{6,22},{7,23},{8,24},{9,... | collective-permute-start | bytes 1671176 | tf_op jit(solution)/shard_map/ppermute | solution.py:49
  382.9 15.1 %collective-permute-start.136 = (f32[1088,128]{1,0:T(8,128)S(1)}, f32[1088,128]{1,0:T(8,128)}, u32[]{:S(2)}, u32[]{:S(2)}) collective-permute-start(f32[1088,128]{1,0:T(8,128)S(1)} %pad_maximum_fusion.2.refs_0_), channel_id=1, source_target_pairs={{0,8},{1,9},{2,10},{3,11},{4,12},{5,13},{6,14},{7,15},{8,0},{9,1},... | collective-permute-start | bytes 1671176 | tf_op jit(solution)/shard_map/ppermute | solution.py:49
  389.8 9.1 %collective-permute-start.149 = (f32[1088,128]{1,0:T(8,128)}, f32[1088,128]{1,0:T(8,128)}, u32[]{:S(2)}, u32[]{:S(2)}) collective-permute-start(f32[1088,128]{1,0:T(8,128)} %collective-permute-done.145.refs_9_), channel_id=1, source_target_pairs={{0,4},{1,5},{2,6},{3,7},{4,0},{5,1},{6,2},{7,3},{8,12},{9,13},{10,... | collective-permute-start | bytes 1671176 | tf_op jit(solution)/shard_map/ppermute | solution.py:49
  (148 other events, 944.0 us)

commit v6 on v5

--- a/solution.py
+++ b/solution.py
@@ -412,12 +412,26 @@
     return (kinds, 2 * width // 128, 128)
 
 
-def reduce_first(x, w_reduce, mask):
+def reduce_first(x, w_reduce, sizes):
     rows, d_in = x.shape
     mid = w_reduce.shape[2]
 
-    def body(x_ref, w_ref, mask_ref, red_ref, stats_ref):
+    def body(sizes_ref, x_ref, w_ref, mask_ref, red_ref, stats_ref):
         k = pl.program_id(0)
+
+        @pl.when(k == 0)
+        def _():
+            at = lax.broadcasted_iota(jnp.int32, (rows, 1), 0)
+            inside = at < 0
+            for slot in range(SLOTS):
+                side = sizes_ref[slot]
+                image = (at < IMG_ROWS) & ((at & (SLOTS - 1)) == slot)
+                image &= ((at >> 4) < side) & (((at >> 1) & (MAPW - 1)) < side)
+                first = IMG_ROWS + slot * PIECES * TILE * TILE
+                tile = (at >= first) & (at < first + PIECES * TILE * TILE) & (at * 0 < side)
+                inside |= image | tile
+            mask_ref[...] = jnp.where(inside, 1.0, 0.0)
+
         part = dot(x_ref[...], w_ref[0])
 
         @pl.when(k == 0)
@@ -435,12 +449,12 @@
     return call(
         body,
         d_in // CH,
-        [cols(rows), pl.BlockSpec((1, CH, mid), lambda k: (0, k, 0)), full((rows, 1))],
-        [full((rows, mid)), full(payload(mid))],
-        [near((rows, mid)), near(payload(mid))],
+        [smem(), cols(rows), pl.BlockSpec((1, CH, mid), lambda k: (0, k, 0))],
+        [full((rows, 1)), full((rows, mid)), full(payload(mid))],
+        [near((rows, 1)), near((rows, mid)), near(payload(mid))],
         name="reduce_first",
         flops=2 * rows * d_in * mid,
-    )(x, w_reduce, mask)
+    )(sizes, x, w_reduce)
 
 
 def spatial_stage(number, red, members, table, mask, w9, select):
@@ -1036,7 +1050,7 @@
             (got,) = yield "deep", [(send, dict(dz=step))]
             step *= 2
             if step == self.grid.z:
-                if gate:
+                if gate and len(gate) > 2:
                     got, _ = lax.optimization_barrier((got, gate[2]))
                 return keep[0] + got[0]
             half = keep.shape[0] // 2
@@ -1047,15 +1061,15 @@
         for group in self.grid.far():
             flat = flat + sum(self.grid.swap(flat, **step) for step in group)
         got = yield "plane", [(flat, dict(dx=1)), (flat, dict(dy=1)), (flat, dict(dy=1, dx=1))]
-        out.extend([flat] + list(lax.optimization_barrier(tuple(got))))
-
-    def by_halves(self, kernel, own, peer, keep, send, out, after=None, gate=None):
+        out.extend([flat] + list(got))
+
+    def by_halves(self, kernel, own, peer, keep, send, out, after=None, gate=None, kind="plane"):
         (got,) = yield "core", [(send, dict(dc=1))]
         if after:
             got, _ = lax.optimization_barrier((got, after[0]))
         x_keep, x_send, y_keep, y_send = kernel(self.me, own, peer, keep, got, self.grid.z)
         self.begun = x_keep
-        got = yield "plane", [(x_send, dict(dx=1)), (y_send, dict(dy=1))]
+        got = yield kind, [(x_send, dict(dx=1)), (y_send, dict(dy=1))]
         got = lax.optimization_barrier(tuple(got))
         if after is not None:
             after.append(got[0])
@@ -1163,16 +1177,6 @@
     return image, tile.reshape(-1, TILE, TILE, width)
 
 
-def row_mask(map_sizes, rows):
-    row = jnp.arange(MAP)
-    col = jnp.arange(MAPW)
-    inside = (row[:, None, None] < map_sizes[None, None, :]) & (col[None, :, None] < map_sizes[None, None, :])
-    image = inside.astype(F32).reshape(IMG_ROWS)
-    tile = jnp.repeat((map_sizes > 0).astype(F32), PIECES * TILE * TILE)
-    pad = jnp.zeros((rows - IMG_ROWS - tile.shape[0],), F32)
-    return jnp.concatenate([image, tile, pad])[:, None]
-
-
 def core_halves(value, core, nz):
     deep = value.shape[1] // (2 * nz)
     low = [value[:, 2 * z * deep : (2 * z + 1) * deep] for z in range(nz)]
@@ -1215,10 +1219,8 @@
     chip = (y % 2) * 2 + x % 2
     turned = (x % 2) * 2 + y % 2
     me = jnp.stack([core, chip, z, turned]).astype(jnp.int32)
-    mask = row_mask(map_sizes, rows)
     w9 = w_spatial.reshape(BLOCKS, 9, mid, mid)
     start = to_rows(images, tile_maps, rows)
-    grad = to_rows(grad_images, grad_tiles, rows)
     select = core_select(core, mid, nz)
     collect = Collect(grid, me)
     bulk = Bulk(grid, ROOM)
@@ -1235,7 +1237,9 @@
 
     acts, lows, reds, spas, exps = [start], [], [], [], []
     mr1, mr2, mr3, hid1, hid2 = [], [], [], [], []
-    red, stats = reduce_first(start, w_reduce, mask)
+    mask, red, stats = reduce_first(start, w_reduce, map_sizes)
+    grad_images, grad_tiles, stats = lax.optimization_barrier((grad_images, grad_tiles, stats))
+    grad = to_rows(grad_images, grad_tiles, rows)
     low = start
     for b in range(BLOCKS):
         reds.append(red)
@@ -1243,6 +1247,8 @@
             b, red, moments(stats), table, mask, w9, select
         )
         mr1.append(mr)
+        if b == 0:
+            stats, grad = lax.optimization_barrier((stats, grad))
         hid1.append([])
         bulk.add(("h", b), collect.hidden(keep, send, hid1[b]))
         keep, send = core_halves(low, core, nz)

time: 413 us -> 410 us (level)
  transfers between devices with their start and end apart: 152 -> 152, of which waited for: 90 -> 89; matrix products, arithmetic and copies ran while one was open for 3% -> 3% of each run, Pallas kernels for 12% -> 12%
where the time goes in v6:
time: 410 us; the launch traced here: 409 us
  starting transfers between devices  161 us (39%)
  waiting for transfers between devices  143 us (35%)
  Pallas kernels  79 us (19%)
  local copies, waits for them, and re-layouts  15.8 us (4%)
  other arithmetic  8.92 us (2%)
    ppermute x152, starting transfers between devices, swap(): return lax.ppermute(value, AXES, pairs)  161 us
    ppermute x152, waiting for transfers between devices, swap(): return lax.ppermute(value, AXES, pairs)  143 us
    pallas_call x2, Pallas kernels, back_spatial(): call(body, 3, [smem(), full((rows, mid)), full((rows, mid)), full((8, mid...  10.3 us
    pallas_call x2, Pallas kernels, back_expand(): call(body, d_in // CH, [smem(), cols(rows), cols(rows), full((8, d_in)),...  9.35 us
    pallas_call x2, Pallas kernels, spatial_stage(): call(body, 3, [full((rows, mid)), full(table.shape), full((rows, 1)), pl....  9.27 us
    pallas_call x2, Pallas kernels, expand_stage(): call(body, d_in // CH, [full((rows, mid)), full(table.shape), full((rows,...  8.72 us
  transfers between devices with their start and end apart: 152, of which 89 were waited for; matrix products, arithmetic and copies ran while one was open for 3% of the time, Pallas kernels for 12%

profile of v6, /device:TPU:0, one launch (start us, length us, event | category | flops | bytes accessed | tf_op | source)
XLA Modules:
  0.0 409.1 jit_solution(17480025231760025321)
XLA Ops:
  3.6 3.4 reduce_first.1
  10.8 4.0 collective-permute-start.3
  19.0 3.7 collective-permute-start.6
  24.5 2.7 collective-permute-done.5.refs_2_
  27.2 4.6 %spatial_stage.2 = (f32[8,512]{1,0:T(8,128)S(1)}, f32[192,256]{1,0:T(8,128)S(1)}, f32[192,256]{1,0:T(8,128)S(1)}, f32[192,512]{1,0:T(8,128)S(1)}, f32[3,8,128]{2,1,0:T(8,128)S(1)}) custom-call(f32[192,512]{1,0:T(8,128)S(1)} %get-tuple-element.232.red_ref, f32[8,512]{1,0:T(8,128)S(1)} %pad_maximum_fusion.21.table_ref, ...), custom_call_target="tpu_custom_call" | custom-call | tf_op jit(solution)/shard_map/spatial_stage/pallas_call | solution.py:492
  41.4 2.3 collective-permute-start.13
  46.7 4.4 %expand_stage.2 = (f32[8,512]{1,0:T(8,128)S(1)}, f32[192,512]{1,0:T(8,128)S(1)}, f32[192,2048]{1,0:T(8,128)}, f32[3,32,128]{2,1,0:T(8,128)S(1)}) custom-call(f32[192,512]{1,0:T(8,128)S(1)} %get-tuple-element.236.spa_ref, f32[8,512]{1,0:T(8,128)S(1)} %pad_maximum_fusion.21.table_ref, f32[192,1]{1,0:T(8,128)S(1)} %get-tuple-element.233.mask_ref, ...), custom_call_target="tpu_custom_call" | custom-call | tf_op jit(solution)/shard_map/expand_stage/pallas_call | solution.py:548
  61.8 2.6 collective-permute-start.24
  67.3 2.9 collective-permute-done.22.h3
  72.4 5.3 %join_stage.1 = (f32[8,2048]{1,0:T(8,128)S(1)}, f32[192,2048]{1,0:T(8,128)}, f32[192,2048]{1,0:T(8,128)}, f32[192,512]{1,0:T(8,128)S(1)}, f32[3,8,128]{2,1,0:T(8,128)S(1)}) custom-call(f32[192,2048]{1,0:T(8,128)} %get-tuple-element.245.exp_ref, f32[4,2048]{1,0:T(4,128)S(1)} %pad_maximum_fusion.20.table_ref.outer_ref, ...), custom_call_target="tpu_custom_call" | custom-call | tf_op jit(solution)/shard_map/join_stage/pallas_call | solution.py:610
  90.6 2.9 collective-permute-start.31
  95.3 4.6 %spatial_stage.3 = (f32[8,512]{1,0:T(8,128)S(1)}, f32[192,256]{1,0:T(8,128)S(1)}, f32[192,256]{1,0:T(8,128)S(1)}, f32[192,512]{1,0:T(8,128)S(1)}, f32[3,8,128]{2,1,0:T(8,128)S(1)}) custom-call(f32[192,512]{1,0:T(8,128)S(1)} %get-tuple-element.256.red_ref, f32[8,512]{1,0:T(8,128)S(1)} %pad_maximum_fusion.21.table_ref, ...), custom_call_target="tpu_custom_call" | custom-call | tf_op jit(solution)/shard_map/spatial_stage/pallas_call | solution.py:492
  107.5 2.3 collective-permute-start.42
  114.7 4.4 %expand_stage.3 = (f32[8,512]{1,0:T(8,128)S(1)}, f32[192,512]{1,0:T(8,128)S(1)}, f32[192,2048]{1,0:T(8,128)}, f32[3,32,128]{2,1,0:T(8,128)S(1)}) custom-call(f32[192,512]{1,0:T(8,128)S(1)} %get-tuple-element.258.spa_ref, f32[8,512]{1,0:T(8,128)S(1)} %pad_maximum_fusion.21.table_ref, f32[192,1]{1,0:T(8,128)S(1)} %get-tuple-element.233.mask_ref, ...), custom_call_target="tpu_custom_call" | custom-call | tf_op jit(solution)/shard_map/expand_stage/pallas_call | solution.py:548
  129.8 2.2 collective-permute-start.53
  137.0 4.7 %turn_stage.1 = (f32[8,2048]{1,0:T(8,128)S(1)}, f32[98,2048]{1,0:T(8,128)}, f32[72,2048]{1,0:T(8,128)}, f32[192,2048]{1,0:T(8,128)}, f32[2,32,128]{2,1,0:T(8,128)S(1)}) custom-call(f32[192,2048]{1,0:T(8,128)} %get-tuple-element.265.exp_ref, f32[4,2048]{1,0:T(4,128)S(1)} %pad_maximum_fusion.20.table_ref.outer_ref, f32[192,2048]{1,0:T(8,128)} %get-tuple-element.266.act_ref, ...), custom_call_target="tpu_custom_call" | custom-call | tf_op jit(solution)/shard_map/turn_stage/pallas_call | solution.py:666
  142.9 2.2 collective-permute-start.57
  150.3 2.1 collective-permute-start.60
  157.5 4.7 %back_expand.2 = (f32[2,2048]{1,0:T(2,128)S(1)}, f32[192,1024]{1,0:T(8,128)S(1)}, f32[192,1024]{1,0:T(8,128)S(1)}, f32[192,512]{1,0:T(8,128)S(1)}, f32[2,8,128]{2,1,0:T(8,128)S(1)}) custom-call(s32[4]{0:T(128)S(1)} %pad_add_fusion.me_ref, f32[192,2048]{1,0:T(8,128)} %get-tuple-element.281.pre3_ref, f32[192,2048]{1,0:T(8,128)} %get-tuple-element.265.exp_ref, ...), custom_call_target="tpu_custom_call" | custom-call | tf_op jit(solution)/shard_map/back_expand/pallas_call | solution.py:750
  163.0 2.3 collective-permute-done.61
  165.2 2.0 collective-permute-start.64
  181.8 5.1 %back_spatial.2 = (f32[2,512]{1,0:T(2,128)S(1)}, f32[192,128]{1,0:T(8,128)S(1)}, f32[192,128]{1,0:T(8,128)S(1)}, f32[192,128]{1,0:T(8,128)S(1)}, f32[192,128]{1,...) custom-call(s32[4]{0:T(128)S(1)} %pad_add_fusion.me_ref, f32[192,512]{1,0:T(8,128)S(1)} %get-tuple-element.285.pre2_ref, ...), custom_call_target="tpu_custom_call" | custom-call | tf_op jit(solution)/shard_map/back_spatial/pallas_call | solution.py:817
  195.8 2.0 collective-permute-start.78
  208.5 2.2 weight_spatial.2
  210.9 5.2 %back_reduce.1 = (f32[2,512]{1,0:T(2,128)S(1)}, f32[192,512]{1,0:T(8,128)S(1)}, f32[192,2048]{1,0:T(8,128)}, f32[2,32,128]{2,1,0:T(8,128)S(1)}) custom-call(f32[192,512]{1,0:T(8,128)S(1)} %get-tuple-element.294.pre1_ref, f32[192,512]{1,0:T(8,128)S(1)} %get-tuple-element.256.red_ref, f32[8,512]{1,0:T(8,128)S(1)} %get-tuple-element.286.mr1_ref, ...), custom_call_target="tpu_custom_call" | custom-call | tf_op jit(solution)/shard_map/back_reduce/pallas_call | solution.py:906
  225.9 6.0 %collective-permute-done.90 = f32[2,9,64,128]{3,2,1,0:T(8,128)S(1)} collective-permute-done((f32[2,9,64,128]{3,2,1,0:T(8,128)S(1)}, f32[2,9,64,128]{3,2,1,0:T(8,128)S(1)}, u32[]{:S(2)}, u32[]{:S(2)}) %collective-permute-start.90) | collective-permute-done | bytes 589856 | tf_op jit(solution)/shard_map/ppermute | solution.py:49
  238.9 4.6 %back_expand.3 = (f32[2,2048]{1,0:T(2,128)S(1)}, f32[192,1024]{1,0:T(8,128)S(1)}, f32[192,1024]{1,0:T(8,128)S(1)}, f32[192,512]{1,0:T(8,128)S(1)}, f32[2,8,128]{2,1,0:T(8,128)S(1)}) custom-call(s32[4]{0:T(128)S(1)} %pad_add_fusion.me_ref, f32[192,2048]{1,0:T(8,128)} %get-tuple-element.325.pre3_ref, f32[192,2048]{1,0:T(8,128)} %get-tuple-element.245.exp_ref, ...), custom_call_target="tpu_custom_call" | custom-call | tf_op jit(solution)/shard_map/back_expand/pallas_call | solution.py:750
  248.6 9.3 %collective-permute-done.95 = f32[2,4,128,128]{3,2,1,0:T(8,128)S(1)} collective-permute-done((f32[2,4,128,128]{3,2,1,0:T(8,128)S(1)}, f32[2,4,128,128]{3,2,1,0:T(8,128)S(1)}, u32[]{:S(2)}, u32[]{:S(2)}) %collective-permute-start.95) | collective-permute-done | bytes 524320 | tf_op jit(solution)/shard_map/ppermute | solution.py:49
  261.2 2.1 collective-permute-done.99
  277.2 5.1 %back_spatial.3 = (f32[2,512]{1,0:T(2,128)S(1)}, f32[192,128]{1,0:T(8,128)S(1)}, f32[192,128]{1,0:T(8,128)S(1)}, f32[192,128]{1,0:T(8,128)S(1)}, f32[192,128]{1,...) custom-call(s32[4]{0:T(128)S(1)} %pad_add_fusion.me_ref, f32[192,512]{1,0:T(8,128)S(1)} %get-tuple-element.347.pre2_ref, ...), custom_call_target="tpu_custom_call" | custom-call | tf_op jit(solution)/shard_map/back_spatial/pallas_call | solution.py:817
  287.2 2.1 collective-permute-start.113
  293.4 2.4 collective-permute-done.113
  301.7 2.2 weight_spatial.3
  307.8 4.6 %back_reduce_last.1 = (f32[2,512]{1,0:T(2,128)S(1)}, f32[192,512]{1,0:T(8,128)S(1)}, f32[98,2048]{1,0:T(8,128)}, f32[72,2048]{1,0:T(8,128)}) custom-call(f32[192,512]{1,0:T(8,128)S(1)} %get-tuple-element.367.pre1_ref, f32[192,512]{1,0:T(8,128)S(1)} %get-tuple-element.232.red_ref, f32[8,512]{1,0:T(8,128)S(1)} %get-tuple-element.348.mr1_ref, ...), custom_call_target="tpu_custom_call" | custom-call | tf_op jit(solution)/shard_map/back_reduce_last/pallas_call | solution.py:882
  314.1 2.1 weight_reduce.3
  321.6 9.1 %collective-permute-done.143 = f32[2,256,128]{2,1,0:T(8,128)S(1)} collective-permute-done((f32[2,256,128]{2,1,0:T(8,128)S(1)}, f32[2,256,128]{2,1,0:T(8,128)S(1)}, u32[]{:S(2)}, u32[]{:S(2)}) %collective-permute-start.143) | collective-permute-done | bytes 262176 | tf_op jit(solution)/shard_map/ppermute | solution.py:49
  334.6 3.5 collective-permute-done.128
  339.1 2.6 collective-permute-done.129
  341.7 2.3 collective-permute-start.130
  344.6 2.2 collective-permute-start.133
  351.6 2.1 collective-permute-start.131
  353.7 2.3 collective-permute-done.133
  356.0 2.2 collective-permute-start.134
  359.5 3.9 collective-permute-done.134
  367.1 7.9 %collective-permute-done.147.refs_11_ = f32[1088,128]{1,0:T(8,128)} collective-permute-done((f32[1088,128]{1,0:T(8,128)S(1)}, f32[1088,128]{1,0:T(8,128)}, u32[]{:S(2)}, u32[]{:S(2)}) %collective-permute-start.147) | collective-permute-done | bytes 557088 | tf_op jit(solution)/shard_map/ppermute | solution.py:49
  376.1 10.5 %collective-permute-done.136.refs_1_ = f32[1088,128]{1,0:T(8,128)} collective-permute-done((f32[1088,128]{1,0:T(8,128)S(1)}, f32[1088,128]{1,0:T(8,128)}, u32[]{:S(2)}, u32[]{:S(2)}) %collective-permute-start.136) | collective-permute-done | bytes 557088 | tf_op jit(solution)/shard_map/ppermute | solution.py:49
  389.0 2.3 reshape.145
  401.2 7.8 %place_slices.1 = (f32[2,512,512]{2,1,0:T(8,128)}, f32[2,9,128,512]{3,2,1,0:T(8,128)}, f32[2,128,2048]{2,1,0:T(8,128)}) custom-call(s32[4]{0:T(128)S(1)} %pad_add_fusion.me_ref, f32[1088,128]{1,0:T(8,128)} %copy-done.27, f32[1088,128]{1,0:T(8,128)} %collective-permute-done.136.refs_1_, f32[1088,128]{1,0:T(8,128)} %collective-permute-done.137.refs_2_, ...), custom_call_target="tpu_custom_call" | custom-call | tf_op jit(solution)/shard_map/place_slices/pallas_call | solution.py:1153
  (484 shorter events, 223.1 us)
Async XLA Ops:
  8.9 23.0 %collective-permute-start.7 = (f32[192,1024]{1,0:T(8,128)}, f32[192,1024]{1,0:T(8,128)}, u32[]{:S(2)}, u32[]{:S(2)}) collective-permute-start(f32[192,1024]{1,0:T(8,128)} %get-tuple-element.515), channel_id=1, source_target_pairs={{0,4},{1,5},{2,6},{3,7},{4,0},{5,1},{6,2},{7,3},{8,12},{9,13},{10,... | collective-permute-start | bytes 2359304 | tf_op jit(solution)/shard_map/ppermute | solution.py:49
  39.2 7.5 %collective-permute-start.15 = (f32[3,8,128]{2,1,0:T(8,128)S(1)}, f32[3,8,128]{2,1,0:T(8,128)S(1)}, u32[]{:S(2)}, u32[]{:S(2)}) collective-permute-start(f32[3,8,128]{2,1,0:T(8,128)S(1)} %pad_maximum_fusion.27.refs_0_), channel_id=1, source_target_pairs={{0,3},{1,2},{2,1},{3,0},{4,7},{5,6},{6,5},{7,4},{8,11},{9,10},{10,... | collective-permute-start | bytes 36872 | tf_op jit(solution)/shard_map/ppermute | solution.py:49
  43.7 9.0 %collective-permute-start.17 = (f32[384,256]{1,0:T(8,128)S(1)}, f32[384,256]{1,0:T(8,128)S(1)}, u32[]{:S(2)}, u32[]{:S(2)}) collective-permute-start(f32[384,256]{1,0:T(8,128)S(1)} %constant_dynamic-update-slice_fusion.h0), channel_id=1, source_target_pairs={{0,8},{1,9},{2,10},{3,11},{4,12},{5,13},{6,14},{7,15},{8,0},{9,1},... | collective-permute-start | bytes 1179656 | tf_op jit(solution)/shard_map/ppermute | solution.py:49
  45.2 8.4 %collective-permute-start.18 = (f32[384,256]{1,0:T(8,128)S(1)}, f32[384,256]{1,0:T(8,128)S(1)}, u32[]{:S(2)}, u32[]{:S(2)}) collective-permute-start(f32[384,256]{1,0:T(8,128)S(1)} %constant_dynamic-update-slice_fusion.h0), channel_id=1, source_target_pairs={{0,16},{1,17},{2,18},{3,19},{4,20},{5,21},{6,22},{7,23},{8,24},{9,... | collective-permute-start | bytes 1179656 | tf_op jit(solution)/shard_map/ppermute | solution.py:49
  60.0 12.3 %collective-permute-start.26 = (f32[3,32,128]{2,1,0:T(8,128)S(1)}, f32[3,32,128]{2,1,0:T(8,128)S(1)}, u32[]{:S(2)}, u32[]{:S(2)}) collective-permute-start(f32[3,32,128]{2,1,0:T(8,128)S(1)} %pad_maximum_fusion.17.refs_0_), channel_id=1, source_target_pairs={{0,3},{1,2},{2,1},{3,0},{4,7},{5,6},{6,5},{7,4},{8,11},{9,10},{10,... | collective-permute-start | bytes 147464 | tf_op jit(solution)/shard_map/ppermute | solution.py:49
  61.5 10.8 %collective-permute-start.25 = (f32[3,32,128]{2,1,0:T(8,128)S(1)}, f32[3,32,128]{2,1,0:T(8,128)S(1)}, u32[]{:S(2)}, u32[]{:S(2)}) collective-permute-start(f32[3,32,128]{2,1,0:T(8,128)S(1)} %pad_maximum_fusion.17.refs_0_), channel_id=1, source_target_pairs={{0,2},{1,3},{2,0},{3,1},{4,6},{5,7},{6,4},{7,5},{8,10},{9,11},{10,... | collective-permute-start | bytes 147464 | tf_op jit(solution)/shard_map/ppermute | solution.py:49
  61.8 10.5 %collective-permute-start.24 = (f32[3,32,128]{2,1,0:T(8,128)S(1)}, f32[3,32,128]{2,1,0:T(8,128)S(1)}, u32[]{:S(2)}, u32[]{:S(2)}) collective-permute-start(f32[3,32,128]{2,1,0:T(8,128)S(1)} %pad_maximum_fusion.17.refs_0_), channel_id=1, source_target_pairs={{0,1},{1,0},{2,3},{3,2},{4,5},{5,4},{6,7},{7,6},{8,9},{9,8},{10,11... | collective-permute-start | bytes 147464 | tf_op jit(solution)/shard_map/ppermute | solution.py:49
  80.2 19.8 %collective-permute-start.34 = (f32[192,1024]{1,0:T(8,128)S(1)}, f32[192,1024]{1,0:T(8,128)S(1)}, u32[]{:S(2)}, u32[]{:S(2)}) collective-permute-start(f32[192,1024]{1,0:T(8,128)S(1)} %get-tuple-element.489), channel_id=1, source_target_pairs={{0,4},{1,5},{2,6},{3,7},{4,0},{5,1},{6,2},{7,3},{8,12},{9,13},{10,... | collective-permute-start | bytes 2359304 | tf_op jit(solution)/shard_map/ppermute | solution.py:49
  112.0 9.1 %collective-permute-start.44 = (f32[384,256]{1,0:T(8,128)S(1)}, f32[384,256]{1,0:T(8,128)S(1)}, u32[]{:S(2)}, u32[]{:S(2)}) collective-permute-start(f32[384,256]{1,0:T(8,128)S(1)} %constant_dynamic-update-slice_fusion.2.h0), channel_id=1, source_target_pairs={{0,8},{1,9},{2,10},{3,11},{4,12},{5,13},{6,14},{7,15},{8,0},{9,1},... | collective-permute-start | bytes 1179656 | tf_op jit(solution)/shard_map/ppermute | solution.py:49
  113.3 8.4 %collective-permute-start.45 = (f32[384,256]{1,0:T(8,128)S(1)}, f32[384,256]{1,0:T(8,128)S(1)}, u32[]{:S(2)}, u32[]{:S(2)}) collective-permute-start(f32[384,256]{1,0:T(8,128)S(1)} %constant_dynamic-update-slice_fusion.2.h0), channel_id=1, source_target_pairs={{0,16},{1,17},{2,18},{3,19},{4,20},{5,21},{6,22},{7,23},{8,24},{9,... | collective-permute-start | bytes 1179656 | tf_op jit(solution)/shard_map/ppermute | solution.py:49
  162.3 9.1 %collective-permute-start.66 = (f32[192,1024]{1,0:T(8,128)S(1)}, f32[192,1024]{1,0:T(8,128)S(1)}, u32[]{:S(2)}, u32[]{:S(2)}) collective-permute-start(f32[192,1024]{1,0:T(8,128)S(1)} %get-tuple-element.290), channel_id=1, source_target_pairs={{0,4},{1,5},{2,6},{3,7},{4,0},{5,1},{6,2},{7,3},{8,12},{9,13},{10,... | collective-permute-start | bytes 2359304 | tf_op jit(solution)/shard_map/ppermute | solution.py:49
  162.4 9.0 %collective-permute-start.65 = (f32[192,512]{1,0:T(8,128)S(1)}, f32[192,512]{1,0:T(8,128)S(1)}, u32[]{:S(2)}, u32[]{:S(2)}) collective-permute-start(f32[192,512]{1,0:T(8,128)S(1)} %copy-done.16), channel_id=1, source_target_pairs={{0,4},{1,5},{2,6},{3,7},{4,0},{5,1},{6,2},{7,3},{8,12},{9,13},{10,... | collective-permute-start | bytes 1179656 | tf_op jit(solution)/shard_map/ppermute | solution.py:49
  172.7 15.5 %collective-permute-start.71 = (f32[2,4,128,128]{3,2,1,0:T(8,128)S(1)}, f32[2,4,128,128]{3,2,1,0:T(8,128)S(1)}, u32[]{:S(2)}, u32[]{:S(2)}) collective-permute-start(f32[2,4,128,128]{3,2,1,0:T(8,128)S(1)} %get-tuple-element.297), channel_id=1, source_target_pairs={{0,8},{1,9},{2,10},{3,11},{4,12},{5,13},{6,14},{7,15},{8,0},{9,1},... | collective-permute-start | bytes 1572872 | tf_op jit(solution)/shard_map/ppermute | solution.py:49
  173.8 14.4 %collective-permute-start.72 = (f32[2,4,128,128]{3,2,1,0:T(8,128)S(1)}, f32[2,4,128,128]{3,2,1,0:T(8,128)S(1)}, u32[]{:S(2)}, u32[]{:S(2)}) collective-permute-start(f32[2,4,128,128]{3,2,1,0:T(8,128)S(1)} %get-tuple-element.298), channel_id=1, source_target_pairs={{0,16},{1,17},{2,18},{3,19},{4,20},{5,21},{6,22},{7,23},{8,24},{9,... | collective-permute-start | bytes 1572872 | tf_op jit(solution)/shard_map/ppermute | solution.py:49
  201.4 16.5 %collective-permute-start.84 = (f32[1,4,128,128]{3,2,1,0:T(8,128)S(1)}, f32[1,4,128,128]{3,2,1,0:T(8,128)S(1)}, u32[]{:S(2)}, u32[]{:S(2)}) collective-permute-start(f32[1,4,128,128]{3,2,1,0:T(8,128)S(1)} %get-tuple-element.328), channel_id=1, source_target_pairs={{0,16},{1,17},{2,18},{3,19},{4,20},{5,21},{6,22},{7,23},{8,24},{9,... | collective-permute-start | bytes 786440 | tf_op jit(solution)/shard_map/ppermute | solution.py:49
  203.1 14.8 %collective-permute-start.85 = (f32[1,4,128,128]{3,2,1,0:T(8,128)S(1)}, f32[1,4,128,128]{3,2,1,0:T(8,128)S(1)}, u32[]{:S(2)}, u32[]{:S(2)}) collective-permute-start(f32[1,4,128,128]{3,2,1,0:T(8,128)S(1)} %get-tuple-element.329), channel_id=1, source_target_pairs={{0,8},{1,9},{2,10},{3,11},{4,12},{5,13},{6,14},{7,15},{8,0},{9,1},... | collective-permute-start | bytes 786440 | tf_op jit(solution)/shard_map/ppermute | solution.py:49
  216.1 8.3 %collective-permute-start.89 = (f32[192,512]{1,0:T(8,128)S(1)}, f32[192,512]{1,0:T(8,128)S(1)}, u32[]{:S(2)}, u32[]{:S(2)}) collective-permute-start(f32[192,512]{1,0:T(8,128)S(1)} %get-tuple-element.333.keep_ref), channel_id=1, source_target_pairs={{0,4},{1,5},{2,6},{3,7},{4,0},{5,1},{6,2},{7,3},{8,12},{9,13},{10,... | collective-permute-start | bytes 1179656 | tf_op jit(solution)/shard_map/ppermute | solution.py:49
  216.6 15.3 %collective-permute-start.90 = (f32[2,9,64,128]{3,2,1,0:T(8,128)S(1)}, f32[2,9,64,128]{3,2,1,0:T(8,128)S(1)}, u32[]{:S(2)}, u32[]{:S(2)}) collective-permute-start(f32[2,9,64,128]{3,2,1,0:T(8,128)S(1)} %get-tuple-element.337), channel_id=1, source_target_pairs={{0,1},{1,0},{2,3},{3,2},{4,5},{5,4},{6,7},{7,6},{8,9},{9,8},{10,11... | collective-permute-start | bytes 1769480 | tf_op jit(solution)/shard_map/ppermute | solution.py:49
  243.5 23.4 %collective-permute-start.101 = (f32[192,1024]{1,0:T(8,128)S(1)}, f32[192,1024]{1,0:T(8,128)S(1)}, u32[]{:S(2)}, u32[]{:S(2)}) collective-permute-start(f32[192,1024]{1,0:T(8,128)S(1)} %get-tuple-element.355), channel_id=1, source_target_pairs={{0,4},{1,5},{2,6},{3,7},{4,0},{5,1},{6,2},{7,3},{8,12},{9,13},{10,... | collective-permute-start | bytes 2359304 | tf_op jit(solution)/shard_map/ppermute | solution.py:49
  243.6 14.3 %collective-permute-start.95 = (f32[2,4,128,128]{3,2,1,0:T(8,128)S(1)}, f32[2,4,128,128]{3,2,1,0:T(8,128)S(1)}, u32[]{:S(2)}, u32[]{:S(2)}) collective-permute-start(f32[2,4,128,128]{3,2,1,0:T(8,128)S(1)} %get-tuple-element.350), channel_id=1, source_target_pairs={{0,8},{1,9},{2,10},{3,11},{4,12},{5,13},{6,14},{7,15},{8,0},{9,1},... | collective-permute-start | bytes 1572872 | tf_op jit(solution)/shard_map/ppermute | solution.py:49
  244.7 14.0 %collective-permute-start.96 = (f32[2,4,128,128]{3,2,1,0:T(8,128)S(1)}, f32[2,4,128,128]{3,2,1,0:T(8,128)S(1)}, u32[]{:S(2)}, u32[]{:S(2)}) collective-permute-start(f32[2,4,128,128]{3,2,1,0:T(8,128)S(1)} %get-tuple-element.351), channel_id=1, source_target_pairs={{0,16},{1,17},{2,18},{3,19},{4,20},{5,21},{6,22},{7,23},{8,24},{9,... | collective-permute-start | bytes 1572872 | tf_op jit(solution)/shard_map/ppermute | solution.py:49
  245.1 21.8 %collective-permute-start.100 = (f32[192,512]{1,0:T(8,128)S(1)}, f32[192,512]{1,0:T(8,128)S(1)}, u32[]{:S(2)}, u32[]{:S(2)}) collective-permute-start(f32[192,512]{1,0:T(8,128)S(1)} %copy-done.14), channel_id=1, source_target_pairs={{0,4},{1,5},{2,6},{3,7},{4,0},{5,1},{6,2},{7,3},{8,12},{9,13},{10,... | collective-permute-start | bytes 1179656 | tf_op jit(solution)/shard_map/ppermute | solution.py:49
  246.9 23.8 %collective-permute-start.103 = (f32[1,9,64,128]{3,2,1,0:T(8,128)S(1)}, f32[1,9,64,128]{3,2,1,0:T(8,128)S(1)}, u32[]{:S(2)}, u32[]{:S(2)}) collective-permute-start(f32[1,9,64,128]{3,2,1,0:T(8,128)S(1)} %slice_add_fusion.1), channel_id=1, source_target_pairs={{0,2},{1,3},{2,0},{3,1},{4,6},{5,7},{6,4},{7,5},{8,10},{9,11},{10,... | collective-permute-start | bytes 884744 | tf_op jit(solution)/shard_map/ppermute | solution.py:49
  268.3 15.3 %collective-permute-start.108 = (f32[2,4,128,128]{3,2,1,0:T(8,128)S(1)}, f32[2,4,128,128]{3,2,1,0:T(8,128)S(1)}, u32[]{:S(2)}, u32[]{:S(2)}) collective-permute-start(f32[2,4,128,128]{3,2,1,0:T(8,128)S(1)} %get-tuple-element.369), channel_id=1, source_target_pairs={{0,8},{1,9},{2,10},{3,11},{4,12},{5,13},{6,14},{7,15},{8,0},{9,1},... | collective-permute-start | bytes 1572872 | tf_op jit(solution)/shard_map/ppermute | solution.py:49
  269.4 14.2 %collective-permute-start.109 = (f32[2,4,128,128]{3,2,1,0:T(8,128)S(1)}, f32[2,4,128,128]{3,2,1,0:T(8,128)S(1)}, u32[]{:S(2)}, u32[]{:S(2)}) collective-permute-start(f32[2,4,128,128]{3,2,1,0:T(8,128)S(1)} %get-tuple-element.370), channel_id=1, source_target_pairs={{0,16},{1,17},{2,18},{3,19},{4,20},{5,21},{6,22},{7,23},{8,24},{9,... | collective-permute-start | bytes 1572872 | tf_op jit(solution)/shard_map/ppermute | solution.py:49
  287.2 8.5 %collective-permute-start.113 = (f32[1,256,128]{2,1,0:T(8,128)S(1)}, f32[1,256,128]{2,1,0:T(8,128)S(1)}, u32[]{:S(2)}, u32[]{:S(2)}) collective-permute-start(f32[1,256,128]{2,1,0:T(8,128)S(1)} %fusion.16), channel_id=1, source_target_pairs={{0,2},{1,3},{2,0},{3,1},{4,6},{5,7},{6,4},{7,5},{8,10},{9,11},{10,... | collective-permute-start | bytes 393224 | tf_op jit(solution)/shard_map/ppermute | solution.py:49
  303.9 14.9 %collective-permute-start.127 = (f32[2,9,64,128]{3,2,1,0:T(8,128)S(1)}, f32[2,9,64,128]{3,2,1,0:T(8,128)S(1)}, u32[]{:S(2)}, u32[]{:S(2)}) collective-permute-start(f32[2,9,64,128]{3,2,1,0:T(8,128)S(1)} %get-tuple-element.412), channel_id=1, source_target_pairs={{0,1},{1,0},{2,3},{3,2},{4,5},{5,4},{6,7},{7,6},{8,9},{9,8},{10,11... | collective-permute-start | bytes 1769480 | tf_op jit(solution)/shard_map/ppermute | solution.py:49
  305.3 12.6 %collective-permute-start.125 = (f32[1,4,128,128]{3,2,1,0:T(8,128)S(1)}, f32[1,4,128,128]{3,2,1,0:T(8,128)S(1)}, u32[]{:S(2)}, u32[]{:S(2)}) collective-permute-start(f32[1,4,128,128]{3,2,1,0:T(8,128)S(1)} %get-tuple-element.410), channel_id=1, source_target_pairs={{0,16},{1,17},{2,18},{3,19},{4,20},{5,21},{6,22},{7,23},{8,24},{9,... | collective-permute-start | bytes 786440 | tf_op jit(solution)/shard_map/ppermute | solution.py:49
  306.7 11.2 %collective-permute-start.126 = (f32[1,4,128,128]{3,2,1,0:T(8,128)S(1)}, f32[1,4,128,128]{3,2,1,0:T(8,128)S(1)}, u32[]{:S(2)}, u32[]{:S(2)}) collective-permute-start(f32[1,4,128,128]{3,2,1,0:T(8,128)S(1)} %get-tuple-element.411), channel_id=1, source_target_pairs={{0,8},{1,9},{2,10},{3,11},{4,12},{5,13},{6,14},{7,15},{8,0},{9,1},... | collective-permute-start | bytes 786440 | tf_op jit(solution)/shard_map/ppermute | solution.py:49
  316.2 14.7 %collective-permute-start.122 = (f32[2,4,128,128]{3,2,1,0:T(8,128)S(1)}, f32[2,4,128,128]{3,2,1,0:T(8,128)S(1)}, u32[]{:S(2)}, u32[]{:S(2)}) collective-permute-start(f32[2,4,128,128]{3,2,1,0:T(8,128)S(1)} %get-tuple-element.403), channel_id=1, source_target_pairs={{0,8},{1,9},{2,10},{3,11},{4,12},{5,13},{6,14},{7,15},{8,0},{9,1},... | collective-permute-start | bytes 1572872 | tf_op jit(solution)/shard_map/ppermute | solution.py:49
  317.2 13.7 %collective-permute-start.123 = (f32[2,4,128,128]{3,2,1,0:T(8,128)S(1)}, f32[2,4,128,128]{3,2,1,0:T(8,128)S(1)}, u32[]{:S(2)}, u32[]{:S(2)}) collective-permute-start(f32[2,4,128,128]{3,2,1,0:T(8,128)S(1)} %get-tuple-element.404), channel_id=1, source_target_pairs={{0,16},{1,17},{2,18},{3,19},{4,20},{5,21},{6,22},{7,23},{8,24},{9,... | collective-permute-start | bytes 1572872 | tf_op jit(solution)/shard_map/ppermute | solution.py:49
  319.0 11.8 %collective-permute-start.143 = (f32[2,256,128]{2,1,0:T(8,128)S(1)}, f32[2,256,128]{2,1,0:T(8,128)S(1)}, u32[]{:S(2)}, u32[]{:S(2)}) collective-permute-start(f32[2,256,128]{2,1,0:T(8,128)S(1)} %pad_maximum_fusion.11), channel_id=1, source_target_pairs={{0,1},{1,0},{2,3},{3,2},{4,5},{5,4},{6,7},{7,6},{8,9},{9,8},{10,11... | collective-permute-start | bytes 786440 | tf_op jit(solution)/shard_map/ppermute | solution.py:49
  319.8 27.0 %collective-permute-start.135 = (f32[1,9,64,128]{3,2,1,0:T(8,128)S(1)}, f32[1,9,64,128]{3,2,1,0:T(8,128)S(1)}, u32[]{:S(2)}, u32[]{:S(2)}) collective-permute-start(f32[1,9,64,128]{3,2,1,0:T(8,128)S(1)} %slice_add_fusion), channel_id=1, source_target_pairs={{0,2},{1,3},{2,0},{3,1},{4,6},{5,7},{6,4},{7,5},{8,10},{9,11},{10,... | collective-permute-start | bytes 884744 | tf_op jit(solution)/shard_map/ppermute | solution.py:49
  330.8 16.0 %collective-permute-start.144 = (f32[1,256,128]{2,1,0:T(8,128)S(1)}, f32[1,256,128]{2,1,0:T(8,128)S(1)}, u32[]{:S(2)}, u32[]{:S(2)}) collective-permute-start(f32[1,256,128]{2,1,0:T(8,128)S(1)} %slice_add_fusion.18), channel_id=1, source_target_pairs={{0,2},{1,3},{2,0},{3,1},{4,6},{5,7},{6,4},{7,5},{8,10},{9,11},{10,... | collective-permute-start | bytes 393224 | tf_op jit(solution)/shard_map/ppermute | solution.py:49
  332.3 9.3 %collective-permute-start.129 = (f32[1,4,128,128]{3,2,1,0:T(8,128)S(1)}, f32[1,4,128,128]{3,2,1,0:T(8,128)S(1)}, u32[]{:S(2)}, u32[]{:S(2)}) collective-permute-start(f32[1,4,128,128]{3,2,1,0:T(8,128)S(1)} %get-tuple-element.424), channel_id=1, source_target_pairs={{0,8},{1,9},{2,10},{3,11},{4,12},{5,13},{6,14},{7,15},{8,0},{9,1},... | collective-permute-start | bytes 786440 | tf_op jit(solution)/shard_map/ppermute | solution.py:49
  333.5 11.0 %collective-permute-start.132 = (f32[1,4,128,128]{3,2,1,0:T(8,128)S(1)}, f32[1,4,128,128]{3,2,1,0:T(8,128)S(1)}, u32[]{:S(2)}, u32[]{:S(2)}) collective-permute-start(f32[1,4,128,128]{3,2,1,0:T(8,128)S(1)} %get-tuple-element.510), channel_id=1, source_target_pairs={{0,8},{1,9},{2,10},{3,11},{4,12},{5,13},{6,14},{7,15},{8,0},{9,1},... | collective-permute-start | bytes 786440 | tf_op jit(solution)/shard_map/ppermute | solution.py:49
  341.7 9.8 %collective-permute-start.130 = (f32[2,256,128]{2,1,0:T(8,128)S(1)}, f32[2,256,128]{2,1,0:T(8,128)S(1)}, u32[]{:S(2)}, u32[]{:S(2)}) collective-permute-start(f32[2,256,128]{2,1,0:T(8,128)S(1)} %pad_maximum_fusion.9), channel_id=1, source_target_pairs={{0,1},{1,0},{2,3},{3,2},{4,5},{5,4},{6,7},{7,6},{8,9},{9,8},{10,11... | collective-permute-start | bytes 786440 | tf_op jit(solution)/shard_map/ppermute | solution.py:49
  344.6 11.4 %collective-permute-start.133 = (f32[2,256,128]{2,1,0:T(8,128)S(1)}, f32[2,256,128]{2,1,0:T(8,128)S(1)}, u32[]{:S(2)}, u32[]{:S(2)}) collective-permute-start(f32[2,256,128]{2,1,0:T(8,128)S(1)} %pad_maximum_fusion.10), channel_id=1, source_target_pairs={{0,1},{1,0},{2,3},{3,2},{4,5},{5,4},{6,7},{7,6},{8,9},{9,8},{10,11... | collective-permute-start | bytes 786440 | tf_op jit(solution)/shard_map/ppermute | solution.py:49
  347.0 17.6 %collective-permute-start.145 = (f32[1088,128]{1,0:T(8,128)S(1)}, f32[1088,128]{1,0:T(8,128)}, u32[]{:S(2)}, u32[]{:S(2)}) collective-permute-start(f32[1088,128]{1,0:T(8,128)S(1)} %pad_maximum_fusion.3.refs_8_), channel_id=1, source_target_pairs={{0,8},{1,9},{2,10},{3,11},{4,12},{5,13},{6,14},{7,15},{8,0},{9,1},... | collective-permute-start | bytes 1671176 | tf_op jit(solution)/shard_map/ppermute | solution.py:49
  348.0 19.0 %collective-permute-start.146 = (f32[1088,128]{1,0:T(8,128)S(1)}, f32[1088,128]{1,0:T(8,128)S(1)}, u32[]{:S(2)}, u32[]{:S(2)}) collective-permute-start(f32[1088,128]{1,0:T(8,128)S(1)} %pad_maximum_fusion.3.refs_8_), channel_id=1, source_target_pairs={{0,16},{1,17},{2,18},{3,19},{4,20},{5,21},{6,22},{7,23},{8,24},{9,... | collective-permute-start | bytes 1671176 | tf_op jit(solution)/shard_map/ppermute | solution.py:49
  348.9 26.1 %collective-permute-start.147 = (f32[1088,128]{1,0:T(8,128)S(1)}, f32[1088,128]{1,0:T(8,128)}, u32[]{:S(2)}, u32[]{:S(2)}) collective-permute-start(f32[1088,128]{1,0:T(8,128)S(1)} %pad_maximum_fusion.3.refs_8_), channel_id=1, source_target_pairs={{0,24},{1,25},{2,26},{3,27},{4,28},{5,29},{6,30},{7,31},{8,16},{9,... | collective-permute-start | bytes 1671176 | tf_op jit(solution)/shard_map/ppermute | solution.py:49
  351.6 7.9 %collective-permute-start.131 = (f32[1,256,128]{2,1,0:T(8,128)S(1)}, f32[1,256,128]{2,1,0:T(8,128)S(1)}, u32[]{:S(2)}, u32[]{:S(2)}) collective-permute-start(f32[1,256,128]{2,1,0:T(8,128)S(1)} %slice_add_fusion.28), channel_id=1, source_target_pairs={{0,2},{1,3},{2,0},{3,1},{4,6},{5,7},{6,4},{7,5},{8,10},{9,11},{10,... | collective-permute-start | bytes 393224 | tf_op jit(solution)/shard_map/ppermute | solution.py:49
  363.5 23.1 %collective-permute-start.136 = (f32[1088,128]{1,0:T(8,128)S(1)}, f32[1088,128]{1,0:T(8,128)}, u32[]{:S(2)}, u32[]{:S(2)}) collective-permute-start(f32[1088,128]{1,0:T(8,128)S(1)} %pad_maximum_fusion.2.refs_0_), channel_id=1, source_target_pairs={{0,8},{1,9},{2,10},{3,11},{4,12},{5,13},{6,14},{7,15},{8,0},{9,1},... | collective-permute-start | bytes 1671176 | tf_op jit(solution)/shard_map/ppermute | solution.py:49
  364.5 29.6 %collective-permute-start.148 = (f32[1088,128]{1,0:T(8,128)S(1)}, f32[1088,128]{1,0:T(8,128)}, u32[]{:S(2)}, u32[]{:S(2)}) collective-permute-start(f32[1088,128]{1,0:T(8,128)S(1)} %pad_maximum_fusion.3.refs_8_), channel_id=1, source_target_pairs={{0,4},{1,5},{2,6},{3,7},{4,0},{5,1},{6,2},{7,3},{8,12},{9,13},{10,... | collective-permute-start | bytes 1671176 | tf_op jit(solution)/shard_map/ppermute | solution.py:49
  364.6 30.0 %collective-permute-start.139 = (f32[1088,128]{1,0:T(8,128)S(1)}, f32[1088,128]{1,0:T(8,128)}, u32[]{:S(2)}, u32[]{:S(2)}) collective-permute-start(f32[1088,128]{1,0:T(8,128)S(1)} %pad_maximum_fusion.2.refs_0_), channel_id=1, source_target_pairs={{0,4},{1,5},{2,6},{3,7},{4,0},{5,1},{6,2},{7,3},{8,12},{9,13},{10,... | collective-permute-start | bytes 1671176 | tf_op jit(solution)/shard_map/ppermute | solution.py:49
  367.1 27.6 %collective-permute-start.138 = (f32[1088,128]{1,0:T(8,128)S(1)}, f32[1088,128]{1,0:T(8,128)}, u32[]{:S(2)}, u32[]{:S(2)}) collective-permute-start(f32[1088,128]{1,0:T(8,128)S(1)} %pad_maximum_fusion.2.refs_0_), channel_id=1, source_target_pairs={{0,24},{1,25},{2,26},{3,27},{4,28},{5,29},{6,30},{7,31},{8,16},{9,... | collective-permute-start | bytes 1671176 | tf_op jit(solution)/shard_map/ppermute | solution.py:49
  375.0 21.3 %collective-permute-start.137 = (f32[1088,128]{1,0:T(8,128)S(1)}, f32[1088,128]{1,0:T(8,128)}, u32[]{:S(2)}, u32[]{:S(2)}) collective-permute-start(f32[1088,128]{1,0:T(8,128)S(1)} %pad_maximum_fusion.2.refs_0_), channel_id=1, source_target_pairs={{0,16},{1,17},{2,18},{3,19},{4,20},{5,21},{6,22},{7,23},{8,24},{9,... | collective-permute-start | bytes 1671176 | tf_op jit(solution)/shard_map/ppermute | solution.py:49
  386.6 9.7 %collective-permute-start.149 = (f32[1088,128]{1,0:T(8,128)}, f32[1088,128]{1,0:T(8,128)}, u32[]{:S(2)}, u32[]{:S(2)}) collective-permute-start(f32[1088,128]{1,0:T(8,128)} %collective-permute-done.145.refs_9_), channel_id=1, source_target_pairs={{0,4},{1,5},{2,6},{3,7},{4,0},{5,1},{6,2},{7,3},{8,12},{9,13},{10,... | collective-permute-start | bytes 1671176 | tf_op jit(solution)/shard_map/ppermute | solution.py:49
  (149 other events, 947.8 us)

commit v7 on v6

--- a/solution.py
+++ b/solution.py
@@ -570,14 +570,16 @@
     return (value - pick(mr_ref, k, stream, 0)) * pick(mr_ref, k, stream, 1)
 
 
-def join_stage(number, exp, members, table, act, mask, w_reduce):
+def join_stage(number, me, nz, exp, members, table, act, mask, w_reduce):
     rows, d_in = exp.shape
     mid = w_reduce.shape[2]
     size = len(members)
 
-    def body(exp_ref, table_ref, act_ref, mask_ref, w_ref, *refs):
+    deep = d_in // nz // 2
+
+    def body(me_ref, exp_ref, table_ref, act_ref, mask_ref, w_ref, *refs):
         gain_ref, bias_ref = out_rows(table_ref, number - 1)
-        got, (mr_ref, out_ref, low_ref, red_ref, stats_ref) = refs[:size], refs[size:]
+        got, (mr_ref, out_ref, keep_ref, send_ref, red_ref, stats_ref, low_ref) = refs[:size], refs[size:]
         k = pl.program_id(0)
 
         @pl.when(k == 0)
@@ -593,6 +595,10 @@
             out = z * sigmoid(z) * mask_ref[lo:hi, :]
             out_ref[lo:hi, :] = out
             low_ref[lo:hi, :] = rounded(out)
+        for j in range(CH // 2 // deep):
+            for ref, core in ((keep_ref, me_ref[0]), (send_ref, 1 - me_ref[0])):
+                at = pl.ds(pl.multiple_of((2 * j + core) * deep, 128), deep)
+                ref[:, j * deep : (j + 1) * deep] = low_ref[:, at]
         part = dot(low_ref[...].astype(BF), w_ref[0])
 
         @pl.when(k == 0)
@@ -611,6 +617,7 @@
         body,
         d_in // CH,
         [
+            smem(),
             cols(rows),
             cols(table.shape[0]),
             cols(rows),
@@ -618,12 +625,13 @@
             pl.BlockSpec((1, CH, mid), lambda k: (number, k, 0)),
         ]
         + [full(payload(d_in))] * size,
-        [full((8, d_in)), cols(rows), cols(rows), full((rows, mid)), full(payload(mid))],
-        [near((8, d_in)), far((rows, d_in)), far((rows, d_in)), near((rows, mid)), near(payload(mid))],
+        [full((8, d_in)), cols(rows)] + [pl.BlockSpec((rows, CH // 2), lambda k: (0, k))] * 2 + [full((rows, mid)), full(payload(mid))],
+        [near((8, d_in))] + [far((rows, d_in))] + [far((rows, d_in // 2))] * 2 + [near((rows, mid)), near(payload(mid))],
+        [pltpu.VMEM((rows, CH), F32)],
         name="join_stage",
         flops=2 * rows * d_in * mid,
         transcendentals=rows * d_in,
-    )(exp, table, act, mask, w_reduce, *members)
+    )(me, exp, table, act, mask, w_reduce, *members)
 
 
 def put_places(value, image_ref, tile_ref):
@@ -1240,7 +1248,6 @@
     mask, red, stats = reduce_first(start, w_reduce, map_sizes)
     grad_images, grad_tiles, stats = lax.optimization_barrier((grad_images, grad_tiles, stats))
     grad = to_rows(grad_images, grad_tiles, rows)
-    low = start
     for b in range(BLOCKS):
         reds.append(red)
         mr, keep, send, spa, stats = spatial_stage(
@@ -1251,7 +1258,7 @@
             stats, grad = lax.optimization_barrier((stats, grad))
         hid1.append([])
         bulk.add(("h", b), collect.hidden(keep, send, hid1[b]))
-        keep, send = core_halves(low, core, nz)
+        keep, send = core_halves(start, core, nz) if b == 0 else (low_keep, low_send)
         peer = grid.swap(send, dc=1)
         stats, keep, peer = lax.optimization_barrier((stats, keep, peer))
         lows.append((keep, peer))
@@ -1264,8 +1271,8 @@
         exp = away(exp)
         exps.append(exp)
         if b + 1 < BLOCKS:
-            mr, out, low, red, stats = join_stage(
-                b + 1, exp, moments(stats), outer, acts[b], mask, w_reduce
+            mr, out, low_keep, low_send, red, stats = join_stage(
+                b + 1, me, nz, exp, moments(stats), outer, acts[b], mask, w_reduce
             )
             mr3.append(mr)
             acts.append(away(out))

time: 410 us -> 405 us (0.988)
  transfers between devices with their start and end apart: 152 -> 152, of which waited for: 89 -> 92; matrix products, arithmetic and copies ran while one was open for 3% -> 4% of each run, Pallas kernels for 12% -> 12%
where the time goes in v7:
time: 405 us; the launch traced here: 404 us
  starting transfers between devices  160 us (40%)
  waiting for transfers between devices  142 us (35%)
  Pallas kernels  79.9 us (20%)
  local copies, waits for them, and re-layouts  13.8 us (3%)
  other arithmetic  6.77 us (2%)
    ppermute x152, starting transfers between devices, swap(): return lax.ppermute(value, AXES, pairs)  160 us
    ppermute x152, waiting for transfers between devices, swap(): return lax.ppermute(value, AXES, pairs)  142 us
    pallas_call x2, Pallas kernels, back_spatial(): call(body, 3, [smem(), full((rows, mid)), full((rows, mid)), full((8, mid...  10.5 us
    pallas_call x2, Pallas kernels, back_expand(): call(body, d_in // CH, [smem(), cols(rows), cols(rows), full((8, d_in)),...  9.37 us
    pallas_call x2, Pallas kernels, spatial_stage(): call(body, 3, [full((rows, mid)), full(table.shape), full((rows, 1)), pl....  9.28 us
    pallas_call x2, Pallas kernels, expand_stage(): call(body, d_in // CH, [full((rows, mid)), full(table.shape), full((rows,...  8.74 us
  transfers between devices with their start and end apart: 152, of which 92 were waited for; matrix products, arithmetic and copies ran while one was open for 4% of the time, Pallas kernels for 12%

profile of v7, /device:TPU:0, one launch (start us, length us, event | category | flops | bytes accessed | tf_op | source)
XLA Modules:
  0.0 404.3 jit_solution(16759157905923932819)
XLA Ops:
  3.6 3.4 reduce_first.1
  11.5 4.0 collective-permute-start.3
  17.1 2.0 collective-permute-done.2
  19.6 3.7 collective-permute-start.6
  25.2 2.7 collective-permute-done.5.refs_2_
  27.9 4.6 %spatial_stage.2 = (f32[8,512]{1,0:T(8,128)S(1)}, f32[192,256]{1,0:T(8,128)S(1)}, f32[192,256]{1,0:T(8,128)S(1)}, f32[192,512]{1,0:T(8,128)S(1)}, f32[3,8,128]{2,1,0:T(8,128)S(1)}) custom-call(f32[192,512]{1,0:T(8,128)S(1)} %get-tuple-element.233.red_ref, f32[8,512]{1,0:T(8,128)S(1)} %pad_maximum_fusion.19.table_ref, ...), custom_call_target="tpu_custom_call" | custom-call | tf_op jit(solution)/shard_map/spatial_stage/pallas_call | solution.py:492
  42.1 2.3 collective-permute-start.13
  47.4 4.4 %expand_stage.2 = (f32[8,512]{1,0:T(8,128)S(1)}, f32[192,512]{1,0:T(8,128)S(1)}, f32[192,2048]{1,0:T(8,128)}, f32[3,32,128]{2,1,0:T(8,128)S(1)}) custom-call(f32[192,512]{1,0:T(8,128)S(1)} %get-tuple-element.237.spa_ref, f32[8,512]{1,0:T(8,128)S(1)} %pad_maximum_fusion.19.table_ref, f32[192,1]{1,0:T(8,128)S(1)} %get-tuple-element.234.mask_ref, ...), custom_call_target="tpu_custom_call" | custom-call | tf_op jit(solution)/shard_map/expand_stage/pallas_call | solution.py:548
  65.5 2.6 collective-permute-start.24
  70.7 5.3 %join_stage.1 = (f32[8,2048]{1,0:T(8,128)S(1)}, f32[192,2048]{1,0:T(8,128)}, f32[192,1024]{1,0:T(8,128)}, f32[192,1024]{1,0:T(8,128)}, f32[192,512]{1,0:T(8,128)S(1)}, /*index=5*/f32[3,8,128]{2,1,0:T(8,128)S(1)}) custom-call(s32[4]{0:T(128)S(1)} %pad_add_fusion.me_ref, f32[192,2048]{1,0:T(8,128)} %get-tuple-element.246.exp_ref, ...), custom_call_target="tpu_custom_call" | custom-call | tf_op jit(solution)/shard_map/join_stage/pallas_call | solution.py:616
  90.7 4.6 %spatial_stage.3 = (f32[8,512]{1,0:T(8,128)S(1)}, f32[192,256]{1,0:T(8,128)S(1)}, f32[192,256]{1,0:T(8,128)S(1)}, f32[192,512]{1,0:T(8,128)S(1)}, f32[3,8,128]{2,1,0:T(8,128)S(1)}) custom-call(f32[192,512]{1,0:T(8,128)S(1)} %get-tuple-element.257.red_ref, f32[8,512]{1,0:T(8,128)S(1)} %pad_maximum_fusion.19.table_ref, ...), custom_call_target="tpu_custom_call" | custom-call | tf_op jit(solution)/shard_map/spatial_stage/pallas_call | solution.py:492
  110.2 4.4 %expand_stage.3 = (f32[8,512]{1,0:T(8,128)S(1)}, f32[192,512]{1,0:T(8,128)S(1)}, f32[192,2048]{1,0:T(8,128)}, f32[3,32,128]{2,1,0:T(8,128)S(1)}) custom-call(f32[192,512]{1,0:T(8,128)S(1)} %get-tuple-element.259.spa_ref, f32[8,512]{1,0:T(8,128)S(1)} %pad_maximum_fusion.19.table_ref, f32[192,1]{1,0:T(8,128)S(1)} %get-tuple-element.234.mask_ref, ...), custom_call_target="tpu_custom_call" | custom-call | tf_op jit(solution)/shard_map/expand_stage/pallas_call | solution.py:548
  127.5 2.4 collective-permute-start.51
  132.5 4.7 %turn_stage.1 = (f32[8,2048]{1,0:T(8,128)S(1)}, f32[98,2048]{1,0:T(8,128)}, f32[72,2048]{1,0:T(8,128)}, f32[192,2048]{1,0:T(8,128)}, f32[2,32,128]{2,1,0:T(8,128)S(1)}) custom-call(f32[192,2048]{1,0:T(8,128)} %get-tuple-element.267.exp_ref, f32[4,2048]{1,0:T(4,128)S(1)} %pad_maximum_fusion.18.table_ref.outer_ref, f32[192,2048]{1,0:T(8,128)} %get-tuple-element.268.act_ref, ...), custom_call_target="tpu_custom_call" | custom-call | tf_op jit(solution)/shard_map/turn_stage/pallas_call | solution.py:674
  138.3 2.0 collective-permute-start.57
  144.7 2.0 collective-permute-start.60
  151.9 4.7 %back_expand.2 = (f32[2,2048]{1,0:T(2,128)S(1)}, f32[192,1024]{1,0:T(8,128)S(1)}, f32[192,1024]{1,0:T(8,128)S(1)}, f32[192,512]{1,0:T(8,128)S(1)}, f32[2,8,128]{2,1,0:T(8,128)S(1)}) custom-call(s32[4]{0:T(128)S(1)} %pad_add_fusion.me_ref, f32[192,2048]{1,0:T(8,128)} %get-tuple-element.283.pre3_ref, f32[192,2048]{1,0:T(8,128)} %get-tuple-element.267.exp_ref, ...), custom_call_target="tpu_custom_call" | custom-call | tf_op jit(solution)/shard_map/back_expand/pallas_call | solution.py:758
  157.3 2.3 collective-permute-done.61
  159.6 2.1 collective-permute-start.64
  176.2 5.2 %back_spatial.2 = (f32[2,512]{1,0:T(2,128)S(1)}, f32[192,128]{1,0:T(8,128)S(1)}, f32[192,128]{1,0:T(8,128)S(1)}, f32[192,128]{1,0:T(8,128)S(1)}, f32[192,128]{1,...) custom-call(s32[4]{0:T(128)S(1)} %pad_add_fusion.me_ref, f32[192,512]{1,0:T(8,128)S(1)} %get-tuple-element.287.pre2_ref, ...), custom_call_target="tpu_custom_call" | custom-call | tf_op jit(solution)/shard_map/back_spatial/pallas_call | solution.py:825
  190.2 2.1 collective-permute-start.78
  203.0 2.2 weight_spatial.2
  205.3 5.2 %back_reduce.1 = (f32[2,512]{1,0:T(2,128)S(1)}, f32[192,512]{1,0:T(8,128)S(1)}, f32[192,2048]{1,0:T(8,128)}, f32[2,32,128]{2,1,0:T(8,128)S(1)}) custom-call(f32[192,512]{1,0:T(8,128)S(1)} %get-tuple-element.296.pre1_ref, f32[192,512]{1,0:T(8,128)S(1)} %get-tuple-element.257.red_ref, f32[8,512]{1,0:T(8,128)S(1)} %get-tuple-element.288.mr1_ref, ...), custom_call_target="tpu_custom_call" | custom-call | tf_op jit(solution)/shard_map/back_reduce/pallas_call | solution.py:914
  220.3 6.0 %collective-permute-done.90 = f32[2,9,64,128]{3,2,1,0:T(8,128)S(1)} collective-permute-done((f32[2,9,64,128]{3,2,1,0:T(8,128)S(1)}, f32[2,9,64,128]{3,2,1,0:T(8,128)S(1)}, u32[]{:S(2)}, u32[]{:S(2)}) %collective-permute-start.90) | collective-permute-done | bytes 589856 | tf_op jit(solution)/shard_map/ppermute | solution.py:49
  233.4 4.6 %back_expand.3 = (f32[2,2048]{1,0:T(2,128)S(1)}, f32[192,1024]{1,0:T(8,128)S(1)}, f32[192,1024]{1,0:T(8,128)S(1)}, f32[192,512]{1,0:T(8,128)S(1)}, f32[2,8,128]{2,1,0:T(8,128)S(1)}) custom-call(s32[4]{0:T(128)S(1)} %pad_add_fusion.me_ref, f32[192,2048]{1,0:T(8,128)} %get-tuple-element.327.pre3_ref, f32[192,2048]{1,0:T(8,128)} %get-tuple-element.246.exp_ref, ...), custom_call_target="tpu_custom_call" | custom-call | tf_op jit(solution)/shard_map/back_expand/pallas_call | solution.py:758
  243.0 9.5 %collective-permute-done.95 = f32[2,4,128,128]{3,2,1,0:T(8,128)S(1)} collective-permute-done((f32[2,4,128,128]{3,2,1,0:T(8,128)S(1)}, f32[2,4,128,128]{3,2,1,0:T(8,128)S(1)}, u32[]{:S(2)}, u32[]{:S(2)}) %collective-permute-start.95) | collective-permute-done | bytes 524320 | tf_op jit(solution)/shard_map/ppermute | solution.py:49
  255.7 2.1 collective-permute-done.99
  271.7 5.4 %back_spatial.3 = (f32[2,512]{1,0:T(2,128)S(1)}, f32[192,128]{1,0:T(8,128)S(1)}, f32[192,128]{1,0:T(8,128)S(1)}, f32[192,128]{1,0:T(8,128)S(1)}, f32[192,128]{1,...) custom-call(s32[4]{0:T(128)S(1)} %pad_add_fusion.me_ref, f32[192,512]{1,0:T(8,128)S(1)} %get-tuple-element.349.pre2_ref, ...), custom_call_target="tpu_custom_call" | custom-call | tf_op jit(solution)/shard_map/back_spatial/pallas_call | solution.py:825
  281.9 2.1 collective-permute-start.113
  288.0 2.4 collective-permute-done.113
  291.8 2.0 collective-permute-start.119
  296.3 2.7 weight_spatial.3
  302.4 4.6 %back_reduce_last.1 = (f32[2,512]{1,0:T(2,128)S(1)}, f32[192,512]{1,0:T(8,128)S(1)}, f32[98,2048]{1,0:T(8,128)}, f32[72,2048]{1,0:T(8,128)}) custom-call(f32[192,512]{1,0:T(8,128)S(1)} %get-tuple-element.369.pre1_ref, f32[192,512]{1,0:T(8,128)S(1)} %get-tuple-element.233.red_ref, f32[8,512]{1,0:T(8,128)S(1)} %get-tuple-element.350.mr1_ref, ...), custom_call_target="tpu_custom_call" | custom-call | tf_op jit(solution)/shard_map/back_reduce_last/pallas_call | solution.py:890
  308.7 2.1 weight_reduce.3
  316.8 9.1 %collective-permute-done.143 = f32[2,256,128]{2,1,0:T(8,128)S(1)} collective-permute-done((f32[2,256,128]{2,1,0:T(8,128)S(1)}, f32[2,256,128]{2,1,0:T(8,128)S(1)}, u32[]{:S(2)}, u32[]{:S(2)}) %collective-permute-start.143) | collective-permute-done | bytes 262176 | tf_op jit(solution)/shard_map/ppermute | solution.py:49
  329.7 3.2 collective-permute-done.128
  334.3 2.5 collective-permute-done.129
  336.9 2.3 collective-permute-start.130
  339.8 2.2 collective-permute-start.133
  346.8 2.0 collective-permute-start.131
  348.9 2.3 collective-permute-done.133
  351.2 2.3 collective-permute-start.134
  354.7 3.8 collective-permute-done.134
  360.3 2.1 collective-permute-done.146.refs_10_
  362.4 7.7 %collective-permute-done.147.refs_11_ = f32[1088,128]{1,0:T(8,128)} collective-permute-done((f32[1088,128]{1,0:T(8,128)S(1)}, f32[1088,128]{1,0:T(8,128)}, u32[]{:S(2)}, u32[]{:S(2)}) %collective-permute-start.147) | collective-permute-done | bytes 557088 | tf_op jit(solution)/shard_map/ppermute | solution.py:49
  371.3 10.5 %collective-permute-done.136.refs_1_ = f32[1088,128]{1,0:T(8,128)} collective-permute-done((f32[1088,128]{1,0:T(8,128)S(1)}, f32[1088,128]{1,0:T(8,128)}, u32[]{:S(2)}, u32[]{:S(2)}) %collective-permute-start.136) | collective-permute-done | bytes 557088 | tf_op jit(solution)/shard_map/ppermute | solution.py:49
  384.2 2.3 reshape.145
  396.3 7.8 %place_slices.1 = (f32[2,512,512]{2,1,0:T(8,128)}, f32[2,9,128,512]{3,2,1,0:T(8,128)}, f32[2,128,2048]{2,1,0:T(8,128)}) custom-call(s32[4]{0:T(128)S(1)} %pad_add_fusion.me_ref, f32[1088,128]{1,0:T(8,128)} %copy-done.10, f32[1088,128]{1,0:T(8,128)} %collective-permute-done.136.refs_1_, f32[1088,128]{1,0:T(8,128)} %collective-permute-done.137.refs_2_, ...), custom_call_target="tpu_custom_call" | custom-call | tf_op jit(solution)/shard_map/place_slices/pallas_call | solution.py:1161
  (444 shorter events, 220.0 us)
Async XLA Ops:
  8.6 24.0 %collective-permute-start.7 = (f32[192,1024]{1,0:T(8,128)}, f32[192,1024]{1,0:T(8,128)}, u32[]{:S(2)}, u32[]{:S(2)}) collective-permute-start(f32[192,1024]{1,0:T(8,128)} %get-tuple-element.507), channel_id=1, source_target_pairs={{0,4},{1,5},{2,6},{3,7},{4,0},{5,1},{6,2},{7,3},{8,12},{9,13},{10,... | collective-permute-start | bytes 2359304 | tf_op jit(solution)/shard_map/ppermute | solution.py:49
  39.9 7.5 %collective-permute-start.15 = (f32[3,8,128]{2,1,0:T(8,128)S(1)}, f32[3,8,128]{2,1,0:T(8,128)S(1)}, u32[]{:S(2)}, u32[]{:S(2)}) collective-permute-start(f32[3,8,128]{2,1,0:T(8,128)S(1)} %pad_maximum_fusion.25.refs_0_), channel_id=1, source_target_pairs={{0,3},{1,2},{2,1},{3,0},{4,7},{5,6},{6,5},{7,4},{8,11},{9,10},{10,... | collective-permute-start | bytes 36872 | tf_op jit(solution)/shard_map/ppermute | solution.py:49
  44.3 9.0 %collective-permute-start.17 = (f32[384,256]{1,0:T(8,128)S(1)}, f32[384,256]{1,0:T(8,128)S(1)}, u32[]{:S(2)}, u32[]{:S(2)}) collective-permute-start(f32[384,256]{1,0:T(8,128)S(1)} %constant_dynamic-update-slice_fusion.h0), channel_id=1, source_target_pairs={{0,8},{1,9},{2,10},{3,11},{4,12},{5,13},{6,14},{7,15},{8,0},{9,1},... | collective-permute-start | bytes 1179656 | tf_op jit(solution)/shard_map/ppermute | solution.py:49
  45.8 8.4 %collective-permute-start.18 = (f32[384,256]{1,0:T(8,128)S(1)}, f32[384,256]{1,0:T(8,128)S(1)}, u32[]{:S(2)}, u32[]{:S(2)}) collective-permute-start(f32[384,256]{1,0:T(8,128)S(1)} %constant_dynamic-update-slice_fusion.h0), channel_id=1, source_target_pairs={{0,16},{1,17},{2,18},{3,19},{4,20},{5,21},{6,22},{7,23},{8,24},{9,... | collective-permute-start | bytes 1179656 | tf_op jit(solution)/shard_map/ppermute | solution.py:49
  60.7 7.5 %collective-permute-start.22 = (f32[192,256]{1,0:T(8,128)}, f32[192,256]{1,0:T(8,128)}, u32[]{:S(2)}, u32[]{:S(2)}) collective-permute-start(f32[192,256]{1,0:T(8,128)} %slice.776), channel_id=1, source_target_pairs={{0,16},{1,17},{2,18},{3,19},{4,20},{5,21},{6,22},{7,23},{8,24},{9,... | collective-permute-start | bytes 589832 | tf_op jit(solution)/shard_map/ppermute | solution.py:49
  76.0 19.4 %collective-permute-start.34 = (f32[192,1024]{1,0:T(8,128)}, f32[192,1024]{1,0:T(8,128)S(1)}, u32[]{:S(2)}, u32[]{:S(2)}) collective-permute-start(f32[192,1024]{1,0:T(8,128)} %get-tuple-element.262), channel_id=1, source_target_pairs={{0,4},{1,5},{2,6},{3,7},{4,0},{5,1},{6,2},{7,3},{8,12},{9,13},{10,... | collective-permute-start | bytes 2359304 | tf_op jit(solution)/shard_map/ppermute | solution.py:49
  107.9 8.7 %collective-permute-start.44 = (f32[384,256]{1,0:T(8,128)S(1)}, f32[384,256]{1,0:T(8,128)S(1)}, u32[]{:S(2)}, u32[]{:S(2)}) collective-permute-start(f32[384,256]{1,0:T(8,128)S(1)} %constant_dynamic-update-slice_fusion.2.h0), channel_id=1, source_target_pairs={{0,8},{1,9},{2,10},{3,11},{4,12},{5,13},{6,14},{7,15},{8,0},{9,1},... | collective-permute-start | bytes 1179656 | tf_op jit(solution)/shard_map/ppermute | solution.py:49
  108.7 8.7 %collective-permute-start.45 = (f32[384,256]{1,0:T(8,128)S(1)}, f32[384,256]{1,0:T(8,128)S(1)}, u32[]{:S(2)}, u32[]{:S(2)}) collective-permute-start(f32[384,256]{1,0:T(8,128)S(1)} %constant_dynamic-update-slice_fusion.2.h0), channel_id=1, source_target_pairs={{0,16},{1,17},{2,18},{3,19},{4,20},{5,21},{6,22},{7,23},{8,24},{9,... | collective-permute-start | bytes 1179656 | tf_op jit(solution)/shard_map/ppermute | solution.py:49
  156.6 9.1 %collective-permute-start.66 = (f32[192,1024]{1,0:T(8,128)S(1)}, f32[192,1024]{1,0:T(8,128)S(1)}, u32[]{:S(2)}, u32[]{:S(2)}) collective-permute-start(f32[192,1024]{1,0:T(8,128)S(1)} %get-tuple-element.292), channel_id=1, source_target_pairs={{0,4},{1,5},{2,6},{3,7},{4,0},{5,1},{6,2},{7,3},{8,12},{9,13},{10,... | collective-permute-start | bytes 2359304 | tf_op jit(solution)/shard_map/ppermute | solution.py:49
  156.7 9.0 %collective-permute-start.65 = (f32[192,512]{1,0:T(8,128)S(1)}, f32[192,512]{1,0:T(8,128)S(1)}, u32[]{:S(2)}, u32[]{:S(2)}) collective-permute-start(f32[192,512]{1,0:T(8,128)S(1)} %get-tuple-element.290.own_ref), channel_id=1, source_target_pairs={{0,4},{1,5},{2,6},{3,7},{4,0},{5,1},{6,2},{7,3},{8,12},{9,13},{10,... | collective-permute-start | bytes 1179656 | tf_op jit(solution)/shard_map/ppermute | solution.py:49
  167.1 15.5 %collective-permute-start.71 = (f32[2,4,128,128]{3,2,1,0:T(8,128)S(1)}, f32[2,4,128,128]{3,2,1,0:T(8,128)S(1)}, u32[]{:S(2)}, u32[]{:S(2)}) collective-permute-start(f32[2,4,128,128]{3,2,1,0:T(8,128)S(1)} %get-tuple-element.299), channel_id=1, source_target_pairs={{0,8},{1,9},{2,10},{3,11},{4,12},{5,13},{6,14},{7,15},{8,0},{9,1},... | collective-permute-start | bytes 1572872 | tf_op jit(solution)/shard_map/ppermute | solution.py:49
  168.1 14.5 %collective-permute-start.72 = (f32[2,4,128,128]{3,2,1,0:T(8,128)S(1)}, f32[2,4,128,128]{3,2,1,0:T(8,128)S(1)}, u32[]{:S(2)}, u32[]{:S(2)}) collective-permute-start(f32[2,4,128,128]{3,2,1,0:T(8,128)S(1)} %get-tuple-element.300), channel_id=1, source_target_pairs={{0,16},{1,17},{2,18},{3,19},{4,20},{5,21},{6,22},{7,23},{8,24},{9,... | collective-permute-start | bytes 1572872 | tf_op jit(solution)/shard_map/ppermute | solution.py:49
  195.9 16.5 %collective-permute-start.84 = (f32[1,4,128,128]{3,2,1,0:T(8,128)S(1)}, f32[1,4,128,128]{3,2,1,0:T(8,128)S(1)}, u32[]{:S(2)}, u32[]{:S(2)}) collective-permute-start(f32[1,4,128,128]{3,2,1,0:T(8,128)S(1)} %get-tuple-element.330), channel_id=1, source_target_pairs={{0,16},{1,17},{2,18},{3,19},{4,20},{5,21},{6,22},{7,23},{8,24},{9,... | collective-permute-start | bytes 786440 | tf_op jit(solution)/shard_map/ppermute | solution.py:49
  197.5 14.9 %collective-permute-start.85 = (f32[1,4,128,128]{3,2,1,0:T(8,128)S(1)}, f32[1,4,128,128]{3,2,1,0:T(8,128)S(1)}, u32[]{:S(2)}, u32[]{:S(2)}) collective-permute-start(f32[1,4,128,128]{3,2,1,0:T(8,128)S(1)} %get-tuple-element.331), channel_id=1, source_target_pairs={{0,8},{1,9},{2,10},{3,11},{4,12},{5,13},{6,14},{7,15},{8,0},{9,1},... | collective-permute-start | bytes 786440 | tf_op jit(solution)/shard_map/ppermute | solution.py:49
  210.5 8.3 %collective-permute-start.89 = (f32[192,512]{1,0:T(8,128)S(1)}, f32[192,512]{1,0:T(8,128)S(1)}, u32[]{:S(2)}, u32[]{:S(2)}) collective-permute-start(f32[192,512]{1,0:T(8,128)S(1)} %get-tuple-element.335.keep_ref), channel_id=1, source_target_pairs={{0,4},{1,5},{2,6},{3,7},{4,0},{5,1},{6,2},{7,3},{8,12},{9,13},{10,... | collective-permute-start | bytes 1179656 | tf_op jit(solution)/shard_map/ppermute | solution.py:49
  211.0 15.3 %collective-permute-start.90 = (f32[2,9,64,128]{3,2,1,0:T(8,128)S(1)}, f32[2,9,64,128]{3,2,1,0:T(8,128)S(1)}, u32[]{:S(2)}, u32[]{:S(2)}) collective-permute-start(f32[2,9,64,128]{3,2,1,0:T(8,128)S(1)} %get-tuple-element.339), channel_id=1, source_target_pairs={{0,1},{1,0},{2,3},{3,2},{4,5},{5,4},{6,7},{7,6},{8,9},{9,8},{10,11... | collective-permute-start | bytes 1769480 | tf_op jit(solution)/shard_map/ppermute | solution.py:49
  238.0 23.4 %collective-permute-start.101 = (f32[192,1024]{1,0:T(8,128)S(1)}, f32[192,1024]{1,0:T(8,128)S(1)}, u32[]{:S(2)}, u32[]{:S(2)}) collective-permute-start(f32[192,1024]{1,0:T(8,128)S(1)} %get-tuple-element.357), channel_id=1, source_target_pairs={{0,4},{1,5},{2,6},{3,7},{4,0},{5,1},{6,2},{7,3},{8,12},{9,13},{10,... | collective-permute-start | bytes 2359304 | tf_op jit(solution)/shard_map/ppermute | solution.py:49
  238.1 14.3 %collective-permute-start.95 = (f32[2,4,128,128]{3,2,1,0:T(8,128)S(1)}, f32[2,4,128,128]{3,2,1,0:T(8,128)S(1)}, u32[]{:S(2)}, u32[]{:S(2)}) collective-permute-start(f32[2,4,128,128]{3,2,1,0:T(8,128)S(1)} %get-tuple-element.352), channel_id=1, source_target_pairs={{0,8},{1,9},{2,10},{3,11},{4,12},{5,13},{6,14},{7,15},{8,0},{9,1},... | collective-permute-start | bytes 1572872 | tf_op jit(solution)/shard_map/ppermute | solution.py:49
  239.2 14.0 %collective-permute-start.96 = (f32[2,4,128,128]{3,2,1,0:T(8,128)S(1)}, f32[2,4,128,128]{3,2,1,0:T(8,128)S(1)}, u32[]{:S(2)}, u32[]{:S(2)}) collective-permute-start(f32[2,4,128,128]{3,2,1,0:T(8,128)S(1)} %get-tuple-element.353), channel_id=1, source_target_pairs={{0,16},{1,17},{2,18},{3,19},{4,20},{5,21},{6,22},{7,23},{8,24},{9,... | collective-permute-start | bytes 1572872 | tf_op jit(solution)/shard_map/ppermute | solution.py:49
  239.6 21.9 %collective-permute-start.100 = (f32[192,512]{1,0:T(8,128)S(1)}, f32[192,512]{1,0:T(8,128)S(1)}, u32[]{:S(2)}, u32[]{:S(2)}) collective-permute-start(f32[192,512]{1,0:T(8,128)S(1)} %copy-done.7), channel_id=1, source_target_pairs={{0,4},{1,5},{2,6},{3,7},{4,0},{5,1},{6,2},{7,3},{8,12},{9,13},{10,... | collective-permute-start | bytes 1179656 | tf_op jit(solution)/shard_map/ppermute | solution.py:49
  241.3 23.9 %collective-permute-start.103 = (f32[1,9,64,128]{3,2,1,0:T(8,128)S(1)}, f32[1,9,64,128]{3,2,1,0:T(8,128)S(1)}, u32[]{:S(2)}, u32[]{:S(2)}) collective-permute-start(f32[1,9,64,128]{3,2,1,0:T(8,128)S(1)} %slice_add_fusion.1), channel_id=1, source_target_pairs={{0,2},{1,3},{2,0},{3,1},{4,6},{5,7},{6,4},{7,5},{8,10},{9,11},{10,... | collective-permute-start | bytes 884744 | tf_op jit(solution)/shard_map/ppermute | solution.py:49
  262.8 15.5 %collective-permute-start.108 = (f32[2,4,128,128]{3,2,1,0:T(8,128)S(1)}, f32[2,4,128,128]{3,2,1,0:T(8,128)S(1)}, u32[]{:S(2)}, u32[]{:S(2)}) collective-permute-start(f32[2,4,128,128]{3,2,1,0:T(8,128)S(1)} %get-tuple-element.371), channel_id=1, source_target_pairs={{0,8},{1,9},{2,10},{3,11},{4,12},{5,13},{6,14},{7,15},{8,0},{9,1},... | collective-permute-start | bytes 1572872 | tf_op jit(solution)/shard_map/ppermute | solution.py:49
  263.9 14.4 %collective-permute-start.109 = (f32[2,4,128,128]{3,2,1,0:T(8,128)S(1)}, f32[2,4,128,128]{3,2,1,0:T(8,128)S(1)}, u32[]{:S(2)}, u32[]{:S(2)}) collective-permute-start(f32[2,4,128,128]{3,2,1,0:T(8,128)S(1)} %get-tuple-element.372), channel_id=1, source_target_pairs={{0,16},{1,17},{2,18},{3,19},{4,20},{5,21},{6,22},{7,23},{8,24},{9,... | collective-permute-start | bytes 1572872 | tf_op jit(solution)/shard_map/ppermute | solution.py:49
  281.9 8.5 %collective-permute-start.113 = (f32[1,256,128]{2,1,0:T(8,128)S(1)}, f32[1,256,128]{2,1,0:T(8,128)S(1)}, u32[]{:S(2)}, u32[]{:S(2)}) collective-permute-start(f32[1,256,128]{2,1,0:T(8,128)S(1)} %fusion.14), channel_id=1, source_target_pairs={{0,2},{1,3},{2,0},{3,1},{4,6},{5,7},{6,4},{7,5},{8,10},{9,11},{10,... | collective-permute-start | bytes 393224 | tf_op jit(solution)/shard_map/ppermute | solution.py:49
  291.8 7.2 %collective-permute-start.119 = (f32[2,8,128]{2,1,0:T(8,128)S(1)}, f32[2,8,128]{2,1,0:T(8,128)S(1)}, u32[]{:S(2)}, u32[]{:S(2)}) collective-permute-start(f32[2,8,128]{2,1,0:T(8,128)S(1)} %add_add_fusion.8.refs_0_), channel_id=1, source_target_pairs={{0,3},{1,2},{2,1},{3,0},{4,7},{5,6},{6,5},{7,4},{8,11},{9,10},{10,... | collective-permute-start | bytes 24584 | tf_op jit(solution)/shard_map/ppermute | solution.py:49
  299.1 14.9 %collective-permute-start.127 = (f32[2,9,64,128]{3,2,1,0:T(8,128)S(1)}, f32[2,9,64,128]{3,2,1,0:T(8,128)S(1)}, u32[]{:S(2)}, u32[]{:S(2)}) collective-permute-start(f32[2,9,64,128]{3,2,1,0:T(8,128)S(1)} %get-tuple-element.414), channel_id=1, source_target_pairs={{0,1},{1,0},{2,3},{3,2},{4,5},{5,4},{6,7},{7,6},{8,9},{9,8},{10,11... | collective-permute-start | bytes 1769480 | tf_op jit(solution)/shard_map/ppermute | solution.py:49
  300.0 12.6 %collective-permute-start.125 = (f32[1,4,128,128]{3,2,1,0:T(8,128)S(1)}, f32[1,4,128,128]{3,2,1,0:T(8,128)S(1)}, u32[]{:S(2)}, u32[]{:S(2)}) collective-permute-start(f32[1,4,128,128]{3,2,1,0:T(8,128)S(1)} %get-tuple-element.412), channel_id=1, source_target_pairs={{0,16},{1,17},{2,18},{3,19},{4,20},{5,21},{6,22},{7,23},{8,24},{9,... | collective-permute-start | bytes 786440 | tf_op jit(solution)/shard_map/ppermute | solution.py:49
  301.4 11.2 %collective-permute-start.126 = (f32[1,4,128,128]{3,2,1,0:T(8,128)S(1)}, f32[1,4,128,128]{3,2,1,0:T(8,128)S(1)}, u32[]{:S(2)}, u32[]{:S(2)}) collective-permute-start(f32[1,4,128,128]{3,2,1,0:T(8,128)S(1)} %get-tuple-element.413), channel_id=1, source_target_pairs={{0,8},{1,9},{2,10},{3,11},{4,12},{5,13},{6,14},{7,15},{8,0},{9,1},... | collective-permute-start | bytes 786440 | tf_op jit(solution)/shard_map/ppermute | solution.py:49
  310.8 15.2 %collective-permute-start.122 = (f32[2,4,128,128]{3,2,1,0:T(8,128)S(1)}, f32[2,4,128,128]{3,2,1,0:T(8,128)S(1)}, u32[]{:S(2)}, u32[]{:S(2)}) collective-permute-start(f32[2,4,128,128]{3,2,1,0:T(8,128)S(1)} %get-tuple-element.405), channel_id=1, source_target_pairs={{0,8},{1,9},{2,10},{3,11},{4,12},{5,13},{6,14},{7,15},{8,0},{9,1},... | collective-permute-start | bytes 1572872 | tf_op jit(solution)/shard_map/ppermute | solution.py:49
  311.9 14.2 %collective-permute-start.123 = (f32[2,4,128,128]{3,2,1,0:T(8,128)S(1)}, f32[2,4,128,128]{3,2,1,0:T(8,128)S(1)}, u32[]{:S(2)}, u32[]{:S(2)}) collective-permute-start(f32[2,4,128,128]{3,2,1,0:T(8,128)S(1)} %get-tuple-element.406), channel_id=1, source_target_pairs={{0,16},{1,17},{2,18},{3,19},{4,20},{5,21},{6,22},{7,23},{8,24},{9,... | collective-permute-start | bytes 1572872 | tf_op jit(solution)/shard_map/ppermute | solution.py:49
  314.1 11.8 %collective-permute-start.143 = (f32[2,256,128]{2,1,0:T(8,128)S(1)}, f32[2,256,128]{2,1,0:T(8,128)S(1)}, u32[]{:S(2)}, u32[]{:S(2)}) collective-permute-start(f32[2,256,128]{2,1,0:T(8,128)S(1)} %pad_maximum_fusion.9), channel_id=1, source_target_pairs={{0,1},{1,0},{2,3},{3,2},{4,5},{5,4},{6,7},{7,6},{8,9},{9,8},{10,11... | collective-permute-start | bytes 786440 | tf_op jit(solution)/shard_map/ppermute | solution.py:49
  314.9 27.1 %collective-permute-start.135 = (f32[1,9,64,128]{3,2,1,0:T(8,128)S(1)}, f32[1,9,64,128]{3,2,1,0:T(8,128)S(1)}, u32[]{:S(2)}, u32[]{:S(2)}) collective-permute-start(f32[1,9,64,128]{3,2,1,0:T(8,128)S(1)} %slice_add_fusion), channel_id=1, source_target_pairs={{0,2},{1,3},{2,0},{3,1},{4,6},{5,7},{6,4},{7,5},{8,10},{9,11},{10,... | collective-permute-start | bytes 884744 | tf_op jit(solution)/shard_map/ppermute | solution.py:49
  325.9 16.1 %collective-permute-start.144 = (f32[1,256,128]{2,1,0:T(8,128)S(1)}, f32[1,256,128]{2,1,0:T(8,128)S(1)}, u32[]{:S(2)}, u32[]{:S(2)}) collective-permute-start(f32[1,256,128]{2,1,0:T(8,128)S(1)} %slice_add_fusion.18), channel_id=1, source_target_pairs={{0,2},{1,3},{2,0},{3,1},{4,6},{5,7},{6,4},{7,5},{8,10},{9,11},{10,... | collective-permute-start | bytes 393224 | tf_op jit(solution)/shard_map/ppermute | solution.py:49
  327.5 9.3 %collective-permute-start.129 = (f32[1,4,128,128]{3,2,1,0:T(8,128)S(1)}, f32[1,4,128,128]{3,2,1,0:T(8,128)S(1)}, u32[]{:S(2)}, u32[]{:S(2)}) collective-permute-start(f32[1,4,128,128]{3,2,1,0:T(8,128)S(1)} %get-tuple-element.426), channel_id=1, source_target_pairs={{0,8},{1,9},{2,10},{3,11},{4,12},{5,13},{6,14},{7,15},{8,0},{9,1},... | collective-permute-start | bytes 786440 | tf_op jit(solution)/shard_map/ppermute | solution.py:49
  328.6 11.1 %collective-permute-start.132 = (f32[1,4,128,128]{3,2,1,0:T(8,128)S(1)}, f32[1,4,128,128]{3,2,1,0:T(8,128)S(1)}, u32[]{:S(2)}, u32[]{:S(2)}) collective-permute-start(f32[1,4,128,128]{3,2,1,0:T(8,128)S(1)} %get-tuple-element.502), channel_id=1, source_target_pairs={{0,8},{1,9},{2,10},{3,11},{4,12},{5,13},{6,14},{7,15},{8,0},{9,1},... | collective-permute-start | bytes 786440 | tf_op jit(solution)/shard_map/ppermute | solution.py:49
  336.9 9.9 %collective-permute-start.130 = (f32[2,256,128]{2,1,0:T(8,128)S(1)}, f32[2,256,128]{2,1,0:T(8,128)S(1)}, u32[]{:S(2)}, u32[]{:S(2)}) collective-permute-start(f32[2,256,128]{2,1,0:T(8,128)S(1)} %pad_maximum_fusion.7), channel_id=1, source_target_pairs={{0,1},{1,0},{2,3},{3,2},{4,5},{5,4},{6,7},{7,6},{8,9},{9,8},{10,11... | collective-permute-start | bytes 786440 | tf_op jit(solution)/shard_map/ppermute | solution.py:49
  339.8 11.4 %collective-permute-start.133 = (f32[2,256,128]{2,1,0:T(8,128)S(1)}, f32[2,256,128]{2,1,0:T(8,128)S(1)}, u32[]{:S(2)}, u32[]{:S(2)}) collective-permute-start(f32[2,256,128]{2,1,0:T(8,128)S(1)} %pad_maximum_fusion.8), channel_id=1, source_target_pairs={{0,1},{1,0},{2,3},{3,2},{4,5},{5,4},{6,7},{7,6},{8,9},{9,8},{10,11... | collective-permute-start | bytes 786440 | tf_op jit(solution)/shard_map/ppermute | solution.py:49
  342.1 17.7 %collective-permute-start.145 = (f32[1088,128]{1,0:T(8,128)S(1)}, f32[1088,128]{1,0:T(8,128)}, u32[]{:S(2)}, u32[]{:S(2)}) collective-permute-start(f32[1088,128]{1,0:T(8,128)S(1)} %pad_maximum_fusion.1.refs_8_), channel_id=1, source_target_pairs={{0,8},{1,9},{2,10},{3,11},{4,12},{5,13},{6,14},{7,15},{8,0},{9,1},... | collective-permute-start | bytes 1671176 | tf_op jit(solution)/shard_map/ppermute | solution.py:49
  343.2 19.2 %collective-permute-start.146 = (f32[1088,128]{1,0:T(8,128)S(1)}, f32[1088,128]{1,0:T(8,128)S(1)}, u32[]{:S(2)}, u32[]{:S(2)}) collective-permute-start(f32[1088,128]{1,0:T(8,128)S(1)} %pad_maximum_fusion.1.refs_8_), channel_id=1, source_target_pairs={{0,16},{1,17},{2,18},{3,19},{4,20},{5,21},{6,22},{7,23},{8,24},{9,... | collective-permute-start | bytes 1671176 | tf_op jit(solution)/shard_map/ppermute | solution.py:49
  344.1 26.1 %collective-permute-start.147 = (f32[1088,128]{1,0:T(8,128)S(1)}, f32[1088,128]{1,0:T(8,128)}, u32[]{:S(2)}, u32[]{:S(2)}) collective-permute-start(f32[1088,128]{1,0:T(8,128)S(1)} %pad_maximum_fusion.1.refs_8_), channel_id=1, source_target_pairs={{0,24},{1,25},{2,26},{3,27},{4,28},{5,29},{6,30},{7,31},{8,16},{9,... | collective-permute-start | bytes 1671176 | tf_op jit(solution)/shard_map/ppermute | solution.py:49
  346.8 7.9 %collective-permute-start.131 = (f32[1,256,128]{2,1,0:T(8,128)S(1)}, f32[1,256,128]{2,1,0:T(8,128)S(1)}, u32[]{:S(2)}, u32[]{:S(2)}) collective-permute-start(f32[1,256,128]{2,1,0:T(8,128)S(1)} %slice_add_fusion.28), channel_id=1, source_target_pairs={{0,2},{1,3},{2,0},{3,1},{4,6},{5,7},{6,4},{7,5},{8,10},{9,11},{10,... | collective-permute-start | bytes 393224 | tf_op jit(solution)/shard_map/ppermute | solution.py:49
  351.2 7.3 %collective-permute-start.134 = (f32[1,256,128]{2,1,0:T(8,128)S(1)}, f32[1,256,128]{2,1,0:T(8,128)S(1)}, u32[]{:S(2)}, u32[]{:S(2)}) collective-permute-start(f32[1,256,128]{2,1,0:T(8,128)S(1)} %slice_add_fusion.23), channel_id=1, source_target_pairs={{0,2},{1,3},{2,0},{3,1},{4,6},{5,7},{6,4},{7,5},{8,10},{9,11},{10,... | collective-permute-start | bytes 393224 | tf_op jit(solution)/shard_map/ppermute | solution.py:49
  358.6 23.1 %collective-permute-start.136 = (f32[1088,128]{1,0:T(8,128)S(1)}, f32[1088,128]{1,0:T(8,128)}, u32[]{:S(2)}, u32[]{:S(2)}) collective-permute-start(f32[1088,128]{1,0:T(8,128)S(1)} %pad_maximum_fusion.refs_0_), channel_id=1, source_target_pairs={{0,8},{1,9},{2,10},{3,11},{4,12},{5,13},{6,14},{7,15},{8,0},{9,1},... | collective-permute-start | bytes 1671176 | tf_op jit(solution)/shard_map/ppermute | solution.py:49
  359.8 29.4 %collective-permute-start.148 = (f32[1088,128]{1,0:T(8,128)S(1)}, f32[1088,128]{1,0:T(8,128)}, u32[]{:S(2)}, u32[]{:S(2)}) collective-permute-start(f32[1088,128]{1,0:T(8,128)S(1)} %pad_maximum_fusion.1.refs_8_), channel_id=1, source_target_pairs={{0,4},{1,5},{2,6},{3,7},{4,0},{5,1},{6,2},{7,3},{8,12},{9,13},{10,... | collective-permute-start | bytes 1671176 | tf_op jit(solution)/shard_map/ppermute | solution.py:49
  359.8 29.9 %collective-permute-start.139 = (f32[1088,128]{1,0:T(8,128)S(1)}, f32[1088,128]{1,0:T(8,128)}, u32[]{:S(2)}, u32[]{:S(2)}) collective-permute-start(f32[1088,128]{1,0:T(8,128)S(1)} %pad_maximum_fusion.refs_0_), channel_id=1, source_target_pairs={{0,4},{1,5},{2,6},{3,7},{4,0},{5,1},{6,2},{7,3},{8,12},{9,13},{10,... | collective-permute-start | bytes 1671176 | tf_op jit(solution)/shard_map/ppermute | solution.py:49
  362.4 27.4 %collective-permute-start.138 = (f32[1088,128]{1,0:T(8,128)S(1)}, f32[1088,128]{1,0:T(8,128)}, u32[]{:S(2)}, u32[]{:S(2)}) collective-permute-start(f32[1088,128]{1,0:T(8,128)S(1)} %pad_maximum_fusion.refs_0_), channel_id=1, source_target_pairs={{0,24},{1,25},{2,26},{3,27},{4,28},{5,29},{6,30},{7,31},{8,16},{9,... | collective-permute-start | bytes 1671176 | tf_op jit(solution)/shard_map/ppermute | solution.py:49
  370.2 21.4 %collective-permute-start.137 = (f32[1088,128]{1,0:T(8,128)S(1)}, f32[1088,128]{1,0:T(8,128)}, u32[]{:S(2)}, u32[]{:S(2)}) collective-permute-start(f32[1088,128]{1,0:T(8,128)S(1)} %pad_maximum_fusion.refs_0_), channel_id=1, source_target_pairs={{0,16},{1,17},{2,18},{3,19},{4,20},{5,21},{6,22},{7,23},{8,24},{9,... | collective-permute-start | bytes 1671176 | tf_op jit(solution)/shard_map/ppermute | solution.py:49
  381.7 9.8 %collective-permute-start.149 = (f32[1088,128]{1,0:T(8,128)}, f32[1088,128]{1,0:T(8,128)}, u32[]{:S(2)}, u32[]{:S(2)}) collective-permute-start(f32[1088,128]{1,0:T(8,128)} %collective-permute-done.145.refs_9_), channel_id=1, source_target_pairs={{0,4},{1,5},{2,6},{3,7},{4,0},{5,1},{6,2},{7,3},{8,12},{9,13},{10,... | collective-permute-start | bytes 1671176 | tf_op jit(solution)/shard_map/ppermute | solution.py:49
  (130 other events, 748.3 us)
